TPU v7x, 32 devices: a whole 2x2x4 slice. The times are simulated.
32 devices in a mesh: wshard: 4 (over y, x), ctx: 8 (over z, core).
Axes of the slice: x: 2, y: 2, z: 4, core: 2. Of those that a mesh axis runs over, the one named last changes fastest.
Arguments:
- tokens: bfloat16 [2, 4, 1024, 768], P(None, 'wshard', 'ctx'), may hold values from -6 to 6
- gain_one: bfloat16 [768], P('wshard'), may hold values from 0.099609375 to 1.8984375
- w_qkv: bfloat16 [768, 2304], P('wshard'), may hold values from -0.21875 to 0.21875
- w_out: bfloat16 [768, 768], P('wshard'), may hold values from -1.75 to 1.75
- gain_two: bfloat16 [768], P('wshard'), may hold values from 0.099609375 to 1.8984375
- w_up: bfloat16 [768, 3072], P('wshard'), may hold values from -0.21875 to 0.21875
- w_down: bfloat16 [3072, 768], P('wshard'), may hold values from -0.109375 to 0.109375
- cotangent: bfloat16 [2, 4, 1024, 768], P(None, 'wshard', 'ctx'), may hold values from -6 to 6
Outputs:
- result: bfloat16 [2, 4, 1024, 768], P(None, 'wshard', 'ctx')
- grad_tokens: float32 [2, 4, 1024, 768], P(None, 'wshard', 'ctx')
- grad_gain_one: float32 [768], P('wshard')
- grad_qkv: float32 [768, 2304], P('wshard')
- grad_out: float32 [768, 768], P('wshard')
- grad_gain_two: float32 [768], P('wshard')
- grad_up: float32 [768, 3072], P('wshard')
- grad_down: float32 [3072, 768], P('wshard')
All inputs are finite; a program needn't handle non-finite values.
Results may differ from a plain program's by a relative error of at most 0.02.
Values may be sent and summed in bfloat16 or wider, within the bound.
No kernel may reach another device: no remote copies, remote signals or barrier semaphores. Data moves between devices by JAX's collectives and lax.ppermute only.
A program may use at most 192 MiB of HBM per device.

v0:
```python
import jax
import jax.numpy as jnp
from jax import lax
from jax.sharding import PartitionSpec as P

D = 768
HEADS = 12
HEAD_DIM = 64


EPSILON = 1e-05


def passed_along(value, axis, by):
    count = lax.axis_size(axis)
    return lax.ppermute(value, axis, [(i, (i + by) % count) for i in range(count)])


def layer_norm(inputs, scaling):
    centred = inputs - jnp.mean(inputs, axis=-1, keepdims=True)
    variance = jnp.mean(centred * centred, axis=-1, keepdims=True)
    return centred * lax.rsqrt(variance + EPSILON) * scaling


def gelu_smooth(values_in):
    return jax.nn.gelu(values_in, approximate=True)


def contract_rows(left_side, right_side):
    return lax.dot_general(
        left_side, right_side, (((0,), (0,)), ((), ())), preferred_element_type=jnp.float32
    )


def times_rows(left_side, right_side):
    return lax.dot_general(
        left_side, right_side, (((1,), (1,)), ((), ())), preferred_element_type=jnp.float32
    )


def pair_grads(query_h, dout_h, log_total, row_delta, query_pos, key_h, value_h, key_pos):
    scaling = HEAD_DIM ** (-0.5)
    scores = (
        jnp.einsum("qhe,khe->hqk", query_h, key_h, preferred_element_type=jnp.float32) * scaling
    )
    visible = key_pos[None, None, :] <= query_pos[None, :, None]
    magnitude = jnp.sqrt(scores * scores + 1.0)
    tilted = scores / magnitude
    chance = jnp.exp(jnp.where(visible, magnitude - log_total[:, :, None], -1e30))
    signed = (tilted * chance).astype(jnp.bfloat16)
    d_signed = jnp.einsum("qhe,khe->hqk", dout_h, value_h, preferred_element_type=jnp.float32)
    slope = 1.0 / (magnitude * magnitude * magnitude) + tilted * tilted
    d_scores = (chance * (d_signed * slope - tilted * row_delta[:, :, None])).astype(jnp.bfloat16)
    d_query = (
        jnp.einsum("hqk,khe->qhe", d_scores, key_h, preferred_element_type=jnp.float32) * scaling
    )
    d_key = (
        jnp.einsum("hqk,qhe->khe", d_scores, query_h, preferred_element_type=jnp.float32) * scaling
    )
    d_value = jnp.einsum("hqk,qhe->khe", signed, dout_h, preferred_element_type=jnp.float32)
    return (d_query, d_key, d_value)


def keep_state(loop_state):
    return loop_state


def local(tokens, gain_one, w_qkv, w_out, gain_two, w_up, w_down, cotangent):
    gathered = (
        lax.all_gather(gain_one, "wshard", axis=0, tiled=True),
        lax.all_gather(w_qkv, "wshard", axis=0, tiled=True),
        lax.all_gather(w_out, "wshard", axis=0, tiled=True),
        lax.all_gather(gain_two, "wshard", axis=0, tiled=True),
        lax.all_gather(w_up, "wshard", axis=0, tiled=True),
        lax.all_gather(w_down, "wshard", axis=0, tiled=True),
    )
    full_gain_one, full_qkv, full_out, full_gain_two, full_up, full_down = gathered
    gain_first = full_gain_one.astype(jnp.float32)
    gain_second = full_gain_two.astype(jnp.float32)
    cycle_size = lax.axis_size("ctx")
    cycle_place = lax.axis_index("ctx")
    micro_count = tokens.shape[0]
    local_len = tokens.shape[2]
    scaling = HEAD_DIM ** (-0.5)
    query_pos = cycle_place * local_len + jnp.arange(local_len, dtype=jnp.int32)
    sum_gain_one = jnp.zeros((D,), jnp.float32)
    sum_gain_two = jnp.zeros((D,), jnp.float32)
    sum_qkv = jnp.zeros(full_qkv.shape, jnp.float32)
    sum_out = jnp.zeros(full_out.shape, jnp.float32)
    sum_up = jnp.zeros(full_up.shape, jnp.float32)
    sum_down = jnp.zeros(full_down.shape, jnp.float32)
    results = []
    grad_list = []
    for micro_index in range(micro_count):
        inputs = tokens[micro_index, 0].astype(jnp.float32)
        normed_f, norm_back = jax.vjp(layer_norm, inputs, gain_first)
        normed = normed_f.astype(jnp.bfloat16)
        mixed_all = jnp.dot(normed, full_qkv, preferred_element_type=jnp.float32).astype(
            jnp.bfloat16
        )
        keys_flat = mixed_all[:, D : 2 * D]
        values_flat = mixed_all[:, 2 * D :]
        query_h = mixed_all[:, :D].reshape(local_len, HEADS, HEAD_DIM)
        key_h = keys_flat.reshape(local_len, HEADS, HEAD_DIM)
        value_h = values_flat.reshape(local_len, HEADS, HEAD_DIM)
        start_state = (
            jnp.zeros((HEADS, local_len, HEAD_DIM), jnp.float32),
            jnp.ones((HEADS, local_len), jnp.float32),
            jnp.zeros((HEADS, local_len), jnp.float32),
        )
        shard_piece = (
            lax.all_gather(keys_flat, "ctx", axis=0, tiled=True),
            lax.all_gather(values_flat, "ctx", axis=0, tiled=True),
        )

        def compute(loop_state):
            accumulated, top_value, totals = loop_state
            key_piece = shard_piece[0].reshape(-1, HEADS, HEAD_DIM)
            value_piece = shard_piece[1].reshape(-1, HEADS, HEAD_DIM)
            key_pos = jnp.arange(key_piece.shape[0], dtype=jnp.int32)
            scores = (
                jnp.einsum("qhe,khe->hqk", query_h, key_piece, preferred_element_type=jnp.float32)
                * scaling
            )
            visible = key_pos[None, None, :] <= query_pos[None, :, None]
            magnitude = jnp.sqrt(scores * scores + 1.0)
            new_top = jnp.maximum(top_value, jnp.max(jnp.where(visible, magnitude, 0.0), axis=-1))
            weighted = jnp.exp(jnp.where(visible, magnitude - new_top[:, :, None], -1e30))
            signed = (scores / magnitude * weighted).astype(jnp.bfloat16)
            accumulated = jnp.einsum(
                "hqk,khe->hqe", signed, value_piece, preferred_element_type=jnp.float32
            )
            totals = jnp.sum(weighted, axis=-1)
            return (accumulated, new_top, totals)

        accumulated, top_value, totals = lax.cond(
            jnp.int32(0) <= query_pos[-1], compute, keep_state, start_state
        )
        attended_h = accumulated / totals[:, :, None]
        log_total = top_value + jnp.log(totals)
        attended = jnp.transpose(attended_h, (1, 0, 2)).reshape(local_len, D)
        attended_low = attended.astype(jnp.bfloat16)
        hidden = inputs + jnp.dot(attended_low, full_out, preferred_element_type=jnp.float32)
        normed_two_f, norm_two_back = jax.vjp(layer_norm, hidden, gain_second)
        normed_two = normed_two_f.astype(jnp.bfloat16)
        upward = jnp.dot(normed_two, full_up, preferred_element_type=jnp.float32)
        active_f, gelu_back = jax.vjp(gelu_smooth, upward)
        active = active_f.astype(jnp.bfloat16)
        result_rows = hidden + jnp.dot(active, full_down, preferred_element_type=jnp.float32)
        results.append(result_rows.astype(jnp.bfloat16))
        d_result = cotangent[micro_index, 0]
        sum_down = sum_down + contract_rows(active, d_result)
        d_active = times_rows(d_result, full_down)
        d_upward = gelu_back(d_active)[0].astype(jnp.bfloat16)
        sum_up = sum_up + contract_rows(normed_two, d_upward)
        d_normed_two = times_rows(d_upward, full_up)
        d_hidden_norm, d_gain_two = norm_two_back(d_normed_two)
        sum_gain_two = sum_gain_two + d_gain_two
        d_hidden = d_result.astype(jnp.float32) + d_hidden_norm
        d_branch = d_hidden.astype(jnp.bfloat16)
        sum_out = sum_out + contract_rows(attended_low, d_branch)
        d_attended = times_rows(d_branch, full_out).astype(jnp.bfloat16)
        dout_h = d_attended.reshape(local_len, HEADS, HEAD_DIM)
        row_delta = jnp.einsum("qhe,hqe->hq", dout_h.astype(jnp.float32), attended_h)
        zero_block = jnp.zeros((local_len, HEADS, HEAD_DIM), jnp.float32)

        def turn_keys(turn_index, loop_state):
            key_b, value_b, d_key_b, d_value_b, d_query = loop_state
            owner_index = (cycle_place + turn_index) % cycle_size
            key_pos = owner_index * local_len + jnp.arange(local_len, dtype=jnp.int32)

            def work(partial_sums):
                contrib = pair_grads(
                    query_h, dout_h, log_total, row_delta, query_pos, key_b, value_b, key_pos
                )
                return (
                    partial_sums[0] + contrib[0],
                    partial_sums[1] + contrib[1],
                    partial_sums[2] + contrib[2],
                )

            needed = (turn_index == 0) | (cycle_place + turn_index >= cycle_size)
            d_query, d_key_b, d_value_b = lax.cond(
                needed, work, keep_state, (d_query, d_key_b, d_value_b)
            )
            key_b, value_b = passed_along((key_b, value_b), "ctx", -1)
            d_key_b, d_value_b = (
                passed_along(d_key_b.astype(jnp.bfloat16), "ctx", -1).astype(d_key_b.dtype),
                passed_along(d_value_b.astype(jnp.bfloat16), "ctx", -1).astype(d_value_b.dtype),
            )
            return (key_b, value_b, d_key_b, d_value_b, d_query)

        final_state = lax.fori_loop(
            0, cycle_size, turn_keys, (key_h, value_h, zero_block, zero_block, zero_block)
        )
        d_key = final_state[2]
        d_value = final_state[3]
        d_query = final_state[4]
        d_mixed = jnp.concatenate(
            [
                d_query.reshape(local_len, D),
                d_key.reshape(local_len, D),
                d_value.reshape(local_len, D),
            ],
            axis=1,
        ).astype(jnp.bfloat16)
        sum_qkv = sum_qkv + contract_rows(normed, d_mixed)
        d_normed = times_rows(d_mixed, full_qkv)
        d_inputs_norm, d_gain_one = norm_back(d_normed)
        sum_gain_one = sum_gain_one + d_gain_one
        grad_list.append(d_hidden + d_inputs_norm)
    shares = (
        lax.psum_scatter(
            sum_gain_one.astype(jnp.bfloat16), "wshard", scatter_dimension=0, tiled=True
        ).astype(jnp.float32),
        lax.psum_scatter(
            sum_qkv.astype(jnp.bfloat16), "wshard", scatter_dimension=0, tiled=True
        ).astype(jnp.float32),
        lax.psum_scatter(
            sum_out.astype(jnp.bfloat16), "wshard", scatter_dimension=0, tiled=True
        ).astype(jnp.float32),
        lax.psum_scatter(
            sum_gain_two.astype(jnp.bfloat16), "wshard", scatter_dimension=0, tiled=True
        ).astype(jnp.float32),
        lax.psum_scatter(
            sum_up.astype(jnp.bfloat16), "wshard", scatter_dimension=0, tiled=True
        ).astype(jnp.float32),
        lax.psum_scatter(
            sum_down.astype(jnp.bfloat16), "wshard", scatter_dimension=0, tiled=True
        ).astype(jnp.float32),
    )
    summed = (
        lax.psum(shares[0].astype(jnp.bfloat16), "ctx").astype(jnp.float32),
        lax.psum(shares[1].astype(jnp.bfloat16), "ctx").astype(jnp.float32),
        lax.psum(shares[2].astype(jnp.bfloat16), "ctx").astype(jnp.float32),
        lax.psum(shares[3].astype(jnp.bfloat16), "ctx").astype(jnp.float32),
        lax.psum(shares[4].astype(jnp.bfloat16), "ctx").astype(jnp.float32),
        lax.psum(shares[5].astype(jnp.bfloat16), "ctx").astype(jnp.float32),
    )
    result_out = jnp.stack(results)[:, None]
    grad_out_tokens = jnp.stack(grad_list)[:, None]
    return (
        result_out,
        grad_out_tokens,
        summed[0],
        summed[1],
        summed[2],
        summed[3],
        summed[4],
        summed[5],
    )


def solution(mesh):
    placed = (
        P(None, "wshard", "ctx", None),
        P("wshard"),
        P("wshard", None),
        P("wshard", None),
        P("wshard"),
        P("wshard", None),
        P("wshard", None),
        P(None, "wshard", "ctx", None),
    )
    return jax.shard_map(
        local,
        mesh=mesh,
        in_specs=placed,
        out_specs=(
            P(None, "wshard", "ctx", None),
            P(None, "wshard", "ctx", None),
            P("wshard"),
            P("wshard", None),
            P("wshard", None),
            P("wshard"),
            P("wshard", None),
            P("wshard", None),
        ),
        check_vma=False,
    )
```

profile of v0, /device:TPU:0, one launch (start us, length us, event | category | flops | bytes accessed | tf_op | source)
XLA Modules:
  0.0 898.1 jit_solution(4168062707646784133)
XLA Ops:
  11.7 11.3 %all-reduce.7 = (bf16[768]{0:T(1024)(128)(2,1)S(1)}, bf16[768]{0:T(1024)(128)(2,1)S(1)}) all-reduce(bf16[768]{0:T(1024)(128)(2,1)S(1)} %dynamic-update-slice, bf16[768]{0:T(1024)(128)(2,1)S(1)} %dynamic-update-slice.1), channel_id=1, replica_groups=mesh['wshard'=4,'ctx'=8] {'wshard'}, use_global_device_ids=true, to_apply=%add | all-reduce | flops 1536 | bytes 6144
  24.5 35.4 %all-gather.9.cloned.1.call-done = bf16[768,2304]{1,0:T(8,128)(2,1)} async-done(((bf16[192,2304]{1,0:T(8,128)(2,1)}), bf16[768,2304]{1,0:T(8,128)(2,1)}) %all-gather.9.cloned.1.call-update) | async-done | bytes 3538960 | tf_op jit(solution)/shard_map/all_gather | solution.py:71
  75.4 13.2 %all-gather.21.cloned.1.call-done = bf16[1024,768]{1,0:T(8,128)(2,1)} async-done(((bf16[128,768]{1,0:T(8,128)(2,1)}), bf16[1024,768]{1,0:T(8,128)(2,1)}) %all-gather.21.cloned.1.call-update) | async-done | bytes 1572880 | tf_op jit(solution)/shard_map/all_gather | solution.py:112
  88.6 26.8 %all-gather.23.cloned.1.call-done = bf16[1024,768]{1,0:T(8,128)(2,1)} async-done(((bf16[128,768]{1,0:T(8,128)(2,1)}), bf16[1024,768]{1,0:T(8,128)(2,1)}) %all-gather.23.cloned.1.call-update) | async-done | bytes 1572880 | tf_op jit(solution)/shard_map/all_gather | solution.py:113
  115.4 23.0 %conditional.5 = (f32[12,128,64]{1,2,0:T(8,128)S(1)}, f32[12,128]{1,0:T(8,128)}, f32[12,128]{1,0:T(8,128)}, f32[12,128]{1,0:T(8,128)S(1)}) conditional(s32[]{:T(128)} %bitcast.13, () %tuple.114, (bf16[1024,768]{1,0:T(8,128)(2,1)}, bf16[128,12,64]{0,2,1:T(8,128)(2,1)S(1)}, s32[128]{0:T(128)}, bf16[1024,768]{1,0:T(8,128)(2,1)}) %tuple.260), branch_computations={%region_10.11_spmd, %region_11.14_spmd} | conditional | flops 432667136 | bytes 43109036 | solution.py:136
  120.1 5.9 select_reduce_fusion.1
  126.7 5.6 fusion.10
  132.2 5.5 fusion.9
  138.5 3.1 all-gather.11.cloned.1.call-done
  141.5 26.7 %all-gather.13.cloned.1.call-done = bf16[1024,768]{1,0:T(8,128)(2,1)} async-done(((bf16[128,768]{1,0:T(8,128)(2,1)}), bf16[1024,768]{1,0:T(8,128)(2,1)}) %all-gather.13.cloned.1.call-update) | async-done | bytes 1572880 | tf_op jit(solution)/shard_map/all_gather | solution.py:113
  168.2 24.5 %conditional.4 = (f32[12,128,64]{1,2,0:T(8,128)S(1)}, f32[12,128]{1,0:T(8,128)}, f32[12,128]{1,0:T(8,128)}, f32[12,128]{1,0:T(8,128)S(1)}) conditional(s32[]{:T(128)} %bitcast.13, () %tuple.112, (bf16[1024,768]{1,0:T(8,128)(2,1)}, bf16[128,12,64]{0,2,1:T(8,128)(2,1)S(1)}, s32[128]{0:T(128)}, bf16[1024,768]{1,0:T(8,128)(2,1)}) %tuple.261), branch_computations={%region_2.0_spmd, %region_3.6_spmd} | conditional | flops 432667136 | bytes 42582644 | solution.py:136
  174.2 5.9 select_reduce_fusion
  180.8 5.3 fusion.5
  186.0 5.5 fusion.4
  194.2 3.1 all-gather.15.cloned.1.call-done
  203.6 52.6 %all-gather.17.cloned.1.call-done = bf16[768,3072]{1,0:T(8,128)(2,1)} async-done(((bf16[192,3072]{1,0:T(8,128)(2,1)}), bf16[768,3072]{1,0:T(8,128)(2,1)}) %all-gather.17.cloned.1.call-update) | async-done | bytes 4718608 | tf_op jit(solution)/shard_map/all_gather | solution.py:74
  256.2 4.5 fusion.128
  262.6 52.5 %all-gather.19.cloned.1.call-done = bf16[3072,768]{1,0:T(8,128)(2,1)} async-done(((bf16[768,768]{1,0:T(8,128)(2,1)}), bf16[3072,768]{1,0:T(8,128)(2,1)}) %all-gather.19.cloned.1.call-update) | async-done | bytes 4718608 | tf_op jit(solution)/shard_map/all_gather | solution.py:75
  315.1 4.9 fusion.61
  320.0 4.3 fusion.136
  336.7 139.2 %while.49 = (s32[]{:T(128)}, bf16[128,12,64]{0,2,1:T(8,128)(2,1)S(1)}, bf16[128,12,64]{0,2,1:T(8,128)(2,1)S(1)}, f32[128,12,64]{0,2,1:T(8,128)S(1)}, f32[128,12,...) while((s32[]{:T(128)}, ...), condition=%wide.region_29.30_spmd.clone, body=%wide.region_26.29_spmd.clone.sunk | while | flops 131449096 | bytes 16021677 | solution.py:193
  337.1 4.0 conditional.11
  353.7 7.8 collective-permute-start.6
  361.7 3.0 collective-permute-done.6
  371.2 7.8 collective-permute-start.6
  379.2 3.0 collective-permute-done.6
  388.7 7.8 collective-permute-start.6
  396.7 3.0 collective-permute-done.6
  406.1 7.8 collective-permute-start.6
  414.2 3.0 collective-permute-done.6
  423.6 7.8 collective-permute-start.6
  431.6 3.0 collective-permute-done.6
  441.1 7.8 collective-permute-start.6
  449.1 3.0 collective-permute-done.6
  458.6 7.8 collective-permute-start.6
  466.6 3.0 collective-permute-done.6
  487.3 136.2 %while.48 = (s32[]{:T(128)}, bf16[128,12,64]{0,2,1:T(8,128)(2,1)S(1)}, bf16[128,12,64]{0,2,1:T(8,128)(2,1)S(1)}, f32[128,12,64]{0,2,1:T(8,128)S(1)}, f32[128,12,...) while((s32[]{:T(128)}, ...), condition=%wide.region_21.22_spmd.clone, body=%wide.region_18.21_spmd.clone.sunk | while | flops 131449096 | bytes 15235217 | solution.py:193
  487.5 3.6 conditional.10
  491.1 3.8 collective-permute-start.2
  495.1 3.0 collective-permute-done.2
  504.6 7.3 collective-permute-start.2
  512.1 3.0 collective-permute-done.2
  521.6 7.3 collective-permute-start.2
  529.2 3.0 collective-permute-done.2
  538.6 7.3 collective-permute-start.2
  546.2 3.0 collective-permute-done.2
  555.7 7.3 collective-permute-start.2
  563.2 3.0 collective-permute-done.2
  572.7 7.3 collective-permute-start.2
  580.3 3.0 collective-permute-done.2
  589.7 7.3 collective-permute-start.2
  606.8 7.3 collective-permute-start.2
  614.3 3.0 collective-permute-done.2
  625.6 3.1 add_convert_fusion.2
  631.3 3.7 add_convert_fusion.1
  638.6 4.0 add_convert_fusion
  643.3 3.9 fusion.92
  651.7 9.6 %all-reduce.6 = (bf16[768]{0:T(1024)(128)(2,1)}, bf16[768]{0:T(1024)(128)(2,1)S(1)}) all-reduce(bf16[768]{0:T(1024)(128)(2,1)} %add_convert_fusion.5, bf16[768]{0:T(1024)(128)(2,1)} %add_convert_fusion.4), channel_id=2, replica_groups=mesh['wshard'=4,'ctx'=8] {'wshard'}, use_global_device_ids=true, to_apply=%region_34.35.clone | all-reduce | flops 1536 | bytes 6144
  663.1 15.9 %all-reduce.4 = (bf16[192]{0:T(256)(128)(2,1)}, bf16[192]{0:T(256)(128)(2,1)S(1)}) all-reduce(bf16[192]{0:T(256)(128)(2,1)} %dynamic-slice.3, bf16[192]{0:T(256)(128)(2,1)} %dynamic-slice.5), channel_id=1, replica_groups=mesh['wshard'=4,'ctx'=8] {'ctx'}, use_global_device_ids=true, to_apply=%region_35.36 | all-reduce | flops 384 | bytes 1536 | tf_op jit(solution)/shard_map/psum | solution.py:233
  680.8 56.0 %reduce-scatter.9.cloned.1.call-done = bf16[192,3072]{1,0:T(8,128)(2,1)} async-done(((bf16[768,3072]{1,0:T(8,128)(2,1)}), bf16[192,3072]{1,0:T(8,128)(2,1)}) %reduce-scatter.9.cloned.1.call-update) | async-done | bytes 1179664 | tf_op jit(solution)/shard_map/reduce_scatter | solution.py:225
  736.8 60.0 %reduce-scatter.11.cloned.1.call-done = bf16[768,768]{1,0:T(8,128)(2,1)} async-done(((bf16[3072,768]{1,0:T(8,128)(2,1)}), bf16[768,768]{1,0:T(8,128)(2,1)}) %reduce-scatter.11.cloned.1.call-update) | async-done | bytes 1179664 | tf_op jit(solution)/shard_map/reduce_scatter | solution.py:228
  796.8 3.9 fusion.64
  800.8 3.5 fusion.65
  806.4 78.2 %all-reduce.10.cloned.1.call-done = (bf16[192,2304]{1,0:T(8,128)(2,1)}, bf16[192,768]{1,0:T(8,128)(2,1)}, bf16[192,3072]{1,0:T(8,128)(2,1)}, bf16[768,768]{1,0:T(8,128)(2,1)}) async-done(((bf16[192,2304]{1,0:T(8,128)(2,1)}, bf16[192,768]{1,0:T(8,128)(2,1)}, bf16[192,3072]{1,0:T(8,128)(2,1)}, bf16[768,768]{1,0:T(8,128)(2,1)}), (bf16[192,2304]{1,0:T(8,128)(2,1)}, bf16[192,768]{1,0:T(8,128)(2,1)}, ...) | async-done | bytes 3538960 | tf_op jit(solution)/shard_map/psum | solution.py:234
  (611 shorter events, 213.8 us)
Async XLA Ops:
  7.2 52.7 %all-gather.9.cloned.1.call-start = ((), (), s32[]{:S(2)}) async-start(), calls=%async_computation.4 | async-start | bytes 4423680 | tf_op jit(solution)/shard_map/all_gather | solution.py:71
  7.9 80.7 %all-gather.21.cloned.1.call-start = ((), (), s32[]{:S(2)}) async-start(), calls=%async_computation.10 | async-start | bytes 1769472 | tf_op jit(solution)/shard_map/all_gather | solution.py:112
  63.4 52.1 %all-gather.23.cloned.1.call-start = ((), (), s32[]{:S(2)}) async-start(), calls=%async_computation.11 | async-start | bytes 1769472 | tf_op jit(solution)/shard_map/all_gather | solution.py:113
  64.1 77.4 %all-gather.11.cloned.1.call-start = ((), (), s32[]{:S(2)}) async-start(), calls=%async_computation.5 | async-start | bytes 1769472 | tf_op jit(solution)/shard_map/all_gather | solution.py:112
  67.7 100.5 %all-gather.13.cloned.1.call-start = ((), (), s32[]{:S(2)}) async-start(), calls=%async_computation.6 | async-start | bytes 1769472 | tf_op jit(solution)/shard_map/all_gather | solution.py:113
  68.3 128.9 %all-gather.15.cloned.1.call-start = ((), (), s32[]{:S(2)}) async-start(), calls=%async_computation.7 | async-start | bytes 1474560 | tf_op jit(solution)/shard_map/all_gather | solution.py:72
  68.9 187.2 %all-gather.17.cloned.1.call-start = ((), (), s32[]{:S(2)}) async-start(), calls=%async_computation.8 | async-start | bytes 5898240 | tf_op jit(solution)/shard_map/all_gather | solution.py:74
  69.7 245.4 %all-gather.19.cloned.1.call-start = ((), (), s32[]{:S(2)}) async-start(), calls=%async_computation.9 | async-start | bytes 5898240 | tf_op jit(solution)/shard_map/all_gather | solution.py:75
  70.4 610.3 %reduce-scatter.7.cloned.1.call-start = ((), (), s32[]{:S(2)}) async-start(), calls=%async_computation.13 | async-start | bytes 1474560 | tf_op jit(solution)/shard_map/reduce_scatter | solution.py:219
  341.1 6.0 collective-permute-start.6
  344.0 5.3 collective-permute-start.7
  344.7 6.6 collective-permute-start.4
  344.8 8.7 collective-permute-start.5
  353.7 11.0 %collective-permute-start.6 = (bf16[128,12,64]{0,2,1:T(8,128)(2,1)S(1)}, bf16[128,12,64]{0,2,1:T(8,128)(2,1)S(1)}, u32[]{:S(2)}, u32[]{:S(2)}) collective-permute-start(bf16[128,12,64]{0,2,1:T(8,128)(2,1)S(1)} %convert_element_type.474), channel_id=1, source_target_pairs={{0,7},{1,0},{2,1},{3,2},{4,3},{5,4},{6,5},{7,6},{8,15},{9,8},{10,9... | collective-permute-start | bytes 589832 | tf_op jit(solution)/shard_map/while/body/eval_jaxpr/ppermute | solution.py:16
  361.5 7.3 collective-permute-start.4
  361.6 9.3 %collective-permute-start.5 = (bf16[128,12,64]{0,2,1:T(8,128)(2,1)S(1)}, bf16[128,12,64]{0,2,1:T(8,128)(2,1)S(1)}, u32[]{:S(2)}, u32[]{:S(2)}) collective-permute-start(bf16[128,12,64]{0,2,1:T(8,128)(2,1)S(1)} %copy.114), channel_id=1, source_target_pairs={{0,7},{1,0},{2,1},{3,2},{4,3},{5,4},{6,5},{7,6},{8,15},{9,8},{10,9... | collective-permute-start | bytes 589832 | tf_op jit(solution)/shard_map/while/body/eval_jaxpr/ppermute | solution.py:16
  371.2 11.0 %collective-permute-start.6 = (bf16[128,12,64]{0,2,1:T(8,128)(2,1)S(1)}, bf16[128,12,64]{0,2,1:T(8,128)(2,1)S(1)}, u32[]{:S(2)}, u32[]{:S(2)}) collective-permute-start(bf16[128,12,64]{0,2,1:T(8,128)(2,1)S(1)} %convert_element_type.474), channel_id=1, source_target_pairs={{0,7},{1,0},{2,1},{3,2},{4,3},{5,4},{6,5},{7,6},{8,15},{9,8},{10,9... | collective-permute-start | bytes 589832 | tf_op jit(solution)/shard_map/while/body/eval_jaxpr/ppermute | solution.py:16
  379.0 7.3 collective-permute-start.4
  379.1 9.3 %collective-permute-start.5 = (bf16[128,12,64]{0,2,1:T(8,128)(2,1)S(1)}, bf16[128,12,64]{0,2,1:T(8,128)(2,1)S(1)}, u32[]{:S(2)}, u32[]{:S(2)}) collective-permute-start(bf16[128,12,64]{0,2,1:T(8,128)(2,1)S(1)} %copy.114), channel_id=1, source_target_pairs={{0,7},{1,0},{2,1},{3,2},{4,3},{5,4},{6,5},{7,6},{8,15},{9,8},{10,9... | collective-permute-start | bytes 589832 | tf_op jit(solution)/shard_map/while/body/eval_jaxpr/ppermute | solution.py:16
  388.7 11.0 %collective-permute-start.6 = (bf16[128,12,64]{0,2,1:T(8,128)(2,1)S(1)}, bf16[128,12,64]{0,2,1:T(8,128)(2,1)S(1)}, u32[]{:S(2)}, u32[]{:S(2)}) collective-permute-start(bf16[128,12,64]{0,2,1:T(8,128)(2,1)S(1)} %convert_element_type.474), channel_id=1, source_target_pairs={{0,7},{1,0},{2,1},{3,2},{4,3},{5,4},{6,5},{7,6},{8,15},{9,8},{10,9... | collective-permute-start | bytes 589832 | tf_op jit(solution)/shard_map/while/body/eval_jaxpr/ppermute | solution.py:16
  396.5 5.3 collective-permute-start.7
  396.5 7.3 collective-permute-start.4
  396.6 9.3 %collective-permute-start.5 = (bf16[128,12,64]{0,2,1:T(8,128)(2,1)S(1)}, bf16[128,12,64]{0,2,1:T(8,128)(2,1)S(1)}, u32[]{:S(2)}, u32[]{:S(2)}) collective-permute-start(bf16[128,12,64]{0,2,1:T(8,128)(2,1)S(1)} %copy.114), channel_id=1, source_target_pairs={{0,7},{1,0},{2,1},{3,2},{4,3},{5,4},{6,5},{7,6},{8,15},{9,8},{10,9... | collective-permute-start | bytes 589832 | tf_op jit(solution)/shard_map/while/body/eval_jaxpr/ppermute | solution.py:16
  406.1 11.0 %collective-permute-start.6 = (bf16[128,12,64]{0,2,1:T(8,128)(2,1)S(1)}, bf16[128,12,64]{0,2,1:T(8,128)(2,1)S(1)}, u32[]{:S(2)}, u32[]{:S(2)}) collective-permute-start(bf16[128,12,64]{0,2,1:T(8,128)(2,1)S(1)} %convert_element_type.474), channel_id=1, source_target_pairs={{0,7},{1,0},{2,1},{3,2},{4,3},{5,4},{6,5},{7,6},{8,15},{9,8},{10,9... | collective-permute-start | bytes 589832 | tf_op jit(solution)/shard_map/while/body/eval_jaxpr/ppermute | solution.py:16
  413.9 5.3 collective-permute-start.7
  414.0 7.3 collective-permute-start.4
  414.1 9.3 %collective-permute-start.5 = (bf16[128,12,64]{0,2,1:T(8,128)(2,1)S(1)}, bf16[128,12,64]{0,2,1:T(8,128)(2,1)S(1)}, u32[]{:S(2)}, u32[]{:S(2)}) collective-permute-start(bf16[128,12,64]{0,2,1:T(8,128)(2,1)S(1)} %copy.114), channel_id=1, source_target_pairs={{0,7},{1,0},{2,1},{3,2},{4,3},{5,4},{6,5},{7,6},{8,15},{9,8},{10,9... | collective-permute-start | bytes 589832 | tf_op jit(solution)/shard_map/while/body/eval_jaxpr/ppermute | solution.py:16
  423.6 11.0 %collective-permute-start.6 = (bf16[128,12,64]{0,2,1:T(8,128)(2,1)S(1)}, bf16[128,12,64]{0,2,1:T(8,128)(2,1)S(1)}, u32[]{:S(2)}, u32[]{:S(2)}) collective-permute-start(bf16[128,12,64]{0,2,1:T(8,128)(2,1)S(1)} %convert_element_type.474), channel_id=1, source_target_pairs={{0,7},{1,0},{2,1},{3,2},{4,3},{5,4},{6,5},{7,6},{8,15},{9,8},{10,9... | collective-permute-start | bytes 589832 | tf_op jit(solution)/shard_map/while/body/eval_jaxpr/ppermute | solution.py:16
  431.5 7.3 collective-permute-start.4
  431.6 9.3 %collective-permute-start.5 = (bf16[128,12,64]{0,2,1:T(8,128)(2,1)S(1)}, bf16[128,12,64]{0,2,1:T(8,128)(2,1)S(1)}, u32[]{:S(2)}, u32[]{:S(2)}) collective-permute-start(bf16[128,12,64]{0,2,1:T(8,128)(2,1)S(1)} %copy.114), channel_id=1, source_target_pairs={{0,7},{1,0},{2,1},{3,2},{4,3},{5,4},{6,5},{7,6},{8,15},{9,8},{10,9... | collective-permute-start | bytes 589832 | tf_op jit(solution)/shard_map/while/body/eval_jaxpr/ppermute | solution.py:16
  441.1 11.0 %collective-permute-start.6 = (bf16[128,12,64]{0,2,1:T(8,128)(2,1)S(1)}, bf16[128,12,64]{0,2,1:T(8,128)(2,1)S(1)}, u32[]{:S(2)}, u32[]{:S(2)}) collective-permute-start(bf16[128,12,64]{0,2,1:T(8,128)(2,1)S(1)} %convert_element_type.474), channel_id=1, source_target_pairs={{0,7},{1,0},{2,1},{3,2},{4,3},{5,4},{6,5},{7,6},{8,15},{9,8},{10,9... | collective-permute-start | bytes 589832 | tf_op jit(solution)/shard_map/while/body/eval_jaxpr/ppermute | solution.py:16
  449.0 7.3 collective-permute-start.4
  449.1 9.3 %collective-permute-start.5 = (bf16[128,12,64]{0,2,1:T(8,128)(2,1)S(1)}, bf16[128,12,64]{0,2,1:T(8,128)(2,1)S(1)}, u32[]{:S(2)}, u32[]{:S(2)}) collective-permute-start(bf16[128,12,64]{0,2,1:T(8,128)(2,1)S(1)} %copy.114), channel_id=1, source_target_pairs={{0,7},{1,0},{2,1},{3,2},{4,3},{5,4},{6,5},{7,6},{8,15},{9,8},{10,9... | collective-permute-start | bytes 589832 | tf_op jit(solution)/shard_map/while/body/eval_jaxpr/ppermute | solution.py:16
  458.6 11.0 %collective-permute-start.6 = (bf16[128,12,64]{0,2,1:T(8,128)(2,1)S(1)}, bf16[128,12,64]{0,2,1:T(8,128)(2,1)S(1)}, u32[]{:S(2)}, u32[]{:S(2)}) collective-permute-start(bf16[128,12,64]{0,2,1:T(8,128)(2,1)S(1)} %convert_element_type.474), channel_id=1, source_target_pairs={{0,7},{1,0},{2,1},{3,2},{4,3},{5,4},{6,5},{7,6},{8,15},{9,8},{10,9... | collective-permute-start | bytes 589832 | tf_op jit(solution)/shard_map/while/body/eval_jaxpr/ppermute | solution.py:16
  466.5 7.3 collective-permute-start.4
  466.6 9.3 %collective-permute-start.5 = (bf16[128,12,64]{0,2,1:T(8,128)(2,1)S(1)}, bf16[128,12,64]{0,2,1:T(8,128)(2,1)S(1)}, u32[]{:S(2)}, u32[]{:S(2)}) collective-permute-start(bf16[128,12,64]{0,2,1:T(8,128)(2,1)S(1)} %copy.114), channel_id=1, source_target_pairs={{0,7},{1,0},{2,1},{3,2},{4,3},{5,4},{6,5},{7,6},{8,15},{9,8},{10,9... | collective-permute-start | bytes 589832 | tf_op jit(solution)/shard_map/while/body/eval_jaxpr/ppermute | solution.py:16
  485.8 195.0 %reduce-scatter.5.cloned.1.call-start = ((), (), s32[]{:S(2)}) async-start(), calls=%async_computation.12 | async-start | bytes 4423680 | tf_op jit(solution)/shard_map/reduce_scatter | solution.py:216
  491.1 6.9 collective-permute-start.2
  495.0 7.3 collective-permute-start
  495.0 9.3 %collective-permute-start.1 = (bf16[128,12,64]{0,2,1:T(8,128)(2,1)S(1)}, bf16[128,12,64]{0,2,1:T(8,128)(2,1)S(1)}, u32[]{:S(2)}, u32[]{:S(2)}) collective-permute-start(bf16[128,12,64]{0,2,1:T(8,128)(2,1)S(1)} %copy.132), channel_id=1, source_target_pairs={{0,7},{1,0},{2,1},{3,2},{4,3},{5,4},{6,5},{7,6},{8,15},{9,8},{10,9... | collective-permute-start | bytes 589832 | tf_op jit(solution)/shard_map/while/body/eval_jaxpr/ppermute | solution.py:16
  504.6 10.5 %collective-permute-start.2 = (bf16[128,12,64]{0,2,1:T(8,128)(2,1)S(1)}, bf16[128,12,64]{0,2,1:T(8,128)(2,1)S(1)}, u32[]{:S(2)}, u32[]{:S(2)}) collective-permute-start(bf16[128,12,64]{0,2,1:T(8,128)(2,1)S(1)} %convert_element_type.469), channel_id=1, source_target_pairs={{0,7},{1,0},{2,1},{3,2},{4,3},{5,4},{6,5},{7,6},{8,15},{9,8},{10,9... | collective-permute-start | bytes 589832 | tf_op jit(solution)/shard_map/while/body/eval_jaxpr/ppermute | solution.py:16
  512.0 7.3 collective-permute-start
  512.1 9.3 %collective-permute-start.1 = (bf16[128,12,64]{0,2,1:T(8,128)(2,1)S(1)}, bf16[128,12,64]{0,2,1:T(8,128)(2,1)S(1)}, u32[]{:S(2)}, u32[]{:S(2)}) collective-permute-start(bf16[128,12,64]{0,2,1:T(8,128)(2,1)S(1)} %copy.132), channel_id=1, source_target_pairs={{0,7},{1,0},{2,1},{3,2},{4,3},{5,4},{6,5},{7,6},{8,15},{9,8},{10,9... | collective-permute-start | bytes 589832 | tf_op jit(solution)/shard_map/while/body/eval_jaxpr/ppermute | solution.py:16
  521.6 10.5 %collective-permute-start.2 = (bf16[128,12,64]{0,2,1:T(8,128)(2,1)S(1)}, bf16[128,12,64]{0,2,1:T(8,128)(2,1)S(1)}, u32[]{:S(2)}, u32[]{:S(2)}) collective-permute-start(bf16[128,12,64]{0,2,1:T(8,128)(2,1)S(1)} %convert_element_type.469), channel_id=1, source_target_pairs={{0,7},{1,0},{2,1},{3,2},{4,3},{5,4},{6,5},{7,6},{8,15},{9,8},{10,9... | collective-permute-start | bytes 589832 | tf_op jit(solution)/shard_map/while/body/eval_jaxpr/ppermute | solution.py:16
  529.0 7.3 collective-permute-start
  529.1 9.3 %collective-permute-start.1 = (bf16[128,12,64]{0,2,1:T(8,128)(2,1)S(1)}, bf16[128,12,64]{0,2,1:T(8,128)(2,1)S(1)}, u32[]{:S(2)}, u32[]{:S(2)}) collective-permute-start(bf16[128,12,64]{0,2,1:T(8,128)(2,1)S(1)} %copy.132), channel_id=1, source_target_pairs={{0,7},{1,0},{2,1},{3,2},{4,3},{5,4},{6,5},{7,6},{8,15},{9,8},{10,9... | collective-permute-start | bytes 589832 | tf_op jit(solution)/shard_map/while/body/eval_jaxpr/ppermute | solution.py:16
  538.6 10.5 %collective-permute-start.2 = (bf16[128,12,64]{0,2,1:T(8,128)(2,1)S(1)}, bf16[128,12,64]{0,2,1:T(8,128)(2,1)S(1)}, u32[]{:S(2)}, u32[]{:S(2)}) collective-permute-start(bf16[128,12,64]{0,2,1:T(8,128)(2,1)S(1)} %convert_element_type.469), channel_id=1, source_target_pairs={{0,7},{1,0},{2,1},{3,2},{4,3},{5,4},{6,5},{7,6},{8,15},{9,8},{10,9... | collective-permute-start | bytes 589832 | tf_op jit(solution)/shard_map/while/body/eval_jaxpr/ppermute | solution.py:16
  546.1 7.3 collective-permute-start
  546.1 9.3 %collective-permute-start.1 = (bf16[128,12,64]{0,2,1:T(8,128)(2,1)S(1)}, bf16[128,12,64]{0,2,1:T(8,128)(2,1)S(1)}, u32[]{:S(2)}, u32[]{:S(2)}) collective-permute-start(bf16[128,12,64]{0,2,1:T(8,128)(2,1)S(1)} %copy.132), channel_id=1, source_target_pairs={{0,7},{1,0},{2,1},{3,2},{4,3},{5,4},{6,5},{7,6},{8,15},{9,8},{10,9... | collective-permute-start | bytes 589832 | tf_op jit(solution)/shard_map/while/body/eval_jaxpr/ppermute | solution.py:16
  555.7 10.5 %collective-permute-start.2 = (bf16[128,12,64]{0,2,1:T(8,128)(2,1)S(1)}, bf16[128,12,64]{0,2,1:T(8,128)(2,1)S(1)}, u32[]{:S(2)}, u32[]{:S(2)}) collective-permute-start(bf16[128,12,64]{0,2,1:T(8,128)(2,1)S(1)} %convert_element_type.469), channel_id=1, source_target_pairs={{0,7},{1,0},{2,1},{3,2},{4,3},{5,4},{6,5},{7,6},{8,15},{9,8},{10,9... | collective-permute-start | bytes 589832 | tf_op jit(solution)/shard_map/while/body/eval_jaxpr/ppermute | solution.py:16
  563.1 7.3 collective-permute-start
  563.2 9.3 %collective-permute-start.1 = (bf16[128,12,64]{0,2,1:T(8,128)(2,1)S(1)}, bf16[128,12,64]{0,2,1:T(8,128)(2,1)S(1)}, u32[]{:S(2)}, u32[]{:S(2)}) collective-permute-start(bf16[128,12,64]{0,2,1:T(8,128)(2,1)S(1)} %copy.132), channel_id=1, source_target_pairs={{0,7},{1,0},{2,1},{3,2},{4,3},{5,4},{6,5},{7,6},{8,15},{9,8},{10,9... | collective-permute-start | bytes 589832 | tf_op jit(solution)/shard_map/while/body/eval_jaxpr/ppermute | solution.py:16
  572.7 10.5 %collective-permute-start.2 = (bf16[128,12,64]{0,2,1:T(8,128)(2,1)S(1)}, bf16[128,12,64]{0,2,1:T(8,128)(2,1)S(1)}, u32[]{:S(2)}, u32[]{:S(2)}) collective-permute-start(bf16[128,12,64]{0,2,1:T(8,128)(2,1)S(1)} %convert_element_type.469), channel_id=1, source_target_pairs={{0,7},{1,0},{2,1},{3,2},{4,3},{5,4},{6,5},{7,6},{8,15},{9,8},{10,9... | collective-permute-start | bytes 589832 | tf_op jit(solution)/shard_map/while/body/eval_jaxpr/ppermute | solution.py:16
  580.1 7.3 collective-permute-start
  580.2 9.3 %collective-permute-start.1 = (bf16[128,12,64]{0,2,1:T(8,128)(2,1)S(1)}, bf16[128,12,64]{0,2,1:T(8,128)(2,1)S(1)}, u32[]{:S(2)}, u32[]{:S(2)}) collective-permute-start(bf16[128,12,64]{0,2,1:T(8,128)(2,1)S(1)} %copy.132), channel_id=1, source_target_pairs={{0,7},{1,0},{2,1},{3,2},{4,3},{5,4},{6,5},{7,6},{8,15},{9,8},{10,9... | collective-permute-start | bytes 589832 | tf_op jit(solution)/shard_map/while/body/eval_jaxpr/ppermute | solution.py:16
  589.7 10.5 %collective-permute-start.2 = (bf16[128,12,64]{0,2,1:T(8,128)(2,1)S(1)}, bf16[128,12,64]{0,2,1:T(8,128)(2,1)S(1)}, u32[]{:S(2)}, u32[]{:S(2)}) collective-permute-start(bf16[128,12,64]{0,2,1:T(8,128)(2,1)S(1)} %convert_element_type.469), channel_id=1, source_target_pairs={{0,7},{1,0},{2,1},{3,2},{4,3},{5,4},{6,5},{7,6},{8,15},{9,8},{10,9... | collective-permute-start | bytes 589832 | tf_op jit(solution)/shard_map/while/body/eval_jaxpr/ppermute | solution.py:16
  597.1 7.3 collective-permute-start
  597.2 9.3 %collective-permute-start.1 = (bf16[128,12,64]{0,2,1:T(8,128)(2,1)S(1)}, bf16[128,12,64]{0,2,1:T(8,128)(2,1)S(1)}, u32[]{:S(2)}, u32[]{:S(2)}) collective-permute-start(bf16[128,12,64]{0,2,1:T(8,128)(2,1)S(1)} %copy.132), channel_id=1, source_target_pairs={{0,7},{1,0},{2,1},{3,2},{4,3},{5,4},{6,5},{7,6},{8,15},{9,8},{10,9... | collective-permute-start | bytes 589832 | tf_op jit(solution)/shard_map/while/body/eval_jaxpr/ppermute | solution.py:16
  606.8 10.5 %collective-permute-start.2 = (bf16[128,12,64]{0,2,1:T(8,128)(2,1)S(1)}, bf16[128,12,64]{0,2,1:T(8,128)(2,1)S(1)}, u32[]{:S(2)}, u32[]{:S(2)}) collective-permute-start(bf16[128,12,64]{0,2,1:T(8,128)(2,1)S(1)} %convert_element_type.469), channel_id=1, source_target_pairs={{0,7},{1,0},{2,1},{3,2},{4,3},{5,4},{6,5},{7,6},{8,15},{9,8},{10,9... | collective-permute-start | bytes 589832 | tf_op jit(solution)/shard_map/while/body/eval_jaxpr/ppermute | solution.py:16
  614.2 7.3 collective-permute-start
  614.2 9.3 %collective-permute-start.1 = (bf16[128,12,64]{0,2,1:T(8,128)(2,1)S(1)}, bf16[128,12,64]{0,2,1:T(8,128)(2,1)S(1)}, u32[]{:S(2)}, u32[]{:S(2)}) collective-permute-start(bf16[128,12,64]{0,2,1:T(8,128)(2,1)S(1)} %copy.132), channel_id=1, source_target_pairs={{0,7},{1,0},{2,1},{3,2},{4,3},{5,4},{6,5},{7,6},{8,15},{9,8},{10,9... | collective-permute-start | bytes 589832 | tf_op jit(solution)/shard_map/while/body/eval_jaxpr/ppermute | solution.py:16
  628.7 108.0 %reduce-scatter.9.cloned.1.call-start = ((), (), s32[]{:S(2)}) async-start(), calls=%async_computation.14 | async-start | bytes 5898240 | tf_op jit(solution)/shard_map/reduce_scatter | solution.py:225
  635.1 161.6 %reduce-scatter.11.cloned.1.call-start = ((), (), s32[]{:S(2)}) async-start(), calls=%async_computation.15 | async-start | bytes 5898240 | tf_op jit(solution)/shard_map/reduce_scatter | solution.py:228
  642.6 242.1 %all-reduce.10.cloned.1.call-start = ((), (), s32[]{:S(2)}) async-start(), calls=%async_computation.16 | async-start | bytes 7077888 | tf_op jit(solution)/shard_map/psum | solution.py:234
  (128 other events, 775.2 us)
Sparse Core Ops, SparseCore 0:
  9.9 49.9 all-gather.8
  63.5 25.0 all-gather.20
  90.8 24.5 all-gather.22
  116.9 24.5 all-gather.10
  143.6 24.5 all-gather.12
  169.9 27.2 all-gather.14
  199.0 57.0 all-gather.16
  258.0 57.0 all-gather.18
  485.9 28.9 reduce-scatter.6
  628.8 47.7 reduce-scatter.4
  679.6 57.0 reduce-scatter.8
  739.6 57.0 reduce-scatter.10
  799.4 85.2 all-reduce.9
where the time goes:
time: 904 us; the launch traced here: 898 us
  waiting for transfers between devices  557 us (62%)
  starting transfers between devices  117 us (13%)
  matrix products  90.3 us (10%)
  other arithmetic  44.4 us (5%)
  blocking collectives  36.8 us (4%)
  local copies, waits for them, and re-layouts  31.8 us (4%)
  between operations  17.5 us (2%)
    ppermute x64, waiting for transfers between devices, passed_along(): lax.ppermute(value, axis, [(i, (i + by) % count) for i in range(count)])  146 us
    ppermute x64, starting transfers between devices, passed_along(): lax.ppermute(value, axis, [(i, (i + by) % count) for i in range(count)])  117 us
    psum x1, waiting for transfers between devices, local(): lax.psum(shares[1].astype(jnp.bfloat16), 'ctx').astype(jnp.float32)  78.2 us
    reduce_scatter x1, waiting for transfers between devices, local(): lax.psum_scatter(sum_down.astype(jnp.bfloat16), 'wshard', scatter_dimensi...  60 us
    reduce_scatter x1, waiting for transfers between devices, local(): lax.psum_scatter(sum_up.astype(jnp.bfloat16), 'wshard', scatter_dimension...  56 us
    all_gather x2, waiting for transfers between devices, local(): lax.all_gather(values_flat, 'ctx', axis=0, tiled=True)  53.5 us
    all_gather x1, waiting for transfers between devices, local(): lax.all_gather(w_up, 'wshard', axis=0, tiled=True)  52.6 us
    all_gather x1, waiting for transfers between devices, local(): lax.all_gather(w_down, 'wshard', axis=0, tiled=True)  52.5 us
  transfers between devices with their start and end apart: 77, of which 75 were waited for; matrix products, arithmetic and copies ran while one was open for 13% of the time, Pallas kernels for 0%

commit v1 on v0

--- a/solution.py
+++ b/solution.py
@@ -1,6 +1,10 @@
+import functools
+
 import jax
 import jax.numpy as jnp
 from jax import lax
+from jax.experimental import pallas as pl
+from jax.experimental.pallas import tpu as pltpu
 from jax.sharding import PartitionSpec as P
 
 D = 768
@@ -65,7 +69,7 @@
     return loop_state
 
 
-def local(tokens, gain_one, w_qkv, w_out, gain_two, w_up, w_down, cotangent):
+def local_any(tokens, gain_one, w_qkv, w_out, gain_two, w_up, w_down, cotangent):
     gathered = (
         lax.all_gather(gain_one, "wshard", axis=0, tiled=True),
         lax.all_gather(w_qkv, "wshard", axis=0, tiled=True),
@@ -251,6 +255,399 @@
     )
 
 
+BF = jnp.bfloat16
+F32 = jnp.float32
+TILE = 256
+VMEM_LIMIT = 56 * 1024 * 1024
+
+
+def nn(a, b):
+    return lax.dot_general(a, b, (((1,), (0,)), ((), ())), preferred_element_type=F32)
+
+
+def nt(a, b):
+    return lax.dot_general(a, b, (((1,), (1,)), ((), ())), preferred_element_type=F32)
+
+
+def tn(a, b):
+    return lax.dot_general(a, b, (((0,), (0,)), ((), ())), preferred_element_type=F32)
+
+
+def normalised(x):
+    centred = x - jnp.mean(x, axis=-1, keepdims=True)
+    variance = jnp.mean(centred * centred, axis=-1, keepdims=True)
+    inverse = lax.rsqrt(variance + EPSILON)
+    return centred * inverse, inverse
+
+
+def norm_back(xhat, inverse, gain, dy):
+    g = dy * gain
+    mean_g = jnp.mean(g, axis=-1, keepdims=True)
+    mean_gx = jnp.mean(g * xhat, axis=-1, keepdims=True)
+    return (g - mean_g - xhat * mean_gx) * inverse
+
+
+def causal_tile():
+    rows = lax.broadcasted_iota(jnp.int32, (TILE, TILE), 0)
+    cols = lax.broadcasted_iota(jnp.int32, (TILE, TILE), 1)
+    return rows <= cols
+
+
+def attend_kernel(x_ref, gain_ref, w_ref, normed_ref, kv_ref, mixt_ref, att_ref, low_ref, lse_ref, s_ref):
+    length = x_ref.shape[0]
+
+    @pl.when(pl.program_id(0) == 0)
+    def _():
+        for row in range(0, length, TILE):
+            xhat, _ = normalised(x_ref[row : row + TILE, :].astype(F32))
+            normed_ref[row : row + TILE, :] = (xhat * gain_ref[...]).astype(BF)
+
+    mix = nn(normed_ref[...], w_ref[0]).astype(BF)
+    kv_ref[0] = mix[:, HEAD_DIM:]
+    mixt_ref[0] = mix.T
+    keys = mix[:, HEAD_DIM : 2 * HEAD_DIM]
+    for block in range(length // TILE):
+        here = slice(block * TILE, (block + 1) * TILE)
+        queries = mixt_ref[0, 0:HEAD_DIM, here] * BF(HEAD_DIM**-0.5)
+        top = jnp.zeros((1, TILE), F32)
+        for other in range(block + 1):
+            there = slice(other * TILE, (other + 1) * TILE)
+            s = nn(keys[there, :], queries)
+            s_ref[there, :] = s
+            size = jnp.abs(s)
+            if other == block:
+                size = jnp.where(causal_tile(), size, 0.0)
+            top = jnp.maximum(top, jnp.max(size, axis=0, keepdims=True))
+        top = jnp.sqrt(top * top + 1.0)
+        total = jnp.zeros((1, TILE), F32)
+        acc = jnp.zeros((HEAD_DIM, TILE), F32)
+        for other in range(block + 1):
+            there = slice(other * TILE, (other + 1) * TILE)
+            s = s_ref[there, :]
+            square = s * s + 1.0
+            r = lax.rsqrt(square)
+            p = jnp.exp(square * r - top)
+            if other == block:
+                p = jnp.where(causal_tile(), p, 0.0)
+            total = total + jnp.sum(p, axis=0, keepdims=True)
+            signed = (s * r * p).astype(BF)
+            acc = acc + nn(mixt_ref[0, 2 * HEAD_DIM :, there], signed)
+        att = acc / total
+        att_ref[0, :, here] = att
+        low_ref[0, :, here] = att.astype(BF)
+        lse_ref[0, :, here] = top + jnp.log(total)
+
+
+def attend(x, gain, w):
+    length, heads = x.shape[0], w.shape[0]
+    whole = lambda h: (0, 0)
+    head = lambda h: (h, 0, 0)
+    return pl.pallas_call(
+        attend_kernel,
+        grid=(heads,),
+        in_specs=[
+            pl.BlockSpec((length, D), whole),
+            pl.BlockSpec((1, D), whole),
+            pl.BlockSpec((1, D, 3 * HEAD_DIM), head),
+        ],
+        out_specs=[
+            pl.BlockSpec((length, D), whole),
+            pl.BlockSpec((1, length, 2 * HEAD_DIM), head),
+            pl.BlockSpec((1, 3 * HEAD_DIM, length), head),
+            pl.BlockSpec((1, HEAD_DIM, length), head),
+            pl.BlockSpec((1, HEAD_DIM, length), head),
+            pl.BlockSpec((1, 1, length), head),
+        ],
+        out_shape=[
+            jax.ShapeDtypeStruct((length, D), BF),
+            jax.ShapeDtypeStruct((heads, length, 2 * HEAD_DIM), BF),
+            jax.ShapeDtypeStruct((heads, 3 * HEAD_DIM, length), BF),
+            jax.ShapeDtypeStruct((heads, HEAD_DIM, length), F32),
+            jax.ShapeDtypeStruct((heads, HEAD_DIM, length), BF),
+            jax.ShapeDtypeStruct((heads, 1, length), F32),
+        ],
+        scratch_shapes=[pltpu.VMEM((length, TILE), F32)],
+        compiler_params=pltpu.CompilerParams(vmem_limit_bytes=VMEM_LIMIT),
+        cost_estimate=pl.CostEstimate(flops=3 * 10**9, bytes_accessed=6 * 10**6, transcendentals=4 * 10**6),
+        name="attend",
+    )(x, gain, w)
+
+
+def attend_back_kernel(kv_ref, mixt_ref, att_ref, lse_ref, dout_ref, dmix_ref, dq_ref, dk_ref, dv_ref):
+    length = kv_ref.shape[1]
+    scale = BF(HEAD_DIM**-0.5)
+    keys = kv_ref[0, :, :HEAD_DIM]
+    values = kv_ref[0, :, HEAD_DIM:]
+    for block in range(length // TILE):
+        here = slice(block * TILE, (block + 1) * TILE)
+        queries = mixt_ref[0, 0:HEAD_DIM, here] * scale
+        dout = dout_ref[0, :, here]
+        delta = jnp.sum(dout.astype(F32) * att_ref[0, :, here], axis=0, keepdims=True)
+        lse = lse_ref[0, :, here]
+        acc = jnp.zeros((HEAD_DIM, TILE), F32)
+        for other in range(block + 1):
+            there = slice(other * TILE, (other + 1) * TILE)
+            s = nn(keys[there, :], queries)
+            ds = nn(values[there, :], dout)
+            square = s * s + 1.0
+            r = lax.rsqrt(square)
+            chance = jnp.exp(square * r - lse)
+            if other == block:
+                chance = jnp.where(causal_tile(), chance, 0.0)
+            tilted = s * r
+            signed = (tilted * chance).astype(BF)
+            slope = r * r * r + tilted * tilted
+            dsc = (chance * (ds * slope - tilted * delta)).astype(BF)
+            acc = acc + nn(mixt_ref[0, HEAD_DIM : 2 * HEAD_DIM, there], dsc)
+            dk = nt(dsc, queries)
+            dv = nt(signed, dout)
+            if other == block:
+                dk_ref[there, :] = dk
+                dv_ref[there, :] = dv
+            else:
+                dk_ref[there, :] += dk
+                dv_ref[there, :] += dv
+        dq_ref[:, here] = acc * HEAD_DIM**-0.5
+    dmix_ref[0, :, 0:HEAD_DIM] = dq_ref[...].T.astype(BF)
+    dmix_ref[0, :, HEAD_DIM : 2 * HEAD_DIM] = dk_ref[...].astype(BF)
+    dmix_ref[0, :, 2 * HEAD_DIM :] = dv_ref[...].astype(BF)
+
+
+def attend_back(kv, mixt, att, lse, dout):
+    heads, length = kv.shape[0], kv.shape[1]
+    head = lambda h: (h, 0, 0)
+    return pl.pallas_call(
+        attend_back_kernel,
+        grid=(heads,),
+        in_specs=[
+            pl.BlockSpec((1, length, 2 * HEAD_DIM), head),
+            pl.BlockSpec((1, 3 * HEAD_DIM, length), head),
+            pl.BlockSpec((1, HEAD_DIM, length), head),
+            pl.BlockSpec((1, 1, length), head),
+            pl.BlockSpec((1, HEAD_DIM, length), head),
+        ],
+        out_specs=pl.BlockSpec((1, length, 3 * HEAD_DIM), head),
+        out_shape=jax.ShapeDtypeStruct((heads, length, 3 * HEAD_DIM), BF),
+        scratch_shapes=[
+            pltpu.VMEM((HEAD_DIM, length), F32),
+            pltpu.VMEM((length, HEAD_DIM), F32),
+            pltpu.VMEM((length, HEAD_DIM), F32),
+        ],
+        compiler_params=pltpu.CompilerParams(vmem_limit_bytes=VMEM_LIMIT),
+        cost_estimate=pl.CostEstimate(flops=3 * 10**9, bytes_accessed=6 * 10**6, transcendentals=4 * 10**6),
+        name="attend_back",
+    )(kv, mixt, att, lse, dout)
+
+
+def pick(value, index, axis=0):
+    return lax.dynamic_index_in_dim(value, index, axis, keepdims=False)
+
+
+def across_w(value, flip):
+    return lax.ppermute(value, "wshard", [(i, i ^ flip) for i in range(4)])
+
+
+def across_core(value):
+    return lax.ppermute(value, "ctx", [(i, i ^ 1) for i in range(8)])
+
+
+def across_z(value, flip):
+    return lax.ppermute(value, "ctx", [(i, i ^ (2 * flip)) for i in range(8)])
+
+
+def along_z(value, by):
+    return lax.ppermute(value, "ctx", [(i, i + 2 * by) for i in range(8) if 0 <= i + 2 * by < 8])
+
+
+Z_GROUPS = [[0, 2, 4, 6], [1, 3, 5, 7]]
+
+
+def gather_w(shard):
+    place = lax.axis_index("wshard")
+    half = shard.shape[0] // 2
+    from_x = across_w(shard, 1)
+    from_y = across_w(shard, 2)
+    corner = jnp.concatenate([across_w(from_x[:half], 2), across_w(from_y[half:], 1)])
+    stacked = jnp.stack([shard, from_x, from_y, corner])
+    return jnp.stack([pick(stacked, place ^ j) for j in range(4)])
+
+
+def gather_z(block):
+    z = lax.axis_index("ctx") // 2
+    up1, down1 = along_z(block, 1), along_z(block, -1)
+    up2, down2 = along_z(up1, 1), along_z(down1, -1)
+    up3, down3 = along_z(up2, 1), along_z(down2, -1)
+    line = jnp.stack([up3, up2, up1, block, down1, down2, down3])
+    return lax.dynamic_slice_in_dim(line, 3 - z, 4, 0)
+
+
+def scatter_w(partial, x_first):
+    place = lax.axis_index("wshard")
+    y, x = place // 2, place % 2
+    grid = partial.reshape((2, 2) + partial.shape[1:])
+    if x_first:
+        first = pick(grid, x, 1) + across_w(pick(grid, 1 - x, 1), 1)
+        return pick(first, y) + across_w(pick(first, 1 - y), 2)
+    first = pick(grid, y, 0) + across_w(pick(grid, 1 - y, 0), 2)
+    return pick(first, x) + across_w(pick(first, 1 - x), 1)
+
+
+def scatter_z(partial):
+    z = lax.axis_index("ctx") // 2
+    high, low = z // 2, z % 2
+    grid = partial.reshape((2, 2) + partial.shape[1:])
+    first = pick(grid, low, 1) + across_z(pick(grid, 1 - low, 1), 1)
+    return pick(first, high) + across_z(pick(first, 1 - high), 2)
+
+
+def unscatter_z(slot):
+    z = lax.axis_index("ctx") // 2
+    high, low = z // 2, z % 2
+    other = across_z(slot, 2)
+    pair = jnp.where(high == 0, jnp.stack([slot, other]), jnp.stack([other, slot]))
+    far = across_z(pair, 1)
+    return jnp.where(low == 0, jnp.stack([pair, far], 1), jnp.stack([far, pair], 1)).reshape((4,) + slot.shape)
+
+
+def total_z(partial):
+    rows = partial.shape[0] // 4
+    return unscatter_z(scatter_z(partial.reshape((4, rows) + partial.shape[1:]))).reshape(partial.shape)
+
+
+def local_grid(tokens, gain_one, w_qkv, w_out, gain_two, w_up, w_down, cotangent):
+    core = lax.axis_index("ctx") % 2
+    z = lax.axis_index("ctx") // 2
+    block = tokens.shape[2]
+    quarter = D // 4
+    own_heads = HEADS // 4
+
+    tok = tokens[:, 0]
+    other_tok = across_core(pick(tok, 1 - core))
+    own_tok = pick(tok, core)
+    x_block = jnp.where(core == 0, jnp.concatenate([own_tok, other_tok]), jnp.concatenate([other_tok, own_tok]))
+    x_all = gather_z(x_block).reshape(-1, D)
+
+    shard_rows = w_qkv.shape[0]
+    w_heads = pick(w_qkv.reshape(shard_rows, 3, 4, own_heads, HEAD_DIM), z, 2)
+    w_heads = w_heads.transpose(2, 0, 1, 3).reshape(own_heads * shard_rows, 3 * HEAD_DIM)
+    first = gather_w(jnp.concatenate([w_heads, gain_one[None], gain_two[None], jnp.zeros((14, quarter), BF)]))
+    gains = first[:, own_heads * shard_rows :, :]
+    gain_first = gains[:, 0].reshape(1, D).astype(F32)
+    gain_second = gains[:, 1].reshape(1, D).astype(F32)
+    w_heads = first[:, : own_heads * shard_rows].reshape(4, own_heads, shard_rows, 3 * HEAD_DIM)
+    w_heads = w_heads.transpose(1, 0, 2, 3).reshape(own_heads, D, 3 * HEAD_DIM)
+
+    full_out = gather_w(w_out).reshape(D, D)
+    half = w_down.shape[0] // 2
+    up_half = pick(w_up.reshape(shard_rows, 4, 2, half), core, 2).reshape(shard_rows, 4 * half)
+    full_up = gather_w(up_half).reshape(D, 4 * half)
+    full_down = gather_w(pick(w_down.reshape(2, half, D), core)).reshape(4 * half, D)
+
+    cot = cotangent[:, 0]
+    other_cot = across_core(cot)
+    cots = jnp.where(core == 0, jnp.stack([cot, other_cot], 1), jnp.stack([other_cot, cot], 1))
+    cots = cots.reshape(2, 2 * block, D)
+    cot_mine = pick(cots, core)
+    cot_both = jnp.concatenate([cot_mine, pick(cots, 1 - core)])
+
+    normed_all, kv, mixt, att, att_low, lse = attend(x_all, gain_first, w_heads)
+    att_home = lax.all_to_all(
+        att_low.reshape(quarter, -1), "ctx", 1, 0, tiled=True, axis_index_groups=Z_GROUPS
+    )
+
+    x_own = x_block.astype(F32)
+    hidden = x_own + tn(att_home, full_out)
+    xhat_two, inverse_two = normalised(hidden)
+    normed_two = (xhat_two * gain_second).astype(BF)
+    normed_both = jnp.concatenate([normed_two, across_core(normed_two)])
+    upward = nn(normed_both, full_up)
+    active_f, gelu_back = jax.vjp(gelu_smooth, upward)
+    active = active_f.astype(BF)
+    down = nn(active, full_down)
+    rows = 2 * block
+    result = hidden + down[:rows] + across_core(down[rows:].astype(BF)).astype(F32)
+    result = result.astype(BF)
+
+    grad_down = tn(active, cot_both).astype(BF)
+    d_upward = gelu_back(nt(cot_both, full_down))[0].astype(BF)
+    d_normed = nt(d_upward, full_up)
+    grad_up = tn(normed_both, d_upward).astype(BF)
+    d_normed_two = d_normed[:rows] + across_core(d_normed[rows:].astype(BF)).astype(F32)
+    d_gain_two = jnp.sum(d_normed_two * xhat_two, axis=0)
+    d_hidden = cot_mine.astype(F32) + norm_back(xhat_two, inverse_two, gain_second, d_normed_two)
+    d_branch = d_hidden.astype(BF)
+    d_att = nt(full_out, d_branch).astype(BF)
+    dout = lax.all_to_all(d_att, "ctx", 0, 1, tiled=True, axis_index_groups=Z_GROUPS)
+    grad_out = nn(att_home, d_branch).astype(BF)
+
+    d_mix = attend_back(kv, mixt, att, lse, dout.reshape(own_heads, HEAD_DIM, -1))
+    d_first = sum(nt(d_mix[h], w_heads[h]) for h in range(own_heads))
+    xhat_all, _ = normalised(x_all.astype(F32))
+    d_gain_one = jnp.sum(d_first * xhat_all, axis=0)
+    grad_heads = jnp.stack([tn(normed_all, d_mix[h]) for h in range(own_heads)]).astype(BF)
+    d_first = scatter_z(d_first.astype(BF).reshape(4, rows, D)).astype(F32)
+    xhat_one, inverse_one = normalised(x_own)
+    grad_tok = d_hidden + norm_back(xhat_one, inverse_one, gain_first, d_first)
+
+    sum_up = total_z(scatter_w(grad_up.reshape(4, shard_rows, 4 * half), True))
+    sum_down = total_z(scatter_w(grad_down.reshape(4, half, D), False))
+    other_up, other_down = across_core(sum_up), across_core(sum_down)
+    pair_up = jnp.where(core == 0, jnp.stack([sum_up, other_up]), jnp.stack([other_up, sum_up]))
+    out_up = pair_up.reshape(2, shard_rows, 4, half).transpose(1, 2, 0, 3).reshape(shard_rows, 8 * half).astype(F32)
+    pair_down = jnp.where(core == 0, jnp.stack([sum_down, other_down]), jnp.stack([other_down, sum_down]))
+    out_down = pair_down.reshape(2 * half, D).astype(F32)
+
+    part = shard_rows // 2
+    grid_out = grad_out.reshape(4, 2, part, D)
+    sum_out = pick(grid_out, core, 1) + across_core(pick(grid_out, 1 - core, 1))
+    sum_out = total_z(scatter_w(sum_out, True))
+    other_out = across_core(sum_out)
+    out_out = jnp.where(core == 0, jnp.concatenate([sum_out, other_out]), jnp.concatenate([other_out, sum_out]))
+    out_out = out_out.astype(F32)
+
+    grid_heads = grad_heads.reshape(own_heads, 4, 2, part, 3 * HEAD_DIM).transpose(1, 2, 0, 3, 4)
+    grid_heads = grid_heads.reshape(4, 2, own_heads * part, 3 * HEAD_DIM)
+    extra = jnp.stack([d_gain_one, d_gain_two]).astype(BF).reshape(2, 4, quarter).transpose(1, 0, 2)
+    extra = jnp.stack([extra, jnp.zeros_like(extra)], 1)
+    extra = jnp.pad(extra, ((0, 0), (0, 0), (0, 14), (0, 0)))
+    both = jnp.concatenate([grid_heads, extra], 2)
+    sum_heads = pick(both, core, 1) + across_core(pick(both, 1 - core, 1))
+    sum_heads = gather_z(scatter_w(sum_heads, False))
+    other_heads = across_core(sum_heads)
+    pair = jnp.where(core == 0, jnp.stack([sum_heads, other_heads]), jnp.stack([other_heads, sum_heads]))
+    pair = pair.astype(F32)
+    out_gains = jnp.sum(pair[0, :, own_heads * part :], axis=0)
+    heads_out = pair[:, :, : own_heads * part].reshape(2, 4, own_heads, part, 3, HEAD_DIM)
+    out_qkv = heads_out.transpose(0, 3, 4, 1, 2, 5).reshape(shard_rows, 3 * D)
+
+    result = result.reshape(2, block, D)
+    grad_tok = grad_tok.reshape(2, block, D)
+    result_kept, result_got = pick(result, core), across_core(pick(result, 1 - core))
+    grad_kept, grad_got = pick(grad_tok, core), across_core(pick(grad_tok, 1 - core))
+    out_result = jnp.where(core == 0, jnp.stack([result_kept, result_got]), jnp.stack([result_got, result_kept]))
+    out_tokens = jnp.where(core == 0, jnp.stack([grad_kept, grad_got]), jnp.stack([grad_got, grad_kept]))
+    return (
+        out_result[:, None],
+        out_tokens[:, None],
+        out_gains[0],
+        out_qkv,
+        out_out,
+        out_gains[1],
+        out_up,
+        out_down,
+    )
+
+
+def local(tokens, *rest):
+    fits = (
+        lax.axis_size("wshard") == 4
+        and lax.axis_size("ctx") == 8
+        and tokens.shape[:2] == (2, 1)
+        and tokens.shape[2] % 128 == 0
+    )
+    return (local_grid if fits else local_any)(tokens, *rest)
+
+
 def solution(mesh):
     placed = (
         P(None, "wshard", "ctx", None),

time: 904 us -> 364 us (0.40)
  waiting for transfers between devices: 557 us -> 100 us
  matrix products: 90.3 us -> 25.6 us
  blocking collectives: 36.8 us -> 0 us
  local copies, waits for them, and re-layouts: 31.8 us -> 68.5 us
  Pallas kernels: 0 us -> 25.9 us
  starting transfers between devices: 117 us -> 99.4 us
  between operations: 17.5 us -> 2.49 us
    all_gather x8 -> x0, waiting for transfers between devices: 213 us -> none  [the longest x2 53.5 us: local(): lax.all_gather(values_flat, 'ctx', axis=0, tiled=True)]
    reduce_scatter x4 -> x0, waiting for transfers between devices: 116 us -> none  [the longest x1 60 us: local(): lax.psum_scatter(sum_down.astype(jnp.bfloat16), 'wshard', scatter_dimensi...]
    psum x1 -> x0, waiting for transfers between devices: 78.2 us -> none  [local(): lax.psum(shares[1].astype(jnp.bfloat16), 'ctx').astype(jnp.float32)]
    dot_general x38 -> x15, matrix products: 90.3 us -> 25.6 us  [the longest x6 9.23 us: nt(): lax.dot_general(a, b, (((1,), (1,)), ((), ())), preferred_element_type=F32)]
    ppermute x64 -> x63, waiting for transfers between devices: 146 us -> 89 us  [the longest x14 40.9 us: across_z(): return lax.ppermute(value, 'ctx', [(i, i ^ 2 * flip) for i in range(8)])]
    ppermute x64 -> x63, starting transfers between devices: 117 us -> 89.9 us  [the longest x12 43.9 us: along_z(): lax.ppermute(value, 'ctx', [(i, i + 2 * by) for i in range(8) if 0 <= i +...]
    pallas_call x0 -> x2, Pallas kernels: none -> 25.9 us  [the longest x1 13.1 us: attend(): pl.pallas_call(attend_kernel, grid=(heads,), in_specs=[pl.BlockSpec((leng...]
    unnamed x2 -> x0, blocking collectives: 20.9 us -> none
  transfers between devices with their start and end apart: 77 -> 65, of which waited for: 75 -> 23; matrix products, arithmetic and copies ran while one was open for 13% -> 29% of each run, Pallas kernels for 0% -> 4%
where the time goes in v1:
time: 364 us; the launch traced here: 358 us
  waiting for transfers between devices  100 us (27%)
  starting transfers between devices  99.4 us (27%)
  local copies, waits for them, and re-layouts  68.5 us (19%)
  other arithmetic  35.5 us (10%)
  Pallas kernels  25.9 us (7%)
  matrix products  25.6 us (7%)
    ppermute x12, starting transfers between devices, along_z(): lax.ppermute(value, 'ctx', [(i, i + 2 * by) for i in range(8) if 0 <= i +...  43.9 us
    ppermute x14, waiting for transfers between devices, across_z(): return lax.ppermute(value, 'ctx', [(i, i ^ 2 * flip) for i in range(8)])  40.9 us
    ppermute x24, waiting for transfers between devices, across_w(): return lax.ppermute(value, 'wshard', [(i, i ^ flip) for i in range(4)])  31.8 us
    ppermute x24, starting transfers between devices, across_w(): return lax.ppermute(value, 'wshard', [(i, i ^ flip) for i in range(4)])  27 us
    unnamed x134, local copies, waits for them, and re-layouts  19.4 us
    ppermute x14, starting transfers between devices, across_z(): return lax.ppermute(value, 'ctx', [(i, i ^ 2 * flip) for i in range(8)])  16.8 us
    ppermute x12, waiting for transfers between devices, along_z(): lax.ppermute(value, 'ctx', [(i, i + 2 * by) for i in range(8) if 0 <= i +...  16.2 us
    pallas_call x1, Pallas kernels, attend(): pl.pallas_call(attend_kernel, grid=(heads,), in_specs=[pl.BlockSpec((leng...  13.1 us
  transfers between devices with their start and end apart: 65, of which 23 were waited for; matrix products, arithmetic and copies ran while one was open for 29% of the time, Pallas kernels for 4%

profile of v1, /device:TPU:0, one launch (start us, length us, event | category | flops | bytes accessed | tf_op | source)
XLA Modules:
  0.0 357.5 jit_solution(2082121941914006742)
XLA Ops:
  0.6 3.0 collective-permute-start.12
  10.4 1.8 dynamic-slice_bitcast_fusion.19
  18.4 2.0 collective-permute-start.17
  27.4 1.9 collective-permute-start.21
  29.3 8.7 %collective-permute-done.9 = bf16[296,192]{0,1:T(8,128)(2,1)S(1)} collective-permute-done((bf16[296,192]{0,1:T(8,128)(2,1)S(1)}, bf16[296,192]{0,1:T(8,128)(2,1)S(1)}, u32[]{:S(2)}, u32[]{:S(2)}) %collective-permute-start.9) | collective-permute-done | bytes 113696 | tf_op jit(solution)/shard_map/ppermute | solution.py:447
  38.0 1.8 collective-permute-start.14
  45.7 1.9 collective-permute-start.13
  50.1 3.5 collective-permute-done.13
  53.6 3.7 %collective-permute-start.1 = (bf16[256,768]{1,0:T(8,128)(2,1)S(1)}, bf16[256,768]{1,0:T(8,128)(2,1)S(1)}, u32[]{:S(2)}, u32[]{:S(2)}) collective-permute-start(bf16[256,768]{1,0:T(8,128)(2,1)S(1)} %get-tuple-element.65), channel_id=1, source_target_pairs={{0,2},{1,3},{2,4},{3,5},{4,6},{5,7},{8,10},{9,11},{10,12},{11,13},... | collective-permute-start | bytes 1179656 | tf_op jit(solution)/shard_map/ppermute | solution.py:459
  70.6 3.5 collective-permute-start.2
  75.6 2.0 collective-permute-done.22
  81.1 4.4 %collective-permute-start.3 = (bf16[256,768]{1,0:T(8,128)(2,1)S(1)}, bf16[256,768]{1,0:T(8,128)(2,1)S(1)}, u32[]{:S(2)}, u32[]{:S(2)}) collective-permute-start(bf16[256,768]{1,0:T(8,128)(2,1)S(1)} %collective-permute-done.2), channel_id=1, source_target_pairs={{0,2},{1,3},{2,4},{3,5},{4,6},{5,7},{8,10},{9,11},{10,12},{11,13},... | collective-permute-start | bytes 1179656 | tf_op jit(solution)/shard_map/ppermute | solution.py:459
  87.0 13.0 %collective-permute-start.6 = (bf16[256,768]{1,0:T(8,128)(2,1)S(1)}, bf16[256,768]{1,0:T(8,128)(2,1)S(1)}, u32[]{:S(2)}, u32[]{:S(2)}) collective-permute-start(bf16[256,768]{1,0:T(8,128)(2,1)S(1)} %collective-permute-done.5), channel_id=1, source_target_pairs={{2,0},{3,1},{4,2},{5,3},{6,4},{7,5},{10,8},{11,9},{12,10},{13,11},... | collective-permute-start | bytes 1179656 | tf_op jit(solution)/shard_map/ppermute | solution.py:459
  101.7 13.1 %attend.1 = (bf16[1024,768]{1,0:T(8,128)(2,1)}, bf16[3,1024,128]{2,1,0:T(8,128)(2,1)}, bf16[3,192,1024]{2,1,0:T(8,128)(2,1)}, f32[3,64,1024]{2,1,0:T(8,128)}, bf...) custom-call(bf16[1024,768]{1,0:T(8,128)(2,1)} %bitcast.294, f32[1,768]{1,0:T(1,128)} %reshape.669.gain_ref, ...), custom_call_target="tpu_custom_call" | custom-call | flops 3000000000 | bytes 6000000 | tf_op jit(solution)/shard_map/attend/pallas_call | solution.py:345
  114.8 2.0 all_to_all.26
  116.8 1.8 copy.102
  118.6 5.5 %all-to-all-start = ((bf16[192,4,256]{2,0,1:T(8,128)(2,1)}), bf16[192,4,256]{2,0,1:T(8,128)(2,1)}, u32[]{:S(2)}, u32[]{:S(2)}) async-start(bf16[192,4,256]{2,0,1:T(8,128)(2,1)} %copy.102), calls=%async_computation | async-start | bytes 786432 | tf_op jit(solution)/shard_map/all_to_all | solution.py:554
  124.1 1.7 pad_maximum_fusion.3
  127.8 5.5 %all-to-all-done = bf16[192,4,256]{2,0,1:T(8,128)(2,1)} async-done(((bf16[192,4,256]{2,0,1:T(8,128)(2,1)}), bf16[192,4,256]{2,0,1:T(8,128)(2,1)}, u32[]{:S(2)}, u32[]{:S(2)}) %all-to-all-start) | async-done | bytes 393248 | tf_op jit(solution)/shard_map/all_to_all | solution.py:554
  137.6 2.6 copy.105
  140.2 3.3 fusion.37
  143.5 1.9 fusion.54
  145.5 3.2 fusion.8
  148.7 1.7 convolution_convert_fusion
  152.6 2.4 convolution_convert_fusion.1
  163.7 4.0 %all-to-all-start.1 = ((bf16[4,192,256]{2,1,0:T(8,128)(2,1)}), bf16[4,192,256]{2,1,0:T(8,128)(2,1)S(1)}, u32[]{:S(2)}, u32[]{:S(2)}) async-start(bf16[4,192,256]{2,1,0:T(8,128)(2,1)} %bitcast.47), calls=%async_computation.1 | async-start | bytes 786432 | tf_op jit(solution)/shard_map/all_to_all | solution.py:580
  167.9 2.5 convolution_convert_fusion.2
  170.5 1.9 dynamic-slice_bitcast_fusion.5
  173.7 5.6 %all-to-all-done.1 = bf16[4,192,256]{2,1,0:T(8,128)(2,1)S(1)} async-done(((bf16[4,192,256]{2,1,0:T(8,128)(2,1)}), bf16[4,192,256]{2,1,0:T(8,128)(2,1)S(1)}, u32[]{:S(2)}, u32[]{:S(2)}) %all-to-all-start.1) | async-done | bytes 393248 | tf_op jit(solution)/shard_map/all_to_all | solution.py:580
  180.6 12.8 %attend_back.1 = bf16[3,1024,192]{2,1,0:T(8,128)(2,1)} custom-call(bf16[3,1024,128]{2,1,0:T(8,128)(2,1)} %get-tuple-element.15.kv_ref, bf16[3,192,1024]{2,1,0:T(8,128)(2,1)} %get-tuple-element.16.mixt_ref, f32[3,64,1024]{2,1,0:T(8,128)} %get-tuple-element.17.att_ref, f32[3,1,1024]{2,1,0:T(1,128)} %get-tuple-element.18.lse_ref, ...), custom_call_target="tpu_custom_call" | custom-call | flops 3000000000 | bytes 6000000 | tf_op jit(solution)/shard_map/attend_back/pallas_call | solution.py:419
  193.4 1.7 fusion.14
  197.8 2.1 multiply_reduce_fusion
  203.0 2.2 copy.113
  208.3 1.8 bitcast_add_fusion.1
  210.8 6.2 %collective-permute-done.42 = bf16[2,96,768]{2,1,0:T(8,128)(2,1)S(1)} collective-permute-done((bf16[2,96,768]{2,1,0:T(8,128)(2,1)S(1)}, bf16[2,96,768]{2,1,0:T(8,128)(2,1)S(1)}, u32[]{:S(2)}, u32[]{:S(2)}) %collective-permute-start.42) | collective-permute-done | bytes 294944 | tf_op jit(solution)/shard_map/ppermute | solution.py:447
  219.1 10.0 %collective-permute-done.43 = bf16[96,768]{1,0:T(8,128)(2,1)S(1)} collective-permute-done((bf16[96,768]{1,0:T(8,128)(2,1)S(1)}, bf16[96,768]{1,0:T(8,128)(2,1)S(1)}, u32[]{:S(2)}, u32[]{:S(2)}) %collective-permute-start.43) | collective-permute-done | bytes 147488 | tf_op jit(solution)/shard_map/ppermute | solution.py:447
  229.1 2.1 collective-permute-start.44
  233.6 2.1 collective-permute-start.45
  236.8 1.7 collective-permute-done.45
  238.5 2.0 collective-permute-start.46
  241.2 2.3 collective-permute-done.46
  243.5 2.0 collective-permute-start.47
  245.5 2.4 collective-permute-done.47
  250.4 2.5 collective-permute-start.29
  254.4 3.9 %collective-permute-start.34 = (bf16[304,192]{0,1:T(8,128)(2,1)S(1)}, bf16[304,192]{0,1:T(8,128)(2,1)S(1)}, u32[]{:S(2)}, u32[]{:S(2)}) collective-permute-start(bf16[304,192]{0,1:T(8,128)(2,1)S(1)} %bitcast_add_fusion.15), channel_id=1, source_target_pairs={{0,2},{1,3},{2,4},{3,5},{4,6},{5,7},{8,10},{9,11},{10,12},{11,13},... | collective-permute-start | bytes 350216 | tf_op jit(solution)/shard_map/ppermute | solution.py:459
  259.6 2.7 collective-permute-start.58
  262.4 9.6 %collective-permute-done.34 = bf16[304,192]{0,1:T(8,128)(2,1)S(1)} collective-permute-done((bf16[304,192]{0,1:T(8,128)(2,1)S(1)}, bf16[304,192]{0,1:T(8,128)(2,1)S(1)}, u32[]{:S(2)}, u32[]{:S(2)}) %collective-permute-start.34) | collective-permute-done | bytes 116768 | tf_op jit(solution)/shard_map/ppermute | solution.py:459
  271.9 4.4 %collective-permute-start.35 = (bf16[304,192]{0,1:T(8,128)(2,1)S(1)}, bf16[304,192]{0,1:T(8,128)(2,1)S(1)}, u32[]{:S(2)}, u32[]{:S(2)}) collective-permute-start(bf16[304,192]{0,1:T(8,128)(2,1)S(1)} %collective-permute-done.34), channel_id=1, source_target_pairs={{0,2},{1,3},{2,4},{3,5},{4,6},{5,7},{8,10},{9,11},{10,12},{11,13},... | collective-permute-start | bytes 350216 | tf_op jit(solution)/shard_map/ppermute | solution.py:459
  278.5 2.2 collective-permute-done.35
  280.7 4.4 %collective-permute-start.36 = (bf16[304,192]{0,1:T(8,128)(2,1)S(1)}, bf16[304,192]{0,1:T(8,128)(2,1)S(1)}, u32[]{:S(2)}, u32[]{:S(2)}) collective-permute-start(bf16[304,192]{0,1:T(8,128)(2,1)S(1)} %collective-permute-done.35), channel_id=1, source_target_pairs={{0,2},{1,3},{2,4},{3,5},{4,6},{5,7},{8,10},{9,11},{10,12},{11,13},... | collective-permute-start | bytes 350216 | tf_op jit(solution)/shard_map/ppermute | solution.py:459
  286.6 2.2 collective-permute-start.52
  290.0 2.9 collective-permute-done.39
  294.5 8.1 %collective-permute-done.52 = bf16[48,1536]{1,0:T(8,128)(2,1)S(1)} collective-permute-done((bf16[48,1536]{1,0:T(8,128)(2,1)S(1)}, bf16[48,1536]{1,0:T(8,128)(2,1)S(1)}, u32[]{:S(2)}, u32[]{:S(2)}) %collective-permute-start.52) | collective-permute-done | bytes 147488 | tf_op jit(solution)/shard_map/ppermute | solution.py:455
  302.7 9.2 %collective-permute-done.59 = bf16[96,768]{1,0:T(8,128)(2,1)S(1)} collective-permute-done((bf16[96,768]{1,0:T(8,128)(2,1)S(1)}, bf16[96,768]{1,0:T(8,128)(2,1)S(1)}, u32[]{:S(2)}, u32[]{:S(2)}) %collective-permute-start.59) | collective-permute-done | bytes 147488 | tf_op jit(solution)/shard_map/ppermute | solution.py:455
  311.9 3.1 collective-permute-done.53
  315.1 3.0 collective-permute-done.60
  318.3 6.7 %collective-permute-done.54 = bf16[2,48,1536]{2,1,0:T(8,128)(2,1)S(1)} collective-permute-done((bf16[2,48,1536]{2,1,0:T(8,128)(2,1)S(1)}, bf16[2,48,1536]{2,1,0:T(8,128)(2,1)S(1)}, u32[]{:S(2)}, u32[]{:S(2)}) %collective-permute-start.54) | collective-permute-done | bytes 294944 | tf_op jit(solution)/shard_map/ppermute | solution.py:455
  326.1 3.3 collective-permute-done.61
  330.1 3.1 reshape.665
  333.2 6.4 %copy.126 = f32[2,96,3,4,3,64]{5,4,3,2,1,0:T(4,128)} copy(f32[2,96,3,4,3,64]{1,4,5,2,3,0:T(4,128)} %bitcast.295) | data formatting | bytes 3538944
  339.6 5.9 %reshape.678 = f32[192,2304]{1,0:T(8,128)} reshape(f32[2,96,3,4,3,64]{5,4,3,2,1,0:T(4,128)} %copy.126) | data formatting | bytes 3538944
  349.0 1.8 copy.115
  350.8 2.9 reshape.672
  353.8 1.9 maximum_select_fusion.2
  (365 shorter events, 103.3 us)
Async XLA Ops:
  0.6 24.3 %collective-permute-start.12 = (bf16[192,768]{1,0:T(8,128)(2,1)}, bf16[192,768]{1,0:T(8,128)(2,1)S(1)}, u32[]{:S(2)}, u32[]{:S(2)}) collective-permute-start(bf16[192,768]{1,0:T(8,128)(2,1)} %param.11), channel_id=1, source_target_pairs={{0,16},{8,24},{16,0},{24,8},{1,17},{9,25},{17,1},{25,9},{2,18},{10... | collective-permute-start | bytes 884744 | tf_op jit(solution)/shard_map/ppermute | solution.py:447
  3.7 22.1 %collective-permute-start.11 = (bf16[192,768]{1,0:T(8,128)(2,1)}, bf16[192,768]{1,0:T(8,128)(2,1)}, u32[]{:S(2)}, u32[]{:S(2)}) collective-permute-start(bf16[192,768]{1,0:T(8,128)(2,1)} %param.11), channel_id=1, source_target_pairs={{0,8},{8,0},{16,24},{24,16},{1,9},{9,1},{17,25},{25,17},{2,10},{10... | collective-permute-start | bytes 884744 | tf_op jit(solution)/shard_map/ppermute | solution.py:447
  9.8 11.5 %collective-permute-start.8 = (bf16[592,192]{0,1:T(8,128)(2,1)}, bf16[592,192]{0,1:T(8,128)(2,1)S(1)}, u32[]{:S(2)}, u32[]{:S(2)}) collective-permute-start(bf16[592,192]{0,1:T(8,128)(2,1)} %maximum_maximum_fusion), channel_id=1, source_target_pairs={{0,16},{8,24},{16,0},{24,8},{1,17},{9,25},{17,1},{25,9},{2,18},{10... | collective-permute-start | bytes 681992 | tf_op jit(solution)/shard_map/ppermute | solution.py:447
  10.3 12.6 %collective-permute-start.7 = (bf16[592,192]{0,1:T(8,128)(2,1)}, bf16[592,192]{0,1:T(8,128)(2,1)}, u32[]{:S(2)}, u32[]{:S(2)}) collective-permute-start(bf16[592,192]{0,1:T(8,128)(2,1)} %maximum_maximum_fusion), channel_id=1, source_target_pairs={{0,8},{8,0},{16,24},{24,16},{1,9},{9,1},{17,25},{25,17},{2,10},{10... | collective-permute-start | bytes 681992 | tf_op jit(solution)/shard_map/ppermute | solution.py:447
  12.2 6.2 %collective-permute-start = (bf16[128,768]{1,0:T(8,128)(2,1)}, bf16[128,768]{1,0:T(8,128)(2,1)S(1)}, u32[]{:S(2)}, u32[]{:S(2)}) collective-permute-start(bf16[128,768]{1,0:T(8,128)(2,1)} %get-tuple-element.98), channel_id=1, source_target_pairs={{0,1},{1,0},{2,3},{3,2},{4,5},{5,4},{6,7},{7,6},{8,9},{9,8},{10,11... | collective-permute-start | bytes 589832 | tf_op jit(solution)/shard_map/ppermute | solution.py:451
  18.4 39.8 %collective-permute-start.17 = (bf16[192,1536]{1,0:T(8,128)(2,1)}, bf16[192,1536]{1,0:T(8,128)(2,1)}, u32[]{:S(2)}, u32[]{:S(2)}) collective-permute-start(bf16[192,1536]{1,0:T(8,128)(2,1)} %bitcast.165), channel_id=1, source_target_pairs={{0,16},{8,24},{16,0},{24,8},{1,17},{9,25},{17,1},{25,9},{2,18},{10... | collective-permute-start | bytes 1769480 | tf_op jit(solution)/shard_map/ppermute | solution.py:447
  21.3 6.0 %collective-permute-start.10 = (bf16[296,192]{0,1:T(8,128)(2,1)S(1)}, bf16[296,192]{0,1:T(8,128)(2,1)S(1)}, u32[]{:S(2)}, u32[]{:S(2)}) collective-permute-start(bf16[296,192]{0,1:T(8,128)(2,1)S(1)} %slice.112), channel_id=1, source_target_pairs={{0,8},{8,0},{16,24},{24,16},{1,9},{9,1},{17,25},{25,17},{2,10},{10... | collective-permute-start | bytes 341000 | tf_op jit(solution)/shard_map/ppermute | solution.py:447
  23.8 14.2 %collective-permute-start.9 = (bf16[296,192]{0,1:T(8,128)(2,1)S(1)}, bf16[296,192]{0,1:T(8,128)(2,1)S(1)}, u32[]{:S(2)}, u32[]{:S(2)}) collective-permute-start(bf16[296,192]{0,1:T(8,128)(2,1)S(1)} %slice.111), channel_id=1, source_target_pairs={{0,16},{8,24},{16,0},{24,8},{1,17},{9,25},{17,1},{25,9},{2,18},{10... | collective-permute-start | bytes 341000 | tf_op jit(solution)/shard_map/ppermute | solution.py:447
  25.0 35.6 %collective-permute-start.16 = (bf16[192,1536]{1,0:T(8,128)(2,1)}, bf16[192,1536]{1,0:T(8,128)(2,1)}, u32[]{:S(2)}, u32[]{:S(2)}) collective-permute-start(bf16[192,1536]{1,0:T(8,128)(2,1)} %bitcast.165), channel_id=1, source_target_pairs={{0,8},{8,0},{16,24},{24,16},{1,9},{9,1},{17,25},{25,17},{2,10},{10... | collective-permute-start | bytes 1769480 | tf_op jit(solution)/shard_map/ppermute | solution.py:447
  25.8 19.7 %collective-permute-start.26 = (bf16[2,128,768]{2,1,0:T(8,128)(2,1)}, bf16[2,128,768]{2,1,0:T(8,128)(2,1)}, u32[]{:S(2)}, u32[]{:S(2)}) collective-permute-start(bf16[2,128,768]{2,1,0:T(8,128)(2,1)} %bitcast.41), channel_id=1, source_target_pairs={{0,1},{1,0},{2,3},{3,2},{4,5},{5,4},{6,7},{7,6},{8,9},{9,8},{10,11... | collective-permute-start | bytes 1179656 | tf_op jit(solution)/shard_map/ppermute | solution.py:451
  27.4 35.7 %collective-permute-start.21 = (bf16[384,768]{1,0:T(8,128)(2,1)}, bf16[384,768]{1,0:T(8,128)(2,1)}, u32[]{:S(2)}, u32[]{:S(2)}) collective-permute-start(bf16[384,768]{1,0:T(8,128)(2,1)} %fusion.74), channel_id=1, source_target_pairs={{0,16},{8,24},{16,0},{24,8},{1,17},{9,25},{17,1},{25,9},{2,18},{10... | collective-permute-start | bytes 1769480 | tf_op jit(solution)/shard_map/ppermute | solution.py:447
  38.0 7.6 %collective-permute-start.14 = (bf16[96,768]{1,0:T(8,128)(2,1)}, bf16[96,768]{1,0:T(8,128)(2,1)}, u32[]{:S(2)}, u32[]{:S(2)}) collective-permute-start(bf16[96,768]{1,0:T(8,128)(2,1)} %slice.115), channel_id=1, source_target_pairs={{0,8},{8,0},{16,24},{24,16},{1,9},{9,1},{17,25},{25,17},{2,10},{10... | collective-permute-start | bytes 442376 | tf_op jit(solution)/shard_map/ppermute | solution.py:447
  45.5 21.7 %collective-permute-start.20 = (bf16[384,768]{1,0:T(8,128)(2,1)}, bf16[384,768]{1,0:T(8,128)(2,1)S(1)}, u32[]{:S(2)}, u32[]{:S(2)}) collective-permute-start(bf16[384,768]{1,0:T(8,128)(2,1)} %fusion.74), channel_id=1, source_target_pairs={{0,8},{8,0},{16,24},{24,16},{1,9},{9,1},{17,25},{25,17},{2,10},{10... | collective-permute-start | bytes 1769480 | tf_op jit(solution)/shard_map/ppermute | solution.py:447
  45.7 7.9 %collective-permute-start.13 = (bf16[96,768]{1,0:T(8,128)(2,1)S(1)}, bf16[96,768]{1,0:T(8,128)(2,1)S(1)}, u32[]{:S(2)}, u32[]{:S(2)}) collective-permute-start(bf16[96,768]{1,0:T(8,128)(2,1)S(1)} %copy-done.49), channel_id=1, source_target_pairs={{0,16},{8,24},{16,0},{24,8},{1,17},{9,25},{17,1},{25,9},{2,18},{10... | collective-permute-start | bytes 442376 | tf_op jit(solution)/shard_map/ppermute | solution.py:447
  53.6 14.2 %collective-permute-start.1 = (bf16[256,768]{1,0:T(8,128)(2,1)S(1)}, bf16[256,768]{1,0:T(8,128)(2,1)S(1)}, u32[]{:S(2)}, u32[]{:S(2)}) collective-permute-start(bf16[256,768]{1,0:T(8,128)(2,1)S(1)} %get-tuple-element.65), channel_id=1, source_target_pairs={{0,2},{1,3},{2,4},{3,5},{4,6},{5,7},{8,10},{9,11},{10,12},{11,13},... | collective-permute-start | bytes 1179656 | tf_op jit(solution)/shard_map/ppermute | solution.py:459
  58.3 12.4 %collective-permute-start.4 = (bf16[256,768]{1,0:T(8,128)(2,1)S(1)}, bf16[256,768]{1,0:T(8,128)(2,1)S(1)}, u32[]{:S(2)}, u32[]{:S(2)}) collective-permute-start(bf16[256,768]{1,0:T(8,128)(2,1)S(1)} %get-tuple-element.65), channel_id=1, source_target_pairs={{2,0},{3,1},{4,2},{5,3},{6,4},{7,5},{10,8},{11,9},{12,10},{13,11},... | collective-permute-start | bytes 1179656 | tf_op jit(solution)/shard_map/ppermute | solution.py:459
  60.6 13.6 %collective-permute-start.19 = (bf16[96,1536]{1,0:T(8,128)(2,1)S(1)}, bf16[96,1536]{1,0:T(8,128)(2,1)S(1)}, u32[]{:S(2)}, u32[]{:S(2)}) collective-permute-start(bf16[96,1536]{1,0:T(8,128)(2,1)S(1)} %slice.117), channel_id=1, source_target_pairs={{0,8},{8,0},{16,24},{24,16},{1,9},{9,1},{17,25},{25,17},{2,10},{10... | collective-permute-start | bytes 884744 | tf_op jit(solution)/shard_map/ppermute | solution.py:447
  63.1 12.3 %collective-permute-start.18 = (bf16[96,1536]{1,0:T(8,128)(2,1)S(1)}, bf16[96,1536]{1,0:T(8,128)(2,1)S(1)}, u32[]{:S(2)}, u32[]{:S(2)}) collective-permute-start(bf16[96,1536]{1,0:T(8,128)(2,1)S(1)} %slice.116), channel_id=1, source_target_pairs={{0,16},{8,24},{16,0},{24,8},{1,17},{9,25},{17,1},{25,9},{2,18},{10... | collective-permute-start | bytes 884744 | tf_op jit(solution)/shard_map/ppermute | solution.py:447
  67.2 8.4 %collective-permute-start.23 = (bf16[192,768]{1,0:T(8,128)(2,1)S(1)}, bf16[192,768]{1,0:T(8,128)(2,1)S(1)}, u32[]{:S(2)}, u32[]{:S(2)}) collective-permute-start(bf16[192,768]{1,0:T(8,128)(2,1)S(1)} %slice.119), channel_id=1, source_target_pairs={{0,8},{8,0},{16,24},{24,16},{1,9},{9,1},{17,25},{25,17},{2,10},{10... | collective-permute-start | bytes 884744 | tf_op jit(solution)/shard_map/ppermute | solution.py:447
  67.8 9.8 %collective-permute-start.22 = (bf16[192,768]{1,0:T(8,128)(2,1)S(1)}, bf16[192,768]{1,0:T(8,128)(2,1)S(1)}, u32[]{:S(2)}, u32[]{:S(2)}) collective-permute-start(bf16[192,768]{1,0:T(8,128)(2,1)S(1)} %slice.118), channel_id=1, source_target_pairs={{0,16},{8,24},{16,0},{24,8},{1,17},{9,25},{17,1},{25,9},{2,18},{10... | collective-permute-start | bytes 884744 | tf_op jit(solution)/shard_map/ppermute | solution.py:447
  70.6 10.5 %collective-permute-start.2 = (bf16[256,768]{1,0:T(8,128)(2,1)S(1)}, bf16[256,768]{1,0:T(8,128)(2,1)S(1)}, u32[]{:S(2)}, u32[]{:S(2)}) collective-permute-start(bf16[256,768]{1,0:T(8,128)(2,1)S(1)} %collective-permute-done.1), channel_id=1, source_target_pairs={{0,2},{1,3},{2,4},{3,5},{4,6},{5,7},{8,10},{9,11},{10,12},{11,13},... | collective-permute-start | bytes 1179656 | tf_op jit(solution)/shard_map/ppermute | solution.py:459
  74.1 12.8 %collective-permute-start.5 = (bf16[256,768]{1,0:T(8,128)(2,1)S(1)}, bf16[256,768]{1,0:T(8,128)(2,1)S(1)}, u32[]{:S(2)}, u32[]{:S(2)}) collective-permute-start(bf16[256,768]{1,0:T(8,128)(2,1)S(1)} %collective-permute-done.4), channel_id=1, source_target_pairs={{2,0},{3,1},{4,2},{5,3},{6,4},{7,5},{10,8},{11,9},{12,10},{13,11},... | collective-permute-start | bytes 1179656 | tf_op jit(solution)/shard_map/ppermute | solution.py:459
  81.1 18.9 %collective-permute-start.3 = (bf16[256,768]{1,0:T(8,128)(2,1)S(1)}, bf16[256,768]{1,0:T(8,128)(2,1)S(1)}, u32[]{:S(2)}, u32[]{:S(2)}) collective-permute-start(bf16[256,768]{1,0:T(8,128)(2,1)S(1)} %collective-permute-done.2), channel_id=1, source_target_pairs={{0,2},{1,3},{2,4},{3,5},{4,6},{5,7},{8,10},{9,11},{10,12},{11,13},... | collective-permute-start | bytes 1179656 | tf_op jit(solution)/shard_map/ppermute | solution.py:459
  87.0 13.4 %collective-permute-start.6 = (bf16[256,768]{1,0:T(8,128)(2,1)S(1)}, bf16[256,768]{1,0:T(8,128)(2,1)S(1)}, u32[]{:S(2)}, u32[]{:S(2)}) collective-permute-start(bf16[256,768]{1,0:T(8,128)(2,1)S(1)} %collective-permute-done.5), channel_id=1, source_target_pairs={{2,0},{3,1},{4,2},{5,3},{6,4},{7,5},{10,8},{11,9},{12,10},{13,11},... | collective-permute-start | bytes 1179656 | tf_op jit(solution)/shard_map/ppermute | solution.py:459
  118.6 14.7 %all-to-all-start = ((bf16[192,4,256]{2,0,1:T(8,128)(2,1)}), bf16[192,4,256]{2,0,1:T(8,128)(2,1)}, u32[]{:S(2)}, u32[]{:S(2)}) async-start(bf16[192,4,256]{2,0,1:T(8,128)(2,1)} %copy.102), calls=%async_computation | async-start | bytes 786432 | tf_op jit(solution)/shard_map/all_to_all | solution.py:554
  135.4 4.8 %collective-permute-start.15 = (bf16[256,768]{1,0:T(8,128)(2,1)S(1)}, bf16[256,768]{1,0:T(8,128)(2,1)}, u32[]{:S(2)}, u32[]{:S(2)}) collective-permute-start(bf16[256,768]{1,0:T(8,128)(2,1)S(1)} %multiply_convert_fusion.1), channel_id=1, source_target_pairs={{0,1},{1,0},{2,3},{3,2},{4,5},{5,4},{6,7},{7,6},{8,9},{9,8},{10,11... | collective-permute-start | bytes 1179656 | tf_op jit(solution)/shard_map/ppermute | solution.py:451
  151.9 8.3 %collective-permute-start.27 = (bf16[256,768]{1,0:T(8,128)(2,1)S(1)}, bf16[256,768]{1,0:T(8,128)(2,1)S(1)}, u32[]{:S(2)}, u32[]{:S(2)}) collective-permute-start(bf16[256,768]{1,0:T(8,128)(2,1)S(1)} %slice.177), channel_id=1, source_target_pairs={{0,1},{1,0},{2,3},{3,2},{4,5},{5,4},{6,7},{7,6},{8,9},{9,8},{10,11... | collective-permute-start | bytes 1179656 | tf_op jit(solution)/shard_map/ppermute | solution.py:451
  152.1 9.1 %collective-permute-start.24 = (bf16[256,768]{1,0:T(8,128)(2,1)S(1)}, bf16[256,768]{1,0:T(8,128)(2,1)S(1)}, u32[]{:S(2)}, u32[]{:S(2)}) collective-permute-start(bf16[256,768]{1,0:T(8,128)(2,1)S(1)} %slice.178), channel_id=1, source_target_pairs={{0,1},{1,0},{2,3},{3,2},{4,5},{5,4},{6,7},{7,6},{8,9},{9,8},{10,11... | collective-permute-start | bytes 1179656 | tf_op jit(solution)/shard_map/ppermute | solution.py:451
  156.3 52.0 %collective-permute-start.49 = (bf16[2,192,1536]{2,1,0:T(8,128)(2,1)}, bf16[2,192,1536]{2,1,0:T(8,128)(2,1)}, u32[]{:S(2)}, u32[]{:S(2)}) collective-permute-start(bf16[2,192,1536]{2,1,0:T(8,128)(2,1)} %dynamic-slice_bitcast_fusion.1), channel_id=1, source_target_pairs={{0,8},{8,0},{16,24},{24,16},{1,9},{9,1},{17,25},{25,17},{2,10},{10... | collective-permute-start | bytes 3538952 | tf_op jit(solution)/shard_map/ppermute | solution.py:447
  158.7 58.9 %collective-permute-start.56 = (bf16[2,384,768]{2,1,0:T(8,128)(2,1)}, bf16[2,384,768]{2,1,0:T(8,128)(2,1)}, u32[]{:S(2)}, u32[]{:S(2)}) collective-permute-start(bf16[2,384,768]{2,1,0:T(8,128)(2,1)} %dynamic-slice_bitcast_fusion), channel_id=1, source_target_pairs={{0,16},{8,24},{16,0},{24,8},{1,17},{9,25},{17,1},{25,9},{2,18},{10... | collective-permute-start | bytes 3538952 | tf_op jit(solution)/shard_map/ppermute | solution.py:447
  163.7 15.6 %all-to-all-start.1 = ((bf16[4,192,256]{2,1,0:T(8,128)(2,1)}), bf16[4,192,256]{2,1,0:T(8,128)(2,1)S(1)}, u32[]{:S(2)}, u32[]{:S(2)}) async-start(bf16[4,192,256]{2,1,0:T(8,128)(2,1)} %bitcast.47), calls=%async_computation.1 | async-start | bytes 786432 | tf_op jit(solution)/shard_map/all_to_all | solution.py:580
  167.8 5.1 %collective-permute-start.25 = (bf16[128,768]{1,0:T(8,128)(2,1)S(1)}, bf16[128,768]{1,0:T(8,128)(2,1)S(1)}, u32[]{:S(2)}, u32[]{:S(2)}) collective-permute-start(bf16[128,768]{1,0:T(8,128)(2,1)S(1)} %get-tuple-element.96), channel_id=1, source_target_pairs={{0,1},{1,0},{2,3},{3,2},{4,5},{5,4},{6,7},{7,6},{8,9},{9,8},{10,11... | collective-permute-start | bytes 589832 | tf_op jit(solution)/shard_map/ppermute | solution.py:451
  172.4 32.8 %collective-permute-start.41 = (bf16[4,96,768]{2,1,0:T(8,128)(2,1)}, bf16[4,96,768]{2,1,0:T(8,128)(2,1)}, u32[]{:S(2)}, u32[]{:S(2)}) collective-permute-start(bf16[4,96,768]{2,1,0:T(8,128)(2,1)} %dynamic-slice_bitcast_fusion.5), channel_id=1, source_target_pairs={{0,1},{1,0},{2,3},{3,2},{4,5},{5,4},{6,7},{7,6},{8,9},{9,8},{10,11... | collective-permute-start | bytes 1769480 | tf_op jit(solution)/shard_map/ppermute | solution.py:451
  201.4 47.8 %collective-permute-start.28 = (bf16[2,256,768]{2,1,0:T(8,128)(2,1)}, bf16[2,256,768]{2,1,0:T(8,128)(2,1)}, u32[]{:S(2)}, u32[]{:S(2)}) collective-permute-start(bf16[2,256,768]{2,1,0:T(8,128)(2,1)} %dynamic-slice_bitcast_fusion.2), channel_id=1, source_target_pairs={{0,2},{1,3},{2,0},{3,1},{4,6},{5,7},{6,4},{7,5},{8,10},{9,11},{10,... | collective-permute-start | bytes 2359304 | tf_op jit(solution)/shard_map/ppermute | solution.py:455
  205.2 30.5 %collective-permute-start.31 = (bf16[4,304,192]{1,2,0:T(8,128)(2,1)}, bf16[4,304,192]{1,2,0:T(8,128)(2,1)}, u32[]{:S(2)}, u32[]{:S(2)}) collective-permute-start(bf16[4,304,192]{1,2,0:T(8,128)(2,1)} %bitcast.353), channel_id=1, source_target_pairs={{0,1},{1,0},{2,3},{3,2},{4,5},{5,4},{6,7},{7,6},{8,9},{9,8},{10,11... | collective-permute-start | bytes 1400840 | tf_op jit(solution)/shard_map/ppermute | solution.py:451
  207.5 9.5 %collective-permute-start.42 = (bf16[2,96,768]{2,1,0:T(8,128)(2,1)S(1)}, bf16[2,96,768]{2,1,0:T(8,128)(2,1)S(1)}, u32[]{:S(2)}, u32[]{:S(2)}) collective-permute-start(bf16[2,96,768]{2,1,0:T(8,128)(2,1)S(1)} %dynamic-slice_bitcast_fusion.13), channel_id=1, source_target_pairs={{0,8},{8,0},{16,24},{24,16},{1,9},{9,1},{17,25},{25,17},{2,10},{10... | collective-permute-start | bytes 884744 | tf_op jit(solution)/shard_map/ppermute | solution.py:447
  210.2 42.7 %collective-permute-start.50 = (bf16[192,1536]{1,0:T(8,128)(2,1)S(1)}, bf16[192,1536]{1,0:T(8,128)(2,1)S(1)}, u32[]{:S(2)}, u32[]{:S(2)}) collective-permute-start(bf16[192,1536]{1,0:T(8,128)(2,1)S(1)} %dynamic-slice_bitcast_fusion.4), channel_id=1, source_target_pairs={{0,16},{8,24},{16,0},{24,8},{1,17},{9,25},{17,1},{25,9},{2,18},{10... | collective-permute-start | bytes 1769480 | tf_op jit(solution)/shard_map/ppermute | solution.py:447
  217.1 12.0 %collective-permute-start.43 = (bf16[96,768]{1,0:T(8,128)(2,1)S(1)}, bf16[96,768]{1,0:T(8,128)(2,1)S(1)}, u32[]{:S(2)}, u32[]{:S(2)}) collective-permute-start(bf16[96,768]{1,0:T(8,128)(2,1)S(1)} %dynamic-slice_bitcast_fusion.23), channel_id=1, source_target_pairs={{0,16},{8,24},{16,0},{24,8},{1,17},{9,25},{17,1},{25,9},{2,18},{10... | collective-permute-start | bytes 442376 | tf_op jit(solution)/shard_map/ppermute | solution.py:447
  229.1 4.4 %collective-permute-start.44 = (bf16[2,24,768]{2,1,0:T(8,128)(2,1)S(1)}, bf16[2,24,768]{2,1,0:T(8,128)(2,1)S(1)}, u32[]{:S(2)}, u32[]{:S(2)}) collective-permute-start(bf16[2,24,768]{2,1,0:T(8,128)(2,1)S(1)} %dynamic-slice_bitcast_fusion.25), channel_id=1, source_target_pairs={{0,2},{1,3},{2,0},{3,1},{4,6},{5,7},{6,4},{7,5},{8,10},{9,11},{10,... | collective-permute-start | bytes 221192 | tf_op jit(solution)/shard_map/ppermute | solution.py:455
  231.3 21.8 %collective-permute-start.57 = (bf16[384,768]{1,0:T(8,128)(2,1)S(1)}, bf16[384,768]{1,0:T(8,128)(2,1)S(1)}, u32[]{:S(2)}, u32[]{:S(2)}) collective-permute-start(bf16[384,768]{1,0:T(8,128)(2,1)S(1)} %dynamic-slice_bitcast_fusion.3), channel_id=1, source_target_pairs={{0,8},{8,0},{16,24},{24,16},{1,9},{9,1},{17,25},{25,17},{2,10},{10... | collective-permute-start | bytes 1769480 | tf_op jit(solution)/shard_map/ppermute | solution.py:447
  233.6 4.9 %collective-permute-start.45 = (bf16[24,768]{1,0:T(8,128)(2,1)S(1)}, bf16[24,768]{1,0:T(8,128)(2,1)S(1)}, u32[]{:S(2)}, u32[]{:S(2)}) collective-permute-start(bf16[24,768]{1,0:T(8,128)(2,1)S(1)} %dynamic-slice_bitcast_fusion.26), channel_id=1, source_target_pairs={{0,4},{1,5},{2,6},{3,7},{4,0},{5,1},{6,2},{7,3},{8,12},{9,13},{10,... | collective-permute-start | bytes 110600 | tf_op jit(solution)/shard_map/ppermute | solution.py:455
  238.5 5.0 %collective-permute-start.46 = (bf16[24,768]{1,0:T(8,128)(2,1)S(1)}, bf16[24,768]{1,0:T(8,128)(2,1)S(1)}, u32[]{:S(2)}, u32[]{:S(2)}) collective-permute-start(bf16[24,768]{1,0:T(8,128)(2,1)S(1)} %bitcast_add_fusion.17), channel_id=1, source_target_pairs={{0,4},{1,5},{2,6},{3,7},{4,0},{5,1},{6,2},{7,3},{8,12},{9,13},{10,... | collective-permute-start | bytes 110600 | tf_op jit(solution)/shard_map/ppermute | solution.py:455
  240.6 7.4 %collective-permute-start.32 = (bf16[2,304,192]{1,2,0:T(8,128)(2,1)S(1)}, bf16[2,304,192]{1,2,0:T(8,128)(2,1)S(1)}, u32[]{:S(2)}, u32[]{:S(2)}) collective-permute-start(bf16[2,304,192]{1,2,0:T(8,128)(2,1)S(1)} %dynamic-slice_bitcast_fusion.14), channel_id=1, source_target_pairs={{0,16},{8,24},{16,0},{24,8},{1,17},{9,25},{17,1},{25,9},{2,18},{10... | collective-permute-start | bytes 700424 | tf_op jit(solution)/shard_map/ppermute | solution.py:447
  247.9 11.7 %collective-permute-start.48 = (bf16[96,768]{1,0:T(8,128)(2,1)S(1)}, bf16[96,768]{1,0:T(8,128)(2,1)S(1)}, u32[]{:S(2)}, u32[]{:S(2)}) collective-permute-start(bf16[96,768]{1,0:T(8,128)(2,1)S(1)} %bitcast.356), channel_id=1, source_target_pairs={{0,1},{1,0},{2,3},{3,2},{4,5},{5,4},{6,7},{7,6},{8,9},{9,8},{10,11... | collective-permute-start | bytes 442376 | tf_op jit(solution)/shard_map/ppermute | solution.py:451
  248.1 6.3 %collective-permute-start.33 = (bf16[304,192]{0,1:T(8,128)(2,1)S(1)}, bf16[304,192]{0,1:T(8,128)(2,1)S(1)}, u32[]{:S(2)}, u32[]{:S(2)}) collective-permute-start(bf16[304,192]{0,1:T(8,128)(2,1)S(1)} %dynamic-slice_bitcast_fusion.24), channel_id=1, source_target_pairs={{0,8},{8,0},{16,24},{24,16},{1,9},{9,1},{17,25},{25,17},{2,10},{10... | collective-permute-start | bytes 350216 | tf_op jit(solution)/shard_map/ppermute | solution.py:447
  250.4 42.7 %collective-permute-start.29 = (bf16[256,768]{1,0:T(8,128)(2,1)S(1)}, bf16[256,768]{1,0:T(8,128)(2,1)S(1)}, u32[]{:S(2)}, u32[]{:S(2)}) collective-permute-start(bf16[256,768]{1,0:T(8,128)(2,1)S(1)} %dynamic-slice_bitcast_fusion.8), channel_id=1, source_target_pairs={{0,4},{1,5},{2,6},{3,7},{4,0},{5,1},{6,2},{7,3},{8,12},{9,13},{10,... | collective-permute-start | bytes 1179656 | tf_op jit(solution)/shard_map/ppermute | solution.py:455
  253.0 33.5 %collective-permute-start.51 = (bf16[2,48,1536]{2,1,0:T(8,128)(2,1)S(1)}, bf16[2,48,1536]{2,1,0:T(8,128)(2,1)S(1)}, u32[]{:S(2)}, u32[]{:S(2)}) collective-permute-start(bf16[2,48,1536]{2,1,0:T(8,128)(2,1)S(1)} %dynamic-slice_bitcast_fusion.12), channel_id=1, source_target_pairs={{0,2},{1,3},{2,0},{3,1},{4,6},{5,7},{6,4},{7,5},{8,10},{9,11},{10,... | collective-permute-start | bytes 884744 | tf_op jit(solution)/shard_map/ppermute | solution.py:455
  254.4 17.5 %collective-permute-start.34 = (bf16[304,192]{0,1:T(8,128)(2,1)S(1)}, bf16[304,192]{0,1:T(8,128)(2,1)S(1)}, u32[]{:S(2)}, u32[]{:S(2)}) collective-permute-start(bf16[304,192]{0,1:T(8,128)(2,1)S(1)} %bitcast_add_fusion.15), channel_id=1, source_target_pairs={{0,2},{1,3},{2,4},{3,5},{4,6},{5,7},{8,10},{9,11},{10,12},{11,13},... | collective-permute-start | bytes 350216 | tf_op jit(solution)/shard_map/ppermute | solution.py:459
  258.3 18.0 %collective-permute-start.37 = (bf16[304,192]{0,1:T(8,128)(2,1)S(1)}, bf16[304,192]{0,1:T(8,128)(2,1)S(1)}, u32[]{:S(2)}, u32[]{:S(2)}) collective-permute-start(bf16[304,192]{0,1:T(8,128)(2,1)S(1)} %bitcast_add_fusion.15), channel_id=1, source_target_pairs={{2,0},{3,1},{4,2},{5,3},{6,4},{7,5},{10,8},{11,9},{12,10},{13,11},... | collective-permute-start | bytes 350216 | tf_op jit(solution)/shard_map/ppermute | solution.py:459
  259.6 29.1 %collective-permute-start.58 = (bf16[2,96,768]{2,1,0:T(8,128)(2,1)S(1)}, bf16[2,96,768]{2,1,0:T(8,128)(2,1)S(1)}, u32[]{:S(2)}, u32[]{:S(2)}) collective-permute-start(bf16[2,96,768]{2,1,0:T(8,128)(2,1)S(1)} %dynamic-slice_bitcast_fusion.11), channel_id=1, source_target_pairs={{0,2},{1,3},{2,0},{3,1},{4,6},{5,7},{6,4},{7,5},{8,10},{9,11},{10,... | collective-permute-start | bytes 884744 | tf_op jit(solution)/shard_map/ppermute | solution.py:455
  271.9 8.7 %collective-permute-start.35 = (bf16[304,192]{0,1:T(8,128)(2,1)S(1)}, bf16[304,192]{0,1:T(8,128)(2,1)S(1)}, u32[]{:S(2)}, u32[]{:S(2)}) collective-permute-start(bf16[304,192]{0,1:T(8,128)(2,1)S(1)} %collective-permute-done.34), channel_id=1, source_target_pairs={{0,2},{1,3},{2,4},{3,5},{4,6},{5,7},{8,10},{9,11},{10,12},{11,13},... | collective-permute-start | bytes 350216 | tf_op jit(solution)/shard_map/ppermute | solution.py:459
  276.3 8.7 %collective-permute-start.38 = (bf16[304,192]{0,1:T(8,128)(2,1)S(1)}, bf16[304,192]{0,1:T(8,128)(2,1)S(1)}, u32[]{:S(2)}, u32[]{:S(2)}) collective-permute-start(bf16[304,192]{0,1:T(8,128)(2,1)S(1)} %collective-permute-done.37), channel_id=1, source_target_pairs={{2,0},{3,1},{4,2},{5,3},{6,4},{7,5},{10,8},{11,9},{12,10},{13,11},... | collective-permute-start | bytes 350216 | tf_op jit(solution)/shard_map/ppermute | solution.py:459
  280.7 9.1 %collective-permute-start.36 = (bf16[304,192]{0,1:T(8,128)(2,1)S(1)}, bf16[304,192]{0,1:T(8,128)(2,1)S(1)}, u32[]{:S(2)}, u32[]{:S(2)}) collective-permute-start(bf16[304,192]{0,1:T(8,128)(2,1)S(1)} %collective-permute-done.35), channel_id=1, source_target_pairs={{0,2},{1,3},{2,4},{3,5},{4,6},{5,7},{8,10},{9,11},{10,12},{11,13},... | collective-permute-start | bytes 350216 | tf_op jit(solution)/shard_map/ppermute | solution.py:459
  285.1 7.8 %collective-permute-start.39 = (bf16[304,192]{0,1:T(8,128)(2,1)S(1)}, bf16[304,192]{0,1:T(8,128)(2,1)S(1)}, u32[]{:S(2)}, u32[]{:S(2)}) collective-permute-start(bf16[304,192]{0,1:T(8,128)(2,1)S(1)} %collective-permute-done.38), channel_id=1, source_target_pairs={{2,0},{3,1},{4,2},{5,3},{6,4},{7,5},{10,8},{11,9},{12,10},{13,11},... | collective-permute-start | bytes 350216 | tf_op jit(solution)/shard_map/ppermute | solution.py:459
  286.6 16.0 %collective-permute-start.52 = (bf16[48,1536]{1,0:T(8,128)(2,1)S(1)}, bf16[48,1536]{1,0:T(8,128)(2,1)S(1)}, u32[]{:S(2)}, u32[]{:S(2)}) collective-permute-start(bf16[48,1536]{1,0:T(8,128)(2,1)S(1)} %dynamic-slice_bitcast_fusion.22), channel_id=1, source_target_pairs={{0,4},{1,5},{2,6},{3,7},{4,0},{5,1},{6,2},{7,3},{8,12},{9,13},{10,... | collective-permute-start | bytes 442376 | tf_op jit(solution)/shard_map/ppermute | solution.py:455
  288.9 23.0 %collective-permute-start.59 = (bf16[96,768]{1,0:T(8,128)(2,1)S(1)}, bf16[96,768]{1,0:T(8,128)(2,1)S(1)}, u32[]{:S(2)}, u32[]{:S(2)}) collective-permute-start(bf16[96,768]{1,0:T(8,128)(2,1)S(1)} %dynamic-slice_bitcast_fusion.21), channel_id=1, source_target_pairs={{0,4},{1,5},{2,6},{3,7},{4,0},{5,1},{6,2},{7,3},{8,12},{9,13},{10,... | collective-permute-start | bytes 442376 | tf_op jit(solution)/shard_map/ppermute | solution.py:455
  293.0 36.7 %collective-permute-start.40 = (bf16[4,304,192]{1,2,0:T(8,128)(2,1)S(1)}, bf16[4,304,192]{1,2,0:T(8,128)(2,1)S(1)}, u32[]{:S(2)}, u32[]{:S(2)}) collective-permute-start(bf16[4,304,192]{1,2,0:T(8,128)(2,1)S(1)} %constant_dynamic-slice_fusion), channel_id=1, source_target_pairs={{0,1},{1,0},{2,3},{3,2},{4,5},{5,4},{6,7},{7,6},{8,9},{9,8},{10,11... | collective-permute-start | bytes 1400840 | tf_op jit(solution)/shard_map/ppermute | solution.py:451
  294.0 31.2 %collective-permute-start.30 = (f32[128,768]{1,0:T(8,128)S(1)}, f32[128,768]{1,0:T(8,128)S(1)}, u32[]{:S(2)}, u32[]{:S(2)}) collective-permute-start(f32[128,768]{1,0:T(8,128)S(1)} %get-tuple-element.90), channel_id=1, source_target_pairs={{0,1},{1,0},{2,3},{3,2},{4,5},{5,4},{6,7},{7,6},{8,9},{9,8},{10,11... | collective-permute-start | bytes 1179656 | tf_op jit(solution)/shard_map/ppermute | solution.py:451
  302.6 12.4 %collective-permute-start.53 = (bf16[48,1536]{1,0:T(8,128)(2,1)S(1)}, bf16[48,1536]{1,0:T(8,128)(2,1)S(1)}, u32[]{:S(2)}, u32[]{:S(2)}) collective-permute-start(bf16[48,1536]{1,0:T(8,128)(2,1)S(1)} %bitcast_add_fusion.13), channel_id=1, source_target_pairs={{0,4},{1,5},{2,6},{3,7},{4,0},{5,1},{6,2},{7,3},{8,12},{9,13},{10,... | collective-permute-start | bytes 442376 | tf_op jit(solution)/shard_map/ppermute | solution.py:455
  311.9 6.2 %collective-permute-start.60 = (bf16[96,768]{1,0:T(8,128)(2,1)S(1)}, bf16[96,768]{1,0:T(8,128)(2,1)S(1)}, u32[]{:S(2)}, u32[]{:S(2)}) collective-permute-start(bf16[96,768]{1,0:T(8,128)(2,1)S(1)} %bitcast_add_fusion.12), channel_id=1, source_target_pairs={{0,4},{1,5},{2,6},{3,7},{4,0},{5,1},{6,2},{7,3},{8,12},{9,13},{10,... | collective-permute-start | bytes 442376 | tf_op jit(solution)/shard_map/ppermute | solution.py:455
  315.0 10.0 %collective-permute-start.54 = (bf16[2,48,1536]{2,1,0:T(8,128)(2,1)S(1)}, bf16[2,48,1536]{2,1,0:T(8,128)(2,1)S(1)}, u32[]{:S(2)}, u32[]{:S(2)}) collective-permute-start(bf16[2,48,1536]{2,1,0:T(8,128)(2,1)S(1)} %maximum_select_fusion.12), channel_id=1, source_target_pairs={{0,2},{1,3},{2,0},{3,1},{4,6},{5,7},{6,4},{7,5},{8,10},{9,11},{10,... | collective-permute-start | bytes 884744 | tf_op jit(solution)/shard_map/ppermute | solution.py:455
  318.1 11.3 %collective-permute-start.61 = (bf16[2,96,768]{2,1,0:T(8,128)(2,1)S(1)}, bf16[2,96,768]{2,1,0:T(8,128)(2,1)S(1)}, u32[]{:S(2)}, u32[]{:S(2)}) collective-permute-start(bf16[2,96,768]{2,1,0:T(8,128)(2,1)S(1)} %maximum_select_fusion.14), channel_id=1, source_target_pairs={{0,2},{1,3},{2,0},{3,1},{4,6},{5,7},{6,4},{7,5},{8,10},{9,11},{10,... | collective-permute-start | bytes 884744 | tf_op jit(solution)/shard_map/ppermute | solution.py:455
  325.1 21.5 %collective-permute-start.55 = (bf16[192,1536]{1,0:T(8,128)(2,1)S(1)}, bf16[192,1536]{1,0:T(8,128)(2,1)}, u32[]{:S(2)}, u32[]{:S(2)}) collective-permute-start(bf16[192,1536]{1,0:T(8,128)(2,1)S(1)} %bitcast.319), channel_id=1, source_target_pairs={{0,1},{1,0},{2,3},{3,2},{4,5},{5,4},{6,7},{7,6},{8,9},{9,8},{10,11... | collective-permute-start | bytes 1769480 | tf_op jit(solution)/shard_map/ppermute | solution.py:451
  329.6 24.2 %collective-permute-start.62 = (bf16[384,768]{1,0:T(8,128)(2,1)S(1)}, bf16[384,768]{1,0:T(8,128)(2,1)}, u32[]{:S(2)}, u32[]{:S(2)}) collective-permute-start(bf16[384,768]{1,0:T(8,128)(2,1)S(1)} %bitcast.320), channel_id=1, source_target_pairs={{0,1},{1,0},{2,3},{3,2},{4,5},{5,4},{6,7},{7,6},{8,9},{9,8},{10,11... | collective-permute-start | bytes 1769480 | tf_op jit(solution)/shard_map/ppermute | solution.py:451
  (59 other events, 458.2 us)

commit v2 on v0

--- a/solution.py
+++ b/solution.py
@@ -1,6 +1,8 @@
 import jax
 import jax.numpy as jnp
 from jax import lax
+from jax.experimental import pallas as pl
+from jax.experimental.pallas import tpu as pltpu
 from jax.sharding import PartitionSpec as P
 
 D = 768
@@ -65,7 +67,7 @@
     return loop_state
 
 
-def local(tokens, gain_one, w_qkv, w_out, gain_two, w_up, w_down, cotangent):
+def local_any(tokens, gain_one, w_qkv, w_out, gain_two, w_up, w_down, cotangent):
     gathered = (
         lax.all_gather(gain_one, "wshard", axis=0, tiled=True),
         lax.all_gather(w_qkv, "wshard", axis=0, tiled=True),
@@ -251,6 +253,803 @@
     )
 
 
+BF = jnp.bfloat16
+F32 = jnp.float32
+TILE = 256
+SHARD = D // 4
+OWN_HEADS = HEADS // 4
+OWN = OWN_HEADS * HEAD_DIM
+MIX = 3 * OWN
+HEAD_ROWS = 160
+PART = SHARD // 2
+QUART = SHARD // 4
+HALF = D // 2
+VMEM_LIMIT = 56 * 1024 * 1024
+WHOLE = pl.BlockSpec(memory_space=pltpu.VMEM)
+ANYWHERE = pl.BlockSpec(memory_space=pl.ANY)
+
+
+def nn(a, b):
+    return lax.dot_general(a, b, (((1,), (0,)), ((), ())), preferred_element_type=F32)
+
+
+def nt(a, b):
+    return lax.dot_general(a, b, (((1,), (1,)), ((), ())), preferred_element_type=F32)
+
+
+def normalised(x):
+    centred = x - jnp.mean(x, axis=-1, keepdims=True)
+    variance = jnp.mean(centred * centred, axis=-1, keepdims=True)
+    inverse = lax.rsqrt(variance + EPSILON)
+    return centred * inverse, inverse
+
+
+def norm_back(xhat, inverse, gain, dy):
+    g = dy * gain
+    mean_g = jnp.mean(g, axis=-1, keepdims=True)
+    mean_gx = jnp.mean(g * xhat, axis=-1, keepdims=True)
+    return (g - mean_g - xhat * mean_gx) * inverse
+
+
+def causal_tile():
+    rows = lax.broadcasted_iota(jnp.int32, (TILE, TILE), 0)
+    cols = lax.broadcasted_iota(jnp.int32, (TILE, TILE), 1)
+    return rows <= cols
+
+
+def call(kernel, name, ins, outs, scratch, flops, args, out_specs=None):
+    moved = sum(a.size * a.dtype.itemsize for a in args)
+    return pl.pallas_call(
+        kernel,
+        in_specs=ins,
+        out_specs=out_specs or [WHOLE] * len(outs),
+        out_shape=[jax.ShapeDtypeStruct(shape, kind) for shape, kind in outs],
+        scratch_shapes=scratch,
+        compiler_params=pltpu.CompilerParams(vmem_limit_bytes=VMEM_LIMIT),
+        cost_estimate=pl.CostEstimate(flops=1000, bytes_accessed=1000, transcendentals=0),
+        name=name,
+    )(*args)
+
+
+def shard_rows_of(pieces, which, first, count):
+    if which < 3:
+        return pieces[which].at[pl.ds(first, count)]
+    half = pieces[3].shape[0]
+    if first < half:
+        return pieces[3].at[pl.ds(first, count)]
+    return pieces[4].at[pl.ds(first - half, count)]
+
+
+def run_copies(pairs, sems):
+    copies = [pltpu.make_async_copy(src, dst, sems.at[i]) for i, (src, dst) in enumerate(pairs)]
+    for copy in copies:
+        copy.start()
+    for copy in copies:
+        copy.wait()
+
+
+def attend_kernel(own, pair, near, far, mid_near, mid_far, w0, w1, w2, w3, w4, gain_ref,
+                  normed_ref, kv_ref, mixt_ref, att_ref, low_ref, lse_ref, wfull_ref, x_ref, s_ref, sems, wsems):
+    z = lax.axis_index("ctx") // 2
+    place = lax.axis_index("wshard")
+    end = (z == 0) | (z == 3)
+    near_slot = jnp.where(z < 2, 2, 1)
+    far_slot = jnp.where(z < 2, 3, 0)
+
+    def line_copies(do):
+        do(pltpu.make_async_copy(own, x_ref.at[z], sems.at[0]))
+        do(pltpu.make_async_copy(pair, x_ref.at[jnp.bitwise_xor(z, 1)], sems.at[1]))
+
+        @pl.when(end)
+        def _():
+            do(pltpu.make_async_copy(near, x_ref.at[near_slot], sems.at[2]))
+            do(pltpu.make_async_copy(far, x_ref.at[far_slot], sems.at[3]))
+
+        @pl.when(jnp.logical_not(end))
+        def _():
+            do(pltpu.make_async_copy(mid_near, x_ref.at[near_slot], sems.at[2]))
+            do(pltpu.make_async_copy(mid_far, x_ref.at[far_slot], sems.at[3]))
+
+    line_copies(lambda copy: copy.start())
+    pieces = (w0, w1, w2, w3, w4)
+    half = w3.shape[0]
+    pairs = []
+    for k in range(4):
+        to = pl.multiple_of(jnp.bitwise_xor(place, k) * SHARD, SHARD)
+        if k < 3:
+            pairs.append((shard_rows_of(pieces, k, 0, SHARD), wfull_ref.at[pl.ds(to, SHARD)]))
+        else:
+            pairs.append((w3, wfull_ref.at[pl.ds(to, half)]))
+            pairs.append((w4.at[pl.ds(0, SHARD - half)], wfull_ref.at[pl.ds(to + half, SHARD - half)]))
+    run_copies(pairs, wsems)
+    line_copies(lambda copy: copy.wait())
+    for row in range(4):
+        here = slice(row * TILE, (row + 1) * TILE)
+        xhat, _ = normalised(x_ref[row].astype(F32))
+        normed = (xhat * gain_ref[...]).astype(BF)
+        normed_ref[here, :] = normed
+        mix = nn(normed, wfull_ref[...]).astype(BF)
+        mixt_ref[:, here] = mix.T
+        for h in range(OWN_HEADS):
+            kv_ref[h, here, 0:HEAD_DIM] = mix[:, OWN + h * HEAD_DIM : OWN + (h + 1) * HEAD_DIM]
+            kv_ref[h, here, HEAD_DIM:] = mix[:, 2 * OWN + h * HEAD_DIM : 2 * OWN + (h + 1) * HEAD_DIM]
+
+    @pl.loop(0, OWN_HEADS)
+    def _(h):
+        base = pl.multiple_of(h * HEAD_DIM, HEAD_DIM)
+        for block in range(4):
+            here = slice(block * TILE, (block + 1) * TILE)
+            queries = mixt_ref[pl.ds(base, HEAD_DIM), here] * BF(HEAD_DIM**-0.5)
+            top = jnp.zeros((1, TILE), F32)
+            for other in range(block + 1):
+                there = slice(other * TILE, (other + 1) * TILE)
+                s = nn(kv_ref[h, there, 0:HEAD_DIM], queries)
+                s_ref[there, :] = s
+                size = jnp.abs(s)
+                if other == block:
+                    size = jnp.where(causal_tile(), size, 0.0)
+                top = jnp.maximum(top, jnp.max(size, axis=0, keepdims=True))
+            top = jnp.sqrt(top * top + 1.0)
+            total = jnp.zeros((1, TILE), F32)
+            acc = jnp.zeros((HEAD_DIM, TILE), F32)
+            for other in range(block + 1):
+                there = slice(other * TILE, (other + 1) * TILE)
+                s = s_ref[there, :]
+                square = s * s + 1.0
+                r = lax.rsqrt(square)
+                p = jnp.exp(square * r - top)
+                if other == block:
+                    p = jnp.where(causal_tile(), p, 0.0)
+                total = total + jnp.sum(p, axis=0, keepdims=True)
+                signed = (s * r * p).astype(BF)
+                acc = acc + nn(mixt_ref[pl.ds(2 * OWN + base, HEAD_DIM), there], signed)
+            att = acc / total
+            att_ref[pl.ds(base, HEAD_DIM), here] = att
+            low_ref[block, pl.ds(base, HEAD_DIM), :] = att.astype(BF)
+            lse_ref[pl.ds(h, 1), here] = top + jnp.log(total)
+
+
+def attend(line, pieces, gain):
+    length = 4 * TILE
+    return call(
+        attend_kernel,
+        "attend",
+        [ANYWHERE] * 11 + [WHOLE],
+        [
+            ((length, D), BF),
+            ((OWN_HEADS, length, 2 * HEAD_DIM), BF),
+            ((MIX, length), BF),
+            ((OWN, length), F32),
+            ((4, OWN, TILE), BF),
+            ((8, length), F32),
+            ((D, MIX), BF),
+        ],
+        [
+            pltpu.VMEM((4, TILE, D), BF),
+            pltpu.VMEM((length, TILE), F32),
+            pltpu.SemaphoreType.DMA((4,)),
+            pltpu.SemaphoreType.DMA((5,)),
+        ],
+        3 * 10**9,
+        (*line, *pieces, gain),
+    )
+
+
+def project_kernel(att_ref, x_ref, gain_ref, b0, b1, b2, b3, hidden_ref, normed_ref, wout_ref, sems):
+    place = lax.axis_index("wshard")
+    pairs = []
+    for k, (ref, first) in enumerate(((b0, TILE), (b1, TILE), (b2, TILE), (b3, b3.shape[0] - SHARD))):
+        to = pl.multiple_of(jnp.bitwise_xor(place, k) * SHARD, SHARD)
+        pairs.append((ref.at[pl.ds(first, SHARD)], wout_ref.at[pl.ds(to, SHARD)]))
+    run_copies(pairs, sems)
+    hidden = x_ref[...].astype(F32) + nn(att_ref[...].T, wout_ref[...])
+    hidden_ref[...] = hidden
+    xhat, _ = normalised(hidden)
+    normed_ref[...] = (xhat * gain_ref[...]).astype(BF)
+
+
+def project(att_home, x_block, gain, shared):
+    rows = x_block.shape[0]
+    own, from_x, from_y, _, low = shared
+    return call(
+        project_kernel,
+        "project",
+        [WHOLE] * 3 + [ANYWHERE] * 4,
+        [((rows, D), F32), ((rows, D), BF), ((D, D), BF)],
+        [pltpu.SemaphoreType.DMA((4,))],
+        3 * 10**8,
+        (att_home, x_block, gain, own, from_x, from_y, low),
+    )
+
+
+SLOPE = (2.0 / 3.141592653589793) ** 0.5
+
+
+def feed_rows(n, cot, up_ref, down_ref, active_ref, dup_ref, here):
+    for first in range(0, D, TILE):
+        cols = slice(first, first + TILE)
+        u = nn(n, up_ref[:, cols])
+        square = u * u
+        t = jnp.tanh(SLOPE * (u + 0.044715 * (square * u)))
+        side = 0.5 + 0.5 * t
+        active_ref[here, cols] = (u * side).astype(BF)
+        grad = side + (0.5 * SLOPE) * u * (1.0 - t * t) * (1.0 + 0.134145 * square)
+        dup_ref[here, cols] = (grad * nt(cot, down_ref[cols, :])).astype(BF)
+    return nn(active_ref[here, :], down_ref[...]), nt(dup_ref[here, :], up_ref[...])
+
+
+def feed_own_kernel(n_ref, cot_ref, up_ref, down_ref, active_ref, dup_ref, out_ref, dout_ref):
+    out_ref[...], dout_ref[...] = feed_rows(
+        n_ref[...], cot_ref[0:TILE, :], up_ref, down_ref, active_ref, dup_ref, slice(0, TILE)
+    )
+
+
+def feed_own(n, shared, up, down):
+    return call(
+        feed_own_kernel,
+        "feed_own",
+        [WHOLE] * 4,
+        [((TILE, D), BF), ((TILE, D), BF), ((TILE, D), F32), ((TILE, D), F32)],
+        [],
+        2 * 10**9,
+        (n, shared[0], up, down),
+    )
+
+
+def feed_near_kernel(nx_ref, ny_ref, cx_ref, cy_ref, up_ref, down_ref, active_ref, dup_ref, out_ref, dout_ref):
+    for k, (n_ref, cot_ref) in enumerate(((nx_ref, cx_ref), (ny_ref, cy_ref))):
+        here = slice(k * TILE, (k + 1) * TILE)
+        out, dout = feed_rows(n_ref[...], cot_ref[0:TILE, :], up_ref, down_ref, active_ref, dup_ref, here)
+        out_ref[here, :], dout_ref[here, :] = out.astype(BF), dout.astype(BF)
+
+
+def feed_near(nx, ny, shared, up, down):
+    return call(
+        feed_near_kernel,
+        "feed_near",
+        [WHOLE] * 6,
+        [((2 * TILE, D), BF)] * 4,
+        [],
+        4 * 10**9,
+        (nx, ny, shared[1], shared[2], up, down),
+    )
+
+
+def feed_far_kernel(na_ref, nb_ref, ca_ref, cb_ref, out_ref, dout_ref, up_ref, down_ref,
+                    active_ref, dup_ref, oa_ref, oaf_ref, ob_ref, obf_ref, da_ref, daf_ref, db_ref, dbf_ref):
+    n = jnp.concatenate([na_ref[...], nb_ref[...]])
+    first = ca_ref.shape[0]
+    cot = jnp.concatenate([ca_ref[...], cb_ref[0 : TILE - first, :]])
+    half = TILE // 2
+    out, dout = feed_rows(n, cot, up_ref, down_ref, active_ref, dup_ref, slice(0, TILE))
+    for far, near, a, af, b, bf in (
+        (out, out_ref, oa_ref, oaf_ref, ob_ref, obf_ref),
+        (dout, dout_ref, da_ref, daf_ref, db_ref, dbf_ref),
+    ):
+        far = far.astype(BF)
+        a[0], a[1] = near[0:half, :], far[0:half]
+        b[0], b[1] = near[TILE + half :, :], far[half:]
+        af[...] = near[TILE : TILE + half, :]
+        bf[...] = near[half:TILE, :]
+
+
+def feed_far(na, nb, shared, out, dout, up, down):
+    half = TILE // 2
+    return call(
+        feed_far_kernel,
+        "feed_far",
+        [WHOLE] * 8,
+        [((TILE, D), BF)] * 2 + [((2, half, D), BF), ((half, D), BF)] * 4,
+        [],
+        2 * 10**9,
+        (na, nb, shared[3], shared[4], out, dout, up, down),
+    )
+
+
+def feed_grads_kernel(n0, n1, n2, n3, n4, c0, c1, c2, c3, c4, a0, a1, a2, d0, d1, d2,
+                      shares_ref, nt_ref, cot_ref, at_ref, dup_ref):
+    first = c3.shape[0]
+    for k, piece in enumerate((n0, n1, n2)):
+        nt_ref[:, k * TILE : (k + 1) * TILE] = piece[...].T
+    nt_ref[:, 3 * TILE :] = jnp.concatenate([n3[...], n4[...]]).T
+    for k, piece in enumerate((c0, c1, c2)):
+        cot_ref[k * TILE : (k + 1) * TILE] = piece[0:TILE, :]
+    cot_ref[3 * TILE : 3 * TILE + first] = c3[...]
+    cot_ref[3 * TILE + first :] = c4[0 : TILE - first, :]
+    at_ref[:, 0:TILE] = a0[...].T
+    at_ref[:, TILE : 3 * TILE] = a1[...].T
+    at_ref[:, 3 * TILE :] = a2[...].T
+    dup_ref[0:TILE] = d0[...]
+    dup_ref[TILE : 3 * TILE] = d1[...]
+    dup_ref[3 * TILE :] = d2[...]
+    rows = D // 8
+    for k in range(8):
+        g = nn(at_ref[k * rows : (k + 1) * rows, :], cot_ref[...]).astype(BF)
+        for side in range(2):
+            shares_ref[k, SHARD + side * rows : SHARD + (side + 1) * rows] = g[:, side * HALF : (side + 1) * HALF]
+    for to in range(4):
+        g = nn(nt_ref[to * SHARD : (to + 1) * SHARD, :], dup_ref[...]).astype(BF)
+        for k in range(8):
+            r, c = (k // 2) * QUART, (k % 2) * HALF
+            shares_ref[k, to * QUART : (to + 1) * QUART] = g[r : r + QUART, c : c + HALF]
+
+
+def feed_grads(ns, shared, actives, dups):
+    length = 4 * TILE
+    return call(
+        feed_grads_kernel,
+        "feed_grads",
+        [WHOLE] * 16,
+        [((8, 2 * SHARD, HALF), BF)],
+        [
+            pltpu.VMEM((D, length), BF),
+            pltpu.VMEM((length, D), BF),
+            pltpu.VMEM((D, length), BF),
+            pltpu.VMEM((length, D), BF),
+        ],
+        3 * 10**9,
+        (*ns, *shared, *actives, *dups),
+    )[0]
+
+
+def summed(keep_ref, a_ref, a_more_ref, b_ref, b_more_ref):
+    first = a_ref[0].astype(F32) + a_more_ref[...].astype(F32)
+    second = b_ref[0].astype(F32) + b_more_ref[...].astype(F32)
+    return keep_ref[...] + jnp.concatenate([first, second])
+
+
+def give_kernel(hidden_ref, keep_ref, a_ref, a_more_ref, b_ref, b_more_ref, rkeep_ref, rsend_ref, result_ref, sems):
+    core = lax.axis_index("ctx") % 2
+    result = (hidden_ref[...] + summed(keep_ref, a_ref, a_more_ref, b_ref, b_more_ref)).astype(BF)
+    half = TILE // 2
+    result_ref[0], result_ref[1] = result[:half], result[half:]
+    run_copies(((result_ref.at[1 - core], rsend_ref), (result_ref.at[core], rkeep_ref)), sems)
+
+
+def give(hidden, keep, parts):
+    half = TILE // 2
+    return call(
+        give_kernel,
+        "give",
+        [WHOLE] * 6,
+        [((half, D), BF)] * 2,
+        [pltpu.VMEM((2, half, D), BF), pltpu.SemaphoreType.DMA((2,))],
+        10**6,
+        (hidden, keep, *parts),
+        [ANYWHERE] * 2,
+    )
+
+
+def turn_kernel(hidden_ref, gain_ref, dkeep_ref, a_ref, a_more_ref, b_ref, b_more_ref, cot_ref, wout_ref,
+                dhidden_ref, datt_ref, dbranch_ref, dgain_ref):
+    gain = gain_ref[...]
+    xhat, inverse = normalised(hidden_ref[...])
+    dy = summed(dkeep_ref, a_ref, a_more_ref, b_ref, b_more_ref)
+    dgain_ref[...] = jnp.sum(dy * xhat, axis=0, keepdims=True)
+    d_hidden = cot_ref[...].astype(F32) + norm_back(xhat, inverse, gain, dy)
+    dhidden_ref[...] = d_hidden
+    d_branch = d_hidden.astype(BF)
+    dbranch_ref[...] = d_branch
+    d_att = nt(wout_ref[...], d_branch).astype(BF)
+    for k in range(4):
+        datt_ref[k] = d_att[k * OWN : (k + 1) * OWN]
+
+
+def turn(hidden, gain, dkeep, parts, cot, w_out):
+    rows = hidden.shape[0]
+    return call(
+        turn_kernel,
+        "turn",
+        [WHOLE] * 9,
+        [((rows, D), F32), ((4, OWN, rows), BF), ((rows, D), BF), ((1, D), F32)],
+        [],
+        6 * 10**8,
+        (hidden, gain, dkeep, *parts, cot, w_out),
+    )
+
+
+def out_grad_kernel(att_ref, dbranch_ref, own_ref, far_ref, send_ref, grad_ref, sems):
+    place = lax.axis_index("wshard")
+    x, y = jnp.bitwise_and(place, 1), place // 2
+    for to in range(4):
+        g = nn(att_ref[to * SHARD : (to + 1) * SHARD, :], dbranch_ref[...])
+        grad_ref[to % 2, to // 2] = g.astype(BF)
+    pairs = (
+        (grad_ref.at[1 - x, y], send_ref.at[0]),
+        (grad_ref.at[1 - x, 1 - y], send_ref.at[1]),
+        (grad_ref.at[x, 1 - y], far_ref),
+        (grad_ref.at[x, y], own_ref),
+    )
+    run_copies(pairs, sems)
+
+
+def out_grad(att_home, d_branch):
+    return call(
+        out_grad_kernel,
+        "out_grad",
+        [WHOLE] * 2,
+        [((SHARD, D), BF), ((SHARD, D), BF), ((2, SHARD, D), BF)],
+        [pltpu.VMEM((2, 2, SHARD, D), BF), pltpu.SemaphoreType.DMA((4,))],
+        3 * 10**8,
+        (att_home, d_branch),
+        [ANYWHERE] * 3,
+    )
+
+
+def attend_back_kernel(kv_ref, mixt_ref, att_ref, lse_ref, dout_ref, normed_ref, w_ref, gain_ref, dgain_ref,
+                       f0_ref, f1_ref, f2_ref, f3_ref, gkeep_ref, gsend_ref,
+                       dq_ref, dk_ref, dv_ref, dm_ref, mix_ref, total_ref, first_ref, head_ref, sems):
+    length = normed_ref.shape[0]
+    scale = BF(HEAD_DIM**-0.5)
+    core = lax.axis_index("ctx") % 2
+    z = lax.axis_index("ctx") // 2
+    place = lax.axis_index("wshard")
+
+    @pl.loop(0, OWN_HEADS)
+    def _(h):
+        base = pl.multiple_of(h * HEAD_DIM, HEAD_DIM)
+        for block in range(4):
+            here = slice(block * TILE, (block + 1) * TILE)
+            queries = mixt_ref[pl.ds(base, HEAD_DIM), here] * scale
+            dout = dout_ref[block, pl.ds(base, HEAD_DIM), :]
+            delta = jnp.sum(dout.astype(F32) * att_ref[pl.ds(base, HEAD_DIM), here], axis=0, keepdims=True)
+            lse = lse_ref[pl.ds(h, 1), here]
+            acc = jnp.zeros((HEAD_DIM, TILE), F32)
+            for other in range(block + 1):
+                there = slice(other * TILE, (other + 1) * TILE)
+                s = nn(kv_ref[h, there, 0:HEAD_DIM], queries)
+                ds = nn(kv_ref[h, there, HEAD_DIM:], dout)
+                square = s * s + 1.0
+                r = lax.rsqrt(square)
+                chance = jnp.exp(square * r - lse)
+                if other == block:
+                    chance = jnp.where(causal_tile(), chance, 0.0)
+                tilted = s * r
+                signed = (tilted * chance).astype(BF)
+                slope = r * r * r + tilted * tilted
+                dsc = (chance * (ds * slope - tilted * delta)).astype(BF)
+                acc = acc + nn(mixt_ref[pl.ds(OWN + base, HEAD_DIM), there], dsc)
+                dk = nt(dsc, queries)
+                dv = nt(signed, dout)
+                if other == block:
+                    dk_ref[there, :] = dk
+                    dv_ref[there, :] = dv
+                else:
+                    dk_ref[there, :] += dk
+                    dv_ref[there, :] += dv
+            dq_ref[:, here] = acc * HEAD_DIM**-0.5
+        dm_ref[h, :, 0:HEAD_DIM] = dq_ref[...].T.astype(BF)
+        dm_ref[h, :, HEAD_DIM : 2 * HEAD_DIM] = dk_ref[...].astype(BF)
+        dm_ref[h, :, 2 * HEAD_DIM :] = dv_ref[...].astype(BF)
+
+    for h in range(OWN_HEADS):
+        for kind in range(3):
+            to = kind * OWN + h * HEAD_DIM
+            mix_ref[:, to : to + HEAD_DIM] = dm_ref[h, :, kind * HEAD_DIM : (kind + 1) * HEAD_DIM]
+    total_ref[...] = jnp.zeros_like(total_ref)
+    for block in range(4):
+        here = slice(block * TILE, (block + 1) * TILE)
+        first = nt(mix_ref[here, :], w_ref[...])
+        first_ref[block] = first.astype(BF)
+        total_ref[...] += jnp.sum(first * normed_ref[here, :].astype(F32), axis=0, keepdims=True)
+    outs = (f3_ref, f2_ref, f1_ref, f0_ref)
+    copies = [
+        pltpu.make_async_copy(first_ref.at[jnp.bitwise_xor(z, 3 - k)], ref, sems.at[k]) for k, ref in enumerate(outs)
+    ]
+    for copy in copies:
+        copy.start()
+    gain_one = total_ref[...] / gain_ref[...]
+    gain_two = dgain_ref[...]
+    for to in range(4):
+        e = jnp.bitwise_xor(place, to)
+        e_x, e_y = jnp.bitwise_and(e, 1), e // 2
+        g = nn(normed_ref[:, to * SHARD : (to + 1) * SHARD].T, mix_ref[...]).astype(BF)
+        span = slice(to * SHARD, (to + 1) * SHARD)
+        gains = jnp.concatenate([gain_one[:, span], gain_two[:, span], jnp.zeros((14, SHARD), F32)], axis=0)
+        gains = jnp.concatenate([gains, jnp.zeros((16, HALF - SHARD), F32)], axis=1).astype(BF)
+        for side in range(2):
+            at = side * PART
+            head_ref[side, e_y, e_x, 0:PART] = g[at : at + PART, 0:HALF]
+            head_ref[side, e_y, e_x, PART : PART + QUART, 0:OWN] = g[at : at + QUART, HALF:]
+            head_ref[side, e_y, e_x, PART : PART + QUART, OWN:] = g[at + QUART : at + PART, HALF:]
+            head_ref[side, e_y, e_x, PART + QUART :] = gains if side == 0 else jnp.zeros_like(gains)
+    more = [
+        pltpu.make_async_copy(head_ref.at[1 - core], gsend_ref, sems.at[4]),
+        pltpu.make_async_copy(head_ref.at[core], gkeep_ref, sems.at[5]),
+    ]
+    for copy in more:
+        copy.start()
+    for copy in copies + more:
+        copy.wait()
+
+
+def attend_back(kv, mixt, att, lse, dout, normed, w, gain, dgain):
+    length = normed.shape[0]
+    return call(
+        attend_back_kernel,
+        "attend_back",
+        [WHOLE] * 9,
+        [((TILE, D), BF)] * 4 + [((2, 2, HEAD_ROWS, HALF), BF)] * 2,
+        [
+            pltpu.VMEM((HEAD_DIM, length), F32),
+            pltpu.VMEM((length, HEAD_DIM), F32),
+            pltpu.VMEM((length, HEAD_DIM), F32),
+            pltpu.VMEM((OWN_HEADS, length, 3 * HEAD_DIM), BF),
+            pltpu.VMEM((length, MIX), BF),
+            pltpu.VMEM((1, D), F32),
+            pltpu.VMEM((4, TILE, D), BF),
+            pltpu.VMEM((2, 2, 2, HEAD_ROWS, HALF), BF),
+            pltpu.SemaphoreType.DMA((6,)),
+        ],
+        5 * 10**9,
+        (kv, mixt, att, lse, dout, normed, w, gain, dgain),
+        [ANYWHERE] * 6,
+    )
+
+
+def is_inner():
+    z = lax.axis_index("ctx") // 2
+    return (z == 1) | (z == 2)
+
+
+def last_kernel(first_ref, pair_ref, middle_ref, x_ref, gain_ref, dhidden_ref, keep_ref, send_ref, grad_ref, sems):
+    core = lax.axis_index("ctx") % 2
+    rows = x_ref.shape[0] // 2
+    dy = first_ref[...].astype(F32) + pair_ref[...].astype(F32)
+    dy = dy + jnp.where(is_inner(), middle_ref[...].astype(F32), 0.0)
+    xhat, inverse = normalised(x_ref[...].astype(F32))
+    grad = dhidden_ref[...] + norm_back(xhat, inverse, gain_ref[...], dy)
+    grad_ref[0], grad_ref[1] = grad[:rows], grad[rows:]
+    run_copies(((grad_ref.at[1 - core], send_ref), (grad_ref.at[core], keep_ref)), sems)
+
+
+def last(*args):
+    rows = TILE // 2
+    return call(
+        last_kernel,
+        "last",
+        [WHOLE] * 6,
+        [((rows, D), F32), ((rows, D), F32)],
+        [pltpu.VMEM((2, rows, D), F32), pltpu.SemaphoreType.DMA((2,))],
+        10**7,
+        args,
+        [ANYWHERE] * 2,
+    )
+
+
+def finish_kernel(*refs):
+    mine, theirs, (gup_ref, gdown_ref, gqkv_ref, gains_ref) = refs[:4], refs[4:8], refs[8:]
+    core = lax.axis_index("ctx") % 2
+    z = lax.axis_index("ctx") // 2
+    rows = D // 8
+    slots = (z, jnp.bitwise_xor(z, 1), jnp.where(z < 2, 2, 1), jnp.where(z < 2, 3, 0))
+    for group, side in ((mine, core), (theirs, 1 - core)):
+        for ref, slot in zip(group, slots):
+            at = pl.multiple_of(slot * QUART, 16)
+            for j in range(4):
+                to = pl.multiple_of(j * D + side * HALF, 128)
+                gup_ref[pl.ds(at, QUART), pl.ds(to, HALF)] = ref[j * QUART : (j + 1) * QUART].astype(F32)
+            at = pl.multiple_of((2 * slot + side) * rows, 32)
+            for half in range(2):
+                share = ref[SHARD + half * rows : SHARD + (half + 1) * rows]
+                gdown_ref[pl.ds(at, rows), half * HALF : (half + 1) * HALF] = share.astype(F32)
+    first = core == 0
+    mine, theirs = [[ref[2 * SHARD :].astype(F32) for ref in group] for group in (mine, theirs)]
+    low = [jnp.where(first, a, b) for a, b in zip(mine, theirs)]
+    high = [jnp.where(first, b, a) for a, b in zip(mine, theirs)]
+    gains_ref[...] = sum(block[PART + QUART :, 0:SHARD] for block in low)
+    for slot in range(4):
+        for side, group in enumerate((low, high)):
+            block = jnp.where(
+                slot == z, group[0], jnp.where(slot == slots[1], group[1], jnp.where(slot == slots[2], group[2], group[3]))
+            )
+            at, to = side * PART, slot * OWN
+            gqkv_ref[at : at + PART, to : to + OWN] = block[0:PART, 0:OWN]
+            gqkv_ref[at : at + PART, D + to : D + to + OWN] = block[0:PART, OWN:]
+            gqkv_ref[at : at + QUART, 2 * D + to : 2 * D + to + OWN] = block[PART : PART + QUART, 0:OWN]
+            gqkv_ref[at + QUART : at + PART, 2 * D + to : 2 * D + to + OWN] = block[PART : PART + QUART, OWN:]
+
+
+def finish(*args):
+    return call(
+        finish_kernel,
+        "finish",
+        [WHOLE] * 8,
+        [((SHARD, 4 * D), F32), ((D, D), F32), ((SHARD, 3 * D), F32), ((16, SHARD), F32)],
+        [],
+        10**7,
+        args,
+    )
+
+
+def pick(value, index, axis=0):
+    return lax.dynamic_index_in_dim(value, index, axis, keepdims=False)
+
+
+def across_w(value, flip):
+    return lax.ppermute(value, "wshard", [(i, i ^ flip) for i in range(4)])
+
+
+def across_core(value):
+    return lax.ppermute(value, "ctx", [(i, i ^ 1) for i in range(8)])
+
+
+def between_z(value, pairs):
+    return lax.ppermute(value, "ctx", [(2 * a + c, 2 * b + c) for a, b in pairs for c in range(2)])
+
+
+Z_GROUPS = [[0, 2, 4, 6], [1, 3, 5, 7]]
+
+
+def after(value, *others):
+    return lax.optimization_barrier((value, *others))[0]
+
+
+PAIRS = [(0, 1), (1, 0), (2, 3), (3, 2)]
+MIDDLE = [(1, 2), (2, 1), (0, 0), (3, 3)]
+
+
+def line_z(block):
+    pair = between_z(block, PAIRS)
+    mid_near = between_z(block, MIDDLE)
+    near = between_z(mid_near, PAIRS)
+    mid_far = between_z(pair, MIDDLE)
+    far = between_z(mid_far, PAIRS)
+    return block, pair, near, far, mid_near, mid_far
+
+
+TO_MIDDLE = [(0, 1), (3, 2)]
+TO_ENDS = [(1, 0), (2, 3)]
+ACROSS = [(1, 2), (2, 1)]
+
+
+def own_slot(slots, x_first):
+    one, two = (1, 2) if x_first else (2, 1)
+    got = across_w(slots[1], one)
+    far = slots[0, 1] + got[1]
+    return (slots[0, 0] + got[0]) + across_w(far, two)
+
+
+def gather_plane(block, *others):
+    half = block.shape[0] // 2
+    from_x, from_y = across_w(block, 1), across_w(block, 2)
+    first, second = from_x[:half], from_y[half:]
+    if others:
+        first, second, *_ = tied(first, second, *others)
+    return block, from_x, from_y, across_w(first, 2), across_w(second, 1)
+
+
+def tied(*values):
+    return lax.optimization_barrier(values)
+
+
+def local_grid(tokens, gain_one, w_qkv, w_out, gain_two, w_up, w_down, cotangent):
+    core = lax.axis_index("ctx") % 2
+    z = lax.axis_index("ctx") // 2
+    place = lax.axis_index("wshard")
+    inner = (z == 1) | (z == 2)
+
+    def both_micros(kept, got):
+        return jnp.where(core == 0, jnp.stack([kept, got]), jnp.stack([got, kept]))[:, None]
+
+    tok, cot = tokens[:, 0], cotangent[:, 0]
+    kept = jnp.concatenate([pick(tok, core), pick(cot, core)])
+    got = across_core(jnp.concatenate([pick(tok, 1 - core), pick(cot, 1 - core)]))
+    half = TILE // 2
+    own = [jnp.where(core == 0, a, b) for a, b in ((kept, got), (got, kept))]
+    x_block = jnp.concatenate([own[0][:half], own[1][:half]])
+    cot = jnp.concatenate([own[0][half:], own[1][half:]])
+
+    w_heads = pick(w_qkv.reshape(SHARD, 3, 4, OWN), z, 2).reshape(SHARD, MIX)
+    gains = jnp.pad(jnp.stack([gain_one, gain_two]), ((0, 30), (0, MIX - SHARD)))
+    w_heads = after(jnp.concatenate([w_heads, gains]), x_block)
+    pair, mid_near = between_z(x_block, PAIRS), between_z(x_block, MIDDLE)
+    heads_x, heads_y = across_w(w_heads, 1), across_w(w_heads, 2)
+    pair, mid_near, heads_x, heads_y = tied(pair, mid_near, heads_x, heads_y)
+    near, mid_far = between_z(mid_near, PAIRS), between_z(pair, MIDDLE)
+    middle = w_heads.shape[0] // 2
+    heads = w_heads, heads_x, heads_y, across_w(heads_x[:middle], 2), across_w(heads_y[middle:], 1)
+    far = between_z(mid_far, PAIRS)
+    shared, *heads = tied(jnp.concatenate([cot, w_out]), *heads)
+    shared_x, shared_y = across_w(shared, 1), across_w(shared, 2)
+    line = x_block, pair, near, far, mid_near, mid_far
+    up, *line = tied(w_up.reshape(SHARD, 4, D).transpose(1, 0, 2), *line)
+    up = lax.all_to_all(up, "wshard", 0, 0, tiled=True).reshape(D, D)
+    at = SHARD - heads[3].shape[0]
+    gains = jnp.stack([heads[k][SHARD : SHARD + 2] for k in range(3)] + [heads[4][at : at + 2]])
+    gains = gains[:, :, :SHARD].astype(F32)
+    gains = jnp.concatenate([pick(gains, place ^ j) for j in range(4)], axis=1)
+    gain_first, gain_second = gains[0:1], gains[1:2]
+
+    normed_all, kv, mixt, att, att_low, lse, w_full = attend(line, heads, gain_first)
+    att_low, up, shared_x, shared_y = tied(att_low, up, shared_x, shared_y)
+    middle = shared.shape[0] // 2
+    shared = shared, shared_x, shared_y, across_w(shared_x[:middle], 2), across_w(shared_y[middle:], 1)
+    att_home = lax.all_to_all(att_low, "ctx", 0, 0, tiled=True, axis_index_groups=Z_GROUPS).reshape(D, -1)
+    hidden, normed_two, wout_full = project(att_home, x_block, gain_second, shared)
+
+    active0, dup0, out0, dout0 = feed_own(normed_two, shared, up, w_down)
+    ns = gather_plane(normed_two, active0)
+    active1, dup1, out1, dout1 = feed_near(ns[1], ns[2], shared, up, w_down)
+    active2, dup2, *parts = feed_far(ns[3], ns[4], shared, out1, dout1, up, w_down)
+    parts, (a, a_far, b, b_far) = parts[:4], parts[4:]
+    got_a, got_b = across_w(a, 1), across_w(b, 2)
+    shares = feed_grads(ns, shared, (active0, active1, active2), (dup0, dup1, dup2))
+    shares, got_a, got_b = tied(shares, got_a, got_b)
+    shares = lax.psum_scatter(shares, "ctx", scatter_dimension=0)
+    more_a, more_b = across_w(a_far + got_a[1], 2), across_w(b_far + got_b[1], 1)
+    d_hidden, d_att, d_branch, d_gain_two = turn(
+        hidden, gain_second, dout0, (got_a, more_a, got_b, more_b), cot, wout_full
+    )
+    d_out = lax.all_to_all(d_att, "ctx", 0, 0, tiled=True, axis_index_groups=Z_GROUPS)
+    out_own, out_far, out_send = out_grad(att_home, d_branch)
+    d_out, out_send = tied(d_out, out_send)
+    out_got = across_w(out_send, 1)
+    *firsts, head_keep, head_send = attend_back(
+        kv, mixt, att, lse, d_out, normed_all, w_full, gain_first, d_gain_two
+    )
+    *firsts, head_keep, head_send, out_got = tied(*firsts, head_keep, head_send, out_got)
+
+    got = between_z(firsts[3], TO_MIDDLE)
+    sum_head = head_keep + across_core(head_send)
+    head_got = across_w(sum_head[1], 2)
+    out_far = across_w(out_far + out_got[1], 2)
+    up_share = lax.all_to_all(shares[:SHARD].reshape(4, QUART, HALF), "wshard", 0, 0, tiled=True)
+    got, head_got, out_far, up_share, *parts = tied(got, head_got, out_far, up_share, *parts)
+
+    both = firsts[2] + jnp.where(inner, got, BF(0))
+    outer, middle = between_z(both, TO_MIDDLE), between_z(both, ACROSS)
+    head_far = across_w(sum_head[0, 1] + head_got[1], 1)
+    head = (sum_head[0, 0] + head_got[0]) + head_far
+    share = jnp.concatenate([up_share.reshape(SHARD, HALF), shares[SHARD:], head])
+    share_pair, share_mid = between_z(share, PAIRS), between_z(share, ACROSS)
+    sum_out = ((out_own + out_got[0]) + out_far).reshape(2, PART, D)
+    sum_out = pick(sum_out, core) + across_core(pick(sum_out, 1 - core))
+    outer, middle, share_pair, share_mid, sum_out, *parts = tied(outer, middle, share_pair, share_mid, sum_out, *parts)
+
+    pair = between_z(firsts[1] + jnp.where(inner, middle, BF(0)), PAIRS)
+    middle = between_z(firsts[3] + outer, ACROSS)
+    share_near, share_far = between_z(share_mid, PAIRS), between_z(share_pair, ACROSS)
+    a, a_far, b, b_far = parts
+    got_a, got_b = across_w(a, 1), across_w(b, 2)
+    sum_out = sum_out + between_z(sum_out, TO_MIDDLE)
+    pair, middle, share_near, share_far, sum_out, got_a, got_b = tied(
+        pair, middle, share_near, share_far, sum_out, got_a, got_b
+    )
+
+    share_last = between_z(share_far, PAIRS)
+    sum_out = sum_out + between_z(sum_out, ACROSS)
+    grad_keep, grad_send = last(firsts[0], pair, middle, x_block, gain_first, d_hidden)
+    more_a, more_b = across_w(a_far + got_a[1], 2), across_w(b_far + got_b[1], 1)
+    shares = share, share_pair, jnp.where(inner, share_mid, share_near), jnp.where(inner, share_far, share_last)
+    result_keep, result_send = give(hidden, out0, (got_a, more_a, got_b, more_b))
+    out_result = both_micros(result_keep, across_core(result_send))
+    out_tokens = both_micros(grad_keep, across_core(grad_send))
+    sum_out = jnp.where(inner, sum_out, between_z(sum_out, TO_ENDS))
+    grad_out = both_micros(sum_out, across_core(sum_out)).reshape(SHARD, D).astype(F32)
+    grad_up, grad_down, grad_qkv, out_gains = finish(*shares, *(across_core(block) for block in shares))
+    return (
+        out_result,
+        out_tokens,
+        out_gains[0],
+        grad_qkv,
+        grad_out,
+        out_gains[1],
+        grad_up,
+        grad_down,
+    )
+
+
+def local(tokens, *rest):
+    fits = (
+        lax.axis_size("wshard") == 4
+        and lax.axis_size("ctx") == 8
+        and tokens.shape[:2] == (2, 1)
+        and 2 * tokens.shape[2] == TILE
+    )
+    return (local_grid if fits else local_any)(tokens, *rest)
+
+
 def solution(mesh):
     placed = (
         P(None, "wshard", "ctx", None),

time: 904 us -> 290 us (0.32)
  waiting for transfers between devices: 557 us -> 91.2 us
  matrix products: 90.3 us -> 0 us
  Pallas kernels: 0 us -> 76 us
  other arithmetic: 44.4 us -> 6.56 us
  blocking collectives: 36.8 us -> 0 us
  starting transfers between devices: 117 us -> 81.5 us
  local copies, waits for them, and re-layouts: 31.8 us -> 18.8 us
    all_gather x8 -> x0, waiting for transfers between devices: 213 us -> none  [the longest x2 53.5 us: local(): lax.all_gather(values_flat, 'ctx', axis=0, tiled=True)]
    reduce_scatter x4 -> x1, waiting for transfers between devices: 116 us -> 0.01 us  [local_grid(): shares = lax.psum_scatter(shares, 'ctx', scatter_dimension=0)]
    dot_general x38 -> x0, matrix products: 90.3 us -> none  [the longest x8 21.2 us: times_rows(): lax.dot_general(left_side, right_side, (((1,), (1,)), ((), ())), preferre...]
    psum x1 -> x0, waiting for transfers between devices: 78.2 us -> none  [local(): lax.psum(shares[1].astype(jnp.bfloat16), 'ctx').astype(jnp.float32)]
    pallas_call x0 -> x12, Pallas kernels: none -> 76 us  [call(): pl.pallas_call(kernel, in_specs=ins, out_specs=out_specs or [WHOLE] * len...]
    ppermute x64 -> x52, waiting for transfers between devices: 146 us -> 77 us  [the longest x18 41.7 us: between_z(): lax.ppermute(value, 'ctx', [(2 * a + c, 2 * b + c) for a, b in pairs for...]
    ppermute x64 -> x52, starting transfers between devices: 117 us -> 67.3 us  [the longest x18 38.2 us: between_z(): lax.ppermute(value, 'ctx', [(2 * a + c, 2 * b + c) for a, b in pairs for...]
    unnamed x2 -> x0, blocking collectives: 20.9 us -> none
  transfers between devices with their start and end apart: 77 -> 57, of which waited for: 75 -> 24; matrix products, arithmetic and copies ran while one was open for 13% -> 5% of each run, Pallas kernels for 0% -> 21%
where the time goes in v2:
time: 290 us; the launch traced here: 289 us
  waiting for transfers between devices  91.2 us (31%)
  starting transfers between devices  81.5 us (28%)
  Pallas kernels  76 us (26%)
  local copies, waits for them, and re-layouts  18.8 us (6%)
  between operations  15 us (5%)
  other arithmetic  6.56 us (2%)
    pallas_call x12, Pallas kernels, call(): pl.pallas_call(kernel, in_specs=ins, out_specs=out_specs or [WHOLE] * len...  76 us
    ppermute x18, waiting for transfers between devices, between_z(): lax.ppermute(value, 'ctx', [(2 * a + c, 2 * b + c) for a, b in pairs for...  41.7 us
    ppermute x18, starting transfers between devices, between_z(): lax.ppermute(value, 'ctx', [(2 * a + c, 2 * b + c) for a, b in pairs for...  38.2 us
    ppermute x24, waiting for transfers between devices, across_w(): return lax.ppermute(value, 'wshard', [(i, i ^ flip) for i in range(4)])  33.3 us
    ppermute x24, starting transfers between devices, across_w(): return lax.ppermute(value, 'wshard', [(i, i ^ flip) for i in range(4)])  27 us
    all_to_all x1, waiting for transfers between devices, local_grid(): lax.all_to_all(d_att, 'ctx', 0, 0, tiled=True, axis_index_groups=Z_GROUPS)  12.2 us
    unnamed x113, local copies, waits for them, and re-layouts  7.5 us
  transfers between devices with their start and end apart: 57, of which 24 were waited for; matrix products, arithmetic and copies ran while one was open for 5% of the time, Pallas kernels for 21%

profile of v2, /device:TPU:0, one launch (start us, length us, event | category | flops | bytes accessed | tf_op | source)
XLA Modules:
  0.0 289.1 jit_solution(6627187559897550920)
XLA Ops:
  7.2 1.3 dynamic-slice_bitcast_fusion.2
  11.2 1.5 collective-permute-start.2
  12.7 4.8 %collective-permute-start.1 = (bf16[256,768]{1,0:T(8,128)(2,1)S(1)}, bf16[256,768]{1,0:T(8,128)(2,1)}, u32[]{:S(2)}, u32[]{:S(2)}) collective-permute-start(bf16[256,768]{1,0:T(8,128)(2,1)S(1)} %pad_maximum_fusion.4.own.x_ref), channel_id=1, source_target_pairs={{0,2},{1,3},{2,0},{3,1},{4,6},{5,7},{6,4},{7,5},{8,10},{9,11},{10,... | collective-permute-start | bytes 1179656 | tf_op jit(solution)/shard_map/ppermute | solution.py:878
  18.6 1.6 collective-permute-start.4
  20.2 1.5 collective-permute-start.3
  21.7 5.6 %collective-permute-done.4.w2 = bf16[224,576]{1,0:T(8,128)(2,1)S(1)} collective-permute-done((bf16[224,576]{1,0:T(8,128)(2,1)S(1)}, bf16[224,576]{1,0:T(8,128)(2,1)S(1)}, u32[]{:S(2)}, u32[]{:S(2)}) %collective-permute-start.4) | collective-permute-done | bytes 258080 | tf_op jit(solution)/shard_map/ppermute | solution.py:870
  27.3 1.2 collective-permute-done.3.w1
  28.5 4.5 %collective-permute-start.6 = (bf16[256,768]{1,0:T(8,128)(2,1)}, bf16[256,768]{1,0:T(8,128)(2,1)}, u32[]{:S(2)}, u32[]{:S(2)}) collective-permute-start(bf16[256,768]{1,0:T(8,128)(2,1)} %collective-permute-done.1.pair), channel_id=1, source_target_pairs={{2,4},{3,5},{4,2},{5,3},{0,0},{1,1},{6,6},{7,7},{10,12},{11,13},{1... | collective-permute-start | bytes 1179656 | tf_op jit(solution)/shard_map/ppermute | solution.py:878
  34.2 1.6 collective-permute-start.9
  37.3 2.0 collective-permute-done.9.w4
  39.3 1.5 collective-permute-done.8.w3
  43.4 6.1 %collective-permute-done.5.near = bf16[256,768]{1,0:T(8,128)(2,1)S(1)} collective-permute-done((bf16[256,768]{1,0:T(8,128)(2,1)}, bf16[256,768]{1,0:T(8,128)(2,1)S(1)}, u32[]{:S(2)}, u32[]{:S(2)}) %collective-permute-start.5) | collective-permute-done | bytes 393248 | tf_op jit(solution)/shard_map/ppermute | solution.py:878
  49.6 6.0 %collective-permute-done.7.far = bf16[256,768]{1,0:T(8,128)(2,1)S(1)} collective-permute-done((bf16[256,768]{1,0:T(8,128)(2,1)}, bf16[256,768]{1,0:T(8,128)(2,1)S(1)}, u32[]{:S(2)}, u32[]{:S(2)}) %collective-permute-start.7) | collective-permute-done | bytes 393248 | tf_op jit(solution)/shard_map/ppermute | solution.py:878
  56.4 3.5 %all-to-all-start = ((bf16[4,192,768]{2,1,0:T(8,128)(2,1)}), bf16[4,192,768]{2,1,0:T(8,128)(2,1)S(1)}, u32[]{:S(2)}, u32[]{:S(2)}) async-start(bf16[4,192,768]{2,1,0:T(8,128)(2,1)} %bitcast.87), calls=%async_computation | async-start | bytes 2359296 | tf_op jit(solution)/shard_map/all_to_all | solution.py:957
  62.0 12.5 %attend.1 = (bf16[1024,768]{1,0:T(8,128)(2,1)}, bf16[3,1024,128]{2,1,0:T(8,128)(2,1)}, bf16[576,1024]{1,0:T(8,128)(2,1)}, f32[192,1024]{1,0:T(8,128)}, bf16[4,19...) custom-call(bf16[256,768]{1,0:T(8,128)(2,1)} %copy-done.4, ...), custom_call_target="tpu_custom_call" | custom-call | flops 1000 | bytes 1000 | tf_op jit(solution)/shard_map/attend/pallas_call | solution.py:302
  74.6 3.5 %all-to-all-start.1 = ((bf16[4,192,256]{2,1,0:T(8,128)(2,1)}), bf16[4,192,256]{2,1,0:T(8,128)(2,1)S(1)}, u32[]{:S(2)}, u32[]{:S(2)}) async-start(bf16[4,192,256]{2,1,0:T(8,128)(2,1)} %get-tuple-element.136), calls=%async_computation.1 | async-start | bytes 786432 | tf_op jit(solution)/shard_map/all_to_all | solution.py:968
  78.3 2.1 collective-permute-start.12
  80.4 5.8 %collective-permute-done.12.b3.cb_ref.c4 = bf16[224,768]{1,0:T(8,128)(2,1)} collective-permute-done((bf16[224,768]{1,0:T(8,128)(2,1)S(1)}, bf16[224,768]{1,0:T(8,128)(2,1)}, u32[]{:S(2)}, u32[]{:S(2)}) %collective-permute-start.12) | collective-permute-done | bytes 344096 | tf_op jit(solution)/shard_map/ppermute | solution.py:870
  86.2 1.7 all-to-all-done.1
  88.6 4.3 %project.1 = (f32[256,768]{1,0:T(8,128)}, bf16[256,768]{1,0:T(8,128)(2,1)}, bf16[768,768]{1,0:T(8,128)(2,1)}) custom-call(bf16[768,256]{1,0:T(8,128)(2,1)} %bitcast.88, bf16[256,768]{1,0:T(8,128)(2,1)} %copy-done.4, f32[1,768]{1,0:T(1,128)} %get-tuple-element.244.gain_ref, bf16[448,768]{1,0:T(8,128)(2,1)} %copy-done.1, bf16[448,768]{1,0:T(8,128)(2,1)} %copy-done.3, ...), custom_call_target="tpu_custom_call" | custom-call | flops 1000 | bytes 1000 | tf_op jit(solution)/shard_map/project/pallas_call | solution.py:302
  92.9 1.8 collective-permute-start.14
  94.7 1.5 collective-permute-start.13
  97.8 4.3 %feed_own.1 = (bf16[256,768]{1,0:T(8,128)(2,1)}, bf16[256,768]{1,0:T(8,128)(2,1)}, f32[256,768]{1,0:T(8,128)}, f32[256,768]{1,0:T(8,128)}) custom-call(bf16[256,768]{1,0:T(8,128)(2,1)} %get-tuple-element.140.n_ref.n0, bf16[448,768]{1,0:T(8,128)(2,1)} %copy-done.1, bf16[768,768]{1,0:T(8,128)(2,1)} %bitcast.84, bf16[768,768]{1,0:T(8,128)(2,1)} %down_ref.5), custom_call_target="tpu_custom_call" | custom-call | flops 1000 | bytes 1000 | tf_op jit(solution)/shard_map/feed_own/pallas_call | solution.py:302
  102.1 3.1 %collective-permute-done.14.ny_ref.n2 = bf16[256,768]{1,0:T(8,128)(2,1)S(1)} collective-permute-done((bf16[256,768]{1,0:T(8,128)(2,1)}, bf16[256,768]{1,0:T(8,128)(2,1)S(1)}, u32[]{:S(2)}, u32[]{:S(2)}) %collective-permute-start.14) | collective-permute-done | bytes 393248 | tf_op jit(solution)/shard_map/ppermute | solution.py:870
  105.3 1.8 collective-permute-start.15
  107.1 1.5 collective-permute-start.16
  108.5 6.1 %feed_near.1 = (bf16[512,768]{1,0:T(8,128)(2,1)}, bf16[512,768]{1,0:T(8,128)(2,1)}, bf16[512,768]{1,0:T(8,128)(2,1)}, bf16[512,768]{1,0:T(8,128)(2,1)}) custom-call(bf16[256,768]{1,0:T(8,128)(2,1)} %copy-done.7, bf16[256,768]{1,0:T(8,128)(2,1)} %copy-done.6, bf16[448,768]{1,0:T(8,128)(2,1)} %copy-done.3, bf16[448,768]{1,0:T(8,128)(2,1)} %copy-done.2, ...), custom_call_target="tpu_custom_call" | custom-call | flops 1000 | bytes 1000 | tf_op jit(solution)/shard_map/feed_near/pallas_call | solution.py:302
  115.5 5.3 %feed_far.1 = (bf16[256,768]{1,0:T(8,128)(2,1)}, bf16[256,768]{1,0:T(8,128)(2,1)}, bf16[2,128,768]{2,1,0:T(8,128)(2,1)}, bf16[128,768]{1,0:T(8,128)(2,1)}, bf16[...) custom-call(bf16[128,768]{1,0:T(8,128)(2,1)} %copy-done.22, ...), custom_call_target="tpu_custom_call" | custom-call | flops 1000 | bytes 1000 | tf_op jit(solution)/shard_map/feed_far/pallas_call | solution.py:302
  121.6 8.0 %feed_grads.1 = bf16[8,384,384]{2,1,0:T(8,128)(2,1)} custom-call(bf16[256,768]{1,0:T(8,128)(2,1)} %get-tuple-element.140.n_ref.n0, bf16[256,768]{1,0:T(8,128)(2,1)} %copy-done.7, bf16[256,768]{1,0:T(8,128)(2,1)} %copy-done.6, bf16[128,768]{1,0:T(8,128)(2,1)} %copy-done.22, bf16[128,768]{1,0:T(8,128)(2,1)} %copy-done.23, bf16[448,768]{1,0:T(8,128)(2,1)} %copy-done.1, ...), custom_call_target="tpu_custom_call" | custom-call | flops 1000 | bytes 1000 | tf_op jit(solution)/shard_map/feed_grads/pallas_call | solution.py:302
  129.6 1.2 collective-permute-done.18.a_ref
  131.7 2.0 collective-permute-start.21
  134.8 2.6 collective-permute-done.21.b_more_ref
  137.3 2.1 collective-permute-done.20.a_more_ref
  140.1 4.3 %turn.1 = (f32[256,768]{1,0:T(8,128)}, bf16[4,192,256]{2,1,0:T(8,128)(2,1)}, bf16[256,768]{1,0:T(8,128)(2,1)}, f32[1,768]{1,0:T(1,128)}) custom-call(f32[256,768]{1,0:T(8,128)} %get-tuple-element.139.hidden_ref, f32[1,768]{1,0:T(1,128)} %get-tuple-element.244.gain_ref, f32[256,768]{1,0:T(8,128)} %get-tuple-element.147.dkeep_ref, ...), custom_call_target="tpu_custom_call" | custom-call | flops 1000 | bytes 1000 | tf_op jit(solution)/shard_map/turn/pallas_call | solution.py:302
  144.4 3.7 %all-to-all-start.2 = ((bf16[4,192,256]{2,1,0:T(8,128)(2,1)}), bf16[4,192,256]{2,1,0:T(8,128)(2,1)S(1)}, u32[]{:S(2)}, u32[]{:S(2)}) async-start(bf16[4,192,256]{2,1,0:T(8,128)(2,1)} %get-tuple-element.165), calls=%async_computation.2 | async-start | bytes 786432 | tf_op jit(solution)/shard_map/all_to_all | solution.py:984
  148.1 2.7 out_grad.1
  150.8 12.2 %all-to-all-done.2.dout_ref = bf16[4,192,256]{2,1,0:T(8,128)(2,1)S(1)} async-done(((bf16[4,192,256]{2,1,0:T(8,128)(2,1)}), bf16[4,192,256]{2,1,0:T(8,128)(2,1)S(1)}, u32[]{:S(2)}, u32[]{:S(2)}) %all-to-all-start.2) | async-done | bytes 393248 | tf_op jit(solution)/shard_map/all_to_all | solution.py:984
  163.0 1.2 collective-permute-start.22
  164.1 17.5 %attend_back.1 = (bf16[256,768]{1,0:T(8,128)(2,1)}, bf16[256,768]{1,0:T(8,128)(2,1)}, bf16[256,768]{1,0:T(8,128)(2,1)}, bf16[256,768]{1,0:T(8,128)(2,1)}, bf16[2...) custom-call(bf16[3,1024,128]{2,1,0:T(8,128)(2,1)} %get-tuple-element.143.kv_ref, ...), custom_call_target="tpu_custom_call" | custom-call | flops 1000 | bytes 1000 | tf_op jit(solution)/shard_map/attend_back/pallas_call | solution.py:302
  182.5 1.4 collective-permute-start.23
  184.0 1.2 add.100
  185.2 1.3 collective-permute-start.25
  186.6 1.7 slice_bitcast_fusion.1
  188.2 3.3 %all-to-all-start.3 = ((bf16[4,48,384]{2,1,0:T(8,128)(2,1)}), bf16[4,48,384]{2,1,0:T(8,128)(2,1)S(1)}, u32[]{:S(2)}, u32[]{:S(2)}) async-start(bf16[4,48,384]{2,1,0:T(8,128)(2,1)} %bitcast.20), calls=%async_computation.4 | async-start | bytes 294912 | tf_op jit(solution)/shard_map/all_to_all | solution.py:997
  191.6 1.5 collective-permute-done.23
  193.1 4.5 %collective-permute-done.25 = bf16[2,160,384]{2,1,0:T(8,128)(2,1)S(1)} collective-permute-done((bf16[2,160,384]{2,1,0:T(8,128)(2,1)S(1)}, bf16[2,160,384]{2,1,0:T(8,128)(2,1)S(1)}, u32[]{:S(2)}, u32[]{:S(2)}) %collective-permute-start.25) | collective-permute-done | bytes 245792 | tf_op jit(solution)/shard_map/ppermute | solution.py:870
  198.8 3.3 %collective-permute-start.27 = (bf16[256,768]{1,0:T(8,128)(2,1)S(1)}, bf16[256,768]{1,0:T(8,128)(2,1)S(1)}, u32[]{:S(2)}, u32[]{:S(2)}) collective-permute-start(bf16[256,768]{1,0:T(8,128)(2,1)S(1)} %select_add_fusion.1), channel_id=1, source_target_pairs={{0,2},{1,3},{6,4},{7,5},{8,10},{9,11},{14,12},{15,13},{16,18},{17,... | collective-permute-start | bytes 1179656 | tf_op jit(solution)/shard_map/ppermute | solution.py:878
  202.2 1.4 collective-permute-start.29
  203.6 3.5 %collective-permute-done.29 = bf16[160,384]{1,0:T(8,128)(2,1)S(1)} collective-permute-done((bf16[160,384]{1,0:T(8,128)(2,1)S(1)}, bf16[160,384]{1,0:T(8,128)(2,1)S(1)}, u32[]{:S(2)}, u32[]{:S(2)}) %collective-permute-start.29) | collective-permute-done | bytes 122912 | tf_op jit(solution)/shard_map/ppermute | solution.py:870
  208.1 2.0 collective-permute-start.30
  210.2 1.4 collective-permute-done.32
  211.7 7.3 %collective-permute-done.30.refs_1_ = bf16[544,384]{1,0:T(8,128)(2,1)S(1)} collective-permute-done((bf16[544,384]{1,0:T(8,128)(2,1)S(1)}, bf16[544,384]{1,0:T(8,128)(2,1)S(1)}, u32[]{:S(2)}, u32[]{:S(2)}) %collective-permute-start.30) | collective-permute-done | bytes 417824 | tf_op jit(solution)/shard_map/ppermute | solution.py:878
  220.0 7.0 %collective-permute-start.37 = (bf16[96,768]{1,0:T(8,128)(2,1)S(1)}, bf16[96,768]{1,0:T(8,128)(2,1)S(1)}, u32[]{:S(2)}, u32[]{:S(2)}) collective-permute-start(bf16[96,768]{1,0:T(8,128)(2,1)S(1)} %bitcast_add_fusion.6), channel_id=1, source_target_pairs={{0,2},{1,3},{6,4},{7,5},{8,10},{9,11},{14,12},{15,13},{16,18},{17,... | collective-permute-start | bytes 442376 | tf_op jit(solution)/shard_map/ppermute | solution.py:878
  227.8 4.0 %collective-permute-start.33 = (bf16[256,768]{1,0:T(8,128)(2,1)S(1)}, bf16[256,768]{1,0:T(8,128)(2,1)S(1)}, u32[]{:S(2)}, u32[]{:S(2)}) collective-permute-start(bf16[256,768]{1,0:T(8,128)(2,1)S(1)} %select_add_fusion), channel_id=1, source_target_pairs={{0,2},{1,3},{2,0},{3,1},{4,6},{5,7},{6,4},{7,5},{8,10},{9,11},{10,... | collective-permute-start | bytes 1179656 | tf_op jit(solution)/shard_map/ppermute | solution.py:878
  231.7 1.3 collective-permute-start.38
  233.6 12.2 %collective-permute-done.33.pair_ref = bf16[256,768]{1,0:T(8,128)(2,1)S(1)} collective-permute-done((bf16[256,768]{1,0:T(8,128)(2,1)S(1)}, bf16[256,768]{1,0:T(8,128)(2,1)S(1)}, u32[]{:S(2)}, u32[]{:S(2)}) %collective-permute-start.33) | collective-permute-done | bytes 393248 | tf_op jit(solution)/shard_map/ppermute | solution.py:878
  246.5 1.4 collective-permute-start.41
  248.5 3.1 %last.1 = (f32[128,768]{1,0:T(8,128)}, f32[128,768]{1,0:T(8,128)}) custom-call(bf16[256,768]{1,0:T(8,128)(2,1)} %get-tuple-element.213.first_ref, bf16[256,768]{1,0:T(8,128)(2,1)} %copy-done.32, bf16[256,768]{1,0:T(8,128)(2,1)} %copy-done.31, bf16[256,768]{1,0:T(8,128)(2,1)} %copy-done.4, f32[1,768]{1,0:T(1,128)} %get-tuple-element.245.gain_ref, ...), custom_call_target="tpu_custom_call" | custom-call | flops 1000 | bytes 1000 | tf_op jit(solution)/shard_map/last/pallas_call | solution.py:302
  251.7 4.5 %collective-permute-start.44 = (bf16[544,384]{1,0:T(8,128)(2,1)S(1)}, bf16[544,384]{1,0:T(8,128)(2,1)S(1)}, u32[]{:S(2)}, u32[]{:S(2)}) collective-permute-start(bf16[544,384]{1,0:T(8,128)(2,1)S(1)} %collective-permute-done.36), channel_id=1, source_target_pairs={{0,2},{1,3},{2,0},{3,1},{4,6},{5,7},{6,4},{7,5},{8,10},{9,11},{10,... | collective-permute-start | bytes 1253384 | tf_op jit(solution)/shard_map/ppermute | solution.py:878
  256.3 1.3 collective-permute-start.50
  258.6 2.6 give.1
  261.3 8.4 %collective-permute-done.50 = bf16[96,768]{1,0:T(8,128)(2,1)S(1)} collective-permute-done((bf16[96,768]{1,0:T(8,128)(2,1)S(1)}, bf16[96,768]{1,0:T(8,128)(2,1)S(1)}, u32[]{:S(2)}, u32[]{:S(2)}) %collective-permute-start.50) | collective-permute-done | bytes 147488 | tf_op jit(solution)/shard_map/ppermute | solution.py:878
  275.6 5.3 %finish.1 = (f32[192,3072]{1,0:T(8,128)}, f32[768,768]{1,0:T(8,128)}, f32[192,2304]{1,0:T(8,128)}, f32[16,192]{1,0:T(8,128)}) custom-call(bf16[544,384]{1,0:T(8,128)(2,1)} %copy-done.12, bf16[544,384]{1,0:T(8,128)(2,1)} %copy-done.26, bf16[544,384]{1,0:T(8,128)(2,1)} %copy-done.10, bf16[544,384]{1,0:T(8,128)(2,1)} %copy-done.11, ...), custom_call_target="tpu_custom_call" | custom-call | flops 1000 | bytes 1000 | tf_op jit(solution)/shard_map/finish/pallas_call | solution.py:302
  280.9 1.3 fusion.17
  (233 shorter events, 32.6 us)
Async XLA Ops:
  8.6 2.3 collective-permute-start
  11.1 25.1 %copy-start.8 = (bf16[128,768]{1,0:T(8,128)(2,1)}, bf16[128,768]{1,0:T(8,128)(2,1)S(1)}, u32[]{:S(2)}) copy-start(bf16[128,768]{1,0:T(8,128)(2,1)S(1)} %get-tuple-element.230) | copy-start | bytes 589828
  11.2 17.4 %collective-permute-start.2 = (bf16[256,768]{1,0:T(8,128)(2,1)S(1)}, bf16[256,768]{1,0:T(8,128)(2,1)}, u32[]{:S(2)}, u32[]{:S(2)}) collective-permute-start(bf16[256,768]{1,0:T(8,128)(2,1)S(1)} %pad_maximum_fusion.4.own.x_ref), channel_id=1, source_target_pairs={{2,4},{3,5},{4,2},{5,3},{0,0},{1,1},{6,6},{7,7},{10,12},{11,13},{1... | collective-permute-start | bytes 1179656 | tf_op jit(solution)/shard_map/ppermute | solution.py:878
  12.7 15.8 %collective-permute-start.1 = (bf16[256,768]{1,0:T(8,128)(2,1)S(1)}, bf16[256,768]{1,0:T(8,128)(2,1)}, u32[]{:S(2)}, u32[]{:S(2)}) collective-permute-start(bf16[256,768]{1,0:T(8,128)(2,1)S(1)} %pad_maximum_fusion.4.own.x_ref), channel_id=1, source_target_pairs={{0,2},{1,3},{2,0},{3,1},{4,6},{5,7},{6,4},{7,5},{8,10},{9,11},{10,... | collective-permute-start | bytes 1179656 | tf_op jit(solution)/shard_map/ppermute | solution.py:878
  18.6 24.1 %copy-start.16 = (bf16[224,576]{1,0:T(8,128)(2,1)}, bf16[224,576]{1,0:T(8,128)(2,1)S(1)}, u32[]{:S(2)}) copy-start(bf16[224,576]{1,0:T(8,128)(2,1)S(1)} %pad_maximum_fusion.6.w0) | copy-start | bytes 774148
  18.6 8.7 %collective-permute-start.4 = (bf16[224,576]{1,0:T(8,128)(2,1)S(1)}, bf16[224,576]{1,0:T(8,128)(2,1)S(1)}, u32[]{:S(2)}, u32[]{:S(2)}) collective-permute-start(bf16[224,576]{1,0:T(8,128)(2,1)S(1)} %pad_maximum_fusion.6.w0), channel_id=1, source_target_pairs={{0,16},{8,24},{16,0},{24,8},{1,17},{9,25},{17,1},{25,9},{2,18},{10... | collective-permute-start | bytes 774152 | tf_op jit(solution)/shard_map/ppermute | solution.py:870
  20.2 8.4 %collective-permute-start.3 = (bf16[224,576]{1,0:T(8,128)(2,1)S(1)}, bf16[224,576]{1,0:T(8,128)(2,1)S(1)}, u32[]{:S(2)}, u32[]{:S(2)}) collective-permute-start(bf16[224,576]{1,0:T(8,128)(2,1)S(1)} %pad_maximum_fusion.6.w0), channel_id=1, source_target_pairs={{0,8},{8,0},{16,24},{24,16},{1,9},{9,1},{17,25},{25,17},{2,10},{10... | collective-permute-start | bytes 774152 | tf_op jit(solution)/shard_map/ppermute | solution.py:870
  28.5 14.1 %collective-permute-start.6 = (bf16[256,768]{1,0:T(8,128)(2,1)}, bf16[256,768]{1,0:T(8,128)(2,1)}, u32[]{:S(2)}, u32[]{:S(2)}) collective-permute-start(bf16[256,768]{1,0:T(8,128)(2,1)} %collective-permute-done.1.pair), channel_id=1, source_target_pairs={{2,4},{3,5},{4,2},{5,3},{0,0},{1,1},{6,6},{7,7},{10,12},{11,13},{1... | collective-permute-start | bytes 1179656 | tf_op jit(solution)/shard_map/ppermute | solution.py:878
  34.2 5.2 %collective-permute-start.9 = (bf16[112,576]{1,0:T(8,128)(2,1)S(1)}, bf16[112,576]{1,0:T(8,128)(2,1)S(1)}, u32[]{:S(2)}, u32[]{:S(2)}) collective-permute-start(bf16[112,576]{1,0:T(8,128)(2,1)S(1)} %slice.105), channel_id=1, source_target_pairs={{0,8},{8,0},{16,24},{24,16},{1,9},{9,1},{17,25},{25,17},{2,10},{10... | collective-permute-start | bytes 387080 | tf_op jit(solution)/shard_map/ppermute | solution.py:870
  35.7 5.1 %collective-permute-start.8 = (bf16[112,576]{1,0:T(8,128)(2,1)S(1)}, bf16[112,576]{1,0:T(8,128)(2,1)S(1)}, u32[]{:S(2)}, u32[]{:S(2)}) collective-permute-start(bf16[112,576]{1,0:T(8,128)(2,1)S(1)} %slice.104), channel_id=1, source_target_pairs={{0,16},{8,24},{16,0},{24,8},{1,17},{9,25},{17,1},{25,9},{2,18},{10... | collective-permute-start | bytes 387080 | tf_op jit(solution)/shard_map/ppermute | solution.py:870
  37.2 37.3 %copy-start.1 = (bf16[448,768]{1,0:T(8,128)(2,1)}, bf16[448,768]{1,0:T(8,128)(2,1)S(1)}, u32[]{:S(2)}) copy-start(bf16[448,768]{1,0:T(8,128)(2,1)S(1)} %pad_maximum_fusion.b0.cot_ref.c0) | copy-start | bytes 2064388
  37.3 12.3 %collective-permute-start.5 = (bf16[256,768]{1,0:T(8,128)(2,1)}, bf16[256,768]{1,0:T(8,128)(2,1)S(1)}, u32[]{:S(2)}, u32[]{:S(2)}) collective-permute-start(bf16[256,768]{1,0:T(8,128)(2,1)} %collective-permute-done.2.mid_near), channel_id=1, source_target_pairs={{0,2},{1,3},{2,0},{3,1},{4,6},{5,7},{6,4},{7,5},{8,10},{9,11},{10,... | collective-permute-start | bytes 1179656 | tf_op jit(solution)/shard_map/ppermute | solution.py:878
  41.5 33.0 %collective-permute-start.11 = (bf16[448,768]{1,0:T(8,128)(2,1)S(1)}, bf16[448,768]{1,0:T(8,128)(2,1)S(1)}, u32[]{:S(2)}, u32[]{:S(2)}) collective-permute-start(bf16[448,768]{1,0:T(8,128)(2,1)S(1)} %pad_maximum_fusion.b0.cot_ref.c0), channel_id=1, source_target_pairs={{0,16},{8,24},{16,0},{24,8},{1,17},{9,25},{17,1},{25,9},{2,18},{10... | collective-permute-start | bytes 2064392 | tf_op jit(solution)/shard_map/ppermute | solution.py:870
  42.0 32.5 %collective-permute-start.10 = (bf16[448,768]{1,0:T(8,128)(2,1)S(1)}, bf16[448,768]{1,0:T(8,128)(2,1)S(1)}, u32[]{:S(2)}, u32[]{:S(2)}) collective-permute-start(bf16[448,768]{1,0:T(8,128)(2,1)S(1)} %pad_maximum_fusion.b0.cot_ref.c0), channel_id=1, source_target_pairs={{0,8},{8,0},{16,24},{24,16},{1,9},{9,1},{17,25},{25,17},{2,10},{10... | collective-permute-start | bytes 2064392 | tf_op jit(solution)/shard_map/ppermute | solution.py:870
  42.7 12.9 %collective-permute-start.7 = (bf16[256,768]{1,0:T(8,128)(2,1)}, bf16[256,768]{1,0:T(8,128)(2,1)S(1)}, u32[]{:S(2)}, u32[]{:S(2)}) collective-permute-start(bf16[256,768]{1,0:T(8,128)(2,1)} %collective-permute-done.6.mid_far), channel_id=1, source_target_pairs={{0,2},{1,3},{2,0},{3,1},{4,6},{5,7},{6,4},{7,5},{8,10},{9,11},{10,... | collective-permute-start | bytes 1179656 | tf_op jit(solution)/shard_map/ppermute | solution.py:878
  56.4 18.2 %all-to-all-start = ((bf16[4,192,768]{2,1,0:T(8,128)(2,1)}), bf16[4,192,768]{2,1,0:T(8,128)(2,1)S(1)}, u32[]{:S(2)}, u32[]{:S(2)}) async-start(bf16[4,192,768]{2,1,0:T(8,128)(2,1)} %bitcast.87), calls=%async_computation | async-start | bytes 2359296 | tf_op jit(solution)/shard_map/all_to_all | solution.py:957
  74.6 13.3 %all-to-all-start.1 = ((bf16[4,192,256]{2,1,0:T(8,128)(2,1)}), bf16[4,192,256]{2,1,0:T(8,128)(2,1)S(1)}, u32[]{:S(2)}, u32[]{:S(2)}) async-start(bf16[4,192,256]{2,1,0:T(8,128)(2,1)} %get-tuple-element.136), calls=%async_computation.1 | async-start | bytes 786432 | tf_op jit(solution)/shard_map/all_to_all | solution.py:968
  78.1 108.5 %reduce-scatter.2.cloned.1.call-start = ((), (), s32[]{:S(2)}) async-start(), calls=%async_computation.5 | async-start | bytes 2654208 | tf_op jit(solution)/shard_map/reduce_scatter | solution.py:979
  78.3 7.8 %collective-permute-start.12 = (bf16[224,768]{1,0:T(8,128)(2,1)S(1)}, bf16[224,768]{1,0:T(8,128)(2,1)}, u32[]{:S(2)}, u32[]{:S(2)}) collective-permute-start(bf16[224,768]{1,0:T(8,128)(2,1)S(1)} %slice.113), channel_id=1, source_target_pairs={{0,8},{8,0},{16,24},{24,16},{1,9},{9,1},{17,25},{25,17},{2,10},{10... | collective-permute-start | bytes 1032200 | tf_op jit(solution)/shard_map/ppermute | solution.py:870
  92.9 12.3 %collective-permute-start.14 = (bf16[256,768]{1,0:T(8,128)(2,1)}, bf16[256,768]{1,0:T(8,128)(2,1)S(1)}, u32[]{:S(2)}, u32[]{:S(2)}) collective-permute-start(bf16[256,768]{1,0:T(8,128)(2,1)} %get-tuple-element.140.n_ref.n0), channel_id=1, source_target_pairs={{0,16},{8,24},{16,0},{24,8},{1,17},{9,25},{17,1},{25,9},{2,18},{10... | collective-permute-start | bytes 1179656 | tf_op jit(solution)/shard_map/ppermute | solution.py:870
  94.7 10.6 %collective-permute-start.13 = (bf16[256,768]{1,0:T(8,128)(2,1)}, bf16[256,768]{1,0:T(8,128)(2,1)S(1)}, u32[]{:S(2)}, u32[]{:S(2)}) collective-permute-start(bf16[256,768]{1,0:T(8,128)(2,1)} %get-tuple-element.140.n_ref.n0), channel_id=1, source_target_pairs={{0,8},{8,0},{16,24},{24,16},{1,9},{9,1},{17,25},{25,17},{2,10},{10... | collective-permute-start | bytes 1179656 | tf_op jit(solution)/shard_map/ppermute | solution.py:870
  97.1 17.5 %collective-permute-start.17 = (bf16[224,768]{1,0:T(8,128)(2,1)S(1)}, bf16[224,768]{1,0:T(8,128)(2,1)S(1)}, u32[]{:S(2)}, u32[]{:S(2)}) collective-permute-start(bf16[224,768]{1,0:T(8,128)(2,1)S(1)} %slice.116), channel_id=1, source_target_pairs={{0,16},{8,24},{16,0},{24,8},{1,17},{9,25},{17,1},{25,9},{2,18},{10... | collective-permute-start | bytes 1032200 | tf_op jit(solution)/shard_map/ppermute | solution.py:870
  105.3 9.3 %collective-permute-start.15 = (bf16[128,768]{1,0:T(8,128)(2,1)S(1)}, bf16[128,768]{1,0:T(8,128)(2,1)S(1)}, u32[]{:S(2)}, u32[]{:S(2)}) collective-permute-start(bf16[128,768]{1,0:T(8,128)(2,1)S(1)} %slice.139), channel_id=1, source_target_pairs={{0,16},{8,24},{16,0},{24,8},{1,17},{9,25},{17,1},{25,9},{2,18},{10... | collective-permute-start | bytes 589832 | tf_op jit(solution)/shard_map/ppermute | solution.py:870
  107.1 7.6 %collective-permute-start.16 = (bf16[128,768]{1,0:T(8,128)(2,1)S(1)}, bf16[128,768]{1,0:T(8,128)(2,1)S(1)}, u32[]{:S(2)}, u32[]{:S(2)}) collective-permute-start(bf16[128,768]{1,0:T(8,128)(2,1)S(1)} %slice.140), channel_id=1, source_target_pairs={{0,8},{8,0},{16,24},{24,16},{1,9},{9,1},{17,25},{25,17},{2,10},{10... | collective-permute-start | bytes 589832 | tf_op jit(solution)/shard_map/ppermute | solution.py:870
  120.7 10.1 %collective-permute-start.18 = (bf16[2,128,768]{2,1,0:T(8,128)(2,1)}, bf16[2,128,768]{2,1,0:T(8,128)(2,1)S(1)}, u32[]{:S(2)}, u32[]{:S(2)}) collective-permute-start(bf16[2,128,768]{2,1,0:T(8,128)(2,1)} %get-tuple-element.158), channel_id=1, source_target_pairs={{0,8},{8,0},{16,24},{24,16},{1,9},{9,1},{17,25},{25,17},{2,10},{10... | collective-permute-start | bytes 1179656 | tf_op jit(solution)/shard_map/ppermute | solution.py:870
  121.3 9.5 %collective-permute-start.19 = (bf16[2,128,768]{2,1,0:T(8,128)(2,1)}, bf16[2,128,768]{2,1,0:T(8,128)(2,1)S(1)}, u32[]{:S(2)}, u32[]{:S(2)}) collective-permute-start(bf16[2,128,768]{2,1,0:T(8,128)(2,1)} %get-tuple-element.159), channel_id=1, source_target_pairs={{0,16},{8,24},{16,0},{24,8},{1,17},{9,25},{17,1},{25,9},{2,18},{10... | collective-permute-start | bytes 1179656 | tf_op jit(solution)/shard_map/ppermute | solution.py:870
  131.7 5.7 %collective-permute-start.21 = (bf16[128,768]{1,0:T(8,128)(2,1)S(1)}, bf16[128,768]{1,0:T(8,128)(2,1)S(1)}, u32[]{:S(2)}, u32[]{:S(2)}) collective-permute-start(bf16[128,768]{1,0:T(8,128)(2,1)S(1)} %bitcast_add_fusion.4), channel_id=1, source_target_pairs={{0,8},{8,0},{16,24},{24,16},{1,9},{9,1},{17,25},{25,17},{2,10},{10... | collective-permute-start | bytes 589832 | tf_op jit(solution)/shard_map/ppermute | solution.py:870
  133.7 5.7 %collective-permute-start.20 = (bf16[128,768]{1,0:T(8,128)(2,1)S(1)}, bf16[128,768]{1,0:T(8,128)(2,1)S(1)}, u32[]{:S(2)}, u32[]{:S(2)}) collective-permute-start(bf16[128,768]{1,0:T(8,128)(2,1)S(1)} %bitcast_add_fusion.5), channel_id=1, source_target_pairs={{0,16},{8,24},{16,0},{24,8},{1,17},{9,25},{17,1},{25,9},{2,18},{10... | collective-permute-start | bytes 589832 | tf_op jit(solution)/shard_map/ppermute | solution.py:870
  144.4 18.5 %all-to-all-start.2 = ((bf16[4,192,256]{2,1,0:T(8,128)(2,1)}), bf16[4,192,256]{2,1,0:T(8,128)(2,1)S(1)}, u32[]{:S(2)}, u32[]{:S(2)}) async-start(bf16[4,192,256]{2,1,0:T(8,128)(2,1)} %get-tuple-element.165), calls=%async_computation.2 | async-start | bytes 786432 | tf_op jit(solution)/shard_map/all_to_all | solution.py:984
  163.0 18.7 %collective-permute-start.22 = (bf16[2,192,768]{2,1,0:T(8,128)(2,1)}, bf16[2,192,768]{2,1,0:T(8,128)(2,1)S(1)}, u32[]{:S(2)}, u32[]{:S(2)}) collective-permute-start(bf16[2,192,768]{2,1,0:T(8,128)(2,1)} %get-tuple-element.178), channel_id=1, source_target_pairs={{0,8},{8,0},{16,24},{24,16},{1,9},{9,1},{17,25},{25,17},{2,10},{10... | collective-permute-start | bytes 1769480 | tf_op jit(solution)/shard_map/ppermute | solution.py:870
  181.6 2.4 collective-permute-start.24
  181.8 9.9 %collective-permute-start.26 = (bf16[192,768]{1,0:T(8,128)(2,1)S(1)}, bf16[192,768]{1,0:T(8,128)(2,1)S(1)}, u32[]{:S(2)}, u32[]{:S(2)}) collective-permute-start(bf16[192,768]{1,0:T(8,128)(2,1)S(1)} %bitcast_add_fusion.1), channel_id=1, source_target_pairs={{0,16},{8,24},{16,0},{24,8},{1,17},{9,25},{17,1},{25,9},{2,18},{10... | collective-permute-start | bytes 884744 | tf_op jit(solution)/shard_map/ppermute | solution.py:870
  182.5 10.6 %collective-permute-start.23 = (bf16[256,768]{1,0:T(8,128)(2,1)}, bf16[256,768]{1,0:T(8,128)(2,1)S(1)}, u32[]{:S(2)}, u32[]{:S(2)}) collective-permute-start(bf16[256,768]{1,0:T(8,128)(2,1)} %get-tuple-element.181), channel_id=1, source_target_pairs={{0,2},{1,3},{6,4},{7,5},{8,10},{9,11},{14,12},{15,13},{16,18},{17,... | collective-permute-start | bytes 1179656 | tf_op jit(solution)/shard_map/ppermute | solution.py:878
  185.2 12.5 %collective-permute-start.25 = (bf16[2,160,384]{2,1,0:T(8,128)(2,1)S(1)}, bf16[2,160,384]{2,1,0:T(8,128)(2,1)S(1)}, u32[]{:S(2)}, u32[]{:S(2)}) collective-permute-start(bf16[2,160,384]{2,1,0:T(8,128)(2,1)S(1)} %slice_bitcast_fusion), channel_id=1, source_target_pairs={{0,16},{8,24},{16,0},{24,8},{1,17},{9,25},{17,1},{25,9},{2,18},{10... | collective-permute-start | bytes 737288 | tf_op jit(solution)/shard_map/ppermute | solution.py:870
  188.2 9.9 %all-to-all-start.3 = ((bf16[4,48,384]{2,1,0:T(8,128)(2,1)}), bf16[4,48,384]{2,1,0:T(8,128)(2,1)S(1)}, u32[]{:S(2)}, u32[]{:S(2)}) async-start(bf16[4,48,384]{2,1,0:T(8,128)(2,1)} %bitcast.20), calls=%async_computation.4 | async-start | bytes 294912 | tf_op jit(solution)/shard_map/all_to_all | solution.py:997
  198.1 13.4 %collective-permute-start.28 = (bf16[256,768]{1,0:T(8,128)(2,1)S(1)}, bf16[256,768]{1,0:T(8,128)(2,1)S(1)}, u32[]{:S(2)}, u32[]{:S(2)}) collective-permute-start(bf16[256,768]{1,0:T(8,128)(2,1)S(1)} %select_add_fusion.1), channel_id=1, source_target_pairs={{2,4},{3,5},{4,2},{5,3},{10,12},{11,13},{12,10},{13,11},{18,20},{1... | collective-permute-start | bytes 1179656 | tf_op jit(solution)/shard_map/ppermute | solution.py:878
  198.8 12.9 %collective-permute-start.27 = (bf16[256,768]{1,0:T(8,128)(2,1)S(1)}, bf16[256,768]{1,0:T(8,128)(2,1)S(1)}, u32[]{:S(2)}, u32[]{:S(2)}) collective-permute-start(bf16[256,768]{1,0:T(8,128)(2,1)S(1)} %select_add_fusion.1), channel_id=1, source_target_pairs={{0,2},{1,3},{6,4},{7,5},{8,10},{9,11},{14,12},{15,13},{16,18},{17,... | collective-permute-start | bytes 1179656 | tf_op jit(solution)/shard_map/ppermute | solution.py:878
  202.2 4.9 %collective-permute-start.29 = (bf16[160,384]{1,0:T(8,128)(2,1)S(1)}, bf16[160,384]{1,0:T(8,128)(2,1)S(1)}, u32[]{:S(2)}, u32[]{:S(2)}) collective-permute-start(bf16[160,384]{1,0:T(8,128)(2,1)S(1)} %fusion.1), channel_id=1, source_target_pairs={{0,8},{8,0},{16,24},{24,16},{1,9},{9,1},{17,25},{25,17},{2,10},{10... | collective-permute-start | bytes 368648 | tf_op jit(solution)/shard_map/ppermute | solution.py:870
  207.2 50.5 %copy-start.12 = (bf16[544,384]{1,0:T(8,128)(2,1)}, bf16[544,384]{1,0:T(8,128)(2,1)S(1)}, u32[]{:S(2)}) copy-start(bf16[544,384]{1,0:T(8,128)(2,1)S(1)} %pad_maximum_fusion.1.refs_0_) | copy-start | bytes 1253380
  207.2 4.5 %collective-permute-start.31 = (bf16[544,384]{1,0:T(8,128)(2,1)S(1)}, bf16[544,384]{1,0:T(8,128)(2,1)S(1)}, u32[]{:S(2)}, u32[]{:S(2)}) collective-permute-start(bf16[544,384]{1,0:T(8,128)(2,1)S(1)} %pad_maximum_fusion.1.refs_0_), channel_id=1, source_target_pairs={{2,4},{3,5},{4,2},{5,3},{10,12},{11,13},{12,10},{13,11},{18,20},{1... | collective-permute-start | bytes 1253384 | tf_op jit(solution)/shard_map/ppermute | solution.py:878
  208.1 11.0 %collective-permute-start.30 = (bf16[544,384]{1,0:T(8,128)(2,1)S(1)}, bf16[544,384]{1,0:T(8,128)(2,1)S(1)}, u32[]{:S(2)}, u32[]{:S(2)}) collective-permute-start(bf16[544,384]{1,0:T(8,128)(2,1)S(1)} %pad_maximum_fusion.1.refs_0_), channel_id=1, source_target_pairs={{0,2},{1,3},{2,0},{3,1},{4,6},{5,7},{6,4},{7,5},{8,10},{9,11},{10,... | collective-permute-start | bytes 1253384 | tf_op jit(solution)/shard_map/ppermute | solution.py:878
  210.1 1.4 collective-permute-start.32
  211.5 35.0 %copy-start.44 = (bf16[128,768]{1,0:T(8,128)(2,1)S(1)}, bf16[128,768]{1,0:T(8,128)(2,1)}, u32[]{:S(2)}) copy-start(bf16[128,768]{1,0:T(8,128)(2,1)} %get-tuple-element.210) | copy-start | bytes 589828
  219.0 38.9 %copy-start.26 = (bf16[544,384]{1,0:T(8,128)(2,1)}, bf16[544,384]{1,0:T(8,128)(2,1)S(1)}, u32[]{:S(2)}) copy-start(bf16[544,384]{1,0:T(8,128)(2,1)S(1)} %collective-permute-done.30.refs_1_) | copy-start | bytes 1253380
  219.1 28.8 %copy-start.43 = (bf16[128,768]{1,0:T(8,128)(2,1)S(1)}, bf16[128,768]{1,0:T(8,128)(2,1)}, u32[]{:S(2)}) copy-start(bf16[128,768]{1,0:T(8,128)(2,1)} %get-tuple-element.208) | copy-start | bytes 589828
  219.1 13.9 %collective-permute-start.34 = (bf16[256,768]{1,0:T(8,128)(2,1)S(1)}, bf16[256,768]{1,0:T(8,128)(2,1)S(1)}, u32[]{:S(2)}, u32[]{:S(2)}) collective-permute-start(bf16[256,768]{1,0:T(8,128)(2,1)S(1)} %add.110), channel_id=1, source_target_pairs={{2,4},{3,5},{4,2},{5,3},{10,12},{11,13},{12,10},{13,11},{18,20},{1... | collective-permute-start | bytes 1179656 | tf_op jit(solution)/shard_map/ppermute | solution.py:878
  220.0 11.8 %collective-permute-start.37 = (bf16[96,768]{1,0:T(8,128)(2,1)S(1)}, bf16[96,768]{1,0:T(8,128)(2,1)S(1)}, u32[]{:S(2)}, u32[]{:S(2)}) collective-permute-start(bf16[96,768]{1,0:T(8,128)(2,1)S(1)} %bitcast_add_fusion.6), channel_id=1, source_target_pairs={{0,2},{1,3},{6,4},{7,5},{8,10},{9,11},{14,12},{15,13},{16,18},{17,... | collective-permute-start | bytes 442376 | tf_op jit(solution)/shard_map/ppermute | solution.py:878
  226.9 18.9 %collective-permute-start.35 = (bf16[544,384]{1,0:T(8,128)(2,1)S(1)}, bf16[544,384]{1,0:T(8,128)(2,1)S(1)}, u32[]{:S(2)}, u32[]{:S(2)}) collective-permute-start(bf16[544,384]{1,0:T(8,128)(2,1)S(1)} %collective-permute-done.31), channel_id=1, source_target_pairs={{0,2},{1,3},{2,0},{3,1},{4,6},{5,7},{6,4},{7,5},{8,10},{9,11},{10,... | collective-permute-start | bytes 1253384 | tf_op jit(solution)/shard_map/ppermute | solution.py:878
  227.0 18.8 %collective-permute-start.36 = (bf16[544,384]{1,0:T(8,128)(2,1)S(1)}, bf16[544,384]{1,0:T(8,128)(2,1)S(1)}, u32[]{:S(2)}, u32[]{:S(2)}) collective-permute-start(bf16[544,384]{1,0:T(8,128)(2,1)S(1)} %collective-permute-done.30.refs_1_), channel_id=1, source_target_pairs={{2,4},{3,5},{4,2},{5,3},{10,12},{11,13},{12,10},{13,11},{18,20},{1... | collective-permute-start | bytes 1253384 | tf_op jit(solution)/shard_map/ppermute | solution.py:878
  227.8 18.0 %collective-permute-start.33 = (bf16[256,768]{1,0:T(8,128)(2,1)S(1)}, bf16[256,768]{1,0:T(8,128)(2,1)S(1)}, u32[]{:S(2)}, u32[]{:S(2)}) collective-permute-start(bf16[256,768]{1,0:T(8,128)(2,1)S(1)} %select_add_fusion), channel_id=1, source_target_pairs={{0,2},{1,3},{2,0},{3,1},{4,6},{5,7},{6,4},{7,5},{8,10},{9,11},{10,... | collective-permute-start | bytes 1179656 | tf_op jit(solution)/shard_map/ppermute | solution.py:878
  231.7 14.0 %collective-permute-start.38 = (bf16[2,128,768]{2,1,0:T(8,128)(2,1)S(1)}, bf16[2,128,768]{2,1,0:T(8,128)(2,1)S(1)}, u32[]{:S(2)}, u32[]{:S(2)}) collective-permute-start(bf16[2,128,768]{2,1,0:T(8,128)(2,1)S(1)} %copy-done.53), channel_id=1, source_target_pairs={{0,8},{8,0},{16,24},{24,16},{1,9},{9,1},{17,25},{25,17},{2,10},{10... | collective-permute-start | bytes 1179656 | tf_op jit(solution)/shard_map/ppermute | solution.py:870
  233.1 12.7 %collective-permute-start.39 = (bf16[2,128,768]{2,1,0:T(8,128)(2,1)S(1)}, bf16[2,128,768]{2,1,0:T(8,128)(2,1)S(1)}, u32[]{:S(2)}, u32[]{:S(2)}) collective-permute-start(bf16[2,128,768]{2,1,0:T(8,128)(2,1)S(1)} %copy-done.52), channel_id=1, source_target_pairs={{0,16},{8,24},{16,0},{24,8},{1,17},{9,25},{17,1},{25,9},{2,18},{10... | collective-permute-start | bytes 1179656 | tf_op jit(solution)/shard_map/ppermute | solution.py:870
  245.8 10.4 %collective-permute-start.49 = (bf16[96,768]{1,0:T(8,128)(2,1)S(1)}, bf16[96,768]{1,0:T(8,128)(2,1)S(1)}, u32[]{:S(2)}, u32[]{:S(2)}) collective-permute-start(bf16[96,768]{1,0:T(8,128)(2,1)S(1)} %add.111), channel_id=1, source_target_pairs={{2,4},{3,5},{4,2},{5,3},{10,12},{11,13},{12,10},{13,11},{18,20},{1... | collective-permute-start | bytes 442376 | tf_op jit(solution)/shard_map/ppermute | solution.py:878
  246.5 11.1 %collective-permute-start.41 = (bf16[128,768]{1,0:T(8,128)(2,1)S(1)}, bf16[128,768]{1,0:T(8,128)(2,1)S(1)}, u32[]{:S(2)}, u32[]{:S(2)}) collective-permute-start(bf16[128,768]{1,0:T(8,128)(2,1)S(1)} %bitcast_add_fusion.2), channel_id=1, source_target_pairs={{0,8},{8,0},{16,24},{24,16},{1,9},{9,1},{17,25},{25,17},{2,10},{10... | collective-permute-start | bytes 589832 | tf_op jit(solution)/shard_map/ppermute | solution.py:870
  247.9 10.0 %collective-permute-start.40 = (bf16[128,768]{1,0:T(8,128)(2,1)S(1)}, bf16[128,768]{1,0:T(8,128)(2,1)S(1)}, u32[]{:S(2)}, u32[]{:S(2)}) collective-permute-start(bf16[128,768]{1,0:T(8,128)(2,1)S(1)} %bitcast_add_fusion.3), channel_id=1, source_target_pairs={{0,16},{8,24},{16,0},{24,8},{1,17},{9,25},{17,1},{25,9},{2,18},{10... | collective-permute-start | bytes 589832 | tf_op jit(solution)/shard_map/ppermute | solution.py:870
  251.7 18.0 %collective-permute-start.43 = (f32[128,768]{1,0:T(8,128)}, f32[128,768]{1,0:T(8,128)S(1)}, u32[]{:S(2)}, u32[]{:S(2)}) collective-permute-start(f32[128,768]{1,0:T(8,128)} %get-tuple-element.218), channel_id=1, source_target_pairs={{0,1},{1,0},{2,3},{3,2},{4,5},{5,4},{6,7},{7,6},{8,9},{9,8},{10,11... | collective-permute-start | bytes 1179656 | tf_op jit(solution)/shard_map/ppermute | solution.py:874
  251.7 19.5 %collective-permute-start.44 = (bf16[544,384]{1,0:T(8,128)(2,1)S(1)}, bf16[544,384]{1,0:T(8,128)(2,1)S(1)}, u32[]{:S(2)}, u32[]{:S(2)}) collective-permute-start(bf16[544,384]{1,0:T(8,128)(2,1)S(1)} %collective-permute-done.36), channel_id=1, source_target_pairs={{0,2},{1,3},{2,0},{3,1},{4,6},{5,7},{6,4},{7,5},{8,10},{9,11},{10,... | collective-permute-start | bytes 1253384 | tf_op jit(solution)/shard_map/ppermute | solution.py:878
  256.3 13.4 %collective-permute-start.50 = (bf16[96,768]{1,0:T(8,128)(2,1)S(1)}, bf16[96,768]{1,0:T(8,128)(2,1)S(1)}, u32[]{:S(2)}, u32[]{:S(2)}) collective-permute-start(bf16[96,768]{1,0:T(8,128)(2,1)S(1)} %add.114), channel_id=1, source_target_pairs={{2,0},{3,1},{4,6},{5,7},{10,8},{11,9},{12,14},{13,15},{18,16},{19,... | collective-permute-start | bytes 442376 | tf_op jit(solution)/shard_map/ppermute | solution.py:878
  257.7 16.0 %collective-permute-start.45 = (bf16[544,384]{1,0:T(8,128)(2,1)S(1)}, bf16[544,384]{1,0:T(8,128)(2,1)S(1)}, u32[]{:S(2)}, u32[]{:S(2)}) collective-permute-start(bf16[544,384]{1,0:T(8,128)(2,1)S(1)} %pad_maximum_fusion.1.refs_0_), channel_id=1, source_target_pairs={{0,1},{1,0},{2,3},{3,2},{4,5},{5,4},{6,7},{7,6},{8,9},{9,8},{10,11... | collective-permute-start | bytes 1253384 | tf_op jit(solution)/shard_map/ppermute | solution.py:874
  257.9 15.8 %collective-permute-start.46 = (bf16[544,384]{1,0:T(8,128)(2,1)S(1)}, bf16[544,384]{1,0:T(8,128)(2,1)S(1)}, u32[]{:S(2)}, u32[]{:S(2)}) collective-permute-start(bf16[544,384]{1,0:T(8,128)(2,1)S(1)} %collective-permute-done.30.refs_1_), channel_id=1, source_target_pairs={{0,1},{1,0},{2,3},{3,2},{4,5},{5,4},{6,7},{7,6},{8,9},{9,8},{10,11... | collective-permute-start | bytes 1253384 | tf_op jit(solution)/shard_map/ppermute | solution.py:874
  269.7 4.1 %collective-permute-start.47 = (bf16[544,384]{1,0:T(8,128)(2,1)S(1)}, bf16[544,384]{1,0:T(8,128)(2,1)S(1)}, u32[]{:S(2)}, u32[]{:S(2)}) collective-permute-start(bf16[544,384]{1,0:T(8,128)(2,1)S(1)} %broadcast_select_fusion.1.refs_2_), channel_id=1, source_target_pairs={{0,1},{1,0},{2,3},{3,2},{4,5},{5,4},{6,7},{7,6},{8,9},{9,8},{10,11... | collective-permute-start | bytes 1253384 | tf_op jit(solution)/shard_map/ppermute | solution.py:874
  269.7 2.2 collective-permute-start.42
  271.2 1.6 collective-permute-start.51
  271.9 1.9 collective-permute-start.48
  (49 other events, 345.0 us)
Sparse Core Ops, SparseCore 0:
  131.0 39.3 reduce-scatter.1

commit v3 on v2

--- a/solution.py
+++ b/solution.py
@@ -264,6 +264,7 @@
 PART = SHARD // 2
 QUART = SHARD // 4
 HALF = D // 2
+MIDDLE_ROW = 224
 VMEM_LIMIT = 56 * 1024 * 1024
 WHOLE = pl.BlockSpec(memory_space=pltpu.VMEM)
 ANYWHERE = pl.BlockSpec(memory_space=pl.ANY)
@@ -328,29 +329,9 @@
         copy.wait()
 
 
-def attend_kernel(own, pair, near, far, mid_near, mid_far, w0, w1, w2, w3, w4, gain_ref,
-                  normed_ref, kv_ref, mixt_ref, att_ref, low_ref, lse_ref, wfull_ref, x_ref, s_ref, sems, wsems):
-    z = lax.axis_index("ctx") // 2
+def attend_kernel(x_ref, w0, w1, w2, w3, w4,
+                  normed_ref, kv_ref, mixt_ref, att_ref, low_ref, lse_ref, wfull_ref, gains_ref, s_ref, g_ref, wsems):
     place = lax.axis_index("wshard")
-    end = (z == 0) | (z == 3)
-    near_slot = jnp.where(z < 2, 2, 1)
-    far_slot = jnp.where(z < 2, 3, 0)
-
-    def line_copies(do):
-        do(pltpu.make_async_copy(own, x_ref.at[z], sems.at[0]))
-        do(pltpu.make_async_copy(pair, x_ref.at[jnp.bitwise_xor(z, 1)], sems.at[1]))
-
-        @pl.when(end)
-        def _():
-            do(pltpu.make_async_copy(near, x_ref.at[near_slot], sems.at[2]))
-            do(pltpu.make_async_copy(far, x_ref.at[far_slot], sems.at[3]))
-
-        @pl.when(jnp.logical_not(end))
-        def _():
-            do(pltpu.make_async_copy(mid_near, x_ref.at[near_slot], sems.at[2]))
-            do(pltpu.make_async_copy(mid_far, x_ref.at[far_slot], sems.at[3]))
-
-    line_copies(lambda copy: copy.start())
     pieces = (w0, w1, w2, w3, w4)
     half = w3.shape[0]
     pairs = []
@@ -361,12 +342,15 @@
         else:
             pairs.append((w3, wfull_ref.at[pl.ds(to, half)]))
             pairs.append((w4.at[pl.ds(0, SHARD - half)], wfull_ref.at[pl.ds(to + half, SHARD - half)]))
+        source = w4.at[pl.ds(SHARD - half, 16)] if k == 3 else pieces[k].at[pl.ds(SHARD, 16)]
+        pairs.append((source, g_ref.at[k]))
     run_copies(pairs, wsems)
-    line_copies(lambda copy: copy.wait())
+    gains = jnp.concatenate([g_ref[jnp.bitwise_xor(place, j)][0:8, 0:SHARD].astype(F32) for j in range(4)], axis=1)
+    gains_ref[...] = gains
     for row in range(4):
         here = slice(row * TILE, (row + 1) * TILE)
         xhat, _ = normalised(x_ref[row].astype(F32))
-        normed = (xhat * gain_ref[...]).astype(BF)
+        normed = (xhat * gains[0:1]).astype(BF)
         normed_ref[here, :] = normed
         mix = nn(normed, wfull_ref[...]).astype(BF)
         mixt_ref[:, here] = mix.T
@@ -409,12 +393,12 @@
             lse_ref[pl.ds(h, 1), here] = top + jnp.log(total)
 
 
-def attend(line, pieces, gain):
+def attend(x_all, pieces):
     length = 4 * TILE
     return call(
         attend_kernel,
         "attend",
-        [ANYWHERE] * 11 + [WHOLE],
+        [WHOLE] + [ANYWHERE] * 5,
         [
             ((length, D), BF),
             ((OWN_HEADS, length, 2 * HEAD_DIM), BF),
@@ -423,42 +407,110 @@
             ((4, OWN, TILE), BF),
             ((8, length), F32),
             ((D, MIX), BF),
+            ((8, D), F32),
         ],
         [
-            pltpu.VMEM((4, TILE, D), BF),
             pltpu.VMEM((length, TILE), F32),
-            pltpu.SemaphoreType.DMA((4,)),
-            pltpu.SemaphoreType.DMA((5,)),
+            pltpu.VMEM((4, 16, MIX), BF),
+            pltpu.SemaphoreType.DMA((9,)),
         ],
         3 * 10**9,
-        (*line, *pieces, gain),
-    )
-
-
-def project_kernel(att_ref, x_ref, gain_ref, b0, b1, b2, b3, hidden_ref, normed_ref, wout_ref, sems):
+        (x_all, *pieces),
+    )
+
+
+def parcel_kernel(cot_ref, wout_ref, wup_ref, x_on_ref, x_ref, y_on_ref, y_ref, sems):
     place = lax.axis_index("wshard")
-    pairs = []
-    for k, (ref, first) in enumerate(((b0, TILE), (b1, TILE), (b2, TILE), (b3, b3.shape[0] - SHARD))):
-        to = pl.multiple_of(jnp.bitwise_xor(place, k) * SHARD, SHARD)
-        pairs.append((ref.at[pl.ds(first, SHARD)], wout_ref.at[pl.ds(to, SHARD)]))
+
+    def columns(k, first, count):
+        at = pl.multiple_of(jnp.bitwise_xor(place, k) * D, D)
+        return wup_ref.at[pl.ds(first, count), pl.ds(at, D)]
+
+    low, high = cot_ref.at[pl.ds(0, MIDDLE_ROW)], cot_ref.at[pl.ds(MIDDLE_ROW, 32)]
+    pairs = (
+        (low, x_on_ref.at[pl.ds(0, MIDDLE_ROW)]),
+        (columns(3, 0, PART), x_on_ref.at[pl.ds(MIDDLE_ROW, PART)]),
+        (high, y_on_ref.at[pl.ds(0, 32)]),
+        (wout_ref, y_on_ref.at[pl.ds(32, SHARD)]),
+        (columns(3, PART, PART), y_on_ref.at[pl.ds(MIDDLE_ROW, PART)]),
+        (columns(1, 0, SHARD), x_ref.at[pl.ds(0, SHARD)]),
+        (high, x_ref.at[pl.ds(SHARD, 32)]),
+        (wout_ref, x_ref.at[pl.ds(SHARD + 32, SHARD)]),
+        (columns(2, 0, SHARD), y_ref.at[pl.ds(0, SHARD)]),
+        (low, y_ref.at[pl.ds(SHARD, MIDDLE_ROW)]),
+    )
     run_copies(pairs, sems)
+
+
+def parcels(cot, w_out, w_up):
+    on, rest = MIDDLE_ROW + PART, SHARD + MIDDLE_ROW
+    return call(
+        parcel_kernel,
+        "parcels",
+        [ANYWHERE] * 3,
+        [((on, D), BF), ((rest, D), BF)] * 2,
+        [pltpu.SemaphoreType.DMA((10,))],
+        10**6,
+        (cot, w_out, w_up),
+    )
+
+
+def assemble_kernel(cot_ref, own_ref, wup_ref, x_on, x_rest, y_on, y_rest, corner_a, corner_b,
+                    wout_ref, up_ref, cots_ref, sems):
+    place = lax.axis_index("wshard")
+    at = [pl.multiple_of(jnp.bitwise_xor(place, k) * SHARD, SHARD) for k in range(4)]
+    half = PART
+    mine = pl.multiple_of(place * D, D)
+    pairs = (
+        (own_ref, wout_ref.at[pl.ds(at[0], SHARD)]),
+        (x_rest.at[pl.ds(SHARD + 32, SHARD)], wout_ref.at[pl.ds(at[1], SHARD)]),
+        (y_on.at[pl.ds(32, SHARD)], wout_ref.at[pl.ds(at[2], SHARD)]),
+        (corner_b.at[pl.ds(32, SHARD)], wout_ref.at[pl.ds(at[3], SHARD)]),
+        (wup_ref.at[:, pl.ds(mine, D)], up_ref.at[pl.ds(at[0], SHARD)]),
+        (x_rest.at[pl.ds(0, SHARD)], up_ref.at[pl.ds(at[1], SHARD)]),
+        (y_rest.at[pl.ds(0, SHARD)], up_ref.at[pl.ds(at[2], SHARD)]),
+        (corner_a.at[pl.ds(MIDDLE_ROW, half)], up_ref.at[pl.ds(at[3], half)]),
+        (corner_b.at[pl.ds(MIDDLE_ROW, half)], up_ref.at[pl.ds(at[3] + half, half)]),
+        (cot_ref, cots_ref.at[pl.ds(0, TILE)]),
+        (x_on.at[pl.ds(0, MIDDLE_ROW)], cots_ref.at[pl.ds(TILE, MIDDLE_ROW)]),
+        (x_rest.at[pl.ds(SHARD, 32)], cots_ref.at[pl.ds(TILE + MIDDLE_ROW, 32)]),
+        (y_rest.at[pl.ds(SHARD, MIDDLE_ROW)], cots_ref.at[pl.ds(2 * TILE, MIDDLE_ROW)]),
+        (y_on.at[pl.ds(0, 32)], cots_ref.at[pl.ds(2 * TILE + MIDDLE_ROW, 32)]),
+        (corner_a.at[pl.ds(0, MIDDLE_ROW)], cots_ref.at[pl.ds(3 * TILE, MIDDLE_ROW)]),
+        (corner_b.at[pl.ds(0, 32)], cots_ref.at[pl.ds(3 * TILE + MIDDLE_ROW, 32)]),
+    )
+    run_copies(pairs, sems)
+
+
+def assemble(cot, w_out, w_up, shared):
+    return call(
+        assemble_kernel,
+        "assemble",
+        [ANYWHERE] * 9,
+        [((D, D), BF), ((D, D), BF), ((4 * TILE, D), BF)],
+        [pltpu.SemaphoreType.DMA((16,))],
+        10**6,
+        (cot, w_out, w_up, *shared),
+    )
+
+
+def project_kernel(att_ref, x_ref, gain_ref, wout_ref, hidden_ref, normed_ref):
     hidden = x_ref[...].astype(F32) + nn(att_ref[...].T, wout_ref[...])
     hidden_ref[...] = hidden
     xhat, _ = normalised(hidden)
-    normed_ref[...] = (xhat * gain_ref[...]).astype(BF)
-
-
-def project(att_home, x_block, gain, shared):
+    normed_ref[...] = (xhat * gain_ref[1:2]).astype(BF)
+
+
+def project(att_home, x_block, gain, w_out):
     rows = x_block.shape[0]
-    own, from_x, from_y, _, low = shared
     return call(
         project_kernel,
         "project",
-        [WHOLE] * 3 + [ANYWHERE] * 4,
-        [((rows, D), F32), ((rows, D), BF), ((D, D), BF)],
-        [pltpu.SemaphoreType.DMA((4,))],
+        [WHOLE] * 4,
+        [((rows, D), F32), ((rows, D), BF)],
+        [],
         3 * 10**8,
-        (att_home, x_block, gain, own, from_x, from_y, low),
+        (att_home, x_block, gain, w_out),
     )
 
 
@@ -484,7 +536,7 @@
     )
 
 
-def feed_own(n, shared, up, down):
+def feed_own(n, cots, up, down):
     return call(
         feed_own_kernel,
         "feed_own",
@@ -492,34 +544,33 @@
         [((TILE, D), BF), ((TILE, D), BF), ((TILE, D), F32), ((TILE, D), F32)],
         [],
         2 * 10**9,
-        (n, shared[0], up, down),
-    )
-
-
-def feed_near_kernel(nx_ref, ny_ref, cx_ref, cy_ref, up_ref, down_ref, active_ref, dup_ref, out_ref, dout_ref):
-    for k, (n_ref, cot_ref) in enumerate(((nx_ref, cx_ref), (ny_ref, cy_ref))):
+        (n, cots, up, down),
+    )
+
+
+def feed_near_kernel(nx_ref, ny_ref, cot_ref, up_ref, down_ref, active_ref, dup_ref, out_ref, dout_ref):
+    for k, n_ref in enumerate((nx_ref, ny_ref)):
         here = slice(k * TILE, (k + 1) * TILE)
-        out, dout = feed_rows(n_ref[...], cot_ref[0:TILE, :], up_ref, down_ref, active_ref, dup_ref, here)
+        out, dout = feed_rows(n_ref[...], cot_ref[(k + 1) * TILE : (k + 2) * TILE, :], up_ref, down_ref, active_ref, dup_ref, here)
         out_ref[here, :], dout_ref[here, :] = out.astype(BF), dout.astype(BF)
 
 
-def feed_near(nx, ny, shared, up, down):
+def feed_near(nx, ny, cots, up, down):
     return call(
         feed_near_kernel,
         "feed_near",
-        [WHOLE] * 6,
+        [WHOLE] * 5,
         [((2 * TILE, D), BF)] * 4,
         [],
         4 * 10**9,
-        (nx, ny, shared[1], shared[2], up, down),
-    )
-
-
-def feed_far_kernel(na_ref, nb_ref, ca_ref, cb_ref, out_ref, dout_ref, up_ref, down_ref,
+        (nx, ny, cots, up, down),
+    )
+
+
+def feed_far_kernel(na_ref, nb_ref, cot_ref, out_ref, dout_ref, up_ref, down_ref,
                     active_ref, dup_ref, oa_ref, oaf_ref, ob_ref, obf_ref, da_ref, daf_ref, db_ref, dbf_ref):
     n = jnp.concatenate([na_ref[...], nb_ref[...]])
-    first = ca_ref.shape[0]
-    cot = jnp.concatenate([ca_ref[...], cb_ref[0 : TILE - first, :]])
+    cot = cot_ref[3 * TILE :, :]
     half = TILE // 2
     out, dout = feed_rows(n, cot, up_ref, down_ref, active_ref, dup_ref, slice(0, TILE))
     for far, near, a, af, b, bf in (
@@ -533,29 +584,24 @@
         bf[...] = near[half:TILE, :]
 
 
-def feed_far(na, nb, shared, out, dout, up, down):
+def feed_far(na, nb, cots, out, dout, up, down):
     half = TILE // 2
     return call(
         feed_far_kernel,
         "feed_far",
-        [WHOLE] * 8,
+        [WHOLE] * 7,
         [((TILE, D), BF)] * 2 + [((2, half, D), BF), ((half, D), BF)] * 4,
         [],
         2 * 10**9,
-        (na, nb, shared[3], shared[4], out, dout, up, down),
-    )
-
-
-def feed_grads_kernel(n0, n1, n2, n3, n4, c0, c1, c2, c3, c4, a0, a1, a2, d0, d1, d2,
-                      shares_ref, nt_ref, cot_ref, at_ref, dup_ref):
-    first = c3.shape[0]
+        (na, nb, cots, out, dout, up, down),
+    )
+
+
+def feed_grads_kernel(n0, n1, n2, n3, n4, cot_ref, a0, a1, a2, d0, d1, d2,
+                      shares_ref, nt_ref, at_ref, dup_ref):
     for k, piece in enumerate((n0, n1, n2)):
         nt_ref[:, k * TILE : (k + 1) * TILE] = piece[...].T
     nt_ref[:, 3 * TILE :] = jnp.concatenate([n3[...], n4[...]]).T
-    for k, piece in enumerate((c0, c1, c2)):
-        cot_ref[k * TILE : (k + 1) * TILE] = piece[0:TILE, :]
-    cot_ref[3 * TILE : 3 * TILE + first] = c3[...]
-    cot_ref[3 * TILE + first :] = c4[0 : TILE - first, :]
     at_ref[:, 0:TILE] = a0[...].T
     at_ref[:, TILE : 3 * TILE] = a1[...].T
     at_ref[:, 3 * TILE :] = a2[...].T
@@ -566,29 +612,31 @@
     for k in range(8):
         g = nn(at_ref[k * rows : (k + 1) * rows, :], cot_ref[...]).astype(BF)
         for side in range(2):
-            shares_ref[k, SHARD + side * rows : SHARD + (side + 1) * rows] = g[:, side * HALF : (side + 1) * HALF]
+            for part in range(2):
+                piece = g[part * QUART : (part + 1) * QUART, side * HALF : (side + 1) * HALF]
+                shares_ref[k, 4 + 2 * side + part] = piece
     for to in range(4):
         g = nn(nt_ref[to * SHARD : (to + 1) * SHARD, :], dup_ref[...]).astype(BF)
+        slot = jnp.bitwise_xor(lax.axis_index("wshard"), to)
         for k in range(8):
             r, c = (k // 2) * QUART, (k % 2) * HALF
-            shares_ref[k, to * QUART : (to + 1) * QUART] = g[r : r + QUART, c : c + HALF]
-
-
-def feed_grads(ns, shared, actives, dups):
+            shares_ref[k, slot] = g[r : r + QUART, c : c + HALF]
+
+
+def feed_grads(ns, cots, actives, dups):
     length = 4 * TILE
     return call(
         feed_grads_kernel,
         "feed_grads",
-        [WHOLE] * 16,
-        [((8, 2 * SHARD, HALF), BF)],
+        [WHOLE] * 12,
+        [((8, 8, QUART, HALF), BF)],
         [
             pltpu.VMEM((D, length), BF),
-            pltpu.VMEM((length, D), BF),
             pltpu.VMEM((D, length), BF),
             pltpu.VMEM((length, D), BF),
         ],
         3 * 10**9,
-        (*ns, *shared, *actives, *dups),
+        (*ns, cots, *actives, *dups),
     )[0]
 
 
@@ -622,7 +670,7 @@
 
 def turn_kernel(hidden_ref, gain_ref, dkeep_ref, a_ref, a_more_ref, b_ref, b_more_ref, cot_ref, wout_ref,
                 dhidden_ref, datt_ref, dbranch_ref, dgain_ref):
-    gain = gain_ref[...]
+    gain = gain_ref[1:2]
     xhat, inverse = normalised(hidden_ref[...])
     dy = summed(dkeep_ref, a_ref, a_more_ref, b_ref, b_more_ref)
     dgain_ref[...] = jnp.sum(dy * xhat, axis=0, keepdims=True)
@@ -648,18 +696,19 @@
     )
 
 
-def out_grad_kernel(att_ref, dbranch_ref, own_ref, far_ref, send_ref, grad_ref, sems):
+def out_grad_kernel(att_ref, dbranch_ref, keep_ref, send_ref, grad_ref, sems):
+    core = lax.axis_index("ctx") % 2
     place = lax.axis_index("wshard")
-    x, y = jnp.bitwise_and(place, 1), place // 2
     for to in range(4):
-        g = nn(att_ref[to * SHARD : (to + 1) * SHARD, :], dbranch_ref[...])
-        grad_ref[to % 2, to // 2] = g.astype(BF)
-    pairs = (
-        (grad_ref.at[1 - x, y], send_ref.at[0]),
-        (grad_ref.at[1 - x, 1 - y], send_ref.at[1]),
-        (grad_ref.at[x, 1 - y], far_ref),
-        (grad_ref.at[x, y], own_ref),
-    )
+        e = jnp.bitwise_xor(place, to)
+        e_x, e_y = jnp.bitwise_and(e, 1), e // 2
+        g = nn(att_ref[to * SHARD : (to + 1) * SHARD, :], dbranch_ref[...]).astype(BF)
+        for side in range(2):
+            for half in range(2):
+                piece = g[side * PART : (side + 1) * PART, half * HALF : (half + 1) * HALF]
+                grad_ref[side, e_y, e_x, half * PART : (half + 1) * PART] = piece
+    rows = pl.ds(HEAD_ROWS, SHARD)
+    pairs = ((grad_ref.at[1 - core], send_ref.at[:, :, rows]), (grad_ref.at[core], keep_ref.at[:, :, rows]))
     run_copies(pairs, sems)
 
 
@@ -668,15 +717,15 @@
         out_grad_kernel,
         "out_grad",
         [WHOLE] * 2,
-        [((SHARD, D), BF), ((SHARD, D), BF), ((2, SHARD, D), BF)],
-        [pltpu.VMEM((2, 2, SHARD, D), BF), pltpu.SemaphoreType.DMA((4,))],
+        [((2, 2, HEAD_ROWS + SHARD, HALF), BF)] * 2,
+        [pltpu.VMEM((2, 2, 2, SHARD, HALF), BF), pltpu.SemaphoreType.DMA((2,))],
         3 * 10**8,
         (att_home, d_branch),
-        [ANYWHERE] * 3,
-    )
-
-
-def attend_back_kernel(kv_ref, mixt_ref, att_ref, lse_ref, dout_ref, normed_ref, w_ref, gain_ref, dgain_ref,
+        [ANYWHERE] * 2,
+    )
+
+
+def attend_back_kernel(kv_ref, mixt_ref, att_ref, lse_ref, dout_ref, normed_ref, w_ref, gain_ref, dgain_ref, _, __,
                        f0_ref, f1_ref, f2_ref, f3_ref, gkeep_ref, gsend_ref,
                        dq_ref, dk_ref, dv_ref, dm_ref, mix_ref, total_ref, first_ref, head_ref, sems):
     length = normed_ref.shape[0]
@@ -738,7 +787,7 @@
     ]
     for copy in copies:
         copy.start()
-    gain_one = total_ref[...] / gain_ref[...]
+    gain_one = total_ref[...] / gain_ref[0:1]
     gain_two = dgain_ref[...]
     for to in range(4):
         e = jnp.bitwise_xor(place, to)
@@ -754,8 +803,8 @@
             head_ref[side, e_y, e_x, PART : PART + QUART, OWN:] = g[at + QUART : at + PART, HALF:]
             head_ref[side, e_y, e_x, PART + QUART :] = gains if side == 0 else jnp.zeros_like(gains)
     more = [
-        pltpu.make_async_copy(head_ref.at[1 - core], gsend_ref, sems.at[4]),
-        pltpu.make_async_copy(head_ref.at[core], gkeep_ref, sems.at[5]),
+        pltpu.make_async_copy(head_ref.at[1 - core], gsend_ref.at[:, :, pl.ds(0, HEAD_ROWS)], sems.at[4]),
+        pltpu.make_async_copy(head_ref.at[core], gkeep_ref.at[:, :, pl.ds(0, HEAD_ROWS)], sems.at[5]),
     ]
     for copy in more:
         copy.start()
@@ -763,14 +812,15 @@
         copy.wait()
 
 
-def attend_back(kv, mixt, att, lse, dout, normed, w, gain, dgain):
+def attend_back(kv, mixt, att, lse, dout, normed, w, gain, dgain, keep, send):
     length = normed.shape[0]
-    return call(
+    return pl.pallas_call(
         attend_back_kernel,
-        "attend_back",
-        [WHOLE] * 9,
-        [((TILE, D), BF)] * 4 + [((2, 2, HEAD_ROWS, HALF), BF)] * 2,
-        [
+        in_specs=[WHOLE] * 9 + [ANYWHERE] * 2,
+        out_specs=[ANYWHERE] * 6,
+        out_shape=[jax.ShapeDtypeStruct((TILE, D), BF)] * 4 + [jax.ShapeDtypeStruct(keep.shape, BF)] * 2,
+        input_output_aliases={9: 4, 10: 5},
+        scratch_shapes=[
             pltpu.VMEM((HEAD_DIM, length), F32),
             pltpu.VMEM((length, HEAD_DIM), F32),
             pltpu.VMEM((length, HEAD_DIM), F32),
@@ -781,10 +831,10 @@
             pltpu.VMEM((2, 2, 2, HEAD_ROWS, HALF), BF),
             pltpu.SemaphoreType.DMA((6,)),
         ],
-        5 * 10**9,
-        (kv, mixt, att, lse, dout, normed, w, gain, dgain),
-        [ANYWHERE] * 6,
-    )
+        compiler_params=pltpu.CompilerParams(vmem_limit_bytes=VMEM_LIMIT),
+        cost_estimate=pl.CostEstimate(flops=1000, bytes_accessed=1000, transcendentals=0),
+        name="attend_back",
+    )(kv, mixt, att, lse, dout, normed, w, gain, dgain, keep, send)
 
 
 def is_inner():
@@ -798,7 +848,7 @@
     dy = first_ref[...].astype(F32) + pair_ref[...].astype(F32)
     dy = dy + jnp.where(is_inner(), middle_ref[...].astype(F32), 0.0)
     xhat, inverse = normalised(x_ref[...].astype(F32))
-    grad = dhidden_ref[...] + norm_back(xhat, inverse, gain_ref[...], dy)
+    grad = dhidden_ref[...] + norm_back(xhat, inverse, gain_ref[0:1], dy)
     grad_ref[0], grad_ref[1] = grad[:rows], grad[rows:]
     run_copies(((grad_ref.at[1 - core], send_ref), (grad_ref.at[core], keep_ref)), sems)
 
@@ -817,31 +867,53 @@
     )
 
 
-def finish_kernel(*refs):
-    mine, theirs, (gup_ref, gdown_ref, gqkv_ref, gains_ref) = refs[:4], refs[4:8], refs[8:]
+def line_slots():
+    z = lax.axis_index("ctx") // 2
+    return z, jnp.bitwise_xor(z, 1), jnp.where(z < 2, 2, 1), jnp.where(z < 2, 3, 0)
+
+
+def finish_feed_kernel(*refs):
+    mine, theirs, (gup_ref, gdown_ref) = refs[:4], refs[4:8], refs[8:]
     core = lax.axis_index("ctx") % 2
-    z = lax.axis_index("ctx") // 2
+    place = lax.axis_index("wshard")
     rows = D // 8
-    slots = (z, jnp.bitwise_xor(z, 1), jnp.where(z < 2, 2, 1), jnp.where(z < 2, 3, 0))
     for group, side in ((mine, core), (theirs, 1 - core)):
-        for ref, slot in zip(group, slots):
+        for ref, slot in zip(group, line_slots()):
             at = pl.multiple_of(slot * QUART, 16)
-            for j in range(4):
-                to = pl.multiple_of(j * D + side * HALF, 128)
-                gup_ref[pl.ds(at, QUART), pl.ds(to, HALF)] = ref[j * QUART : (j + 1) * QUART].astype(F32)
+            for k in range(4):
+                to = pl.multiple_of(jnp.bitwise_xor(place, k) * D + side * HALF, 128)
+                gup_ref[pl.ds(at, QUART), pl.ds(to, HALF)] = ref[k * QUART : (k + 1) * QUART].astype(F32)
             at = pl.multiple_of((2 * slot + side) * rows, 32)
             for half in range(2):
                 share = ref[SHARD + half * rows : SHARD + (half + 1) * rows]
                 gdown_ref[pl.ds(at, rows), half * HALF : (half + 1) * HALF] = share.astype(F32)
-    first = core == 0
-    mine, theirs = [[ref[2 * SHARD :].astype(F32) for ref in group] for group in (mine, theirs)]
+
+
+def finish_feed(*args):
+    return call(
+        finish_feed_kernel, "finish_feed", [WHOLE] * 8, [((SHARD, 4 * D), F32), ((D, D), F32)], [], 10**7, args
+    )
+
+
+def finish_heads_kernel(*refs):
+    mine, theirs, outs, (gout_ref, gqkv_ref, gains_ref) = refs[:4], refs[4:8], refs[8:10], refs[10:]
+    slots = line_slots()
+    first = lax.axis_index("ctx") % 2 == 0
+    out, other_out = [ref[...].astype(F32) for ref in outs]
+    for half in range(2):
+        here, cols = slice(half * PART, (half + 1) * PART), slice(half * HALF, (half + 1) * HALF)
+        gout_ref[0:PART, cols] = jnp.where(first, out[here], other_out[here])
+        gout_ref[PART:, cols] = jnp.where(first, other_out[here], out[here])
+    mine, theirs = [[ref[...].astype(F32) for ref in group] for group in (mine, theirs)]
     low = [jnp.where(first, a, b) for a, b in zip(mine, theirs)]
     high = [jnp.where(first, b, a) for a, b in zip(mine, theirs)]
     gains_ref[...] = sum(block[PART + QUART :, 0:SHARD] for block in low)
     for slot in range(4):
         for side, group in enumerate((low, high)):
             block = jnp.where(
-                slot == z, group[0], jnp.where(slot == slots[1], group[1], jnp.where(slot == slots[2], group[2], group[3]))
+                slot == slots[0],
+                group[0],
+                jnp.where(slot == slots[1], group[1], jnp.where(slot == slots[2], group[2], group[3])),
             )
             at, to = side * PART, slot * OWN
             gqkv_ref[at : at + PART, to : to + OWN] = block[0:PART, 0:OWN]
@@ -850,12 +922,12 @@
             gqkv_ref[at + QUART : at + PART, 2 * D + to : 2 * D + to + OWN] = block[PART : PART + QUART, OWN:]
 
 
-def finish(*args):
-    return call(
-        finish_kernel,
-        "finish",
-        [WHOLE] * 8,
-        [((SHARD, 4 * D), F32), ((D, D), F32), ((SHARD, 3 * D), F32), ((16, SHARD), F32)],
+def finish_heads(*args):
+    return call(
+        finish_heads_kernel,
+        "finish_heads",
+        [WHOLE] * 10,
+        [((SHARD, D), F32), ((SHARD, 3 * D), F32), ((16, SHARD), F32)],
         [],
         10**7,
         args,
@@ -942,92 +1014,83 @@
 
     w_heads = pick(w_qkv.reshape(SHARD, 3, 4, OWN), z, 2).reshape(SHARD, MIX)
     gains = jnp.pad(jnp.stack([gain_one, gain_two]), ((0, 30), (0, MIX - SHARD)))
-    w_heads = after(jnp.concatenate([w_heads, gains]), x_block)
-    pair, mid_near = between_z(x_block, PAIRS), between_z(x_block, MIDDLE)
-    heads_x, heads_y = across_w(w_heads, 1), across_w(w_heads, 2)
-    pair, mid_near, heads_x, heads_y = tied(pair, mid_near, heads_x, heads_y)
-    near, mid_far = between_z(mid_near, PAIRS), between_z(pair, MIDDLE)
-    middle = w_heads.shape[0] // 2
-    heads = w_heads, heads_x, heads_y, across_w(heads_x[:middle], 2), across_w(heads_y[middle:], 1)
-    far = between_z(mid_far, PAIRS)
-    shared, *heads = tied(jnp.concatenate([cot, w_out]), *heads)
-    shared_x, shared_y = across_w(shared, 1), across_w(shared, 2)
-    line = x_block, pair, near, far, mid_near, mid_far
-    up, *line = tied(w_up.reshape(SHARD, 4, D).transpose(1, 0, 2), *line)
-    up = lax.all_to_all(up, "wshard", 0, 0, tiled=True).reshape(D, D)
-    at = SHARD - heads[3].shape[0]
-    gains = jnp.stack([heads[k][SHARD : SHARD + 2] for k in range(3)] + [heads[4][at : at + 2]])
-    gains = gains[:, :, :SHARD].astype(F32)
-    gains = jnp.concatenate([pick(gains, place ^ j) for j in range(4)], axis=1)
-    gain_first, gain_second = gains[0:1], gains[1:2]
-
-    normed_all, kv, mixt, att, att_low, lse, w_full = attend(line, heads, gain_first)
-    att_low, up, shared_x, shared_y = tied(att_low, up, shared_x, shared_y)
-    middle = shared.shape[0] // 2
-    shared = shared, shared_x, shared_y, across_w(shared_x[:middle], 2), across_w(shared_y[middle:], 1)
+    x_all = lax.all_to_all(
+        jnp.broadcast_to(x_block, (4,) + x_block.shape), "ctx", 0, 0, tiled=True, axis_index_groups=Z_GROUPS
+    )
+    x_on, x_rest, y_on, y_rest = parcels(cot, w_out, w_up)
+    x_on, y_on = across_w(x_on, 1), across_w(y_on, 2)
+    x_on, y_on, w_heads = tied(x_on, y_on, jnp.concatenate([w_heads, gains]))
+    heads = gather_plane(w_heads)
+    corner_a, corner_b = across_w(x_on, 2), across_w(y_on, 1)
+    x_rest, y_rest, *heads = tied(x_rest, y_rest, *heads)
+    x_rest, y_rest = across_w(x_rest, 1), across_w(y_rest, 2)
+    normed_all, kv, mixt, att, att_low, lse, w_full, gains = attend(x_all, heads)
+    shared = x_on, x_rest, y_on, y_rest, corner_a, corner_b
+    att_low, *shared = tied(att_low, *shared)
     att_home = lax.all_to_all(att_low, "ctx", 0, 0, tiled=True, axis_index_groups=Z_GROUPS).reshape(D, -1)
-    hidden, normed_two, wout_full = project(att_home, x_block, gain_second, shared)
-
-    active0, dup0, out0, dout0 = feed_own(normed_two, shared, up, w_down)
+    wout_full, up, cots = assemble(cot, w_out, w_up, shared)
+    hidden, normed_two = project(att_home, x_block, gains, wout_full)
+
+    active0, dup0, out0, dout0 = feed_own(normed_two, cots, up, w_down)
     ns = gather_plane(normed_two, active0)
-    active1, dup1, out1, dout1 = feed_near(ns[1], ns[2], shared, up, w_down)
-    active2, dup2, *parts = feed_far(ns[3], ns[4], shared, out1, dout1, up, w_down)
+    active1, dup1, out1, dout1 = feed_near(ns[1], ns[2], cots, up, w_down)
+    active2, dup2, *parts = feed_far(ns[3], ns[4], cots, out1, dout1, up, w_down)
     parts, (a, a_far, b, b_far) = parts[:4], parts[4:]
     got_a, got_b = across_w(a, 1), across_w(b, 2)
-    shares = feed_grads(ns, shared, (active0, active1, active2), (dup0, dup1, dup2))
+    shares = feed_grads(ns, cots, (active0, active1, active2), (dup0, dup1, dup2))
     shares, got_a, got_b = tied(shares, got_a, got_b)
     shares = lax.psum_scatter(shares, "ctx", scatter_dimension=0)
     more_a, more_b = across_w(a_far + got_a[1], 2), across_w(b_far + got_b[1], 1)
     d_hidden, d_att, d_branch, d_gain_two = turn(
-        hidden, gain_second, dout0, (got_a, more_a, got_b, more_b), cot, wout_full
+        hidden, gains, dout0, (got_a, more_a, got_b, more_b), cot, wout_full
     )
     d_out = lax.all_to_all(d_att, "ctx", 0, 0, tiled=True, axis_index_groups=Z_GROUPS)
-    out_own, out_far, out_send = out_grad(att_home, d_branch)
-    d_out, out_send = tied(d_out, out_send)
-    out_got = across_w(out_send, 1)
-    *firsts, head_keep, head_send = attend_back(
-        kv, mixt, att, lse, d_out, normed_all, w_full, gain_first, d_gain_two
-    )
-    *firsts, head_keep, head_send, out_got = tied(*firsts, head_keep, head_send, out_got)
+    keep, send = out_grad(att_home, d_branch)
+    d_out, keep, send = tied(d_out, keep, send)
+    a, a_far, b, b_far = parts
+    got_a, got_b = across_w(a, 1), across_w(b, 2)
+    *firsts, keep, send = attend_back(
+        kv, mixt, att, lse, d_out, normed_all, w_full, gains, d_gain_two, keep, send
+    )
+    *firsts, keep, send, shares, got_a, got_b = tied(*firsts, keep, send, shares, got_a, got_b)
 
     got = between_z(firsts[3], TO_MIDDLE)
-    sum_head = head_keep + across_core(head_send)
-    head_got = across_w(sum_head[1], 2)
-    out_far = across_w(out_far + out_got[1], 2)
-    up_share = lax.all_to_all(shares[:SHARD].reshape(4, QUART, HALF), "wshard", 0, 0, tiled=True)
-    got, head_got, out_far, up_share, *parts = tied(got, head_got, out_far, up_share, *parts)
-
     both = firsts[2] + jnp.where(inner, got, BF(0))
     outer, middle = between_z(both, TO_MIDDLE), between_z(both, ACROSS)
-    head_far = across_w(sum_head[0, 1] + head_got[1], 1)
-    head = (sum_head[0, 0] + head_got[0]) + head_far
-    share = jnp.concatenate([up_share.reshape(SHARD, HALF), shares[SHARD:], head])
-    share_pair, share_mid = between_z(share, PAIRS), between_z(share, ACROSS)
-    sum_out = ((out_own + out_got[0]) + out_far).reshape(2, PART, D)
-    sum_out = pick(sum_out, core) + across_core(pick(sum_out, 1 - core))
-    outer, middle, share_pair, share_mid, sum_out, *parts = tied(outer, middle, share_pair, share_mid, sum_out, *parts)
-
     pair = between_z(firsts[1] + jnp.where(inner, middle, BF(0)), PAIRS)
     middle = between_z(firsts[3] + outer, ACROSS)
-    share_near, share_far = between_z(share_mid, PAIRS), between_z(share_pair, ACROSS)
-    a, a_far, b, b_far = parts
-    got_a, got_b = across_w(a, 1), across_w(b, 2)
-    sum_out = sum_out + between_z(sum_out, TO_MIDDLE)
-    pair, middle, share_near, share_far, sum_out, got_a, got_b = tied(
-        pair, middle, share_near, share_far, sum_out, got_a, got_b
-    )
-
-    share_last = between_z(share_far, PAIRS)
-    sum_out = sum_out + between_z(sum_out, ACROSS)
-    grad_keep, grad_send = last(firsts[0], pair, middle, x_block, gain_first, d_hidden)
+
+    ups = [shares[0]] + [across_w(shares[e], e) for e in (1, 2, 3)]
+    share = jnp.concatenate(ups + [shares[4:].reshape(SHARD, HALF)])
+    share_pair, share_mid = between_z(share, PAIRS), between_z(share, ACROSS)
+    share_near, share_mid_far = between_z(share_mid, TO_ENDS), between_z(share_pair, ACROSS)
+    share_far = between_z(share_mid_far, TO_ENDS)
+    blocks = share, share_pair, jnp.where(inner, share_mid, share_near), jnp.where(inner, share_mid_far, share_far)
+    grad_up, grad_down = finish_feed(*blocks, *(across_core(block) for block in blocks))
+
+    sums, a_far, b_far = tied(keep + across_core(send), a_far, b_far)
+    sums_got = across_w(sums[1], 2)
+    sums_far = across_w(sums[0, 1] + sums_got[1], 1)
+    sums, a_far, b_far = tied((sums[0, 0] + sums_got[0]) + sums_far, a_far, b_far)
     more_a, more_b = across_w(a_far + got_a[1], 2), across_w(b_far + got_b[1], 1)
-    shares = share, share_pair, jnp.where(inner, share_mid, share_near), jnp.where(inner, share_far, share_last)
     result_keep, result_send = give(hidden, out0, (got_a, more_a, got_b, more_b))
     out_result = both_micros(result_keep, across_core(result_send))
+    sums_pair, head_mid = between_z(sums, PAIRS), between_z(sums[:HEAD_ROWS], ACROSS)
+    out = sums[HEAD_ROWS:] + sums_pair[HEAD_ROWS:]
+    head_near = between_z(head_mid, TO_ENDS)
+    sums_far = between_z(jnp.concatenate([sums_pair[:HEAD_ROWS], out]), ACROSS)
+    pair, middle, out_result, sums_far, head_near = tied(pair, middle, out_result, sums_far, head_near)
+    sums_far = jnp.concatenate([sums_far[:HEAD_ROWS], out + sums_far[HEAD_ROWS:]])
+    sums_last = between_z(sums_far, TO_ENDS)
+    grad_keep, grad_send = last(firsts[0], pair, middle, x_block, gains, d_hidden)
     out_tokens = both_micros(grad_keep, across_core(grad_send))
-    sum_out = jnp.where(inner, sum_out, between_z(sum_out, TO_ENDS))
-    grad_out = both_micros(sum_out, across_core(sum_out)).reshape(SHARD, D).astype(F32)
-    grad_up, grad_down, grad_qkv, out_gains = finish(*shares, *(across_core(block) for block in shares))
+    sums_last = jnp.where(inner, sums_far, sums_last)
+    head_near = jnp.where(inner, head_mid, head_near)
+    blocks = sums[:HEAD_ROWS], sums_pair[:HEAD_ROWS], head_near, sums_last[:HEAD_ROWS]
+    others = [across_core(block) for block in (*blocks[:3], sums_last)]
+    grad_out, grad_qkv, out_gains = finish_heads(
+        *blocks, *others[:3], others[3][:HEAD_ROWS], sums_last[HEAD_ROWS:], others[3][HEAD_ROWS:]
+    )
     return (
         out_result,
         out_tokens,

time: 290 us -> 273 us (0.941)
  waiting for transfers between devices: 91.2 us -> 64.3 us
  Pallas kernels: 76 us -> 85 us
  starting transfers between devices: 81.5 us -> 75 us
  local copies, waits for them, and re-layouts: 18.8 us -> 25.2 us
    ppermute x18 -> x15, waiting for transfers between devices: 41.7 us -> 15.9 us  [between_z(): lax.ppermute(value, 'ctx', [(2 * a + c, 2 * b + c) for a, b in pairs for...]
    pallas_call x0 -> x1, Pallas kernels: none -> 17.3 us  [attend_back(): pl.pallas_call(attend_back_kernel, in_specs=[WHOLE] * 9 + [ANYWHERE] * 2,...]
    ppermute x18 -> x15, starting transfers between devices: 38.2 us -> 28.6 us  [between_z(): lax.ppermute(value, 'ctx', [(2 * a + c, 2 * b + c) for a, b in pairs for...]
    pallas_call x12 -> x14, Pallas kernels: 76 us -> 67.7 us  [call(): pl.pallas_call(kernel, in_specs=ins, out_specs=out_specs or [WHOLE] * len...]
    unnamed x113 -> x101, local copies, waits for them, and re-layouts: 7.5 us -> 12.2 us
    all_to_all x1, waiting for transfers between devices: 12.2 us -> 8.99 us  [local_grid(): lax.all_to_all(d_att, 'ctx', 0, 0, tiled=True, axis_index_groups=Z_GROUPS)]
    all_to_all x1, waiting for transfers between devices: 1.69 us -> 4.74 us  [local_grid(): lax.all_to_all(att_low, 'ctx', 0, 0, tiled=True, axis_index_groups=Z_GROUPS)]
    ppermute x24 -> x27, starting transfers between devices: 27 us -> 28.8 us  [across_w(): return lax.ppermute(value, 'wshard', [(i, i ^ flip) for i in range(4)])]
  transfers between devices with their start and end apart: 57 -> 58, of which waited for: 24 -> 21; matrix products, arithmetic and copies ran while one was open for 5% -> 7% of each run, Pallas kernels for 21% -> 27%
where the time goes in v3:
time: 273 us; the launch traced here: 270 us
  Pallas kernels  85 us (31%)
  starting transfers between devices  75 us (27%)
  waiting for transfers between devices  64.3 us (24%)
  local copies, waits for them, and re-layouts  25.2 us (9%)
  between operations  15 us (5%)
  other arithmetic  5.94 us (2%)
    pallas_call x14, Pallas kernels, call(): pl.pallas_call(kernel, in_specs=ins, out_specs=out_specs or [WHOLE] * len...  67.7 us
    ppermute x27, waiting for transfers between devices, across_w(): return lax.ppermute(value, 'wshard', [(i, i ^ flip) for i in range(4)])  32.4 us
    ppermute x27, starting transfers between devices, across_w(): return lax.ppermute(value, 'wshard', [(i, i ^ flip) for i in range(4)])  28.8 us
    ppermute x15, starting transfers between devices, between_z(): lax.ppermute(value, 'ctx', [(2 * a + c, 2 * b + c) for a, b in pairs for...  28.6 us
    pallas_call x1, Pallas kernels, attend_back(): pl.pallas_call(attend_back_kernel, in_specs=[WHOLE] * 9 + [ANYWHERE] * 2,...  17.3 us
    ppermute x15, waiting for transfers between devices, between_z(): lax.ppermute(value, 'ctx', [(2 * a + c, 2 * b + c) for a, b in pairs for...  15.9 us
    unnamed x101, local copies, waits for them, and re-layouts  12.2 us
    all_to_all x1, waiting for transfers between devices, local_grid(): lax.all_to_all(d_att, 'ctx', 0, 0, tiled=True, axis_index_groups=Z_GROUPS)  8.99 us
  transfers between devices with their start and end apart: 58, of which 21 were waited for; matrix products, arithmetic and copies ran while one was open for 7% of the time, Pallas kernels for 27%

profile of v3, /device:TPU:0, one launch (start us, length us, event | category | flops | bytes accessed | tf_op | source)
XLA Modules:
  0.0 270.5 jit_solution(5489390188723131528)
XLA Ops:
  7.2 1.3 dynamic-slice_bitcast_fusion.2
  9.0 1.3 collective-permute-done
  10.6 1.3 broadcast_in_dim.10
  11.9 6.2 %all-to-all-start = ((bf16[4,256,768]{2,1,0:T(8,128)(2,1)}), bf16[4,256,768]{2,1,0:T(8,128)(2,1)S(1)}, u32[]{:S(2)}, u32[]{:S(2)}) async-start(bf16[4,256,768]{2,1,0:T(8,128)(2,1)} %broadcast_in_dim.10), calls=%async_computation | async-start | bytes 3145728 | tf_op jit(solution)/shard_map/all_to_all | solution.py:1017
  18.9 3.1 %parcels.1 = (bf16[320,768]{1,0:T(8,128)(2,1)}, bf16[416,768]{1,0:T(8,128)(2,1)}, bf16[320,768]{1,0:T(8,128)(2,1)}, bf16[416,768]{1,0:T(8,128)(2,1)}) custom-call(bf16[256,768]{1,0:T(8,128)(2,1)} %pad_maximum_fusion.3.cot_ref, bf16[192,768]{1,0:T(8,128)(2,1)} %own_ref.1, bf16[192,3072]{1,0:T(8,128)(2,1)} %wup_ref.3), custom_call_target="tpu_custom_call" | custom-call | flops 1000 | bytes 1000 | tf_op jit(solution)/shard_map/parcels/pallas_call | solution.py:303
  22.0 1.6 collective-permute-start.1
  23.5 1.5 collective-permute-start.2
  25.1 2.9 %reshape.155 = bf16[192,3,4,192]{3,2,1,0:T(4,128)(2,1)S(1)} reshape(bf16[192,2304]{1,0:T(8,128)(2,1)} %param.10) | data formatting | bytes 1769472 | tf_op jit(solution)/shard_map/reshape | solution.py:1015
  29.7 5.6 %collective-permute-done.1.x_on = bf16[320,768]{1,0:T(8,128)(2,1)} collective-permute-done((bf16[320,768]{1,0:T(8,128)(2,1)}, bf16[320,768]{1,0:T(8,128)(2,1)}, u32[]{:S(2)}, u32[]{:S(2)}) %collective-permute-start.1) | collective-permute-done | bytes 491552 | tf_op jit(solution)/shard_map/ppermute | solution.py:942
  36.5 1.5 collective-permute-start.4
  38.6 5.3 %collective-permute-done.4.w2 = bf16[224,576]{1,0:T(8,128)(2,1)S(1)} collective-permute-done((bf16[224,576]{1,0:T(8,128)(2,1)S(1)}, bf16[224,576]{1,0:T(8,128)(2,1)S(1)}, u32[]{:S(2)}, u32[]{:S(2)}) %collective-permute-start.4) | collective-permute-done | bytes 258080 | tf_op jit(solution)/shard_map/ppermute | solution.py:942
  44.6 1.3 collective-permute-done.3.w1
  46.2 2.9 %collective-permute-done.6.w4 = bf16[112,576]{1,0:T(8,128)(2,1)S(1)} collective-permute-done((bf16[112,576]{1,0:T(8,128)(2,1)S(1)}, bf16[112,576]{1,0:T(8,128)(2,1)S(1)}, u32[]{:S(2)}, u32[]{:S(2)}) %collective-permute-start.6) | collective-permute-done | bytes 129056 | tf_op jit(solution)/shard_map/ppermute | solution.py:942
  49.1 2.8 %collective-permute-done.5.w3 = bf16[112,576]{1,0:T(8,128)(2,1)S(1)} collective-permute-done((bf16[112,576]{1,0:T(8,128)(2,1)S(1)}, bf16[112,576]{1,0:T(8,128)(2,1)S(1)}, u32[]{:S(2)}, u32[]{:S(2)}) %collective-permute-start.5) | collective-permute-done | bytes 129056 | tf_op jit(solution)/shard_map/ppermute | solution.py:942
  53.9 2.0 collective-permute-start.10
  57.1 13.4 %attend.1 = (bf16[1024,768]{1,0:T(8,128)(2,1)}, bf16[3,1024,128]{2,1,0:T(8,128)(2,1)}, bf16[576,1024]{1,0:T(8,128)(2,1)}, f32[192,1024]{1,0:T(8,128)}, bf16[4,19...) custom-call(bf16[4,256,768]{2,1,0:T(8,128)(2,1)} %copy-done, ...), custom_call_target="tpu_custom_call" | custom-call | flops 1000 | bytes 1000 | tf_op jit(solution)/shard_map/attend/pallas_call | solution.py:303
  70.5 4.9 %collective-permute-done.9.corner_a = bf16[320,768]{1,0:T(8,128)(2,1)} collective-permute-done((bf16[320,768]{1,0:T(8,128)(2,1)}, bf16[320,768]{1,0:T(8,128)(2,1)}, u32[]{:S(2)}, u32[]{:S(2)}) %collective-permute-start.9) | collective-permute-done | bytes 491552 | tf_op jit(solution)/shard_map/ppermute | solution.py:942
  75.5 4.7 %all-to-all-start.1 = ((bf16[4,192,256]{2,1,0:T(8,128)(2,1)}), bf16[4,192,256]{2,1,0:T(8,128)(2,1)S(1)}, u32[]{:S(2)}, u32[]{:S(2)}) async-start(bf16[4,192,256]{2,1,0:T(8,128)(2,1)} %get-tuple-element.128), calls=%async_computation.1 | async-start | bytes 786432 | tf_op jit(solution)/shard_map/all_to_all | solution.py:1030
  80.2 4.1 %assemble.1 = (bf16[768,768]{1,0:T(8,128)(2,1)}, bf16[768,768]{1,0:T(8,128)(2,1)}, bf16[1024,768]{1,0:T(8,128)(2,1)}) custom-call(bf16[256,768]{1,0:T(8,128)(2,1)} %pad_maximum_fusion.3.cot_ref, bf16[192,768]{1,0:T(8,128)(2,1)} %own_ref.1, bf16[192,3072]{1,0:T(8,128)(2,1)} %wup_ref.3, bf16[320,768]{1,0:T(8,128)(2,1)} %collective-permute-done.1.x_on, ...), custom_call_target="tpu_custom_call" | custom-call | flops 1000 | bytes 1000 | tf_op jit(solution)/shard_map/assemble/pallas_call | solution.py:303
  84.4 4.7 %all-to-all-done.1 = bf16[4,192,256]{2,1,0:T(8,128)(2,1)S(1)} async-done(((bf16[4,192,256]{2,1,0:T(8,128)(2,1)}), bf16[4,192,256]{2,1,0:T(8,128)(2,1)S(1)}, u32[]{:S(2)}, u32[]{:S(2)}) %all-to-all-start.1) | async-done | bytes 393248 | tf_op jit(solution)/shard_map/all_to_all | solution.py:1030
  89.8 3.0 %project.1 = (f32[256,768]{1,0:T(8,128)}, bf16[256,768]{1,0:T(8,128)(2,1)}) custom-call(bf16[768,256]{1,0:T(8,128)(2,1)} %bitcast.50, bf16[256,768]{1,0:T(8,128)(2,1)} %copy-done.1, f32[8,768]{1,0:T(8,128)} %get-tuple-element.129.gain_ref, bf16[768,768]{1,0:T(8,128)(2,1)} %get-tuple-element.136.wout_ref), custom_call_target="tpu_custom_call" | custom-call | flops 1000 | bytes 1000 | tf_op jit(solution)/shard_map/project/pallas_call | solution.py:303
  93.0 1.3 collective-permute-start.11
  94.3 4.6 %feed_own.1 = (bf16[256,768]{1,0:T(8,128)(2,1)}, bf16[256,768]{1,0:T(8,128)(2,1)}, f32[256,768]{1,0:T(8,128)}, f32[256,768]{1,0:T(8,128)}) custom-call(bf16[256,768]{1,0:T(8,128)(2,1)} %get-tuple-element.138.n_ref.n0, bf16[1024,768]{1,0:T(8,128)(2,1)} %get-tuple-element.139.cot_ref, bf16[768,768]{1,0:T(8,128)(2,1)} %get-tuple-element.140.up_ref, ...), custom_call_target="tpu_custom_call" | custom-call | flops 1000 | bytes 1000 | tf_op jit(solution)/shard_map/feed_own/pallas_call | solution.py:303
  99.0 3.1 %collective-permute-done.12.ny_ref.n2 = bf16[256,768]{1,0:T(8,128)(2,1)S(1)} collective-permute-done((bf16[256,768]{1,0:T(8,128)(2,1)}, bf16[256,768]{1,0:T(8,128)(2,1)S(1)}, u32[]{:S(2)}, u32[]{:S(2)}) %collective-permute-start.12) | collective-permute-done | bytes 393248 | tf_op jit(solution)/shard_map/ppermute | solution.py:942
  104.6 6.1 %feed_near.1 = (bf16[512,768]{1,0:T(8,128)(2,1)}, bf16[512,768]{1,0:T(8,128)(2,1)}, bf16[512,768]{1,0:T(8,128)(2,1)}, bf16[512,768]{1,0:T(8,128)(2,1)}) custom-call(bf16[256,768]{1,0:T(8,128)(2,1)} %copy-done.4, bf16[256,768]{1,0:T(8,128)(2,1)} %copy-done.3, bf16[1024,768]{1,0:T(8,128)(2,1)} %get-tuple-element.139.cot_ref, ...), custom_call_target="tpu_custom_call" | custom-call | flops 1000 | bytes 1000 | tf_op jit(solution)/shard_map/feed_near/pallas_call | solution.py:303
  111.5 5.6 %feed_far.1 = (bf16[256,768]{1,0:T(8,128)(2,1)}, bf16[256,768]{1,0:T(8,128)(2,1)}, bf16[2,128,768]{2,1,0:T(8,128)(2,1)}, bf16[128,768]{1,0:T(8,128)(2,1)}, bf16[...) custom-call(bf16[128,768]{1,0:T(8,128)(2,1)} %copy-done.14, ...), custom_call_target="tpu_custom_call" | custom-call | flops 1000 | bytes 1000 | tf_op jit(solution)/shard_map/feed_far/pallas_call | solution.py:303
  117.1 1.3 collective-permute-start.15
  118.4 1.3 collective-permute-start.16
  119.7 7.6 %feed_grads.1 = bf16[8,8,48,384]{3,2,1,0:T(8,128)(2,1)} custom-call(bf16[256,768]{1,0:T(8,128)(2,1)} %get-tuple-element.138.n_ref.n0, bf16[256,768]{1,0:T(8,128)(2,1)} %copy-done.4, bf16[256,768]{1,0:T(8,128)(2,1)} %copy-done.3, bf16[128,768]{1,0:T(8,128)(2,1)} %copy-done.14, bf16[128,768]{1,0:T(8,128)(2,1)} %copy-done.15, ...), custom_call_target="tpu_custom_call" | custom-call | flops 1000 | bytes 1000 | tf_op jit(solution)/shard_map/feed_grads/pallas_call | solution.py:303
  129.2 1.5 collective-permute-start.17
  130.7 3.5 %collective-permute-done.18.b_more_ref = bf16[128,768]{1,0:T(8,128)(2,1)S(1)} collective-permute-done((bf16[128,768]{1,0:T(8,128)(2,1)S(1)}, bf16[128,768]{1,0:T(8,128)(2,1)S(1)}, u32[]{:S(2)}, u32[]{:S(2)}) %collective-permute-start.18) | collective-permute-done | bytes 196640 | tf_op jit(solution)/shard_map/ppermute | solution.py:942
  135.6 4.3 %turn.1 = (f32[256,768]{1,0:T(8,128)}, bf16[4,192,256]{2,1,0:T(8,128)(2,1)}, bf16[256,768]{1,0:T(8,128)(2,1)}, f32[1,768]{1,0:T(1,128)}) custom-call(f32[256,768]{1,0:T(8,128)} %get-tuple-element.137.hidden_ref, f32[8,768]{1,0:T(8,128)} %get-tuple-element.129.gain_ref, f32[256,768]{1,0:T(8,128)} %get-tuple-element.141.dkeep_ref, ...), custom_call_target="tpu_custom_call" | custom-call | flops 1000 | bytes 1000 | tf_op jit(solution)/shard_map/turn/pallas_call | solution.py:303
  139.9 3.7 %all-to-all-start.2 = ((bf16[4,192,256]{2,1,0:T(8,128)(2,1)}), bf16[4,192,256]{2,1,0:T(8,128)(2,1)S(1)}, u32[]{:S(2)}, u32[]{:S(2)}) async-start(bf16[4,192,256]{2,1,0:T(8,128)(2,1)} %get-tuple-element.158), calls=%async_computation.2 | async-start | bytes 786432 | tf_op jit(solution)/shard_map/all_to_all | solution.py:1047
  143.6 1.4 collective-permute-start.19
  146.1 2.6 out_grad.1
  148.7 9.0 %all-to-all-done.2.dout_ref = bf16[4,192,256]{2,1,0:T(8,128)(2,1)S(1)} async-done(((bf16[4,192,256]{2,1,0:T(8,128)(2,1)}), bf16[4,192,256]{2,1,0:T(8,128)(2,1)S(1)}, u32[]{:S(2)}, u32[]{:S(2)}) %all-to-all-start.2) | async-done | bytes 393248 | tf_op jit(solution)/shard_map/all_to_all | solution.py:1047
  158.5 17.3 %attend_back.1 = (bf16[256,768]{1,0:T(8,128)(2,1)}, bf16[256,768]{1,0:T(8,128)(2,1)}, bf16[256,768]{1,0:T(8,128)(2,1)}, bf16[256,768]{1,0:T(8,128)(2,1)}, bf16[2...) custom-call(bf16[3,1024,128]{2,1,0:T(8,128)(2,1)} %get-tuple-element.1, ...), custom_call_target="tpu_custom_call", output_to_operand_aliasing={{4}: (9, {}), {5}: (10, {})} | custom-call | flops 1000 | bytes 1000 | tf_op jit(solution)/shard_map/attend_back/pallas_call | solution.py:817
  176.9 1.5 collective-permute-start.42
  178.4 1.4 bitcast_dynamic-update-slice_fusion
  180.7 1.6 collective-permute-start.44
  183.5 1.5 add.71
  185.1 1.5 collective-permute-start.27
  188.5 1.4 collective-permute-start.46
  190.7 3.9 %collective-permute-start.21 = (bf16[256,768]{1,0:T(8,128)(2,1)S(1)}, bf16[256,768]{1,0:T(8,128)(2,1)}, u32[]{:S(2)}, u32[]{:S(2)}) collective-permute-start(bf16[256,768]{1,0:T(8,128)(2,1)S(1)} %copy-done.23), channel_id=1, source_target_pairs={{0,2},{1,3},{6,4},{7,5},{8,10},{9,11},{14,12},{15,13},{16,18},{17,... | collective-permute-start | bytes 1179656 | tf_op jit(solution)/shard_map/ppermute | solution.py:950
  194.6 1.3 collective-permute-start.47
  195.9 2.6 collective-permute-done.45.refs_1_
  199.2 1.4 collective-permute-start.28
  200.6 4.2 %collective-permute-done.21 = bf16[256,768]{1,0:T(8,128)(2,1)} collective-permute-done((bf16[256,768]{1,0:T(8,128)(2,1)S(1)}, bf16[256,768]{1,0:T(8,128)(2,1)}, u32[]{:S(2)}, u32[]{:S(2)}) %collective-permute-start.21) | collective-permute-done | bytes 393248 | tf_op jit(solution)/shard_map/ppermute | solution.py:950
  205.9 4.8 %collective-permute-start.24 = (bf16[256,768]{1,0:T(8,128)(2,1)S(1)}, bf16[256,768]{1,0:T(8,128)(2,1)S(1)}, u32[]{:S(2)}, u32[]{:S(2)}) collective-permute-start(bf16[256,768]{1,0:T(8,128)(2,1)S(1)} %select_add_fusion.1), channel_id=1, source_target_pairs={{0,2},{1,3},{6,4},{7,5},{8,10},{9,11},{14,12},{15,13},{16,18},{17,... | collective-permute-start | bytes 1179656 | tf_op jit(solution)/shard_map/ppermute | solution.py:950
  211.5 3.3 %collective-permute-start.32 = (bf16[352,384]{1,0:T(8,128)(2,1)S(1)}, bf16[352,384]{1,0:T(8,128)(2,1)S(1)}, u32[]{:S(2)}, u32[]{:S(2)}) collective-permute-start(bf16[352,384]{1,0:T(8,128)(2,1)S(1)} %fusion.2), channel_id=1, source_target_pairs={{0,2},{1,3},{2,0},{3,1},{4,6},{5,7},{6,4},{7,5},{8,10},{9,11},{10,... | collective-permute-start | bytes 811016 | tf_op jit(solution)/shard_map/ppermute | solution.py:950
  215.7 1.6 collective-permute-start.30
  217.6 2.6 collective-permute-done.24
  220.2 1.3 collective-permute-start.49
  222.3 5.6 %collective-permute-start.23 = (bf16[256,768]{1,0:T(8,128)(2,1)S(1)}, bf16[256,768]{1,0:T(8,128)(2,1)S(1)}, u32[]{:S(2)}, u32[]{:S(2)}) collective-permute-start(bf16[256,768]{1,0:T(8,128)(2,1)S(1)} %select_add_fusion), channel_id=1, source_target_pairs={{0,2},{1,3},{2,0},{3,1},{4,6},{5,7},{6,4},{7,5},{8,10},{9,11},{10,... | collective-permute-start | bytes 1179656 | tf_op jit(solution)/shard_map/ppermute | solution.py:950
  227.9 1.3 collective-permute-start.35
  229.2 2.6 give.1
  234.9 3.0 %collective-permute-done.23.pair_ref = bf16[256,768]{1,0:T(8,128)(2,1)S(1)} collective-permute-done((bf16[256,768]{1,0:T(8,128)(2,1)S(1)}, bf16[256,768]{1,0:T(8,128)(2,1)S(1)}, u32[]{:S(2)}, u32[]{:S(2)}) %collective-permute-start.23) | collective-permute-done | bytes 393248 | tf_op jit(solution)/shard_map/ppermute | solution.py:950
  237.9 1.3 collective-permute-done.35
  239.3 1.6 collective-permute-start.37
  242.5 4.1 %finish_feed.1 = (f32[192,3072]{1,0:T(8,128)}, f32[768,768]{1,0:T(8,128)}) custom-call(bf16[384,384]{1,0:T(8,128)(2,1)} %constant_dynamic-update-slice_fusion.refs_0_, bf16[384,384]{1,0:T(8,128)(2,1)} %collective-permute-done.45.refs_1_, bf16[384,384]{1,0:T(8,128)(2,1)} %copy-done.6, bf16[384,384]{1,0:T(8,128)(2,1)} %copy-done.7, ...), custom_call_target="tpu_custom_call" | custom-call | flops 1000 | bytes 1000 | tf_op jit(solution)/shard_map/finish_feed/pallas_call | solution.py:303
  247.3 3.1 %last.1 = (f32[128,768]{1,0:T(8,128)}, f32[128,768]{1,0:T(8,128)}) custom-call(bf16[256,768]{1,0:T(8,128)(2,1)} %get-tuple-element.196.first_ref, bf16[256,768]{1,0:T(8,128)(2,1)} %copy-done.22, bf16[256,768]{1,0:T(8,128)(2,1)} %copy-done.21, bf16[256,768]{1,0:T(8,128)(2,1)} %copy-done.1, f32[8,768]{1,0:T(8,128)} %get-tuple-element.129.gain_ref, ...), custom_call_target="tpu_custom_call" | custom-call | flops 1000 | bytes 1000 | tf_op jit(solution)/shard_map/last/pallas_call | solution.py:303
  250.9 2.3 collective-permute-done.37
  258.9 3.4 %finish_heads.1 = (f32[192,768]{1,0:T(8,128)}, f32[192,2304]{1,0:T(8,128)}, f32[16,192]{1,0:T(8,128)}) custom-call(bf16[160,384]{1,0:T(8,128)(2,1)} %copy-done.19, bf16[160,384]{1,0:T(8,128)(2,1)} %copy-done.9, bf16[160,384]{1,0:T(8,128)(2,1)} %copy-done.20, bf16[160,384]{1,0:T(8,128)(2,1)} %slice.150.refs_3_, bf16[160,384]{1,0:T(8,128)(2,1)} %copy-done.41, ...), custom_call_target="tpu_custom_call" | custom-call | flops 1000 | bytes 1000 | tf_op jit(solution)/shard_map/finish_heads/pallas_call | solution.py:303
  262.3 1.3 fusion.11
  (220 shorter events, 40.2 us)
Async XLA Ops:
  8.5 1.9 collective-permute-start
  11.9 44.1 %all-to-all-start = ((bf16[4,256,768]{2,1,0:T(8,128)(2,1)}), bf16[4,256,768]{2,1,0:T(8,128)(2,1)S(1)}, u32[]{:S(2)}, u32[]{:S(2)}) async-start(bf16[4,256,768]{2,1,0:T(8,128)(2,1)} %broadcast_in_dim.10), calls=%async_computation | async-start | bytes 3145728 | tf_op jit(solution)/shard_map/all_to_all | solution.py:1017
  22.0 13.4 %collective-permute-start.1 = (bf16[320,768]{1,0:T(8,128)(2,1)}, bf16[320,768]{1,0:T(8,128)(2,1)}, u32[]{:S(2)}, u32[]{:S(2)}) collective-permute-start(bf16[320,768]{1,0:T(8,128)(2,1)} %get-tuple-element.111), channel_id=1, source_target_pairs={{0,8},{8,0},{16,24},{24,16},{1,9},{9,1},{17,25},{25,17},{2,10},{10... | collective-permute-start | bytes 1474568 | tf_op jit(solution)/shard_map/ppermute | solution.py:942
  23.5 13.0 %collective-permute-start.2 = (bf16[320,768]{1,0:T(8,128)(2,1)}, bf16[320,768]{1,0:T(8,128)(2,1)}, u32[]{:S(2)}, u32[]{:S(2)}) collective-permute-start(bf16[320,768]{1,0:T(8,128)(2,1)} %get-tuple-element.112), channel_id=1, source_target_pairs={{0,16},{8,24},{16,0},{24,8},{1,17},{9,25},{17,1},{25,9},{2,18},{10... | collective-permute-start | bytes 1474568 | tf_op jit(solution)/shard_map/ppermute | solution.py:942
  29.7 26.3 %copy-start.8 = (bf16[224,576]{1,0:T(8,128)(2,1)}, bf16[224,576]{1,0:T(8,128)(2,1)S(1)}, u32[]{:S(2)}) copy-start(bf16[224,576]{1,0:T(8,128)(2,1)S(1)} %pad_maximum_fusion.4.w0) | copy-start | bytes 774148
  36.5 7.4 %collective-permute-start.4 = (bf16[224,576]{1,0:T(8,128)(2,1)S(1)}, bf16[224,576]{1,0:T(8,128)(2,1)S(1)}, u32[]{:S(2)}, u32[]{:S(2)}) collective-permute-start(bf16[224,576]{1,0:T(8,128)(2,1)S(1)} %pad_maximum_fusion.4.w0), channel_id=1, source_target_pairs={{0,16},{8,24},{16,0},{24,8},{1,17},{9,25},{17,1},{25,9},{2,18},{10... | collective-permute-start | bytes 774152 | tf_op jit(solution)/shard_map/ppermute | solution.py:942
  38.1 7.9 %collective-permute-start.3 = (bf16[224,576]{1,0:T(8,128)(2,1)S(1)}, bf16[224,576]{1,0:T(8,128)(2,1)S(1)}, u32[]{:S(2)}, u32[]{:S(2)}) collective-permute-start(bf16[224,576]{1,0:T(8,128)(2,1)S(1)} %pad_maximum_fusion.4.w0), channel_id=1, source_target_pairs={{0,8},{8,0},{16,24},{24,16},{1,9},{9,1},{17,25},{25,17},{2,10},{10... | collective-permute-start | bytes 774152 | tf_op jit(solution)/shard_map/ppermute | solution.py:942
  44.0 5.2 %collective-permute-start.6 = (bf16[112,576]{1,0:T(8,128)(2,1)S(1)}, bf16[112,576]{1,0:T(8,128)(2,1)S(1)}, u32[]{:S(2)}, u32[]{:S(2)}) collective-permute-start(bf16[112,576]{1,0:T(8,128)(2,1)S(1)} %slice.143), channel_id=1, source_target_pairs={{0,8},{8,0},{16,24},{24,16},{1,9},{9,1},{17,25},{25,17},{2,10},{10... | collective-permute-start | bytes 387080 | tf_op jit(solution)/shard_map/ppermute | solution.py:942
  46.0 5.9 %collective-permute-start.5 = (bf16[112,576]{1,0:T(8,128)(2,1)S(1)}, bf16[112,576]{1,0:T(8,128)(2,1)S(1)}, u32[]{:S(2)}, u32[]{:S(2)}) collective-permute-start(bf16[112,576]{1,0:T(8,128)(2,1)S(1)} %slice.142), channel_id=1, source_target_pairs={{0,16},{8,24},{16,0},{24,8},{1,17},{9,25},{17,1},{25,9},{2,18},{10... | collective-permute-start | bytes 387080 | tf_op jit(solution)/shard_map/ppermute | solution.py:942
  51.9 23.6 %collective-permute-start.7 = (bf16[416,768]{1,0:T(8,128)(2,1)}, bf16[416,768]{1,0:T(8,128)(2,1)S(1)}, u32[]{:S(2)}, u32[]{:S(2)}) collective-permute-start(bf16[416,768]{1,0:T(8,128)(2,1)} %get-tuple-element.125), channel_id=1, source_target_pairs={{0,8},{8,0},{16,24},{24,16},{1,9},{9,1},{17,25},{25,17},{2,10},{10... | collective-permute-start | bytes 1916936 | tf_op jit(solution)/shard_map/ppermute | solution.py:942
  51.9 23.6 %collective-permute-start.8 = (bf16[416,768]{1,0:T(8,128)(2,1)}, bf16[416,768]{1,0:T(8,128)(2,1)}, u32[]{:S(2)}, u32[]{:S(2)}) collective-permute-start(bf16[416,768]{1,0:T(8,128)(2,1)} %get-tuple-element.127), channel_id=1, source_target_pairs={{0,16},{8,24},{16,0},{24,8},{1,17},{9,25},{17,1},{25,9},{2,18},{10... | collective-permute-start | bytes 1916936 | tf_op jit(solution)/shard_map/ppermute | solution.py:942
  52.9 22.5 %collective-permute-start.9 = (bf16[320,768]{1,0:T(8,128)(2,1)}, bf16[320,768]{1,0:T(8,128)(2,1)}, u32[]{:S(2)}, u32[]{:S(2)}) collective-permute-start(bf16[320,768]{1,0:T(8,128)(2,1)} %collective-permute-done.1.x_on), channel_id=1, source_target_pairs={{0,16},{8,24},{16,0},{24,8},{1,17},{9,25},{17,1},{25,9},{2,18},{10... | collective-permute-start | bytes 1474568 | tf_op jit(solution)/shard_map/ppermute | solution.py:942
  53.9 21.5 %collective-permute-start.10 = (bf16[320,768]{1,0:T(8,128)(2,1)}, bf16[320,768]{1,0:T(8,128)(2,1)}, u32[]{:S(2)}, u32[]{:S(2)}) collective-permute-start(bf16[320,768]{1,0:T(8,128)(2,1)} %collective-permute-done.2.y_on), channel_id=1, source_target_pairs={{0,8},{8,0},{16,24},{24,16},{1,9},{9,1},{17,25},{25,17},{2,10},{10... | collective-permute-start | bytes 1474568 | tf_op jit(solution)/shard_map/ppermute | solution.py:942
  75.5 13.6 %all-to-all-start.1 = ((bf16[4,192,256]{2,1,0:T(8,128)(2,1)}), bf16[4,192,256]{2,1,0:T(8,128)(2,1)S(1)}, u32[]{:S(2)}, u32[]{:S(2)}) async-start(bf16[4,192,256]{2,1,0:T(8,128)(2,1)} %get-tuple-element.128), calls=%async_computation.1 | async-start | bytes 786432 | tf_op jit(solution)/shard_map/all_to_all | solution.py:1030
  80.2 95.7 %reduce-scatter.2.cloned.1.call-start = ((), (), s32[]{:S(2)}) async-start(), calls=%async_computation.4 | async-start | bytes 2654208 | tf_op jit(solution)/shard_map/reduce_scatter | solution.py:1042
  92.9 9.1 %collective-permute-start.12 = (bf16[256,768]{1,0:T(8,128)(2,1)}, bf16[256,768]{1,0:T(8,128)(2,1)S(1)}, u32[]{:S(2)}, u32[]{:S(2)}) collective-permute-start(bf16[256,768]{1,0:T(8,128)(2,1)} %get-tuple-element.138.n_ref.n0), channel_id=1, source_target_pairs={{0,16},{8,24},{16,0},{24,8},{1,17},{9,25},{17,1},{25,9},{2,18},{10... | collective-permute-start | bytes 1179656 | tf_op jit(solution)/shard_map/ppermute | solution.py:942
  93.0 10.1 %collective-permute-start.11 = (bf16[256,768]{1,0:T(8,128)(2,1)}, bf16[256,768]{1,0:T(8,128)(2,1)S(1)}, u32[]{:S(2)}, u32[]{:S(2)}) collective-permute-start(bf16[256,768]{1,0:T(8,128)(2,1)} %get-tuple-element.138.n_ref.n0), channel_id=1, source_target_pairs={{0,8},{8,0},{16,24},{24,16},{1,9},{9,1},{17,25},{25,17},{2,10},{10... | collective-permute-start | bytes 1179656 | tf_op jit(solution)/shard_map/ppermute | solution.py:942
  103.1 7.7 %collective-permute-start.13 = (bf16[128,768]{1,0:T(8,128)(2,1)S(1)}, bf16[128,768]{1,0:T(8,128)(2,1)S(1)}, u32[]{:S(2)}, u32[]{:S(2)}) collective-permute-start(bf16[128,768]{1,0:T(8,128)(2,1)S(1)} %slice.144), channel_id=1, source_target_pairs={{0,16},{8,24},{16,0},{24,8},{1,17},{9,25},{17,1},{25,9},{2,18},{10... | collective-permute-start | bytes 589832 | tf_op jit(solution)/shard_map/ppermute | solution.py:942
  103.9 6.9 %collective-permute-start.14 = (bf16[128,768]{1,0:T(8,128)(2,1)S(1)}, bf16[128,768]{1,0:T(8,128)(2,1)S(1)}, u32[]{:S(2)}, u32[]{:S(2)}) collective-permute-start(bf16[128,768]{1,0:T(8,128)(2,1)S(1)} %slice.145), channel_id=1, source_target_pairs={{0,8},{8,0},{16,24},{24,16},{1,9},{9,1},{17,25},{25,17},{2,10},{10... | collective-permute-start | bytes 589832 | tf_op jit(solution)/shard_map/ppermute | solution.py:942
  117.1 10.3 %collective-permute-start.15 = (bf16[2,128,768]{2,1,0:T(8,128)(2,1)}, bf16[2,128,768]{2,1,0:T(8,128)(2,1)S(1)}, u32[]{:S(2)}, u32[]{:S(2)}) collective-permute-start(bf16[2,128,768]{2,1,0:T(8,128)(2,1)} %get-tuple-element.152), channel_id=1, source_target_pairs={{0,8},{8,0},{16,24},{24,16},{1,9},{9,1},{17,25},{25,17},{2,10},{10... | collective-permute-start | bytes 1179656 | tf_op jit(solution)/shard_map/ppermute | solution.py:942
  118.4 9.0 %collective-permute-start.16 = (bf16[2,128,768]{2,1,0:T(8,128)(2,1)}, bf16[2,128,768]{2,1,0:T(8,128)(2,1)S(1)}, u32[]{:S(2)}, u32[]{:S(2)}) collective-permute-start(bf16[2,128,768]{2,1,0:T(8,128)(2,1)} %get-tuple-element.153), channel_id=1, source_target_pairs={{0,16},{8,24},{16,0},{24,8},{1,17},{9,25},{17,1},{25,9},{2,18},{10... | collective-permute-start | bytes 1179656 | tf_op jit(solution)/shard_map/ppermute | solution.py:942
  128.4 5.7 %collective-permute-start.18 = (bf16[128,768]{1,0:T(8,128)(2,1)S(1)}, bf16[128,768]{1,0:T(8,128)(2,1)S(1)}, u32[]{:S(2)}, u32[]{:S(2)}) collective-permute-start(bf16[128,768]{1,0:T(8,128)(2,1)S(1)} %bitcast_add_fusion.2), channel_id=1, source_target_pairs={{0,8},{8,0},{16,24},{24,16},{1,9},{9,1},{17,25},{25,17},{2,10},{10... | collective-permute-start | bytes 589832 | tf_op jit(solution)/shard_map/ppermute | solution.py:942
  129.2 5.7 %collective-permute-start.17 = (bf16[128,768]{1,0:T(8,128)(2,1)S(1)}, bf16[128,768]{1,0:T(8,128)(2,1)S(1)}, u32[]{:S(2)}, u32[]{:S(2)}) collective-permute-start(bf16[128,768]{1,0:T(8,128)(2,1)S(1)} %bitcast_add_fusion.3), channel_id=1, source_target_pairs={{0,16},{8,24},{16,0},{24,8},{1,17},{9,25},{17,1},{25,9},{2,18},{10... | collective-permute-start | bytes 589832 | tf_op jit(solution)/shard_map/ppermute | solution.py:942
  139.9 17.8 %all-to-all-start.2 = ((bf16[4,192,256]{2,1,0:T(8,128)(2,1)}), bf16[4,192,256]{2,1,0:T(8,128)(2,1)S(1)}, u32[]{:S(2)}, u32[]{:S(2)}) async-start(bf16[4,192,256]{2,1,0:T(8,128)(2,1)} %get-tuple-element.158), calls=%async_computation.2 | async-start | bytes 786432 | tf_op jit(solution)/shard_map/all_to_all | solution.py:1047
  143.6 32.2 %collective-permute-start.19 = (bf16[2,128,768]{2,1,0:T(8,128)(2,1)S(1)}, bf16[2,128,768]{2,1,0:T(8,128)(2,1)S(1)}, u32[]{:S(2)}, u32[]{:S(2)}) collective-permute-start(bf16[2,128,768]{2,1,0:T(8,128)(2,1)S(1)} %copy-done.45), channel_id=1, source_target_pairs={{0,8},{8,0},{16,24},{24,16},{1,9},{9,1},{17,25},{25,17},{2,10},{10... | collective-permute-start | bytes 1179656 | tf_op jit(solution)/shard_map/ppermute | solution.py:942
  145.1 30.8 %collective-permute-start.20 = (bf16[2,128,768]{2,1,0:T(8,128)(2,1)S(1)}, bf16[2,128,768]{2,1,0:T(8,128)(2,1)S(1)}, u32[]{:S(2)}, u32[]{:S(2)}) collective-permute-start(bf16[2,128,768]{2,1,0:T(8,128)(2,1)S(1)} %copy-done.44), channel_id=1, source_target_pairs={{0,16},{8,24},{16,0},{24,8},{1,17},{9,25},{17,1},{25,9},{2,18},{10... | collective-permute-start | bytes 1179656 | tf_op jit(solution)/shard_map/ppermute | solution.py:942
  175.8 39.7 %copy-start.12 = (bf16[2,128,768]{2,1,0:T(8,128)(2,1)}, bf16[2,128,768]{2,1,0:T(8,128)(2,1)S(1)}, u32[]{:S(2)}) copy-start(bf16[2,128,768]{2,1,0:T(8,128)(2,1)S(1)} %collective-permute-done.19.a_ref) | copy-start | bytes 1179652
  175.8 39.8 %copy-start.13 = (bf16[2,128,768]{2,1,0:T(8,128)(2,1)}, bf16[2,128,768]{2,1,0:T(8,128)(2,1)S(1)}, u32[]{:S(2)}) copy-start(bf16[2,128,768]{2,1,0:T(8,128)(2,1)S(1)} %collective-permute-done.20.b_ref) | copy-start | bytes 1179652
  175.9 7.6 %collective-permute-start.26 = (bf16[2,2,352,384]{3,2,1,0:T(8,128)(2,1)}, bf16[2,2,352,384]{3,2,1,0:T(8,128)(2,1)S(1)}, u32[]{:S(2)}, u32[]{:S(2)}) collective-permute-start(bf16[2,2,352,384]{3,2,1,0:T(8,128)(2,1)} %get-tuple-element.183), channel_id=1, source_target_pairs={{0,1},{1,0},{2,3},{3,2},{4,5},{5,4},{6,7},{7,6},{8,9},{9,8},{10,11... | collective-permute-start | bytes 3244040 | tf_op jit(solution)/shard_map/ppermute | solution.py:946
  176.9 5.9 %collective-permute-start.42 = (bf16[48,384]{1,0:T(8,128)(2,1)S(1)}, bf16[48,384]{1,0:T(8,128)(2,1)S(1)}, u32[]{:S(2)}, u32[]{:S(2)}) collective-permute-start(bf16[48,384]{1,0:T(8,128)(2,1)S(1)} %get-tuple-element.222), channel_id=1, source_target_pairs={{0,8},{8,0},{16,24},{24,16},{1,9},{9,1},{17,25},{25,17},{2,10},{10... | collective-permute-start | bytes 110600 | tf_op jit(solution)/shard_map/ppermute | solution.py:942
  180.7 6.5 %collective-permute-start.44 = (bf16[48,384]{1,0:T(8,128)(2,1)S(1)}, bf16[48,384]{1,0:T(8,128)(2,1)S(1)}, u32[]{:S(2)}, u32[]{:S(2)}) collective-permute-start(bf16[48,384]{1,0:T(8,128)(2,1)S(1)} %get-tuple-element.220), channel_id=1, source_target_pairs={{0,24},{8,16},{16,8},{24,0},{1,25},{9,17},{17,9},{25,1},{2,26},{10... | collective-permute-start | bytes 110600 | tf_op jit(solution)/shard_map/ppermute | solution.py:942
  182.3 4.3 %collective-permute-start.43 = (bf16[48,384]{1,0:T(8,128)(2,1)S(1)}, bf16[48,384]{1,0:T(8,128)(2,1)S(1)}, u32[]{:S(2)}, u32[]{:S(2)}) collective-permute-start(bf16[48,384]{1,0:T(8,128)(2,1)S(1)} %get-tuple-element.221), channel_id=1, source_target_pairs={{0,16},{8,24},{16,0},{24,8},{1,17},{9,25},{17,1},{25,9},{2,18},{10... | collective-permute-start | bytes 110600 | tf_op jit(solution)/shard_map/ppermute | solution.py:942
  185.1 14.1 %collective-permute-start.27 = (bf16[2,352,384]{2,1,0:T(8,128)(2,1)S(1)}, bf16[2,352,384]{2,1,0:T(8,128)(2,1)S(1)}, u32[]{:S(2)}, u32[]{:S(2)}) collective-permute-start(bf16[2,352,384]{2,1,0:T(8,128)(2,1)S(1)} %slice_bitcast_fusion), channel_id=1, source_target_pairs={{0,16},{8,24},{16,0},{24,8},{1,17},{9,25},{17,1},{25,9},{2,18},{10... | collective-permute-start | bytes 1622024 | tf_op jit(solution)/shard_map/ppermute | solution.py:942
  188.5 6.1 %collective-permute-start.46 = (bf16[384,384]{1,0:T(8,128)(2,1)}, bf16[384,384]{1,0:T(8,128)(2,1)}, u32[]{:S(2)}, u32[]{:S(2)}) collective-permute-start(bf16[384,384]{1,0:T(8,128)(2,1)} %constant_dynamic-update-slice_fusion.refs_0_), channel_id=1, source_target_pairs={{2,4},{3,5},{4,2},{5,3},{10,12},{11,13},{12,10},{13,11},{18,20},{1... | collective-permute-start | bytes 884744 | tf_op jit(solution)/shard_map/ppermute | solution.py:950
  189.9 8.6 %collective-permute-start.45 = (bf16[384,384]{1,0:T(8,128)(2,1)}, bf16[384,384]{1,0:T(8,128)(2,1)}, u32[]{:S(2)}, u32[]{:S(2)}) collective-permute-start(bf16[384,384]{1,0:T(8,128)(2,1)} %constant_dynamic-update-slice_fusion.refs_0_), channel_id=1, source_target_pairs={{0,2},{1,3},{2,0},{3,1},{4,6},{5,7},{6,4},{7,5},{8,10},{9,11},{10,... | collective-permute-start | bytes 884744 | tf_op jit(solution)/shard_map/ppermute | solution.py:950
  190.7 14.1 %collective-permute-start.21 = (bf16[256,768]{1,0:T(8,128)(2,1)S(1)}, bf16[256,768]{1,0:T(8,128)(2,1)}, u32[]{:S(2)}, u32[]{:S(2)}) collective-permute-start(bf16[256,768]{1,0:T(8,128)(2,1)S(1)} %copy-done.23), channel_id=1, source_target_pairs={{0,2},{1,3},{6,4},{7,5},{8,10},{9,11},{14,12},{15,13},{16,18},{17,... | collective-permute-start | bytes 1179656 | tf_op jit(solution)/shard_map/ppermute | solution.py:950
  194.6 16.7 %collective-permute-start.47 = (bf16[384,384]{1,0:T(8,128)(2,1)}, bf16[384,384]{1,0:T(8,128)(2,1)S(1)}, u32[]{:S(2)}, u32[]{:S(2)}) collective-permute-start(bf16[384,384]{1,0:T(8,128)(2,1)} %collective-permute-done.46), channel_id=1, source_target_pairs={{2,0},{3,1},{4,6},{5,7},{10,8},{11,9},{12,14},{13,15},{18,16},{19,... | collective-permute-start | bytes 884744 | tf_op jit(solution)/shard_map/ppermute | solution.py:950
  198.5 17.2 %collective-permute-start.48 = (bf16[384,384]{1,0:T(8,128)(2,1)}, bf16[384,384]{1,0:T(8,128)(2,1)S(1)}, u32[]{:S(2)}, u32[]{:S(2)}) collective-permute-start(bf16[384,384]{1,0:T(8,128)(2,1)} %collective-permute-done.45.refs_1_), channel_id=1, source_target_pairs={{2,4},{3,5},{4,2},{5,3},{10,12},{11,13},{12,10},{13,11},{18,20},{1... | collective-permute-start | bytes 884744 | tf_op jit(solution)/shard_map/ppermute | solution.py:950
  199.2 12.2 %collective-permute-start.28 = (bf16[352,384]{1,0:T(8,128)(2,1)S(1)}, bf16[352,384]{1,0:T(8,128)(2,1)S(1)}, u32[]{:S(2)}, u32[]{:S(2)}) collective-permute-start(bf16[352,384]{1,0:T(8,128)(2,1)S(1)} %fusion), channel_id=1, source_target_pairs={{0,8},{8,0},{16,24},{24,16},{1,9},{9,1},{17,25},{25,17},{2,10},{10... | collective-permute-start | bytes 811016 | tf_op jit(solution)/shard_map/ppermute | solution.py:942
  205.9 14.3 %collective-permute-start.24 = (bf16[256,768]{1,0:T(8,128)(2,1)S(1)}, bf16[256,768]{1,0:T(8,128)(2,1)S(1)}, u32[]{:S(2)}, u32[]{:S(2)}) collective-permute-start(bf16[256,768]{1,0:T(8,128)(2,1)S(1)} %select_add_fusion.1), channel_id=1, source_target_pairs={{0,2},{1,3},{6,4},{7,5},{8,10},{9,11},{14,12},{15,13},{16,18},{17,... | collective-permute-start | bytes 1179656 | tf_op jit(solution)/shard_map/ppermute | solution.py:950
  210.6 6.6 %collective-permute-start.22 = (bf16[256,768]{1,0:T(8,128)(2,1)S(1)}, bf16[256,768]{1,0:T(8,128)(2,1)S(1)}, u32[]{:S(2)}, u32[]{:S(2)}) collective-permute-start(bf16[256,768]{1,0:T(8,128)(2,1)S(1)} %select_add_fusion.1), channel_id=1, source_target_pairs={{2,4},{3,5},{4,2},{5,3},{10,12},{11,13},{12,10},{13,11},{18,20},{1... | collective-permute-start | bytes 1179656 | tf_op jit(solution)/shard_map/ppermute | solution.py:950
  211.4 26.5 %copy-start.6 = (bf16[384,384]{1,0:T(8,128)(2,1)}, bf16[384,384]{1,0:T(8,128)(2,1)S(1)}, u32[]{:S(2)}) copy-start(bf16[384,384]{1,0:T(8,128)(2,1)S(1)} %broadcast_select_fusion.3.refs_2_) | copy-start | bytes 884740
  211.5 35.1 %copy-start.19 = (bf16[160,384]{1,0:T(8,128)(2,1)}, bf16[160,384]{1,0:T(8,128)(2,1)S(1)}, u32[]{:S(2)}) copy-start(bf16[160,384]{1,0:T(8,128)(2,1)S(1)} %slice.124.refs_0_) | copy-start | bytes 368644
  211.5 20.3 %collective-permute-start.32 = (bf16[352,384]{1,0:T(8,128)(2,1)S(1)}, bf16[352,384]{1,0:T(8,128)(2,1)S(1)}, u32[]{:S(2)}, u32[]{:S(2)}) collective-permute-start(bf16[352,384]{1,0:T(8,128)(2,1)S(1)} %fusion.2), channel_id=1, source_target_pairs={{0,2},{1,3},{2,0},{3,1},{4,6},{5,7},{6,4},{7,5},{8,10},{9,11},{10,... | collective-permute-start | bytes 811016 | tf_op jit(solution)/shard_map/ppermute | solution.py:950
  214.9 6.7 %collective-permute-start.34 = (bf16[160,384]{1,0:T(8,128)(2,1)S(1)}, bf16[160,384]{1,0:T(8,128)(2,1)S(1)}, u32[]{:S(2)}, u32[]{:S(2)}) collective-permute-start(bf16[160,384]{1,0:T(8,128)(2,1)S(1)} %slice.124.refs_0_), channel_id=1, source_target_pairs={{2,4},{3,5},{4,2},{5,3},{10,12},{11,13},{12,10},{13,11},{18,20},{1... | collective-permute-start | bytes 368648 | tf_op jit(solution)/shard_map/ppermute | solution.py:950
  215.7 6.6 %collective-permute-start.30 = (bf16[128,768]{1,0:T(8,128)(2,1)S(1)}, bf16[128,768]{1,0:T(8,128)(2,1)S(1)}, u32[]{:S(2)}, u32[]{:S(2)}) collective-permute-start(bf16[128,768]{1,0:T(8,128)(2,1)S(1)} %bitcast_add_fusion), channel_id=1, source_target_pairs={{0,8},{8,0},{16,24},{24,16},{1,9},{9,1},{17,25},{25,17},{2,10},{10... | collective-permute-start | bytes 589832 | tf_op jit(solution)/shard_map/ppermute | solution.py:942
  217.3 10.7 %collective-permute-start.29 = (bf16[128,768]{1,0:T(8,128)(2,1)S(1)}, bf16[128,768]{1,0:T(8,128)(2,1)S(1)}, u32[]{:S(2)}, u32[]{:S(2)}) collective-permute-start(bf16[128,768]{1,0:T(8,128)(2,1)S(1)} %bitcast_add_fusion.1), channel_id=1, source_target_pairs={{0,16},{8,24},{16,0},{24,8},{1,17},{9,25},{17,1},{25,9},{2,18},{10... | collective-permute-start | bytes 589832 | tf_op jit(solution)/shard_map/ppermute | solution.py:942
  220.2 11.9 %collective-permute-start.49 = (bf16[384,384]{1,0:T(8,128)(2,1)S(1)}, bf16[384,384]{1,0:T(8,128)(2,1)S(1)}, u32[]{:S(2)}, u32[]{:S(2)}) collective-permute-start(bf16[384,384]{1,0:T(8,128)(2,1)S(1)} %collective-permute-done.48), channel_id=1, source_target_pairs={{2,0},{3,1},{4,6},{5,7},{10,8},{11,9},{12,14},{13,15},{18,16},{19,... | collective-permute-start | bytes 884744 | tf_op jit(solution)/shard_map/ppermute | solution.py:950
  221.6 13.0 %collective-permute-start.25 = (bf16[256,768]{1,0:T(8,128)(2,1)S(1)}, bf16[256,768]{1,0:T(8,128)(2,1)S(1)}, u32[]{:S(2)}, u32[]{:S(2)}) collective-permute-start(bf16[256,768]{1,0:T(8,128)(2,1)S(1)} %add.70), channel_id=1, source_target_pairs={{2,4},{3,5},{4,2},{5,3},{10,12},{11,13},{12,10},{13,11},{18,20},{1... | collective-permute-start | bytes 1179656 | tf_op jit(solution)/shard_map/ppermute | solution.py:950
  222.3 15.6 %collective-permute-start.23 = (bf16[256,768]{1,0:T(8,128)(2,1)S(1)}, bf16[256,768]{1,0:T(8,128)(2,1)S(1)}, u32[]{:S(2)}, u32[]{:S(2)}) collective-permute-start(bf16[256,768]{1,0:T(8,128)(2,1)S(1)} %select_add_fusion), channel_id=1, source_target_pairs={{0,2},{1,3},{2,0},{3,1},{4,6},{5,7},{6,4},{7,5},{8,10},{9,11},{10,... | collective-permute-start | bytes 1179656 | tf_op jit(solution)/shard_map/ppermute | solution.py:950
  227.9 11.3 %collective-permute-start.35 = (bf16[160,384]{1,0:T(8,128)(2,1)S(1)}, bf16[160,384]{1,0:T(8,128)(2,1)S(1)}, u32[]{:S(2)}, u32[]{:S(2)}) collective-permute-start(bf16[160,384]{1,0:T(8,128)(2,1)S(1)} %collective-permute-done.34), channel_id=1, source_target_pairs={{2,0},{3,1},{4,6},{5,7},{10,8},{11,9},{12,14},{13,15},{18,16},{19,... | collective-permute-start | bytes 368648 | tf_op jit(solution)/shard_map/ppermute | solution.py:950
  231.9 1.7 collective-permute-start.31
  232.0 15.2 %copy-start.9 = (bf16[160,384]{1,0:T(8,128)(2,1)}, bf16[160,384]{1,0:T(8,128)(2,1)S(1)}, u32[]{:S(2)}) copy-start(bf16[160,384]{1,0:T(8,128)(2,1)S(1)} %slice.148.refs_1_) | copy-start | bytes 368644
  232.1 7.2 %collective-permute-start.33 = (bf16[352,384]{1,0:T(8,128)(2,1)S(1)}, bf16[352,384]{1,0:T(8,128)(2,1)S(1)}, u32[]{:S(2)}, u32[]{:S(2)}) collective-permute-start(bf16[352,384]{1,0:T(8,128)(2,1)S(1)} %pad_maximum_fusion.5), channel_id=1, source_target_pairs={{2,4},{3,5},{4,2},{5,3},{10,12},{11,13},{12,10},{13,11},{18,20},{1... | collective-permute-start | bytes 811016 | tf_op jit(solution)/shard_map/ppermute | solution.py:950
  233.6 7.3 %collective-permute-start.50 = (bf16[384,384]{1,0:T(8,128)(2,1)}, bf16[384,384]{1,0:T(8,128)(2,1)S(1)}, u32[]{:S(2)}, u32[]{:S(2)}) collective-permute-start(bf16[384,384]{1,0:T(8,128)(2,1)} %constant_dynamic-update-slice_fusion.refs_0_), channel_id=1, source_target_pairs={{0,1},{1,0},{2,3},{3,2},{4,5},{5,4},{6,7},{7,6},{8,9},{9,8},{10,11... | collective-permute-start | bytes 884744 | tf_op jit(solution)/shard_map/ppermute | solution.py:946
  234.5 6.4 %collective-permute-start.51 = (bf16[384,384]{1,0:T(8,128)(2,1)}, bf16[384,384]{1,0:T(8,128)(2,1)S(1)}, u32[]{:S(2)}, u32[]{:S(2)}) collective-permute-start(bf16[384,384]{1,0:T(8,128)(2,1)} %collective-permute-done.45.refs_1_), channel_id=1, source_target_pairs={{0,1},{1,0},{2,3},{3,2},{4,5},{5,4},{6,7},{7,6},{8,9},{9,8},{10,11... | collective-permute-start | bytes 884744 | tf_op jit(solution)/shard_map/ppermute | solution.py:946
  237.9 3.0 %collective-permute-start.52 = (bf16[384,384]{1,0:T(8,128)(2,1)S(1)}, bf16[384,384]{1,0:T(8,128)(2,1)S(1)}, u32[]{:S(2)}, u32[]{:S(2)}) collective-permute-start(bf16[384,384]{1,0:T(8,128)(2,1)S(1)} %broadcast_select_fusion.3.refs_2_), channel_id=1, source_target_pairs={{0,1},{1,0},{2,3},{3,2},{4,5},{5,4},{6,7},{7,6},{8,9},{9,8},{10,11... | collective-permute-start | bytes 884744 | tf_op jit(solution)/shard_map/ppermute | solution.py:946
  239.2 1.7 collective-permute-start.53
  239.3 13.9 %collective-permute-start.37 = (bf16[352,384]{1,0:T(8,128)(2,1)S(1)}, bf16[352,384]{1,0:T(8,128)(2,1)S(1)}, u32[]{:S(2)}, u32[]{:S(2)}) collective-permute-start(bf16[352,384]{1,0:T(8,128)(2,1)S(1)} %pad_maximum_fusion.6), channel_id=1, source_target_pairs={{2,0},{3,1},{4,6},{5,7},{10,8},{11,9},{12,14},{13,15},{18,16},{19,... | collective-permute-start | bytes 811016 | tf_op jit(solution)/shard_map/ppermute | solution.py:950
  246.6 10.9 %collective-permute-start.38 = (bf16[160,384]{1,0:T(8,128)(2,1)S(1)}, bf16[160,384]{1,0:T(8,128)(2,1)S(1)}, u32[]{:S(2)}, u32[]{:S(2)}) collective-permute-start(bf16[160,384]{1,0:T(8,128)(2,1)S(1)} %slice.124.refs_0_), channel_id=1, source_target_pairs={{0,1},{1,0},{2,3},{3,2},{4,5},{5,4},{6,7},{7,6},{8,9},{9,8},{10,11... | collective-permute-start | bytes 368648 | tf_op jit(solution)/shard_map/ppermute | solution.py:946
  247.2 10.4 %collective-permute-start.39 = (bf16[160,384]{1,0:T(8,128)(2,1)S(1)}, bf16[160,384]{1,0:T(8,128)(2,1)S(1)}, u32[]{:S(2)}, u32[]{:S(2)}) collective-permute-start(bf16[160,384]{1,0:T(8,128)(2,1)S(1)} %slice.148.refs_1_), channel_id=1, source_target_pairs={{0,1},{1,0},{2,3},{3,2},{4,5},{5,4},{6,7},{7,6},{8,9},{9,8},{10,11... | collective-permute-start | bytes 368648 | tf_op jit(solution)/shard_map/ppermute | solution.py:946
  250.4 4.8 %collective-permute-start.36 = (f32[128,768]{1,0:T(8,128)}, f32[128,768]{1,0:T(8,128)S(1)}, u32[]{:S(2)}, u32[]{:S(2)}) collective-permute-start(f32[128,768]{1,0:T(8,128)} %get-tuple-element.201), channel_id=1, source_target_pairs={{0,1},{1,0},{2,3},{3,2},{4,5},{5,4},{6,7},{7,6},{8,9},{9,8},{10,11... | collective-permute-start | bytes 1179656 | tf_op jit(solution)/shard_map/ppermute | solution.py:946
  253.3 3.0 %collective-permute-start.41 = (bf16[352,384]{1,0:T(8,128)(2,1)S(1)}, bf16[352,384]{1,0:T(8,128)(2,1)S(1)}, u32[]{:S(2)}, u32[]{:S(2)}) collective-permute-start(bf16[352,384]{1,0:T(8,128)(2,1)S(1)} %broadcast_select_fusion.4), channel_id=1, source_target_pairs={{0,1},{1,0},{2,3},{3,2},{4,5},{5,4},{6,7},{7,6},{8,9},{9,8},{10,11... | collective-permute-start | bytes 811016 | tf_op jit(solution)/shard_map/ppermute | solution.py:946
  253.4 4.2 %collective-permute-start.40 = (bf16[160,384]{1,0:T(8,128)(2,1)S(1)}, bf16[160,384]{1,0:T(8,128)(2,1)S(1)}, u32[]{:S(2)}, u32[]{:S(2)}) collective-permute-start(bf16[160,384]{1,0:T(8,128)(2,1)S(1)} %broadcast_select_fusion.5.refs_2_), channel_id=1, source_target_pairs={{0,1},{1,0},{2,3},{3,2},{4,5},{5,4},{6,7},{7,6},{8,9},{9,8},{10,11... | collective-permute-start | bytes 368648 | tf_op jit(solution)/shard_map/ppermute | solution.py:946
  (42 other events, 163.7 us)
Sparse Core Ops, SparseCore 0:
  127.5 39.0 reduce-scatter.1

commit v4 on v3

--- a/solution.py
+++ b/solution.py
@@ -330,7 +330,8 @@
 
 
 def attend_kernel(x_ref, w0, w1, w2, w3, w4,
-                  normed_ref, kv_ref, mixt_ref, att_ref, low_ref, lse_ref, wfull_ref, gains_ref, s_ref, g_ref, wsems):
+                  normed_out, kv_out, mixt_out, att_ref, low_ref, lse_ref, wfull_out, gains_ref,
+                  normed_ref, kv_ref, mixt_ref, wfull_ref, s_ref, g_ref, wsems, sems):
     place = lax.axis_index("wshard")
     pieces = (w0, w1, w2, w3, w4)
     half = w3.shape[0]
@@ -357,6 +358,11 @@
         for h in range(OWN_HEADS):
             kv_ref[h, here, 0:HEAD_DIM] = mix[:, OWN + h * HEAD_DIM : OWN + (h + 1) * HEAD_DIM]
             kv_ref[h, here, HEAD_DIM:] = mix[:, 2 * OWN + h * HEAD_DIM : 2 * OWN + (h + 1) * HEAD_DIM]
+
+    pairs = ((normed_ref, normed_out), (kv_ref, kv_out), (mixt_ref, mixt_out), (wfull_ref, wfull_out))
+    copies = [pltpu.make_async_copy(src, dst, sems.at[k]) for k, (src, dst) in enumerate(pairs)]
+    for copy in copies:
+        copy.start()
 
     @pl.loop(0, OWN_HEADS)
     def _(h):
@@ -392,6 +398,9 @@
             low_ref[block, pl.ds(base, HEAD_DIM), :] = att.astype(BF)
             lse_ref[pl.ds(h, 1), here] = top + jnp.log(total)
 
+    for copy in copies:
+        copy.wait()
+
 
 def attend(x_all, pieces):
     length = 4 * TILE
@@ -410,12 +419,18 @@
             ((8, D), F32),
         ],
         [
+            pltpu.VMEM((length, D), BF),
+            pltpu.VMEM((OWN_HEADS, length, 2 * HEAD_DIM), BF),
+            pltpu.VMEM((MIX, length), BF),
+            pltpu.VMEM((D, MIX), BF),
             pltpu.VMEM((length, TILE), F32),
             pltpu.VMEM((4, 16, MIX), BF),
             pltpu.SemaphoreType.DMA((9,)),
+            pltpu.SemaphoreType.DMA((4,)),
         ],
         3 * 10**9,
         (x_all, *pieces),
+        [ANYWHERE] * 3 + [WHOLE] * 3 + [ANYWHERE, WHOLE],
     )
 
 
@@ -725,10 +740,17 @@
     )
 
 
-def attend_back_kernel(kv_ref, mixt_ref, att_ref, lse_ref, dout_ref, normed_ref, w_ref, gain_ref, dgain_ref, _, __,
+def attend_back_kernel(kv_ref, mixt_ref, att_ref, lse_ref, dout_ref, normed_in, w_in, gain_ref, dgain_ref, _, __,
                        f0_ref, f1_ref, f2_ref, f3_ref, gkeep_ref, gsend_ref,
-                       dq_ref, dk_ref, dv_ref, dm_ref, mix_ref, total_ref, first_ref, head_ref, sems):
-    length = normed_ref.shape[0]
+                       dq_ref, dk_ref, dv_ref, dm_ref, mix_ref, total_ref, first_ref, head_ref, sems,
+                       normed_ref, w_ref, in_sems):
+    length = kv_ref.shape[1]
+    loads = [
+        pltpu.make_async_copy(normed_in, normed_ref, in_sems.at[0]),
+        pltpu.make_async_copy(w_in, w_ref, in_sems.at[1]),
+    ]
+    for load in loads:
+        load.start()
     scale = BF(HEAD_DIM**-0.5)
     core = lax.axis_index("ctx") % 2
     z = lax.axis_index("ctx") // 2
@@ -776,6 +798,8 @@
             to = kind * OWN + h * HEAD_DIM
             mix_ref[:, to : to + HEAD_DIM] = dm_ref[h, :, kind * HEAD_DIM : (kind + 1) * HEAD_DIM]
     total_ref[...] = jnp.zeros_like(total_ref)
+    for load in loads:
+        load.wait()
     for block in range(4):
         here = slice(block * TILE, (block + 1) * TILE)
         first = nt(mix_ref[here, :], w_ref[...])
@@ -816,7 +840,7 @@
     length = normed.shape[0]
     return pl.pallas_call(
         attend_back_kernel,
-        in_specs=[WHOLE] * 9 + [ANYWHERE] * 2,
+        in_specs=[WHOLE] * 5 + [ANYWHERE] * 2 + [WHOLE] * 2 + [ANYWHERE] * 2,
         out_specs=[ANYWHERE] * 6,
         out_shape=[jax.ShapeDtypeStruct((TILE, D), BF)] * 4 + [jax.ShapeDtypeStruct(keep.shape, BF)] * 2,
         input_output_aliases={9: 4, 10: 5},
@@ -830,6 +854,9 @@
             pltpu.VMEM((4, TILE, D), BF),
             pltpu.VMEM((2, 2, 2, HEAD_ROWS, HALF), BF),
             pltpu.SemaphoreType.DMA((6,)),
+            pltpu.VMEM((length, D), BF),
+            pltpu.VMEM((D, MIX), BF),
+            pltpu.SemaphoreType.DMA((2,)),
         ],
         compiler_params=pltpu.CompilerParams(vmem_limit_bytes=VMEM_LIMIT),
         cost_estimate=pl.CostEstimate(flops=1000, bytes_accessed=1000, transcendentals=0),
@@ -896,7 +923,7 @@
 
 
 def finish_heads_kernel(*refs):
-    mine, theirs, outs, (gout_ref, gqkv_ref, gains_ref) = refs[:4], refs[4:8], refs[8:10], refs[10:]
+    mine, theirs, outs, (gout_ref, gqkv_ref, one_ref, two_ref) = refs[:4], refs[4:8], refs[8:10], refs[10:]
     slots = line_slots()
     first = lax.axis_index("ctx") % 2 == 0
     out, other_out = [ref[...].astype(F32) for ref in outs]
@@ -907,7 +934,8 @@
     mine, theirs = [[ref[...].astype(F32) for ref in group] for group in (mine, theirs)]
     low = [jnp.where(first, a, b) for a, b in zip(mine, theirs)]
     high = [jnp.where(first, b, a) for a, b in zip(mine, theirs)]
-    gains_ref[...] = sum(block[PART + QUART :, 0:SHARD] for block in low)
+    gains = sum(block[PART + QUART :, 0:SHARD] for block in low)
+    one_ref[...], two_ref[...] = gains[0], gains[1]
     for slot in range(4):
         for side, group in enumerate((low, high)):
             block = jnp.where(
@@ -927,7 +955,7 @@
         finish_heads_kernel,
         "finish_heads",
         [WHOLE] * 10,
-        [((SHARD, D), F32), ((SHARD, 3 * D), F32), ((16, SHARD), F32)],
+        [((SHARD, D), F32), ((SHARD, 3 * D), F32), ((SHARD,), F32), ((SHARD,), F32)],
         [],
         10**7,
         args,
@@ -1088,16 +1116,16 @@
     head_near = jnp.where(inner, head_mid, head_near)
     blocks = sums[:HEAD_ROWS], sums_pair[:HEAD_ROWS], head_near, sums_last[:HEAD_ROWS]
     others = [across_core(block) for block in (*blocks[:3], sums_last)]
-    grad_out, grad_qkv, out_gains = finish_heads(
+    grad_out, grad_qkv, gain_one, gain_two = finish_heads(
         *blocks, *others[:3], others[3][:HEAD_ROWS], sums_last[HEAD_ROWS:], others[3][HEAD_ROWS:]
     )
     return (
         out_result,
         out_tokens,
-        out_gains[0],
+        gain_one,
         grad_qkv,
         grad_out,
-        out_gains[1],
+        gain_two,
         grad_up,
         grad_down,
     )

time: 273 us -> 272 us (level)
  no operation moved by 1% of the time
where the time goes in v4:
time: 272 us; the launch traced here: 269 us
  Pallas kernels  83.7 us (31%)
  starting transfers between devices  75.3 us (28%)
  waiting for transfers between devices  65.4 us (24%)
  local copies, waits for them, and re-layouts  23.8 us (9%)
  between operations  15 us (6%)
  other arithmetic  5.93 us (2%)
    pallas_call x14, Pallas kernels, call(): pl.pallas_call(kernel, in_specs=ins, out_specs=out_specs or [WHOLE] * len...  66.7 us
    ppermute x27, waiting for transfers between devices, across_w(): return lax.ppermute(value, 'wshard', [(i, i ^ flip) for i in range(4)])  33.4 us
    ppermute x15, starting transfers between devices, between_z(): lax.ppermute(value, 'ctx', [(2 * a + c, 2 * b + c) for a, b in pairs for...  28.8 us
    ppermute x27, starting transfers between devices, across_w(): return lax.ppermute(value, 'wshard', [(i, i ^ flip) for i in range(4)])  28.8 us
    pallas_call x1, Pallas kernels, attend_back(): pl.pallas_call(attend_back_kernel, in_specs=[WHOLE] * 5 + [ANYWHERE] * 2...  17.1 us
    ppermute x15, waiting for transfers between devices, between_z(): lax.ppermute(value, 'ctx', [(2 * a + c, 2 * b + c) for a, b in pairs for...  16 us
    unnamed x101, local copies, waits for them, and re-layouts  12.1 us
    all_to_all x1, waiting for transfers between devices, local_grid(): lax.all_to_all(d_att, 'ctx', 0, 0, tiled=True, axis_index_groups=Z_GROUPS)  9 us
  transfers between devices with their start and end apart: 58, of which 21 were waited for; matrix products, arithmetic and copies ran while one was open for 7% of the time, Pallas kernels for 27%

profile of v4, /device:TPU:0, one launch (start us, length us, event | category | flops | bytes accessed | tf_op | source)
XLA Modules:
  0.0 269.1 jit_solution(16521148316460289459)
XLA Ops:
  7.2 1.3 dynamic-slice_bitcast_fusion.2
  9.0 1.3 collective-permute-done
  10.6 1.3 broadcast_in_dim.10
  11.9 6.2 %all-to-all-start = ((bf16[4,256,768]{2,1,0:T(8,128)(2,1)}), bf16[4,256,768]{2,1,0:T(8,128)(2,1)S(1)}, u32[]{:S(2)}, u32[]{:S(2)}) async-start(bf16[4,256,768]{2,1,0:T(8,128)(2,1)} %broadcast_in_dim.10), calls=%async_computation | async-start | bytes 3145728 | tf_op jit(solution)/shard_map/all_to_all | solution.py:1045
  18.9 3.1 %parcels.1 = (bf16[320,768]{1,0:T(8,128)(2,1)}, bf16[416,768]{1,0:T(8,128)(2,1)}, bf16[320,768]{1,0:T(8,128)(2,1)}, bf16[416,768]{1,0:T(8,128)(2,1)}) custom-call(bf16[256,768]{1,0:T(8,128)(2,1)} %pad_maximum_fusion.3.cot_ref, bf16[192,768]{1,0:T(8,128)(2,1)} %own_ref.1, bf16[192,3072]{1,0:T(8,128)(2,1)} %wup_ref.3), custom_call_target="tpu_custom_call" | custom-call | flops 1000 | bytes 1000 | tf_op jit(solution)/shard_map/parcels/pallas_call | solution.py:303
  22.0 1.6 collective-permute-start.1
  23.5 1.5 collective-permute-start.2
  25.1 2.9 %reshape.155 = bf16[192,3,4,192]{3,2,1,0:T(4,128)(2,1)S(1)} reshape(bf16[192,2304]{1,0:T(8,128)(2,1)} %param.10) | data formatting | bytes 1769472 | tf_op jit(solution)/shard_map/reshape | solution.py:1043
  29.7 5.6 %collective-permute-done.1.x_on = bf16[320,768]{1,0:T(8,128)(2,1)} collective-permute-done((bf16[320,768]{1,0:T(8,128)(2,1)}, bf16[320,768]{1,0:T(8,128)(2,1)}, u32[]{:S(2)}, u32[]{:S(2)}) %collective-permute-start.1) | collective-permute-done | bytes 491552 | tf_op jit(solution)/shard_map/ppermute | solution.py:970
  35.3 1.2 collective-permute-done.2.y_on
  36.5 1.5 collective-permute-start.4
  38.6 5.3 %collective-permute-done.4.w2 = bf16[224,576]{1,0:T(8,128)(2,1)S(1)} collective-permute-done((bf16[224,576]{1,0:T(8,128)(2,1)S(1)}, bf16[224,576]{1,0:T(8,128)(2,1)S(1)}, u32[]{:S(2)}, u32[]{:S(2)}) %collective-permute-start.4) | collective-permute-done | bytes 258080 | tf_op jit(solution)/shard_map/ppermute | solution.py:970
  44.6 1.3 collective-permute-done.3.w1
  46.2 2.9 %collective-permute-done.6.w4 = bf16[112,576]{1,0:T(8,128)(2,1)S(1)} collective-permute-done((bf16[112,576]{1,0:T(8,128)(2,1)S(1)}, bf16[112,576]{1,0:T(8,128)(2,1)S(1)}, u32[]{:S(2)}, u32[]{:S(2)}) %collective-permute-start.6) | collective-permute-done | bytes 129056 | tf_op jit(solution)/shard_map/ppermute | solution.py:970
  49.1 2.8 %collective-permute-done.5.w3 = bf16[112,576]{1,0:T(8,128)(2,1)S(1)} collective-permute-done((bf16[112,576]{1,0:T(8,128)(2,1)S(1)}, bf16[112,576]{1,0:T(8,128)(2,1)S(1)}, u32[]{:S(2)}, u32[]{:S(2)}) %collective-permute-start.5) | collective-permute-done | bytes 129056 | tf_op jit(solution)/shard_map/ppermute | solution.py:970
  53.9 2.0 collective-permute-start.10
  57.1 12.4 %attend.1 = (bf16[1024,768]{1,0:T(8,128)(2,1)}, bf16[3,1024,128]{2,1,0:T(8,128)(2,1)}, bf16[576,1024]{1,0:T(8,128)(2,1)}, f32[192,1024]{1,0:T(8,128)}, bf16[4,19...) custom-call(bf16[4,256,768]{2,1,0:T(8,128)(2,1)} %copy-done, ...), custom_call_target="tpu_custom_call" | custom-call | flops 1000 | bytes 1000 | tf_op jit(solution)/shard_map/attend/pallas_call | solution.py:303
  69.5 5.9 %collective-permute-done.9.corner_a = bf16[320,768]{1,0:T(8,128)(2,1)} collective-permute-done((bf16[320,768]{1,0:T(8,128)(2,1)}, bf16[320,768]{1,0:T(8,128)(2,1)}, u32[]{:S(2)}, u32[]{:S(2)}) %collective-permute-start.9) | collective-permute-done | bytes 491552 | tf_op jit(solution)/shard_map/ppermute | solution.py:970
  75.5 4.7 %all-to-all-start.1 = ((bf16[4,192,256]{2,1,0:T(8,128)(2,1)}), bf16[4,192,256]{2,1,0:T(8,128)(2,1)S(1)}, u32[]{:S(2)}, u32[]{:S(2)}) async-start(bf16[4,192,256]{2,1,0:T(8,128)(2,1)} %get-tuple-element.129), calls=%async_computation.1 | async-start | bytes 786432 | tf_op jit(solution)/shard_map/all_to_all | solution.py:1058
  80.2 4.1 %assemble.1 = (bf16[768,768]{1,0:T(8,128)(2,1)}, bf16[768,768]{1,0:T(8,128)(2,1)}, bf16[1024,768]{1,0:T(8,128)(2,1)}) custom-call(bf16[256,768]{1,0:T(8,128)(2,1)} %pad_maximum_fusion.3.cot_ref, bf16[192,768]{1,0:T(8,128)(2,1)} %own_ref.1, bf16[192,3072]{1,0:T(8,128)(2,1)} %wup_ref.3, bf16[320,768]{1,0:T(8,128)(2,1)} %collective-permute-done.1.x_on, ...), custom_call_target="tpu_custom_call" | custom-call | flops 1000 | bytes 1000 | tf_op jit(solution)/shard_map/assemble/pallas_call | solution.py:303
  84.3 4.7 %all-to-all-done.1 = bf16[4,192,256]{2,1,0:T(8,128)(2,1)S(1)} async-done(((bf16[4,192,256]{2,1,0:T(8,128)(2,1)}), bf16[4,192,256]{2,1,0:T(8,128)(2,1)S(1)}, u32[]{:S(2)}, u32[]{:S(2)}) %all-to-all-start.1) | async-done | bytes 393248 | tf_op jit(solution)/shard_map/all_to_all | solution.py:1058
  89.8 3.0 %project.1 = (f32[256,768]{1,0:T(8,128)}, bf16[256,768]{1,0:T(8,128)(2,1)}) custom-call(bf16[768,256]{1,0:T(8,128)(2,1)} %bitcast.48, bf16[256,768]{1,0:T(8,128)(2,1)} %copy-done.1, f32[8,768]{1,0:T(8,128)} %get-tuple-element.130.gain_ref, bf16[768,768]{1,0:T(8,128)(2,1)} %get-tuple-element.137.wout_ref), custom_call_target="tpu_custom_call" | custom-call | flops 1000 | bytes 1000 | tf_op jit(solution)/shard_map/project/pallas_call | solution.py:303
  93.0 1.3 collective-permute-start.11
  94.3 4.6 %feed_own.1 = (bf16[256,768]{1,0:T(8,128)(2,1)}, bf16[256,768]{1,0:T(8,128)(2,1)}, f32[256,768]{1,0:T(8,128)}, f32[256,768]{1,0:T(8,128)}) custom-call(bf16[256,768]{1,0:T(8,128)(2,1)} %get-tuple-element.139.n_ref.n0, bf16[1024,768]{1,0:T(8,128)(2,1)} %get-tuple-element.140.cot_ref, bf16[768,768]{1,0:T(8,128)(2,1)} %get-tuple-element.141.up_ref, ...), custom_call_target="tpu_custom_call" | custom-call | flops 1000 | bytes 1000 | tf_op jit(solution)/shard_map/feed_own/pallas_call | solution.py:303
  99.0 3.1 %collective-permute-done.12.ny_ref.n2 = bf16[256,768]{1,0:T(8,128)(2,1)S(1)} collective-permute-done((bf16[256,768]{1,0:T(8,128)(2,1)}, bf16[256,768]{1,0:T(8,128)(2,1)S(1)}, u32[]{:S(2)}, u32[]{:S(2)}) %collective-permute-start.12) | collective-permute-done | bytes 393248 | tf_op jit(solution)/shard_map/ppermute | solution.py:970
  104.6 6.1 %feed_near.1 = (bf16[512,768]{1,0:T(8,128)(2,1)}, bf16[512,768]{1,0:T(8,128)(2,1)}, bf16[512,768]{1,0:T(8,128)(2,1)}, bf16[512,768]{1,0:T(8,128)(2,1)}) custom-call(bf16[256,768]{1,0:T(8,128)(2,1)} %copy-done.4, bf16[256,768]{1,0:T(8,128)(2,1)} %copy-done.3, bf16[1024,768]{1,0:T(8,128)(2,1)} %get-tuple-element.140.cot_ref, ...), custom_call_target="tpu_custom_call" | custom-call | flops 1000 | bytes 1000 | tf_op jit(solution)/shard_map/feed_near/pallas_call | solution.py:303
  111.5 5.6 %feed_far.1 = (bf16[256,768]{1,0:T(8,128)(2,1)}, bf16[256,768]{1,0:T(8,128)(2,1)}, bf16[2,128,768]{2,1,0:T(8,128)(2,1)}, bf16[128,768]{1,0:T(8,128)(2,1)}, bf16[...) custom-call(bf16[128,768]{1,0:T(8,128)(2,1)} %copy-done.14, ...), custom_call_target="tpu_custom_call" | custom-call | flops 1000 | bytes 1000 | tf_op jit(solution)/shard_map/feed_far/pallas_call | solution.py:303
  117.0 1.3 collective-permute-start.15
  118.4 1.3 collective-permute-start.16
  119.7 7.6 %feed_grads.1 = bf16[8,8,48,384]{3,2,1,0:T(8,128)(2,1)} custom-call(bf16[256,768]{1,0:T(8,128)(2,1)} %get-tuple-element.139.n_ref.n0, bf16[256,768]{1,0:T(8,128)(2,1)} %copy-done.4, bf16[256,768]{1,0:T(8,128)(2,1)} %copy-done.3, bf16[128,768]{1,0:T(8,128)(2,1)} %copy-done.14, bf16[128,768]{1,0:T(8,128)(2,1)} %copy-done.15, ...), custom_call_target="tpu_custom_call" | custom-call | flops 1000 | bytes 1000 | tf_op jit(solution)/shard_map/feed_grads/pallas_call | solution.py:303
  129.2 1.5 collective-permute-start.17
  130.7 3.5 %collective-permute-done.18.b_more_ref = bf16[128,768]{1,0:T(8,128)(2,1)S(1)} collective-permute-done((bf16[128,768]{1,0:T(8,128)(2,1)S(1)}, bf16[128,768]{1,0:T(8,128)(2,1)S(1)}, u32[]{:S(2)}, u32[]{:S(2)}) %collective-permute-start.18) | collective-permute-done | bytes 196640 | tf_op jit(solution)/shard_map/ppermute | solution.py:970
  135.6 4.3 %turn.1 = (f32[256,768]{1,0:T(8,128)}, bf16[4,192,256]{2,1,0:T(8,128)(2,1)}, bf16[256,768]{1,0:T(8,128)(2,1)}, f32[1,768]{1,0:T(1,128)}) custom-call(f32[256,768]{1,0:T(8,128)} %get-tuple-element.138.hidden_ref, f32[8,768]{1,0:T(8,128)} %get-tuple-element.130.gain_ref, f32[256,768]{1,0:T(8,128)} %get-tuple-element.142.dkeep_ref, ...), custom_call_target="tpu_custom_call" | custom-call | flops 1000 | bytes 1000 | tf_op jit(solution)/shard_map/turn/pallas_call | solution.py:303
  139.9 3.7 %all-to-all-start.2 = ((bf16[4,192,256]{2,1,0:T(8,128)(2,1)}), bf16[4,192,256]{2,1,0:T(8,128)(2,1)S(1)}, u32[]{:S(2)}, u32[]{:S(2)}) async-start(bf16[4,192,256]{2,1,0:T(8,128)(2,1)} %get-tuple-element.159), calls=%async_computation.2 | async-start | bytes 786432 | tf_op jit(solution)/shard_map/all_to_all | solution.py:1075
  143.6 1.4 collective-permute-start.19
  146.0 2.6 out_grad.1
  148.7 9.0 %all-to-all-done.2.dout_ref = bf16[4,192,256]{2,1,0:T(8,128)(2,1)S(1)} async-done(((bf16[4,192,256]{2,1,0:T(8,128)(2,1)}), bf16[4,192,256]{2,1,0:T(8,128)(2,1)S(1)}, u32[]{:S(2)}, u32[]{:S(2)}) %all-to-all-start.2) | async-done | bytes 393248 | tf_op jit(solution)/shard_map/all_to_all | solution.py:1075
  158.4 17.1 %attend_back.1 = (bf16[256,768]{1,0:T(8,128)(2,1)}, bf16[256,768]{1,0:T(8,128)(2,1)}, bf16[256,768]{1,0:T(8,128)(2,1)}, bf16[256,768]{1,0:T(8,128)(2,1)}, bf16[2...) custom-call(bf16[3,1024,128]{2,1,0:T(8,128)(2,1)} %get-tuple-element.1, ...), custom_call_target="tpu_custom_call", output_to_operand_aliasing={{4}: (9, {}), {5}: (10, {})} | custom-call | flops 1000 | bytes 1000 | tf_op jit(solution)/shard_map/attend_back/pallas_call | solution.py:841
  176.6 1.4 collective-permute-start.42
  178.0 1.4 bitcast_dynamic-update-slice_fusion
  180.3 1.7 collective-permute-start.44
  183.1 1.5 add.71
  184.7 1.5 collective-permute-start.27
  188.2 1.4 collective-permute-start.46
  190.4 3.8 %collective-permute-start.21 = (bf16[256,768]{1,0:T(8,128)(2,1)S(1)}, bf16[256,768]{1,0:T(8,128)(2,1)}, u32[]{:S(2)}, u32[]{:S(2)}) collective-permute-start(bf16[256,768]{1,0:T(8,128)(2,1)S(1)} %copy-done.23), channel_id=1, source_target_pairs={{0,2},{1,3},{6,4},{7,5},{8,10},{9,11},{14,12},{15,13},{16,18},{17,... | collective-permute-start | bytes 1179656 | tf_op jit(solution)/shard_map/ppermute | solution.py:978
  194.2 1.3 collective-permute-start.47
  195.5 2.6 collective-permute-done.45.refs_1_
  198.9 1.4 collective-permute-start.28
  200.3 4.2 %collective-permute-done.21 = bf16[256,768]{1,0:T(8,128)(2,1)} collective-permute-done((bf16[256,768]{1,0:T(8,128)(2,1)S(1)}, bf16[256,768]{1,0:T(8,128)(2,1)}, u32[]{:S(2)}, u32[]{:S(2)}) %collective-permute-start.21) | collective-permute-done | bytes 393248 | tf_op jit(solution)/shard_map/ppermute | solution.py:978
  205.6 4.8 %collective-permute-start.24 = (bf16[256,768]{1,0:T(8,128)(2,1)S(1)}, bf16[256,768]{1,0:T(8,128)(2,1)S(1)}, u32[]{:S(2)}, u32[]{:S(2)}) collective-permute-start(bf16[256,768]{1,0:T(8,128)(2,1)S(1)} %select_add_fusion.1), channel_id=1, source_target_pairs={{0,2},{1,3},{6,4},{7,5},{8,10},{9,11},{14,12},{15,13},{16,18},{17,... | collective-permute-start | bytes 1179656 | tf_op jit(solution)/shard_map/ppermute | solution.py:978
  211.3 3.3 %collective-permute-start.32 = (bf16[352,384]{1,0:T(8,128)(2,1)S(1)}, bf16[352,384]{1,0:T(8,128)(2,1)S(1)}, u32[]{:S(2)}, u32[]{:S(2)}) collective-permute-start(bf16[352,384]{1,0:T(8,128)(2,1)S(1)} %fusion.2), channel_id=1, source_target_pairs={{0,2},{1,3},{2,0},{3,1},{4,6},{5,7},{6,4},{7,5},{8,10},{9,11},{10,... | collective-permute-start | bytes 811016 | tf_op jit(solution)/shard_map/ppermute | solution.py:978
  215.4 1.6 collective-permute-start.30
  217.3 2.6 collective-permute-done.24
  219.9 1.3 collective-permute-start.49
  222.0 5.9 %collective-permute-start.23 = (bf16[256,768]{1,0:T(8,128)(2,1)S(1)}, bf16[256,768]{1,0:T(8,128)(2,1)S(1)}, u32[]{:S(2)}, u32[]{:S(2)}) collective-permute-start(bf16[256,768]{1,0:T(8,128)(2,1)S(1)} %select_add_fusion), channel_id=1, source_target_pairs={{0,2},{1,3},{2,0},{3,1},{4,6},{5,7},{6,4},{7,5},{8,10},{9,11},{10,... | collective-permute-start | bytes 1179656 | tf_op jit(solution)/shard_map/ppermute | solution.py:978
  227.9 1.3 collective-permute-start.35
  229.2 2.6 give.1
  234.9 2.7 %collective-permute-done.23.pair_ref = bf16[256,768]{1,0:T(8,128)(2,1)S(1)} collective-permute-done((bf16[256,768]{1,0:T(8,128)(2,1)S(1)}, bf16[256,768]{1,0:T(8,128)(2,1)S(1)}, u32[]{:S(2)}, u32[]{:S(2)}) %collective-permute-start.23) | collective-permute-done | bytes 393248 | tf_op jit(solution)/shard_map/ppermute | solution.py:978
  237.6 1.3 collective-permute-done.35
  239.0 1.6 collective-permute-start.37
  242.2 4.1 %finish_feed.1 = (f32[192,3072]{1,0:T(8,128)}, f32[768,768]{1,0:T(8,128)}) custom-call(bf16[384,384]{1,0:T(8,128)(2,1)} %constant_dynamic-update-slice_fusion.refs_0_, bf16[384,384]{1,0:T(8,128)(2,1)} %collective-permute-done.45.refs_1_, bf16[384,384]{1,0:T(8,128)(2,1)} %copy-done.6, bf16[384,384]{1,0:T(8,128)(2,1)} %copy-done.7, ...), custom_call_target="tpu_custom_call" | custom-call | flops 1000 | bytes 1000 | tf_op jit(solution)/shard_map/finish_feed/pallas_call | solution.py:303
  247.0 3.1 %last.1 = (f32[128,768]{1,0:T(8,128)}, f32[128,768]{1,0:T(8,128)}) custom-call(bf16[256,768]{1,0:T(8,128)(2,1)} %get-tuple-element.197.first_ref, bf16[256,768]{1,0:T(8,128)(2,1)} %copy-done.22, bf16[256,768]{1,0:T(8,128)(2,1)} %copy-done.21, bf16[256,768]{1,0:T(8,128)(2,1)} %copy-done.1, f32[8,768]{1,0:T(8,128)} %get-tuple-element.130.gain_ref, ...), custom_call_target="tpu_custom_call" | custom-call | flops 1000 | bytes 1000 | tf_op jit(solution)/shard_map/last/pallas_call | solution.py:303
  250.6 2.5 collective-permute-done.37
  258.9 3.4 %finish_heads.1 = (f32[192,768]{1,0:T(8,128)}, f32[192,2304]{1,0:T(8,128)}, f32[192]{0:T(256)}, f32[192]{0:T(256)}) custom-call(bf16[160,384]{1,0:T(8,128)(2,1)} %copy-done.19, bf16[160,384]{1,0:T(8,128)(2,1)} %copy-done.9, bf16[160,384]{1,0:T(8,128)(2,1)} %copy-done.20, bf16[160,384]{1,0:T(8,128)(2,1)} %slice.142.refs_3_, bf16[160,384]{1,0:T(8,128)(2,1)} %copy-done.41, ...), custom_call_target="tpu_custom_call" | custom-call | flops 1000 | bytes 1000 | tf_op jit(solution)/shard_map/finish_heads/pallas_call | solution.py:303
  (219 shorter events, 39.0 us)
Async XLA Ops:
  8.5 1.9 collective-permute-start
  11.9 44.1 %all-to-all-start = ((bf16[4,256,768]{2,1,0:T(8,128)(2,1)}), bf16[4,256,768]{2,1,0:T(8,128)(2,1)S(1)}, u32[]{:S(2)}, u32[]{:S(2)}) async-start(bf16[4,256,768]{2,1,0:T(8,128)(2,1)} %broadcast_in_dim.10), calls=%async_computation | async-start | bytes 3145728 | tf_op jit(solution)/shard_map/all_to_all | solution.py:1045
  22.0 13.4 %collective-permute-start.1 = (bf16[320,768]{1,0:T(8,128)(2,1)}, bf16[320,768]{1,0:T(8,128)(2,1)}, u32[]{:S(2)}, u32[]{:S(2)}) collective-permute-start(bf16[320,768]{1,0:T(8,128)(2,1)} %get-tuple-element.112), channel_id=1, source_target_pairs={{0,8},{8,0},{16,24},{24,16},{1,9},{9,1},{17,25},{25,17},{2,10},{10... | collective-permute-start | bytes 1474568 | tf_op jit(solution)/shard_map/ppermute | solution.py:970
  23.5 13.0 %collective-permute-start.2 = (bf16[320,768]{1,0:T(8,128)(2,1)}, bf16[320,768]{1,0:T(8,128)(2,1)}, u32[]{:S(2)}, u32[]{:S(2)}) collective-permute-start(bf16[320,768]{1,0:T(8,128)(2,1)} %get-tuple-element.113), channel_id=1, source_target_pairs={{0,16},{8,24},{16,0},{24,8},{1,17},{9,25},{17,1},{25,9},{2,18},{10... | collective-permute-start | bytes 1474568 | tf_op jit(solution)/shard_map/ppermute | solution.py:970
  29.7 26.3 %copy-start.8 = (bf16[224,576]{1,0:T(8,128)(2,1)}, bf16[224,576]{1,0:T(8,128)(2,1)S(1)}, u32[]{:S(2)}) copy-start(bf16[224,576]{1,0:T(8,128)(2,1)S(1)} %pad_maximum_fusion.4.w0) | copy-start | bytes 774148
  36.5 7.4 %collective-permute-start.4 = (bf16[224,576]{1,0:T(8,128)(2,1)S(1)}, bf16[224,576]{1,0:T(8,128)(2,1)S(1)}, u32[]{:S(2)}, u32[]{:S(2)}) collective-permute-start(bf16[224,576]{1,0:T(8,128)(2,1)S(1)} %pad_maximum_fusion.4.w0), channel_id=1, source_target_pairs={{0,16},{8,24},{16,0},{24,8},{1,17},{9,25},{17,1},{25,9},{2,18},{10... | collective-permute-start | bytes 774152 | tf_op jit(solution)/shard_map/ppermute | solution.py:970
  38.1 7.9 %collective-permute-start.3 = (bf16[224,576]{1,0:T(8,128)(2,1)S(1)}, bf16[224,576]{1,0:T(8,128)(2,1)S(1)}, u32[]{:S(2)}, u32[]{:S(2)}) collective-permute-start(bf16[224,576]{1,0:T(8,128)(2,1)S(1)} %pad_maximum_fusion.4.w0), channel_id=1, source_target_pairs={{0,8},{8,0},{16,24},{24,16},{1,9},{9,1},{17,25},{25,17},{2,10},{10... | collective-permute-start | bytes 774152 | tf_op jit(solution)/shard_map/ppermute | solution.py:970
  44.0 5.2 %collective-permute-start.6 = (bf16[112,576]{1,0:T(8,128)(2,1)S(1)}, bf16[112,576]{1,0:T(8,128)(2,1)S(1)}, u32[]{:S(2)}, u32[]{:S(2)}) collective-permute-start(bf16[112,576]{1,0:T(8,128)(2,1)S(1)} %slice.135), channel_id=1, source_target_pairs={{0,8},{8,0},{16,24},{24,16},{1,9},{9,1},{17,25},{25,17},{2,10},{10... | collective-permute-start | bytes 387080 | tf_op jit(solution)/shard_map/ppermute | solution.py:970
  45.9 5.9 %collective-permute-start.5 = (bf16[112,576]{1,0:T(8,128)(2,1)S(1)}, bf16[112,576]{1,0:T(8,128)(2,1)S(1)}, u32[]{:S(2)}, u32[]{:S(2)}) collective-permute-start(bf16[112,576]{1,0:T(8,128)(2,1)S(1)} %slice.134), channel_id=1, source_target_pairs={{0,16},{8,24},{16,0},{24,8},{1,17},{9,25},{17,1},{25,9},{2,18},{10... | collective-permute-start | bytes 387080 | tf_op jit(solution)/shard_map/ppermute | solution.py:970
  51.9 23.6 %collective-permute-start.7 = (bf16[416,768]{1,0:T(8,128)(2,1)}, bf16[416,768]{1,0:T(8,128)(2,1)S(1)}, u32[]{:S(2)}, u32[]{:S(2)}) collective-permute-start(bf16[416,768]{1,0:T(8,128)(2,1)} %get-tuple-element.126), channel_id=1, source_target_pairs={{0,8},{8,0},{16,24},{24,16},{1,9},{9,1},{17,25},{25,17},{2,10},{10... | collective-permute-start | bytes 1916936 | tf_op jit(solution)/shard_map/ppermute | solution.py:970
  51.9 23.6 %collective-permute-start.8 = (bf16[416,768]{1,0:T(8,128)(2,1)}, bf16[416,768]{1,0:T(8,128)(2,1)}, u32[]{:S(2)}, u32[]{:S(2)}) collective-permute-start(bf16[416,768]{1,0:T(8,128)(2,1)} %get-tuple-element.128), channel_id=1, source_target_pairs={{0,16},{8,24},{16,0},{24,8},{1,17},{9,25},{17,1},{25,9},{2,18},{10... | collective-permute-start | bytes 1916936 | tf_op jit(solution)/shard_map/ppermute | solution.py:970
  52.9 22.5 %collective-permute-start.9 = (bf16[320,768]{1,0:T(8,128)(2,1)}, bf16[320,768]{1,0:T(8,128)(2,1)}, u32[]{:S(2)}, u32[]{:S(2)}) collective-permute-start(bf16[320,768]{1,0:T(8,128)(2,1)} %collective-permute-done.1.x_on), channel_id=1, source_target_pairs={{0,16},{8,24},{16,0},{24,8},{1,17},{9,25},{17,1},{25,9},{2,18},{10... | collective-permute-start | bytes 1474568 | tf_op jit(solution)/shard_map/ppermute | solution.py:970
  53.9 21.5 %collective-permute-start.10 = (bf16[320,768]{1,0:T(8,128)(2,1)}, bf16[320,768]{1,0:T(8,128)(2,1)}, u32[]{:S(2)}, u32[]{:S(2)}) collective-permute-start(bf16[320,768]{1,0:T(8,128)(2,1)} %collective-permute-done.2.y_on), channel_id=1, source_target_pairs={{0,8},{8,0},{16,24},{24,16},{1,9},{9,1},{17,25},{25,17},{2,10},{10... | collective-permute-start | bytes 1474568 | tf_op jit(solution)/shard_map/ppermute | solution.py:970
  75.5 13.6 %all-to-all-start.1 = ((bf16[4,192,256]{2,1,0:T(8,128)(2,1)}), bf16[4,192,256]{2,1,0:T(8,128)(2,1)S(1)}, u32[]{:S(2)}, u32[]{:S(2)}) async-start(bf16[4,192,256]{2,1,0:T(8,128)(2,1)} %get-tuple-element.129), calls=%async_computation.1 | async-start | bytes 786432 | tf_op jit(solution)/shard_map/all_to_all | solution.py:1058
  80.2 95.3 %reduce-scatter.2.cloned.1.call-start = ((), (), s32[]{:S(2)}) async-start(), calls=%async_computation.4 | async-start | bytes 2654208 | tf_op jit(solution)/shard_map/reduce_scatter | solution.py:1070
  92.9 9.1 %collective-permute-start.12 = (bf16[256,768]{1,0:T(8,128)(2,1)}, bf16[256,768]{1,0:T(8,128)(2,1)S(1)}, u32[]{:S(2)}, u32[]{:S(2)}) collective-permute-start(bf16[256,768]{1,0:T(8,128)(2,1)} %get-tuple-element.139.n_ref.n0), channel_id=1, source_target_pairs={{0,16},{8,24},{16,0},{24,8},{1,17},{9,25},{17,1},{25,9},{2,18},{10... | collective-permute-start | bytes 1179656 | tf_op jit(solution)/shard_map/ppermute | solution.py:970
  93.0 10.1 %collective-permute-start.11 = (bf16[256,768]{1,0:T(8,128)(2,1)}, bf16[256,768]{1,0:T(8,128)(2,1)S(1)}, u32[]{:S(2)}, u32[]{:S(2)}) collective-permute-start(bf16[256,768]{1,0:T(8,128)(2,1)} %get-tuple-element.139.n_ref.n0), channel_id=1, source_target_pairs={{0,8},{8,0},{16,24},{24,16},{1,9},{9,1},{17,25},{25,17},{2,10},{10... | collective-permute-start | bytes 1179656 | tf_op jit(solution)/shard_map/ppermute | solution.py:970
  103.1 7.6 %collective-permute-start.13 = (bf16[128,768]{1,0:T(8,128)(2,1)S(1)}, bf16[128,768]{1,0:T(8,128)(2,1)S(1)}, u32[]{:S(2)}, u32[]{:S(2)}) collective-permute-start(bf16[128,768]{1,0:T(8,128)(2,1)S(1)} %slice.136), channel_id=1, source_target_pairs={{0,16},{8,24},{16,0},{24,8},{1,17},{9,25},{17,1},{25,9},{2,18},{10... | collective-permute-start | bytes 589832 | tf_op jit(solution)/shard_map/ppermute | solution.py:970
  103.9 6.9 %collective-permute-start.14 = (bf16[128,768]{1,0:T(8,128)(2,1)S(1)}, bf16[128,768]{1,0:T(8,128)(2,1)S(1)}, u32[]{:S(2)}, u32[]{:S(2)}) collective-permute-start(bf16[128,768]{1,0:T(8,128)(2,1)S(1)} %slice.137), channel_id=1, source_target_pairs={{0,8},{8,0},{16,24},{24,16},{1,9},{9,1},{17,25},{25,17},{2,10},{10... | collective-permute-start | bytes 589832 | tf_op jit(solution)/shard_map/ppermute | solution.py:970
  117.0 10.3 %collective-permute-start.15 = (bf16[2,128,768]{2,1,0:T(8,128)(2,1)}, bf16[2,128,768]{2,1,0:T(8,128)(2,1)S(1)}, u32[]{:S(2)}, u32[]{:S(2)}) collective-permute-start(bf16[2,128,768]{2,1,0:T(8,128)(2,1)} %get-tuple-element.153), channel_id=1, source_target_pairs={{0,8},{8,0},{16,24},{24,16},{1,9},{9,1},{17,25},{25,17},{2,10},{10... | collective-permute-start | bytes 1179656 | tf_op jit(solution)/shard_map/ppermute | solution.py:970
  118.4 9.0 %collective-permute-start.16 = (bf16[2,128,768]{2,1,0:T(8,128)(2,1)}, bf16[2,128,768]{2,1,0:T(8,128)(2,1)S(1)}, u32[]{:S(2)}, u32[]{:S(2)}) collective-permute-start(bf16[2,128,768]{2,1,0:T(8,128)(2,1)} %get-tuple-element.154), channel_id=1, source_target_pairs={{0,16},{8,24},{16,0},{24,8},{1,17},{9,25},{17,1},{25,9},{2,18},{10... | collective-permute-start | bytes 1179656 | tf_op jit(solution)/shard_map/ppermute | solution.py:970
  128.4 5.7 %collective-permute-start.18 = (bf16[128,768]{1,0:T(8,128)(2,1)S(1)}, bf16[128,768]{1,0:T(8,128)(2,1)S(1)}, u32[]{:S(2)}, u32[]{:S(2)}) collective-permute-start(bf16[128,768]{1,0:T(8,128)(2,1)S(1)} %bitcast_add_fusion.2), channel_id=1, source_target_pairs={{0,8},{8,0},{16,24},{24,16},{1,9},{9,1},{17,25},{25,17},{2,10},{10... | collective-permute-start | bytes 589832 | tf_op jit(solution)/shard_map/ppermute | solution.py:970
  129.2 5.7 %collective-permute-start.17 = (bf16[128,768]{1,0:T(8,128)(2,1)S(1)}, bf16[128,768]{1,0:T(8,128)(2,1)S(1)}, u32[]{:S(2)}, u32[]{:S(2)}) collective-permute-start(bf16[128,768]{1,0:T(8,128)(2,1)S(1)} %bitcast_add_fusion.3), channel_id=1, source_target_pairs={{0,16},{8,24},{16,0},{24,8},{1,17},{9,25},{17,1},{25,9},{2,18},{10... | collective-permute-start | bytes 589832 | tf_op jit(solution)/shard_map/ppermute | solution.py:970
  139.9 17.8 %all-to-all-start.2 = ((bf16[4,192,256]{2,1,0:T(8,128)(2,1)}), bf16[4,192,256]{2,1,0:T(8,128)(2,1)S(1)}, u32[]{:S(2)}, u32[]{:S(2)}) async-start(bf16[4,192,256]{2,1,0:T(8,128)(2,1)} %get-tuple-element.159), calls=%async_computation.2 | async-start | bytes 786432 | tf_op jit(solution)/shard_map/all_to_all | solution.py:1075
  143.6 31.9 %collective-permute-start.19 = (bf16[2,128,768]{2,1,0:T(8,128)(2,1)S(1)}, bf16[2,128,768]{2,1,0:T(8,128)(2,1)S(1)}, u32[]{:S(2)}, u32[]{:S(2)}) collective-permute-start(bf16[2,128,768]{2,1,0:T(8,128)(2,1)S(1)} %copy-done.45), channel_id=1, source_target_pairs={{0,8},{8,0},{16,24},{24,16},{1,9},{9,1},{17,25},{25,17},{2,10},{10... | collective-permute-start | bytes 1179656 | tf_op jit(solution)/shard_map/ppermute | solution.py:970
  145.0 30.5 %collective-permute-start.20 = (bf16[2,128,768]{2,1,0:T(8,128)(2,1)S(1)}, bf16[2,128,768]{2,1,0:T(8,128)(2,1)S(1)}, u32[]{:S(2)}, u32[]{:S(2)}) collective-permute-start(bf16[2,128,768]{2,1,0:T(8,128)(2,1)S(1)} %copy-done.44), channel_id=1, source_target_pairs={{0,16},{8,24},{16,0},{24,8},{1,17},{9,25},{17,1},{25,9},{2,18},{10... | collective-permute-start | bytes 1179656 | tf_op jit(solution)/shard_map/ppermute | solution.py:970
  175.5 39.8 %copy-start.12 = (bf16[2,128,768]{2,1,0:T(8,128)(2,1)}, bf16[2,128,768]{2,1,0:T(8,128)(2,1)S(1)}, u32[]{:S(2)}) copy-start(bf16[2,128,768]{2,1,0:T(8,128)(2,1)S(1)} %collective-permute-done.19.a_ref) | copy-start | bytes 1179652
  175.5 39.8 %copy-start.13 = (bf16[2,128,768]{2,1,0:T(8,128)(2,1)}, bf16[2,128,768]{2,1,0:T(8,128)(2,1)S(1)}, u32[]{:S(2)}) copy-start(bf16[2,128,768]{2,1,0:T(8,128)(2,1)S(1)} %collective-permute-done.20.b_ref) | copy-start | bytes 1179652
  175.6 7.6 %collective-permute-start.26 = (bf16[2,2,352,384]{3,2,1,0:T(8,128)(2,1)}, bf16[2,2,352,384]{3,2,1,0:T(8,128)(2,1)S(1)}, u32[]{:S(2)}, u32[]{:S(2)}) collective-permute-start(bf16[2,2,352,384]{3,2,1,0:T(8,128)(2,1)} %get-tuple-element.184), channel_id=1, source_target_pairs={{0,1},{1,0},{2,3},{3,2},{4,5},{5,4},{6,7},{7,6},{8,9},{9,8},{10,11... | collective-permute-start | bytes 3244040 | tf_op jit(solution)/shard_map/ppermute | solution.py:974
  176.6 5.9 %collective-permute-start.42 = (bf16[48,384]{1,0:T(8,128)(2,1)S(1)}, bf16[48,384]{1,0:T(8,128)(2,1)S(1)}, u32[]{:S(2)}, u32[]{:S(2)}) collective-permute-start(bf16[48,384]{1,0:T(8,128)(2,1)S(1)} %get-tuple-element.224), channel_id=1, source_target_pairs={{0,8},{8,0},{16,24},{24,16},{1,9},{9,1},{17,25},{25,17},{2,10},{10... | collective-permute-start | bytes 110600 | tf_op jit(solution)/shard_map/ppermute | solution.py:970
  180.3 6.6 %collective-permute-start.44 = (bf16[48,384]{1,0:T(8,128)(2,1)S(1)}, bf16[48,384]{1,0:T(8,128)(2,1)S(1)}, u32[]{:S(2)}, u32[]{:S(2)}) collective-permute-start(bf16[48,384]{1,0:T(8,128)(2,1)S(1)} %get-tuple-element.222), channel_id=1, source_target_pairs={{0,24},{8,16},{16,8},{24,0},{1,25},{9,17},{17,9},{25,1},{2,26},{10... | collective-permute-start | bytes 110600 | tf_op jit(solution)/shard_map/ppermute | solution.py:970
  182.0 4.3 %collective-permute-start.43 = (bf16[48,384]{1,0:T(8,128)(2,1)S(1)}, bf16[48,384]{1,0:T(8,128)(2,1)S(1)}, u32[]{:S(2)}, u32[]{:S(2)}) collective-permute-start(bf16[48,384]{1,0:T(8,128)(2,1)S(1)} %get-tuple-element.223), channel_id=1, source_target_pairs={{0,16},{8,24},{16,0},{24,8},{1,17},{9,25},{17,1},{25,9},{2,18},{10... | collective-permute-start | bytes 110600 | tf_op jit(solution)/shard_map/ppermute | solution.py:970
  184.7 14.1 %collective-permute-start.27 = (bf16[2,352,384]{2,1,0:T(8,128)(2,1)S(1)}, bf16[2,352,384]{2,1,0:T(8,128)(2,1)S(1)}, u32[]{:S(2)}, u32[]{:S(2)}) collective-permute-start(bf16[2,352,384]{2,1,0:T(8,128)(2,1)S(1)} %slice_bitcast_fusion), channel_id=1, source_target_pairs={{0,16},{8,24},{16,0},{24,8},{1,17},{9,25},{17,1},{25,9},{2,18},{10... | collective-permute-start | bytes 1622024 | tf_op jit(solution)/shard_map/ppermute | solution.py:970
  188.2 6.1 %collective-permute-start.46 = (bf16[384,384]{1,0:T(8,128)(2,1)}, bf16[384,384]{1,0:T(8,128)(2,1)}, u32[]{:S(2)}, u32[]{:S(2)}) collective-permute-start(bf16[384,384]{1,0:T(8,128)(2,1)} %constant_dynamic-update-slice_fusion.refs_0_), channel_id=1, source_target_pairs={{2,4},{3,5},{4,2},{5,3},{10,12},{11,13},{12,10},{13,11},{18,20},{1... | collective-permute-start | bytes 884744 | tf_op jit(solution)/shard_map/ppermute | solution.py:978
  189.5 8.6 %collective-permute-start.45 = (bf16[384,384]{1,0:T(8,128)(2,1)}, bf16[384,384]{1,0:T(8,128)(2,1)}, u32[]{:S(2)}, u32[]{:S(2)}) collective-permute-start(bf16[384,384]{1,0:T(8,128)(2,1)} %constant_dynamic-update-slice_fusion.refs_0_), channel_id=1, source_target_pairs={{0,2},{1,3},{2,0},{3,1},{4,6},{5,7},{6,4},{7,5},{8,10},{9,11},{10,... | collective-permute-start | bytes 884744 | tf_op jit(solution)/shard_map/ppermute | solution.py:978
  190.4 14.1 %collective-permute-start.21 = (bf16[256,768]{1,0:T(8,128)(2,1)S(1)}, bf16[256,768]{1,0:T(8,128)(2,1)}, u32[]{:S(2)}, u32[]{:S(2)}) collective-permute-start(bf16[256,768]{1,0:T(8,128)(2,1)S(1)} %copy-done.23), channel_id=1, source_target_pairs={{0,2},{1,3},{6,4},{7,5},{8,10},{9,11},{14,12},{15,13},{16,18},{17,... | collective-permute-start | bytes 1179656 | tf_op jit(solution)/shard_map/ppermute | solution.py:978
  194.2 16.8 %collective-permute-start.47 = (bf16[384,384]{1,0:T(8,128)(2,1)}, bf16[384,384]{1,0:T(8,128)(2,1)S(1)}, u32[]{:S(2)}, u32[]{:S(2)}) collective-permute-start(bf16[384,384]{1,0:T(8,128)(2,1)} %collective-permute-done.46), channel_id=1, source_target_pairs={{2,0},{3,1},{4,6},{5,7},{10,8},{11,9},{12,14},{13,15},{18,16},{19,... | collective-permute-start | bytes 884744 | tf_op jit(solution)/shard_map/ppermute | solution.py:978
  198.2 17.2 %collective-permute-start.48 = (bf16[384,384]{1,0:T(8,128)(2,1)}, bf16[384,384]{1,0:T(8,128)(2,1)S(1)}, u32[]{:S(2)}, u32[]{:S(2)}) collective-permute-start(bf16[384,384]{1,0:T(8,128)(2,1)} %collective-permute-done.45.refs_1_), channel_id=1, source_target_pairs={{2,4},{3,5},{4,2},{5,3},{10,12},{11,13},{12,10},{13,11},{18,20},{1... | collective-permute-start | bytes 884744 | tf_op jit(solution)/shard_map/ppermute | solution.py:978
  198.9 12.2 %collective-permute-start.28 = (bf16[352,384]{1,0:T(8,128)(2,1)S(1)}, bf16[352,384]{1,0:T(8,128)(2,1)S(1)}, u32[]{:S(2)}, u32[]{:S(2)}) collective-permute-start(bf16[352,384]{1,0:T(8,128)(2,1)S(1)} %fusion), channel_id=1, source_target_pairs={{0,8},{8,0},{16,24},{24,16},{1,9},{9,1},{17,25},{25,17},{2,10},{10... | collective-permute-start | bytes 811016 | tf_op jit(solution)/shard_map/ppermute | solution.py:970
  205.6 14.3 %collective-permute-start.24 = (bf16[256,768]{1,0:T(8,128)(2,1)S(1)}, bf16[256,768]{1,0:T(8,128)(2,1)S(1)}, u32[]{:S(2)}, u32[]{:S(2)}) collective-permute-start(bf16[256,768]{1,0:T(8,128)(2,1)S(1)} %select_add_fusion.1), channel_id=1, source_target_pairs={{0,2},{1,3},{6,4},{7,5},{8,10},{9,11},{14,12},{15,13},{16,18},{17,... | collective-permute-start | bytes 1179656 | tf_op jit(solution)/shard_map/ppermute | solution.py:978
  210.4 6.6 %collective-permute-start.22 = (bf16[256,768]{1,0:T(8,128)(2,1)S(1)}, bf16[256,768]{1,0:T(8,128)(2,1)S(1)}, u32[]{:S(2)}, u32[]{:S(2)}) collective-permute-start(bf16[256,768]{1,0:T(8,128)(2,1)S(1)} %select_add_fusion.1), channel_id=1, source_target_pairs={{2,4},{3,5},{4,2},{5,3},{10,12},{11,13},{12,10},{13,11},{18,20},{1... | collective-permute-start | bytes 1179656 | tf_op jit(solution)/shard_map/ppermute | solution.py:978
  211.1 26.5 %copy-start.6 = (bf16[384,384]{1,0:T(8,128)(2,1)}, bf16[384,384]{1,0:T(8,128)(2,1)S(1)}, u32[]{:S(2)}) copy-start(bf16[384,384]{1,0:T(8,128)(2,1)S(1)} %broadcast_select_fusion.3.refs_2_) | copy-start | bytes 884740
  211.2 35.0 %copy-start.19 = (bf16[160,384]{1,0:T(8,128)(2,1)}, bf16[160,384]{1,0:T(8,128)(2,1)S(1)}, u32[]{:S(2)}) copy-start(bf16[160,384]{1,0:T(8,128)(2,1)S(1)} %slice.118.refs_0_) | copy-start | bytes 368644
  211.3 20.6 %collective-permute-start.32 = (bf16[352,384]{1,0:T(8,128)(2,1)S(1)}, bf16[352,384]{1,0:T(8,128)(2,1)S(1)}, u32[]{:S(2)}, u32[]{:S(2)}) collective-permute-start(bf16[352,384]{1,0:T(8,128)(2,1)S(1)} %fusion.2), channel_id=1, source_target_pairs={{0,2},{1,3},{2,0},{3,1},{4,6},{5,7},{6,4},{7,5},{8,10},{9,11},{10,... | collective-permute-start | bytes 811016 | tf_op jit(solution)/shard_map/ppermute | solution.py:978
  214.6 6.7 %collective-permute-start.34 = (bf16[160,384]{1,0:T(8,128)(2,1)S(1)}, bf16[160,384]{1,0:T(8,128)(2,1)S(1)}, u32[]{:S(2)}, u32[]{:S(2)}) collective-permute-start(bf16[160,384]{1,0:T(8,128)(2,1)S(1)} %slice.118.refs_0_), channel_id=1, source_target_pairs={{2,4},{3,5},{4,2},{5,3},{10,12},{11,13},{12,10},{13,11},{18,20},{1... | collective-permute-start | bytes 368648 | tf_op jit(solution)/shard_map/ppermute | solution.py:978
  215.4 6.6 %collective-permute-start.30 = (bf16[128,768]{1,0:T(8,128)(2,1)S(1)}, bf16[128,768]{1,0:T(8,128)(2,1)S(1)}, u32[]{:S(2)}, u32[]{:S(2)}) collective-permute-start(bf16[128,768]{1,0:T(8,128)(2,1)S(1)} %bitcast_add_fusion), channel_id=1, source_target_pairs={{0,8},{8,0},{16,24},{24,16},{1,9},{9,1},{17,25},{25,17},{2,10},{10... | collective-permute-start | bytes 589832 | tf_op jit(solution)/shard_map/ppermute | solution.py:970
  217.0 11.0 %collective-permute-start.29 = (bf16[128,768]{1,0:T(8,128)(2,1)S(1)}, bf16[128,768]{1,0:T(8,128)(2,1)S(1)}, u32[]{:S(2)}, u32[]{:S(2)}) collective-permute-start(bf16[128,768]{1,0:T(8,128)(2,1)S(1)} %bitcast_add_fusion.1), channel_id=1, source_target_pairs={{0,16},{8,24},{16,0},{24,8},{1,17},{9,25},{17,1},{25,9},{2,18},{10... | collective-permute-start | bytes 589832 | tf_op jit(solution)/shard_map/ppermute | solution.py:970
  219.9 12.2 %collective-permute-start.49 = (bf16[384,384]{1,0:T(8,128)(2,1)S(1)}, bf16[384,384]{1,0:T(8,128)(2,1)S(1)}, u32[]{:S(2)}, u32[]{:S(2)}) collective-permute-start(bf16[384,384]{1,0:T(8,128)(2,1)S(1)} %collective-permute-done.48), channel_id=1, source_target_pairs={{2,0},{3,1},{4,6},{5,7},{10,8},{11,9},{12,14},{13,15},{18,16},{19,... | collective-permute-start | bytes 884744 | tf_op jit(solution)/shard_map/ppermute | solution.py:978
  221.3 13.2 %collective-permute-start.25 = (bf16[256,768]{1,0:T(8,128)(2,1)S(1)}, bf16[256,768]{1,0:T(8,128)(2,1)S(1)}, u32[]{:S(2)}, u32[]{:S(2)}) collective-permute-start(bf16[256,768]{1,0:T(8,128)(2,1)S(1)} %add.70), channel_id=1, source_target_pairs={{2,4},{3,5},{4,2},{5,3},{10,12},{11,13},{12,10},{13,11},{18,20},{1... | collective-permute-start | bytes 1179656 | tf_op jit(solution)/shard_map/ppermute | solution.py:978
  222.0 15.6 %collective-permute-start.23 = (bf16[256,768]{1,0:T(8,128)(2,1)S(1)}, bf16[256,768]{1,0:T(8,128)(2,1)S(1)}, u32[]{:S(2)}, u32[]{:S(2)}) collective-permute-start(bf16[256,768]{1,0:T(8,128)(2,1)S(1)} %select_add_fusion), channel_id=1, source_target_pairs={{0,2},{1,3},{2,0},{3,1},{4,6},{5,7},{6,4},{7,5},{8,10},{9,11},{10,... | collective-permute-start | bytes 1179656 | tf_op jit(solution)/shard_map/ppermute | solution.py:978
  227.9 11.0 %collective-permute-start.35 = (bf16[160,384]{1,0:T(8,128)(2,1)S(1)}, bf16[160,384]{1,0:T(8,128)(2,1)S(1)}, u32[]{:S(2)}, u32[]{:S(2)}) collective-permute-start(bf16[160,384]{1,0:T(8,128)(2,1)S(1)} %collective-permute-done.34), channel_id=1, source_target_pairs={{2,0},{3,1},{4,6},{5,7},{10,8},{11,9},{12,14},{13,15},{18,16},{19,... | collective-permute-start | bytes 368648 | tf_op jit(solution)/shard_map/ppermute | solution.py:978
  231.9 1.7 collective-permute-start.31
  232.0 14.9 %copy-start.9 = (bf16[160,384]{1,0:T(8,128)(2,1)}, bf16[160,384]{1,0:T(8,128)(2,1)S(1)}, u32[]{:S(2)}) copy-start(bf16[160,384]{1,0:T(8,128)(2,1)S(1)} %slice.140.refs_1_) | copy-start | bytes 368644
  232.0 6.9 %collective-permute-start.33 = (bf16[352,384]{1,0:T(8,128)(2,1)S(1)}, bf16[352,384]{1,0:T(8,128)(2,1)S(1)}, u32[]{:S(2)}, u32[]{:S(2)}) collective-permute-start(bf16[352,384]{1,0:T(8,128)(2,1)S(1)} %pad_maximum_fusion.5), channel_id=1, source_target_pairs={{2,4},{3,5},{4,2},{5,3},{10,12},{11,13},{12,10},{13,11},{18,20},{1... | collective-permute-start | bytes 811016 | tf_op jit(solution)/shard_map/ppermute | solution.py:978
  233.6 7.0 %collective-permute-start.50 = (bf16[384,384]{1,0:T(8,128)(2,1)}, bf16[384,384]{1,0:T(8,128)(2,1)S(1)}, u32[]{:S(2)}, u32[]{:S(2)}) collective-permute-start(bf16[384,384]{1,0:T(8,128)(2,1)} %constant_dynamic-update-slice_fusion.refs_0_), channel_id=1, source_target_pairs={{0,1},{1,0},{2,3},{3,2},{4,5},{5,4},{6,7},{7,6},{8,9},{9,8},{10,11... | collective-permute-start | bytes 884744 | tf_op jit(solution)/shard_map/ppermute | solution.py:974
  234.5 6.1 %collective-permute-start.51 = (bf16[384,384]{1,0:T(8,128)(2,1)}, bf16[384,384]{1,0:T(8,128)(2,1)S(1)}, u32[]{:S(2)}, u32[]{:S(2)}) collective-permute-start(bf16[384,384]{1,0:T(8,128)(2,1)} %collective-permute-done.45.refs_1_), channel_id=1, source_target_pairs={{0,1},{1,0},{2,3},{3,2},{4,5},{5,4},{6,7},{7,6},{8,9},{9,8},{10,11... | collective-permute-start | bytes 884744 | tf_op jit(solution)/shard_map/ppermute | solution.py:974
  237.6 3.0 %collective-permute-start.52 = (bf16[384,384]{1,0:T(8,128)(2,1)S(1)}, bf16[384,384]{1,0:T(8,128)(2,1)S(1)}, u32[]{:S(2)}, u32[]{:S(2)}) collective-permute-start(bf16[384,384]{1,0:T(8,128)(2,1)S(1)} %broadcast_select_fusion.3.refs_2_), channel_id=1, source_target_pairs={{0,1},{1,0},{2,3},{3,2},{4,5},{5,4},{6,7},{7,6},{8,9},{9,8},{10,11... | collective-permute-start | bytes 884744 | tf_op jit(solution)/shard_map/ppermute | solution.py:974
  238.9 1.7 collective-permute-start.53
  239.0 14.2 %collective-permute-start.37 = (bf16[352,384]{1,0:T(8,128)(2,1)S(1)}, bf16[352,384]{1,0:T(8,128)(2,1)S(1)}, u32[]{:S(2)}, u32[]{:S(2)}) collective-permute-start(bf16[352,384]{1,0:T(8,128)(2,1)S(1)} %pad_maximum_fusion.6), channel_id=1, source_target_pairs={{2,0},{3,1},{4,6},{5,7},{10,8},{11,9},{12,14},{13,15},{18,16},{19,... | collective-permute-start | bytes 811016 | tf_op jit(solution)/shard_map/ppermute | solution.py:978
  246.3 11.3 %collective-permute-start.38 = (bf16[160,384]{1,0:T(8,128)(2,1)S(1)}, bf16[160,384]{1,0:T(8,128)(2,1)S(1)}, u32[]{:S(2)}, u32[]{:S(2)}) collective-permute-start(bf16[160,384]{1,0:T(8,128)(2,1)S(1)} %slice.118.refs_0_), channel_id=1, source_target_pairs={{0,1},{1,0},{2,3},{3,2},{4,5},{5,4},{6,7},{7,6},{8,9},{9,8},{10,11... | collective-permute-start | bytes 368648 | tf_op jit(solution)/shard_map/ppermute | solution.py:974
  246.9 10.7 %collective-permute-start.39 = (bf16[160,384]{1,0:T(8,128)(2,1)S(1)}, bf16[160,384]{1,0:T(8,128)(2,1)S(1)}, u32[]{:S(2)}, u32[]{:S(2)}) collective-permute-start(bf16[160,384]{1,0:T(8,128)(2,1)S(1)} %slice.140.refs_1_), channel_id=1, source_target_pairs={{0,1},{1,0},{2,3},{3,2},{4,5},{5,4},{6,7},{7,6},{8,9},{9,8},{10,11... | collective-permute-start | bytes 368648 | tf_op jit(solution)/shard_map/ppermute | solution.py:974
  250.1 5.1 %collective-permute-start.36 = (f32[128,768]{1,0:T(8,128)}, f32[128,768]{1,0:T(8,128)S(1)}, u32[]{:S(2)}, u32[]{:S(2)}) collective-permute-start(f32[128,768]{1,0:T(8,128)} %get-tuple-element.202), channel_id=1, source_target_pairs={{0,1},{1,0},{2,3},{3,2},{4,5},{5,4},{6,7},{7,6},{8,9},{9,8},{10,11... | collective-permute-start | bytes 1179656 | tf_op jit(solution)/shard_map/ppermute | solution.py:974
  253.2 3.0 %collective-permute-start.41 = (bf16[352,384]{1,0:T(8,128)(2,1)S(1)}, bf16[352,384]{1,0:T(8,128)(2,1)S(1)}, u32[]{:S(2)}, u32[]{:S(2)}) collective-permute-start(bf16[352,384]{1,0:T(8,128)(2,1)S(1)} %broadcast_select_fusion.4), channel_id=1, source_target_pairs={{0,1},{1,0},{2,3},{3,2},{4,5},{5,4},{6,7},{7,6},{8,9},{9,8},{10,11... | collective-permute-start | bytes 811016 | tf_op jit(solution)/shard_map/ppermute | solution.py:974
  253.4 4.2 %collective-permute-start.40 = (bf16[160,384]{1,0:T(8,128)(2,1)S(1)}, bf16[160,384]{1,0:T(8,128)(2,1)S(1)}, u32[]{:S(2)}, u32[]{:S(2)}) collective-permute-start(bf16[160,384]{1,0:T(8,128)(2,1)S(1)} %broadcast_select_fusion.5.refs_2_), channel_id=1, source_target_pairs={{0,1},{1,0},{2,3},{3,2},{4,5},{5,4},{6,7},{7,6},{8,9},{9,8},{10,11... | collective-permute-start | bytes 368648 | tf_op jit(solution)/shard_map/ppermute | solution.py:974
  (42 other events, 163.6 us)
Sparse Core Ops, SparseCore 0:
  127.5 39.0 reduce-scatter.1

commit v5 on v4

--- a/solution.py
+++ b/solution.py
@@ -1050,11 +1050,10 @@
     x_on, y_on, w_heads = tied(x_on, y_on, jnp.concatenate([w_heads, gains]))
     heads = gather_plane(w_heads)
     corner_a, corner_b = across_w(x_on, 2), across_w(y_on, 1)
-    x_rest, y_rest, *heads = tied(x_rest, y_rest, *heads)
+    x_rest, y_rest, corner_a, corner_b = tied(x_rest, y_rest, corner_a, corner_b)
     x_rest, y_rest = across_w(x_rest, 1), across_w(y_rest, 2)
     normed_all, kv, mixt, att, att_low, lse, w_full, gains = attend(x_all, heads)
     shared = x_on, x_rest, y_on, y_rest, corner_a, corner_b
-    att_low, *shared = tied(att_low, *shared)
     att_home = lax.all_to_all(att_low, "ctx", 0, 0, tiled=True, axis_index_groups=Z_GROUPS).reshape(D, -1)
     wout_full, up, cots = assemble(cot, w_out, w_up, shared)
     hidden, normed_two = project(att_home, x_block, gains, wout_full)

time: 272 us -> 273 us (level)
    unnamed x101 -> x105, local copies, waits for them, and re-layouts: 12.1 us -> 13.4 us
  transfers between devices with their start and end apart: 58 -> 58, of which waited for: 21 -> 22; matrix products, arithmetic and copies ran while one was open for 7% -> 7% of each run, Pallas kernels for 27% -> 26%
where the time goes in v5:
time: 273 us; the launch traced here: 271 us
  Pallas kernels  83.8 us (31%)
  starting transfers between devices  74.5 us (27%)
  waiting for transfers between devices  66.8 us (24%)
  local copies, waits for them, and re-layouts  25.1 us (9%)
  between operations  15 us (5%)
  other arithmetic  5.95 us (2%)
    pallas_call x14, Pallas kernels, call(): pl.pallas_call(kernel, in_specs=ins, out_specs=out_specs or [WHOLE] * len...  66.7 us
    ppermute x27, waiting for transfers between devices, across_w(): return lax.ppermute(value, 'wshard', [(i, i ^ flip) for i in range(4)])  34.1 us
    ppermute x15, starting transfers between devices, between_z(): lax.ppermute(value, 'ctx', [(2 * a + c, 2 * b + c) for a, b in pairs for...  28.9 us
    ppermute x27, starting transfers between devices, across_w(): return lax.ppermute(value, 'wshard', [(i, i ^ flip) for i in range(4)])  28 us
    ppermute x15, waiting for transfers between devices, between_z(): lax.ppermute(value, 'ctx', [(2 * a + c, 2 * b + c) for a, b in pairs for...  17.3 us
    pallas_call x1, Pallas kernels, attend_back(): pl.pallas_call(attend_back_kernel, in_specs=[WHOLE] * 5 + [ANYWHERE] * 2...  17.1 us
    unnamed x105, local copies, waits for them, and re-layouts  13.4 us
    all_to_all x1, waiting for transfers between devices, local_grid(): lax.all_to_all(d_att, 'ctx', 0, 0, tiled=True, axis_index_groups=Z_GROUPS)  9.33 us
  transfers between devices with their start and end apart: 58, of which 22 were waited for; matrix products, arithmetic and copies ran while one was open for 7% of the time, Pallas kernels for 26%

profile of v5, /device:TPU:0, one launch (start us, length us, event | category | flops | bytes accessed | tf_op | source)
XLA Modules:
  0.0 271.0 jit_solution(8861859938433736451)
XLA Ops:
  7.2 1.3 dynamic-slice_bitcast_fusion.2
  9.0 1.3 collective-permute-done
  10.6 1.3 broadcast_in_dim.10
  11.9 6.2 %all-to-all-start = ((bf16[4,256,768]{2,1,0:T(8,128)(2,1)}), bf16[4,256,768]{2,1,0:T(8,128)(2,1)S(1)}, u32[]{:S(2)}, u32[]{:S(2)}) async-start(bf16[4,256,768]{2,1,0:T(8,128)(2,1)} %broadcast_in_dim.10), calls=%async_computation | async-start | bytes 3145728 | tf_op jit(solution)/shard_map/all_to_all | solution.py:1045
  18.9 3.0 %parcels.1 = (bf16[320,768]{1,0:T(8,128)(2,1)}, bf16[416,768]{1,0:T(8,128)(2,1)}, bf16[320,768]{1,0:T(8,128)(2,1)}, bf16[416,768]{1,0:T(8,128)(2,1)}) custom-call(bf16[256,768]{1,0:T(8,128)(2,1)} %pad_maximum_fusion.3.cot_ref, bf16[192,768]{1,0:T(8,128)(2,1)} %own_ref.1, bf16[192,3072]{1,0:T(8,128)(2,1)} %wup_ref.3), custom_call_target="tpu_custom_call" | custom-call | flops 1000 | bytes 1000 | tf_op jit(solution)/shard_map/parcels/pallas_call | solution.py:303
  22.0 1.6 collective-permute-start.1
  23.5 1.5 collective-permute-start.2
  25.1 2.9 %reshape.155 = bf16[192,3,4,192]{3,2,1,0:T(4,128)(2,1)S(1)} reshape(bf16[192,2304]{1,0:T(8,128)(2,1)} %param.10) | data formatting | bytes 1769472 | tf_op jit(solution)/shard_map/reshape | solution.py:1043
  29.7 5.6 %collective-permute-done.1.x_on = bf16[320,768]{1,0:T(8,128)(2,1)} collective-permute-done((bf16[320,768]{1,0:T(8,128)(2,1)}, bf16[320,768]{1,0:T(8,128)(2,1)}, u32[]{:S(2)}, u32[]{:S(2)}) %collective-permute-start.1) | collective-permute-done | bytes 491552 | tf_op jit(solution)/shard_map/ppermute | solution.py:970
  35.3 1.2 collective-permute-done.2.y_on
  36.5 1.5 collective-permute-start.7
  39.1 1.5 collective-permute-start.3
  40.6 14.1 %collective-permute-done.4.w2 = bf16[224,576]{1,0:T(8,128)(2,1)S(1)} collective-permute-done((bf16[224,576]{1,0:T(8,128)(2,1)S(1)}, bf16[224,576]{1,0:T(8,128)(2,1)S(1)}, u32[]{:S(2)}, u32[]{:S(2)}) %collective-permute-start.4) | collective-permute-done | bytes 258080 | tf_op jit(solution)/shard_map/ppermute | solution.py:970
  55.4 1.3 collective-permute-done.3.w1
  57.0 1.5 collective-permute-start.9
  59.4 2.1 collective-permute-done.6.w4
  61.5 2.0 collective-permute-done.5.w3
  64.1 1.1 copy-done
  65.3 12.4 %attend.1 = (bf16[1024,768]{1,0:T(8,128)(2,1)}, bf16[3,1024,128]{2,1,0:T(8,128)(2,1)}, bf16[576,1024]{1,0:T(8,128)(2,1)}, f32[192,1024]{1,0:T(8,128)}, bf16[4,19...) custom-call(bf16[4,256,768]{2,1,0:T(8,128)(2,1)} %copy-done, ...), custom_call_target="tpu_custom_call" | custom-call | flops 1000 | bytes 1000 | tf_op jit(solution)/shard_map/attend/pallas_call | solution.py:303
  77.6 4.8 %all-to-all-start.1 = ((bf16[4,192,256]{2,1,0:T(8,128)(2,1)}), bf16[4,192,256]{2,1,0:T(8,128)(2,1)S(1)}, u32[]{:S(2)}, u32[]{:S(2)}) async-start(bf16[4,192,256]{2,1,0:T(8,128)(2,1)} %get-tuple-element.107), calls=%async_computation.1 | async-start | bytes 786432 | tf_op jit(solution)/shard_map/all_to_all | solution.py:1057
  83.3 4.1 %assemble.1 = (bf16[768,768]{1,0:T(8,128)(2,1)}, bf16[768,768]{1,0:T(8,128)(2,1)}, bf16[1024,768]{1,0:T(8,128)(2,1)}) custom-call(bf16[256,768]{1,0:T(8,128)(2,1)} %pad_maximum_fusion.3.cot_ref, bf16[192,768]{1,0:T(8,128)(2,1)} %own_ref.1, bf16[192,3072]{1,0:T(8,128)(2,1)} %wup_ref.3, bf16[320,768]{1,0:T(8,128)(2,1)} %collective-permute-done.1.x_on, ...), custom_call_target="tpu_custom_call" | custom-call | flops 1000 | bytes 1000 | tf_op jit(solution)/shard_map/assemble/pallas_call | solution.py:303
  87.4 3.9 %all-to-all-done.1 = bf16[4,192,256]{2,1,0:T(8,128)(2,1)S(1)} async-done(((bf16[4,192,256]{2,1,0:T(8,128)(2,1)}), bf16[4,192,256]{2,1,0:T(8,128)(2,1)S(1)}, u32[]{:S(2)}, u32[]{:S(2)}) %all-to-all-start.1) | async-done | bytes 393248 | tf_op jit(solution)/shard_map/all_to_all | solution.py:1057
  92.1 3.0 %project.1 = (f32[256,768]{1,0:T(8,128)}, bf16[256,768]{1,0:T(8,128)(2,1)}) custom-call(bf16[768,256]{1,0:T(8,128)(2,1)} %bitcast.48, bf16[256,768]{1,0:T(8,128)(2,1)} %copy-done.1, f32[8,768]{1,0:T(8,128)} %get-tuple-element.108.gain_ref, bf16[768,768]{1,0:T(8,128)(2,1)} %get-tuple-element.117.wout_ref), custom_call_target="tpu_custom_call" | custom-call | flops 1000 | bytes 1000 | tf_op jit(solution)/shard_map/project/pallas_call | solution.py:303
  95.2 1.3 collective-permute-start.11
  96.5 4.7 %feed_own.1 = (bf16[256,768]{1,0:T(8,128)(2,1)}, bf16[256,768]{1,0:T(8,128)(2,1)}, f32[256,768]{1,0:T(8,128)}, f32[256,768]{1,0:T(8,128)}) custom-call(bf16[256,768]{1,0:T(8,128)(2,1)} %get-tuple-element.119.n_ref.n0, bf16[1024,768]{1,0:T(8,128)(2,1)} %get-tuple-element.120.cot_ref, bf16[768,768]{1,0:T(8,128)(2,1)} %get-tuple-element.121.up_ref, ...), custom_call_target="tpu_custom_call" | custom-call | flops 1000 | bytes 1000 | tf_op jit(solution)/shard_map/feed_own/pallas_call | solution.py:303
  101.2 2.5 collective-permute-done.12.ny_ref.n2
  105.5 1.4 collective-permute-start.14
  106.9 6.1 %feed_near.1 = (bf16[512,768]{1,0:T(8,128)(2,1)}, bf16[512,768]{1,0:T(8,128)(2,1)}, bf16[512,768]{1,0:T(8,128)(2,1)}, bf16[512,768]{1,0:T(8,128)(2,1)}) custom-call(bf16[256,768]{1,0:T(8,128)(2,1)} %copy-done.4, bf16[256,768]{1,0:T(8,128)(2,1)} %copy-done.3, bf16[1024,768]{1,0:T(8,128)(2,1)} %get-tuple-element.120.cot_ref, ...), custom_call_target="tpu_custom_call" | custom-call | flops 1000 | bytes 1000 | tf_op jit(solution)/shard_map/feed_near/pallas_call | solution.py:303
  113.8 5.6 %feed_far.1 = (bf16[256,768]{1,0:T(8,128)(2,1)}, bf16[256,768]{1,0:T(8,128)(2,1)}, bf16[2,128,768]{2,1,0:T(8,128)(2,1)}, bf16[128,768]{1,0:T(8,128)(2,1)}, bf16[...) custom-call(bf16[128,768]{1,0:T(8,128)(2,1)} %copy-done.14, ...), custom_call_target="tpu_custom_call" | custom-call | flops 1000 | bytes 1000 | tf_op jit(solution)/shard_map/feed_far/pallas_call | solution.py:303
  120.0 1.3 collective-permute-start.16
  121.2 7.6 %feed_grads.1 = bf16[8,8,48,384]{3,2,1,0:T(8,128)(2,1)} custom-call(bf16[256,768]{1,0:T(8,128)(2,1)} %get-tuple-element.119.n_ref.n0, bf16[256,768]{1,0:T(8,128)(2,1)} %copy-done.4, bf16[256,768]{1,0:T(8,128)(2,1)} %copy-done.3, bf16[128,768]{1,0:T(8,128)(2,1)} %copy-done.14, bf16[128,768]{1,0:T(8,128)(2,1)} %copy-done.15, ...), custom_call_target="tpu_custom_call" | custom-call | flops 1000 | bytes 1000 | tf_op jit(solution)/shard_map/feed_grads/pallas_call | solution.py:303
  130.7 1.6 collective-permute-start.17
  132.3 3.4 %collective-permute-done.18.b_more_ref = bf16[128,768]{1,0:T(8,128)(2,1)S(1)} collective-permute-done((bf16[128,768]{1,0:T(8,128)(2,1)S(1)}, bf16[128,768]{1,0:T(8,128)(2,1)S(1)}, u32[]{:S(2)}, u32[]{:S(2)}) %collective-permute-start.18) | collective-permute-done | bytes 196640 | tf_op jit(solution)/shard_map/ppermute | solution.py:970
  137.2 4.3 %turn.1 = (f32[256,768]{1,0:T(8,128)}, bf16[4,192,256]{2,1,0:T(8,128)(2,1)}, bf16[256,768]{1,0:T(8,128)(2,1)}, f32[1,768]{1,0:T(1,128)}) custom-call(f32[256,768]{1,0:T(8,128)} %get-tuple-element.118.hidden_ref, f32[8,768]{1,0:T(8,128)} %get-tuple-element.108.gain_ref, f32[256,768]{1,0:T(8,128)} %get-tuple-element.122.dkeep_ref, ...), custom_call_target="tpu_custom_call" | custom-call | flops 1000 | bytes 1000 | tf_op jit(solution)/shard_map/turn/pallas_call | solution.py:303
  141.5 3.7 %all-to-all-start.2 = ((bf16[4,192,256]{2,1,0:T(8,128)(2,1)}), bf16[4,192,256]{2,1,0:T(8,128)(2,1)S(1)}, u32[]{:S(2)}, u32[]{:S(2)}) async-start(bf16[4,192,256]{2,1,0:T(8,128)(2,1)} %get-tuple-element.139), calls=%async_computation.2 | async-start | bytes 786432 | tf_op jit(solution)/shard_map/all_to_all | solution.py:1074
  145.2 1.4 collective-permute-start.19
  147.3 2.6 out_grad.1
  150.0 9.3 %all-to-all-done.2.dout_ref = bf16[4,192,256]{2,1,0:T(8,128)(2,1)S(1)} async-done(((bf16[4,192,256]{2,1,0:T(8,128)(2,1)}), bf16[4,192,256]{2,1,0:T(8,128)(2,1)S(1)}, u32[]{:S(2)}, u32[]{:S(2)}) %all-to-all-start.2) | async-done | bytes 393248 | tf_op jit(solution)/shard_map/all_to_all | solution.py:1074
  160.0 17.1 %attend_back.1 = (bf16[256,768]{1,0:T(8,128)(2,1)}, bf16[256,768]{1,0:T(8,128)(2,1)}, bf16[256,768]{1,0:T(8,128)(2,1)}, bf16[256,768]{1,0:T(8,128)(2,1)}, bf16[2...) custom-call(bf16[3,1024,128]{2,1,0:T(8,128)(2,1)} %get-tuple-element.1, ...), custom_call_target="tpu_custom_call", output_to_operand_aliasing={{4}: (9, {}), {5}: (10, {})} | custom-call | flops 1000 | bytes 1000 | tf_op jit(solution)/shard_map/attend_back/pallas_call | solution.py:841
  178.2 1.2 collective-permute-start.42
  179.5 1.4 bitcast_dynamic-update-slice_fusion
  181.8 1.6 collective-permute-start.44
  184.8 1.5 add.71
  186.4 1.3 collective-permute-start.27
  189.6 1.4 collective-permute-start.46
  192.1 3.6 %collective-permute-start.21 = (bf16[256,768]{1,0:T(8,128)(2,1)S(1)}, bf16[256,768]{1,0:T(8,128)(2,1)}, u32[]{:S(2)}, u32[]{:S(2)}) collective-permute-start(bf16[256,768]{1,0:T(8,128)(2,1)S(1)} %copy-done.25), channel_id=1, source_target_pairs={{0,2},{1,3},{6,4},{7,5},{8,10},{9,11},{14,12},{15,13},{16,18},{17,... | collective-permute-start | bytes 1179656 | tf_op jit(solution)/shard_map/ppermute | solution.py:978
  195.7 1.3 collective-permute-start.47
  197.0 2.9 %collective-permute-done.45.refs_1_ = bf16[384,384]{1,0:T(8,128)(2,1)} collective-permute-done((bf16[384,384]{1,0:T(8,128)(2,1)}, bf16[384,384]{1,0:T(8,128)(2,1)}, u32[]{:S(2)}, u32[]{:S(2)}) %collective-permute-start.45) | collective-permute-done | bytes 294944 | tf_op jit(solution)/shard_map/ppermute | solution.py:978
  201.4 5.0 %collective-permute-done.21 = bf16[256,768]{1,0:T(8,128)(2,1)} collective-permute-done((bf16[256,768]{1,0:T(8,128)(2,1)S(1)}, bf16[256,768]{1,0:T(8,128)(2,1)}, u32[]{:S(2)}, u32[]{:S(2)}) %collective-permute-start.21) | collective-permute-done | bytes 393248 | tf_op jit(solution)/shard_map/ppermute | solution.py:978
  207.5 4.8 %collective-permute-start.24 = (bf16[256,768]{1,0:T(8,128)(2,1)S(1)}, bf16[256,768]{1,0:T(8,128)(2,1)S(1)}, u32[]{:S(2)}, u32[]{:S(2)}) collective-permute-start(bf16[256,768]{1,0:T(8,128)(2,1)S(1)} %select_add_fusion.1), channel_id=1, source_target_pairs={{0,2},{1,3},{6,4},{7,5},{8,10},{9,11},{14,12},{15,13},{16,18},{17,... | collective-permute-start | bytes 1179656 | tf_op jit(solution)/shard_map/ppermute | solution.py:978
  213.1 3.3 %collective-permute-start.32 = (bf16[352,384]{1,0:T(8,128)(2,1)S(1)}, bf16[352,384]{1,0:T(8,128)(2,1)S(1)}, u32[]{:S(2)}, u32[]{:S(2)}) collective-permute-start(bf16[352,384]{1,0:T(8,128)(2,1)S(1)} %fusion.2), channel_id=1, source_target_pairs={{0,2},{1,3},{2,0},{3,1},{4,6},{5,7},{6,4},{7,5},{8,10},{9,11},{10,... | collective-permute-start | bytes 811016 | tf_op jit(solution)/shard_map/ppermute | solution.py:978
  217.7 1.3 collective-permute-start.29
  219.1 2.7 collective-permute-done.24
  221.8 1.3 collective-permute-start.49
  223.9 5.9 %collective-permute-start.23 = (bf16[256,768]{1,0:T(8,128)(2,1)S(1)}, bf16[256,768]{1,0:T(8,128)(2,1)S(1)}, u32[]{:S(2)}, u32[]{:S(2)}) collective-permute-start(bf16[256,768]{1,0:T(8,128)(2,1)S(1)} %select_add_fusion), channel_id=1, source_target_pairs={{0,2},{1,3},{2,0},{3,1},{4,6},{5,7},{6,4},{7,5},{8,10},{9,11},{10,... | collective-permute-start | bytes 1179656 | tf_op jit(solution)/shard_map/ppermute | solution.py:978
  229.8 1.3 collective-permute-start.35
  231.1 2.6 give.1
  236.8 2.7 collective-permute-done.23.pair_ref
  239.5 1.3 collective-permute-done.35
  240.9 1.6 collective-permute-start.37
  244.1 4.1 %finish_feed.1 = (f32[192,3072]{1,0:T(8,128)}, f32[768,768]{1,0:T(8,128)}) custom-call(bf16[384,384]{1,0:T(8,128)(2,1)} %constant_dynamic-update-slice_fusion.refs_0_, bf16[384,384]{1,0:T(8,128)(2,1)} %collective-permute-done.45.refs_1_, bf16[384,384]{1,0:T(8,128)(2,1)} %copy-done.6, bf16[384,384]{1,0:T(8,128)(2,1)} %copy-done.7, ...), custom_call_target="tpu_custom_call" | custom-call | flops 1000 | bytes 1000 | tf_op jit(solution)/shard_map/finish_feed/pallas_call | solution.py:303
  248.9 3.1 %last.1 = (f32[128,768]{1,0:T(8,128)}, f32[128,768]{1,0:T(8,128)}) custom-call(bf16[256,768]{1,0:T(8,128)(2,1)} %get-tuple-element.177.first_ref, bf16[256,768]{1,0:T(8,128)(2,1)} %copy-done.24, bf16[256,768]{1,0:T(8,128)(2,1)} %copy-done.23, bf16[256,768]{1,0:T(8,128)(2,1)} %copy-done.1, f32[8,768]{1,0:T(8,128)} %get-tuple-element.108.gain_ref, ...), custom_call_target="tpu_custom_call" | custom-call | flops 1000 | bytes 1000 | tf_op jit(solution)/shard_map/last/pallas_call | solution.py:303
  252.5 2.6 collective-permute-done.37
  260.8 3.4 %finish_heads.1 = (f32[192,768]{1,0:T(8,128)}, f32[192,2304]{1,0:T(8,128)}, f32[192]{0:T(256)}, f32[192]{0:T(256)}) custom-call(bf16[160,384]{1,0:T(8,128)(2,1)} %copy-done.21, bf16[160,384]{1,0:T(8,128)(2,1)} %copy-done.9, bf16[160,384]{1,0:T(8,128)(2,1)} %copy-done.22, bf16[160,384]{1,0:T(8,128)(2,1)} %slice.142.refs_3_, bf16[160,384]{1,0:T(8,128)(2,1)} %copy-done.43, ...), custom_call_target="tpu_custom_call" | custom-call | flops 1000 | bytes 1000 | tf_op jit(solution)/shard_map/finish_heads/pallas_call | solution.py:303
  (223 shorter events, 39.8 us)
Async XLA Ops:
  8.5 1.9 collective-permute-start
  11.9 51.6 %all-to-all-start = ((bf16[4,256,768]{2,1,0:T(8,128)(2,1)}), bf16[4,256,768]{2,1,0:T(8,128)(2,1)S(1)}, u32[]{:S(2)}, u32[]{:S(2)}) async-start(bf16[4,256,768]{2,1,0:T(8,128)(2,1)} %broadcast_in_dim.10), calls=%async_computation | async-start | bytes 3145728 | tf_op jit(solution)/shard_map/all_to_all | solution.py:1045
  22.0 13.4 %collective-permute-start.1 = (bf16[320,768]{1,0:T(8,128)(2,1)}, bf16[320,768]{1,0:T(8,128)(2,1)}, u32[]{:S(2)}, u32[]{:S(2)}) collective-permute-start(bf16[320,768]{1,0:T(8,128)(2,1)} %get-tuple-element.100), channel_id=1, source_target_pairs={{0,8},{8,0},{16,24},{24,16},{1,9},{9,1},{17,25},{25,17},{2,10},{10... | collective-permute-start | bytes 1474568 | tf_op jit(solution)/shard_map/ppermute | solution.py:970
  23.5 13.0 %collective-permute-start.2 = (bf16[320,768]{1,0:T(8,128)(2,1)}, bf16[320,768]{1,0:T(8,128)(2,1)}, u32[]{:S(2)}, u32[]{:S(2)}) collective-permute-start(bf16[320,768]{1,0:T(8,128)(2,1)} %get-tuple-element.101), channel_id=1, source_target_pairs={{0,16},{8,24},{16,0},{24,8},{1,17},{9,25},{17,1},{25,9},{2,18},{10... | collective-permute-start | bytes 1474568 | tf_op jit(solution)/shard_map/ppermute | solution.py:970
  29.7 33.8 %copy-start.8 = (bf16[224,576]{1,0:T(8,128)(2,1)}, bf16[224,576]{1,0:T(8,128)(2,1)S(1)}, u32[]{:S(2)}) copy-start(bf16[224,576]{1,0:T(8,128)(2,1)S(1)} %pad_maximum_fusion.4.w0) | copy-start | bytes 774148
  36.5 20.4 %collective-permute-start.7 = (bf16[320,768]{1,0:T(8,128)(2,1)}, bf16[320,768]{1,0:T(8,128)(2,1)S(1)}, u32[]{:S(2)}, u32[]{:S(2)}) collective-permute-start(bf16[320,768]{1,0:T(8,128)(2,1)} %collective-permute-done.1.x_on), channel_id=1, source_target_pairs={{0,16},{8,24},{16,0},{24,8},{1,17},{9,25},{17,1},{25,9},{2,18},{10... | collective-permute-start | bytes 1474568 | tf_op jit(solution)/shard_map/ppermute | solution.py:970
  38.1 18.9 %collective-permute-start.8 = (bf16[320,768]{1,0:T(8,128)(2,1)}, bf16[320,768]{1,0:T(8,128)(2,1)S(1)}, u32[]{:S(2)}, u32[]{:S(2)}) collective-permute-start(bf16[320,768]{1,0:T(8,128)(2,1)} %collective-permute-done.2.y_on), channel_id=1, source_target_pairs={{0,8},{8,0},{16,24},{24,16},{1,9},{9,1},{17,25},{25,17},{2,10},{10... | collective-permute-start | bytes 1474568 | tf_op jit(solution)/shard_map/ppermute | solution.py:970
  38.6 16.1 %collective-permute-start.4 = (bf16[224,576]{1,0:T(8,128)(2,1)S(1)}, bf16[224,576]{1,0:T(8,128)(2,1)S(1)}, u32[]{:S(2)}, u32[]{:S(2)}) collective-permute-start(bf16[224,576]{1,0:T(8,128)(2,1)S(1)} %pad_maximum_fusion.4.w0), channel_id=1, source_target_pairs={{0,16},{8,24},{16,0},{24,8},{1,17},{9,25},{17,1},{25,9},{2,18},{10... | collective-permute-start | bytes 774152 | tf_op jit(solution)/shard_map/ppermute | solution.py:970
  39.1 17.6 %collective-permute-start.3 = (bf16[224,576]{1,0:T(8,128)(2,1)S(1)}, bf16[224,576]{1,0:T(8,128)(2,1)S(1)}, u32[]{:S(2)}, u32[]{:S(2)}) collective-permute-start(bf16[224,576]{1,0:T(8,128)(2,1)S(1)} %pad_maximum_fusion.4.w0), channel_id=1, source_target_pairs={{0,8},{8,0},{16,24},{24,16},{1,9},{9,1},{17,25},{25,17},{2,10},{10... | collective-permute-start | bytes 774152 | tf_op jit(solution)/shard_map/ppermute | solution.py:970
  54.7 6.8 %collective-permute-start.6 = (bf16[112,576]{1,0:T(8,128)(2,1)S(1)}, bf16[112,576]{1,0:T(8,128)(2,1)S(1)}, u32[]{:S(2)}, u32[]{:S(2)}) collective-permute-start(bf16[112,576]{1,0:T(8,128)(2,1)S(1)} %slice.135), channel_id=1, source_target_pairs={{0,8},{8,0},{16,24},{24,16},{1,9},{9,1},{17,25},{25,17},{2,10},{10... | collective-permute-start | bytes 387080 | tf_op jit(solution)/shard_map/ppermute | solution.py:970
  56.7 6.8 %collective-permute-start.5 = (bf16[112,576]{1,0:T(8,128)(2,1)S(1)}, bf16[112,576]{1,0:T(8,128)(2,1)S(1)}, u32[]{:S(2)}, u32[]{:S(2)}) collective-permute-start(bf16[112,576]{1,0:T(8,128)(2,1)S(1)} %slice.134), channel_id=1, source_target_pairs={{0,16},{8,24},{16,0},{24,8},{1,17},{9,25},{17,1},{25,9},{2,18},{10... | collective-permute-start | bytes 387080 | tf_op jit(solution)/shard_map/ppermute | solution.py:970
  57.0 25.5 %collective-permute-start.9 = (bf16[416,768]{1,0:T(8,128)(2,1)}, bf16[416,768]{1,0:T(8,128)(2,1)S(1)}, u32[]{:S(2)}, u32[]{:S(2)}) collective-permute-start(bf16[416,768]{1,0:T(8,128)(2,1)} %get-tuple-element.113), channel_id=1, source_target_pairs={{0,8},{8,0},{16,24},{24,16},{1,9},{9,1},{17,25},{25,17},{2,10},{10... | collective-permute-start | bytes 1916936 | tf_op jit(solution)/shard_map/ppermute | solution.py:970
  58.5 24.0 %collective-permute-start.10 = (bf16[416,768]{1,0:T(8,128)(2,1)}, bf16[416,768]{1,0:T(8,128)(2,1)}, u32[]{:S(2)}, u32[]{:S(2)}) collective-permute-start(bf16[416,768]{1,0:T(8,128)(2,1)} %get-tuple-element.114), channel_id=1, source_target_pairs={{0,16},{8,24},{16,0},{24,8},{1,17},{9,25},{17,1},{25,9},{2,18},{10... | collective-permute-start | bytes 1916936 | tf_op jit(solution)/shard_map/ppermute | solution.py:970
  77.6 13.7 %all-to-all-start.1 = ((bf16[4,192,256]{2,1,0:T(8,128)(2,1)}), bf16[4,192,256]{2,1,0:T(8,128)(2,1)S(1)}, u32[]{:S(2)}, u32[]{:S(2)}) async-start(bf16[4,192,256]{2,1,0:T(8,128)(2,1)} %get-tuple-element.107), calls=%async_computation.1 | async-start | bytes 786432 | tf_op jit(solution)/shard_map/all_to_all | solution.py:1057
  82.5 94.7 %reduce-scatter.2.cloned.1.call-start = ((), (), s32[]{:S(2)}) async-start(), calls=%async_computation.4 | async-start | bytes 2654208 | tf_op jit(solution)/shard_map/reduce_scatter | solution.py:1069
  95.2 8.5 %collective-permute-start.12 = (bf16[256,768]{1,0:T(8,128)(2,1)}, bf16[256,768]{1,0:T(8,128)(2,1)S(1)}, u32[]{:S(2)}, u32[]{:S(2)}) collective-permute-start(bf16[256,768]{1,0:T(8,128)(2,1)} %get-tuple-element.119.n_ref.n0), channel_id=1, source_target_pairs={{0,16},{8,24},{16,0},{24,8},{1,17},{9,25},{17,1},{25,9},{2,18},{10... | collective-permute-start | bytes 1179656 | tf_op jit(solution)/shard_map/ppermute | solution.py:970
  95.2 9.5 %collective-permute-start.11 = (bf16[256,768]{1,0:T(8,128)(2,1)}, bf16[256,768]{1,0:T(8,128)(2,1)S(1)}, u32[]{:S(2)}, u32[]{:S(2)}) collective-permute-start(bf16[256,768]{1,0:T(8,128)(2,1)} %get-tuple-element.119.n_ref.n0), channel_id=1, source_target_pairs={{0,8},{8,0},{16,24},{24,16},{1,9},{9,1},{17,25},{25,17},{2,10},{10... | collective-permute-start | bytes 1179656 | tf_op jit(solution)/shard_map/ppermute | solution.py:970
  104.6 8.4 %collective-permute-start.13 = (bf16[128,768]{1,0:T(8,128)(2,1)S(1)}, bf16[128,768]{1,0:T(8,128)(2,1)S(1)}, u32[]{:S(2)}, u32[]{:S(2)}) collective-permute-start(bf16[128,768]{1,0:T(8,128)(2,1)S(1)} %slice.136), channel_id=1, source_target_pairs={{0,16},{8,24},{16,0},{24,8},{1,17},{9,25},{17,1},{25,9},{2,18},{10... | collective-permute-start | bytes 589832 | tf_op jit(solution)/shard_map/ppermute | solution.py:970
  105.5 7.6 %collective-permute-start.14 = (bf16[128,768]{1,0:T(8,128)(2,1)S(1)}, bf16[128,768]{1,0:T(8,128)(2,1)S(1)}, u32[]{:S(2)}, u32[]{:S(2)}) collective-permute-start(bf16[128,768]{1,0:T(8,128)(2,1)S(1)} %slice.137), channel_id=1, source_target_pairs={{0,8},{8,0},{16,24},{24,16},{1,9},{9,1},{17,25},{25,17},{2,10},{10... | collective-permute-start | bytes 589832 | tf_op jit(solution)/shard_map/ppermute | solution.py:970
  119.4 9.5 %collective-permute-start.15 = (bf16[2,128,768]{2,1,0:T(8,128)(2,1)}, bf16[2,128,768]{2,1,0:T(8,128)(2,1)S(1)}, u32[]{:S(2)}, u32[]{:S(2)}) collective-permute-start(bf16[2,128,768]{2,1,0:T(8,128)(2,1)} %get-tuple-element.133), channel_id=1, source_target_pairs={{0,8},{8,0},{16,24},{24,16},{1,9},{9,1},{17,25},{25,17},{2,10},{10... | collective-permute-start | bytes 1179656 | tf_op jit(solution)/shard_map/ppermute | solution.py:970
  120.0 9.2 %collective-permute-start.16 = (bf16[2,128,768]{2,1,0:T(8,128)(2,1)}, bf16[2,128,768]{2,1,0:T(8,128)(2,1)S(1)}, u32[]{:S(2)}, u32[]{:S(2)}) collective-permute-start(bf16[2,128,768]{2,1,0:T(8,128)(2,1)} %get-tuple-element.134), channel_id=1, source_target_pairs={{0,16},{8,24},{16,0},{24,8},{1,17},{9,25},{17,1},{25,9},{2,18},{10... | collective-permute-start | bytes 1179656 | tf_op jit(solution)/shard_map/ppermute | solution.py:970
  130.0 5.7 %collective-permute-start.18 = (bf16[128,768]{1,0:T(8,128)(2,1)S(1)}, bf16[128,768]{1,0:T(8,128)(2,1)S(1)}, u32[]{:S(2)}, u32[]{:S(2)}) collective-permute-start(bf16[128,768]{1,0:T(8,128)(2,1)S(1)} %bitcast_add_fusion.2), channel_id=1, source_target_pairs={{0,8},{8,0},{16,24},{24,16},{1,9},{9,1},{17,25},{25,17},{2,10},{10... | collective-permute-start | bytes 589832 | tf_op jit(solution)/shard_map/ppermute | solution.py:970
  130.7 5.7 %collective-permute-start.17 = (bf16[128,768]{1,0:T(8,128)(2,1)S(1)}, bf16[128,768]{1,0:T(8,128)(2,1)S(1)}, u32[]{:S(2)}, u32[]{:S(2)}) collective-permute-start(bf16[128,768]{1,0:T(8,128)(2,1)S(1)} %bitcast_add_fusion.3), channel_id=1, source_target_pairs={{0,16},{8,24},{16,0},{24,8},{1,17},{9,25},{17,1},{25,9},{2,18},{10... | collective-permute-start | bytes 589832 | tf_op jit(solution)/shard_map/ppermute | solution.py:970
  141.5 17.8 %all-to-all-start.2 = ((bf16[4,192,256]{2,1,0:T(8,128)(2,1)}), bf16[4,192,256]{2,1,0:T(8,128)(2,1)S(1)}, u32[]{:S(2)}, u32[]{:S(2)}) async-start(bf16[4,192,256]{2,1,0:T(8,128)(2,1)} %get-tuple-element.139), calls=%async_computation.2 | async-start | bytes 786432 | tf_op jit(solution)/shard_map/all_to_all | solution.py:1074
  145.2 32.0 %collective-permute-start.19 = (bf16[2,128,768]{2,1,0:T(8,128)(2,1)S(1)}, bf16[2,128,768]{2,1,0:T(8,128)(2,1)S(1)}, u32[]{:S(2)}, u32[]{:S(2)}) collective-permute-start(bf16[2,128,768]{2,1,0:T(8,128)(2,1)S(1)} %copy-done.47), channel_id=1, source_target_pairs={{0,8},{8,0},{16,24},{24,16},{1,9},{9,1},{17,25},{25,17},{2,10},{10... | collective-permute-start | bytes 1179656 | tf_op jit(solution)/shard_map/ppermute | solution.py:970
  146.6 30.6 %collective-permute-start.20 = (bf16[2,128,768]{2,1,0:T(8,128)(2,1)S(1)}, bf16[2,128,768]{2,1,0:T(8,128)(2,1)S(1)}, u32[]{:S(2)}, u32[]{:S(2)}) collective-permute-start(bf16[2,128,768]{2,1,0:T(8,128)(2,1)S(1)} %copy-done.46), channel_id=1, source_target_pairs={{0,16},{8,24},{16,0},{24,8},{1,17},{9,25},{17,1},{25,9},{2,18},{10... | collective-permute-start | bytes 1179656 | tf_op jit(solution)/shard_map/ppermute | solution.py:970
  177.1 40.0 %copy-start.12 = (bf16[2,128,768]{2,1,0:T(8,128)(2,1)}, bf16[2,128,768]{2,1,0:T(8,128)(2,1)S(1)}, u32[]{:S(2)}) copy-start(bf16[2,128,768]{2,1,0:T(8,128)(2,1)S(1)} %collective-permute-done.19.a_ref) | copy-start | bytes 1179652
  177.2 40.0 %copy-start.13 = (bf16[2,128,768]{2,1,0:T(8,128)(2,1)}, bf16[2,128,768]{2,1,0:T(8,128)(2,1)S(1)}, u32[]{:S(2)}) copy-start(bf16[2,128,768]{2,1,0:T(8,128)(2,1)S(1)} %collective-permute-done.20.b_ref) | copy-start | bytes 1179652
  177.2 7.6 %collective-permute-start.26 = (bf16[2,2,352,384]{3,2,1,0:T(8,128)(2,1)}, bf16[2,2,352,384]{3,2,1,0:T(8,128)(2,1)S(1)}, u32[]{:S(2)}, u32[]{:S(2)}) collective-permute-start(bf16[2,2,352,384]{3,2,1,0:T(8,128)(2,1)} %get-tuple-element.164), channel_id=1, source_target_pairs={{0,1},{1,0},{2,3},{3,2},{4,5},{5,4},{6,7},{7,6},{8,9},{9,8},{10,11... | collective-permute-start | bytes 3244040 | tf_op jit(solution)/shard_map/ppermute | solution.py:974
  178.2 5.9 %collective-permute-start.42 = (bf16[48,384]{1,0:T(8,128)(2,1)S(1)}, bf16[48,384]{1,0:T(8,128)(2,1)S(1)}, u32[]{:S(2)}, u32[]{:S(2)}) collective-permute-start(bf16[48,384]{1,0:T(8,128)(2,1)S(1)} %get-tuple-element.204), channel_id=1, source_target_pairs={{0,8},{8,0},{16,24},{24,16},{1,9},{9,1},{17,25},{25,17},{2,10},{10... | collective-permute-start | bytes 110600 | tf_op jit(solution)/shard_map/ppermute | solution.py:970
  181.8 6.5 %collective-permute-start.44 = (bf16[48,384]{1,0:T(8,128)(2,1)S(1)}, bf16[48,384]{1,0:T(8,128)(2,1)S(1)}, u32[]{:S(2)}, u32[]{:S(2)}) collective-permute-start(bf16[48,384]{1,0:T(8,128)(2,1)S(1)} %get-tuple-element.202), channel_id=1, source_target_pairs={{0,24},{8,16},{16,8},{24,0},{1,25},{9,17},{17,9},{25,1},{2,26},{10... | collective-permute-start | bytes 110600 | tf_op jit(solution)/shard_map/ppermute | solution.py:970
  183.4 4.3 %collective-permute-start.43 = (bf16[48,384]{1,0:T(8,128)(2,1)S(1)}, bf16[48,384]{1,0:T(8,128)(2,1)S(1)}, u32[]{:S(2)}, u32[]{:S(2)}) collective-permute-start(bf16[48,384]{1,0:T(8,128)(2,1)S(1)} %get-tuple-element.203), channel_id=1, source_target_pairs={{0,16},{8,24},{16,0},{24,8},{1,17},{9,25},{17,1},{25,9},{2,18},{10... | collective-permute-start | bytes 110600 | tf_op jit(solution)/shard_map/ppermute | solution.py:970
  186.4 14.2 %collective-permute-start.27 = (bf16[2,352,384]{2,1,0:T(8,128)(2,1)S(1)}, bf16[2,352,384]{2,1,0:T(8,128)(2,1)S(1)}, u32[]{:S(2)}, u32[]{:S(2)}) collective-permute-start(bf16[2,352,384]{2,1,0:T(8,128)(2,1)S(1)} %slice_bitcast_fusion), channel_id=1, source_target_pairs={{0,16},{8,24},{16,0},{24,8},{1,17},{9,25},{17,1},{25,9},{2,18},{10... | collective-permute-start | bytes 1622024 | tf_op jit(solution)/shard_map/ppermute | solution.py:970
  189.6 6.1 %collective-permute-start.46 = (bf16[384,384]{1,0:T(8,128)(2,1)}, bf16[384,384]{1,0:T(8,128)(2,1)}, u32[]{:S(2)}, u32[]{:S(2)}) collective-permute-start(bf16[384,384]{1,0:T(8,128)(2,1)} %constant_dynamic-update-slice_fusion.refs_0_), channel_id=1, source_target_pairs={{2,4},{3,5},{4,2},{5,3},{10,12},{11,13},{12,10},{13,11},{18,20},{1... | collective-permute-start | bytes 884744 | tf_op jit(solution)/shard_map/ppermute | solution.py:978
  191.0 8.9 %collective-permute-start.45 = (bf16[384,384]{1,0:T(8,128)(2,1)}, bf16[384,384]{1,0:T(8,128)(2,1)}, u32[]{:S(2)}, u32[]{:S(2)}) collective-permute-start(bf16[384,384]{1,0:T(8,128)(2,1)} %constant_dynamic-update-slice_fusion.refs_0_), channel_id=1, source_target_pairs={{0,2},{1,3},{2,0},{3,1},{4,6},{5,7},{6,4},{7,5},{8,10},{9,11},{10,... | collective-permute-start | bytes 884744 | tf_op jit(solution)/shard_map/ppermute | solution.py:978
  192.1 14.3 %collective-permute-start.21 = (bf16[256,768]{1,0:T(8,128)(2,1)S(1)}, bf16[256,768]{1,0:T(8,128)(2,1)}, u32[]{:S(2)}, u32[]{:S(2)}) collective-permute-start(bf16[256,768]{1,0:T(8,128)(2,1)S(1)} %copy-done.25), channel_id=1, source_target_pairs={{0,2},{1,3},{6,4},{7,5},{8,10},{9,11},{14,12},{15,13},{16,18},{17,... | collective-permute-start | bytes 1179656 | tf_op jit(solution)/shard_map/ppermute | solution.py:978
  195.7 17.3 %collective-permute-start.47 = (bf16[384,384]{1,0:T(8,128)(2,1)}, bf16[384,384]{1,0:T(8,128)(2,1)S(1)}, u32[]{:S(2)}, u32[]{:S(2)}) collective-permute-start(bf16[384,384]{1,0:T(8,128)(2,1)} %collective-permute-done.46), channel_id=1, source_target_pairs={{2,0},{3,1},{4,6},{5,7},{10,8},{11,9},{12,14},{13,15},{18,16},{19,... | collective-permute-start | bytes 884744 | tf_op jit(solution)/shard_map/ppermute | solution.py:978
  199.9 17.4 %collective-permute-start.48 = (bf16[384,384]{1,0:T(8,128)(2,1)}, bf16[384,384]{1,0:T(8,128)(2,1)S(1)}, u32[]{:S(2)}, u32[]{:S(2)}) collective-permute-start(bf16[384,384]{1,0:T(8,128)(2,1)} %collective-permute-done.45.refs_1_), channel_id=1, source_target_pairs={{2,4},{3,5},{4,2},{5,3},{10,12},{11,13},{12,10},{13,11},{18,20},{1... | collective-permute-start | bytes 884744 | tf_op jit(solution)/shard_map/ppermute | solution.py:978
  200.6 12.4 %collective-permute-start.28 = (bf16[352,384]{1,0:T(8,128)(2,1)S(1)}, bf16[352,384]{1,0:T(8,128)(2,1)S(1)}, u32[]{:S(2)}, u32[]{:S(2)}) collective-permute-start(bf16[352,384]{1,0:T(8,128)(2,1)S(1)} %fusion), channel_id=1, source_target_pairs={{0,8},{8,0},{16,24},{24,16},{1,9},{9,1},{17,25},{25,17},{2,10},{10... | collective-permute-start | bytes 811016 | tf_op jit(solution)/shard_map/ppermute | solution.py:970
  207.5 14.3 %collective-permute-start.24 = (bf16[256,768]{1,0:T(8,128)(2,1)S(1)}, bf16[256,768]{1,0:T(8,128)(2,1)S(1)}, u32[]{:S(2)}, u32[]{:S(2)}) collective-permute-start(bf16[256,768]{1,0:T(8,128)(2,1)S(1)} %select_add_fusion.1), channel_id=1, source_target_pairs={{0,2},{1,3},{6,4},{7,5},{8,10},{9,11},{14,12},{15,13},{16,18},{17,... | collective-permute-start | bytes 1179656 | tf_op jit(solution)/shard_map/ppermute | solution.py:978
  212.2 5.5 %collective-permute-start.22 = (bf16[256,768]{1,0:T(8,128)(2,1)S(1)}, bf16[256,768]{1,0:T(8,128)(2,1)S(1)}, u32[]{:S(2)}, u32[]{:S(2)}) collective-permute-start(bf16[256,768]{1,0:T(8,128)(2,1)S(1)} %select_add_fusion.1), channel_id=1, source_target_pairs={{2,4},{3,5},{4,2},{5,3},{10,12},{11,13},{12,10},{13,11},{18,20},{1... | collective-permute-start | bytes 1179656 | tf_op jit(solution)/shard_map/ppermute | solution.py:978
  213.0 26.5 %copy-start.6 = (bf16[384,384]{1,0:T(8,128)(2,1)}, bf16[384,384]{1,0:T(8,128)(2,1)S(1)}, u32[]{:S(2)}) copy-start(bf16[384,384]{1,0:T(8,128)(2,1)S(1)} %broadcast_select_fusion.3.refs_2_) | copy-start | bytes 884740
  213.1 35.1 %copy-start.21 = (bf16[160,384]{1,0:T(8,128)(2,1)}, bf16[160,384]{1,0:T(8,128)(2,1)S(1)}, u32[]{:S(2)}) copy-start(bf16[160,384]{1,0:T(8,128)(2,1)S(1)} %slice.118.refs_0_) | copy-start | bytes 368644
  213.1 20.6 %collective-permute-start.32 = (bf16[352,384]{1,0:T(8,128)(2,1)S(1)}, bf16[352,384]{1,0:T(8,128)(2,1)S(1)}, u32[]{:S(2)}, u32[]{:S(2)}) collective-permute-start(bf16[352,384]{1,0:T(8,128)(2,1)S(1)} %fusion.2), channel_id=1, source_target_pairs={{0,2},{1,3},{2,0},{3,1},{4,6},{5,7},{6,4},{7,5},{8,10},{9,11},{10,... | collective-permute-start | bytes 811016 | tf_op jit(solution)/shard_map/ppermute | solution.py:978
  216.5 6.7 %collective-permute-start.34 = (bf16[160,384]{1,0:T(8,128)(2,1)S(1)}, bf16[160,384]{1,0:T(8,128)(2,1)S(1)}, u32[]{:S(2)}, u32[]{:S(2)}) collective-permute-start(bf16[160,384]{1,0:T(8,128)(2,1)S(1)} %slice.118.refs_0_), channel_id=1, source_target_pairs={{2,4},{3,5},{4,2},{5,3},{10,12},{11,13},{12,10},{13,11},{18,20},{1... | collective-permute-start | bytes 368648 | tf_op jit(solution)/shard_map/ppermute | solution.py:978
  217.3 6.6 %collective-permute-start.30 = (bf16[128,768]{1,0:T(8,128)(2,1)S(1)}, bf16[128,768]{1,0:T(8,128)(2,1)S(1)}, u32[]{:S(2)}, u32[]{:S(2)}) collective-permute-start(bf16[128,768]{1,0:T(8,128)(2,1)S(1)} %bitcast_add_fusion), channel_id=1, source_target_pairs={{0,8},{8,0},{16,24},{24,16},{1,9},{9,1},{17,25},{25,17},{2,10},{10... | collective-permute-start | bytes 589832 | tf_op jit(solution)/shard_map/ppermute | solution.py:970
  217.7 12.1 %collective-permute-start.29 = (bf16[128,768]{1,0:T(8,128)(2,1)S(1)}, bf16[128,768]{1,0:T(8,128)(2,1)S(1)}, u32[]{:S(2)}, u32[]{:S(2)}) collective-permute-start(bf16[128,768]{1,0:T(8,128)(2,1)S(1)} %bitcast_add_fusion.1), channel_id=1, source_target_pairs={{0,16},{8,24},{16,0},{24,8},{1,17},{9,25},{17,1},{25,9},{2,18},{10... | collective-permute-start | bytes 589832 | tf_op jit(solution)/shard_map/ppermute | solution.py:970
  221.8 12.3 %collective-permute-start.49 = (bf16[384,384]{1,0:T(8,128)(2,1)S(1)}, bf16[384,384]{1,0:T(8,128)(2,1)S(1)}, u32[]{:S(2)}, u32[]{:S(2)}) collective-permute-start(bf16[384,384]{1,0:T(8,128)(2,1)S(1)} %collective-permute-done.48), channel_id=1, source_target_pairs={{2,0},{3,1},{4,6},{5,7},{10,8},{11,9},{12,14},{13,15},{18,16},{19,... | collective-permute-start | bytes 884744 | tf_op jit(solution)/shard_map/ppermute | solution.py:978
  223.2 13.2 %collective-permute-start.25 = (bf16[256,768]{1,0:T(8,128)(2,1)S(1)}, bf16[256,768]{1,0:T(8,128)(2,1)S(1)}, u32[]{:S(2)}, u32[]{:S(2)}) collective-permute-start(bf16[256,768]{1,0:T(8,128)(2,1)S(1)} %add.70), channel_id=1, source_target_pairs={{2,4},{3,5},{4,2},{5,3},{10,12},{11,13},{12,10},{13,11},{18,20},{1... | collective-permute-start | bytes 1179656 | tf_op jit(solution)/shard_map/ppermute | solution.py:978
  223.9 15.6 %collective-permute-start.23 = (bf16[256,768]{1,0:T(8,128)(2,1)S(1)}, bf16[256,768]{1,0:T(8,128)(2,1)S(1)}, u32[]{:S(2)}, u32[]{:S(2)}) collective-permute-start(bf16[256,768]{1,0:T(8,128)(2,1)S(1)} %select_add_fusion), channel_id=1, source_target_pairs={{0,2},{1,3},{2,0},{3,1},{4,6},{5,7},{6,4},{7,5},{8,10},{9,11},{10,... | collective-permute-start | bytes 1179656 | tf_op jit(solution)/shard_map/ppermute | solution.py:978
  229.8 11.0 %collective-permute-start.35 = (bf16[160,384]{1,0:T(8,128)(2,1)S(1)}, bf16[160,384]{1,0:T(8,128)(2,1)S(1)}, u32[]{:S(2)}, u32[]{:S(2)}) collective-permute-start(bf16[160,384]{1,0:T(8,128)(2,1)S(1)} %collective-permute-done.34), channel_id=1, source_target_pairs={{2,0},{3,1},{4,6},{5,7},{10,8},{11,9},{12,14},{13,15},{18,16},{19,... | collective-permute-start | bytes 368648 | tf_op jit(solution)/shard_map/ppermute | solution.py:978
  233.8 1.7 collective-permute-start.31
  233.9 14.9 %copy-start.9 = (bf16[160,384]{1,0:T(8,128)(2,1)}, bf16[160,384]{1,0:T(8,128)(2,1)S(1)}, u32[]{:S(2)}) copy-start(bf16[160,384]{1,0:T(8,128)(2,1)S(1)} %slice.140.refs_1_) | copy-start | bytes 368644
  234.1 6.7 %collective-permute-start.33 = (bf16[352,384]{1,0:T(8,128)(2,1)S(1)}, bf16[352,384]{1,0:T(8,128)(2,1)S(1)}, u32[]{:S(2)}, u32[]{:S(2)}) collective-permute-start(bf16[352,384]{1,0:T(8,128)(2,1)S(1)} %pad_maximum_fusion.5), channel_id=1, source_target_pairs={{2,4},{3,5},{4,2},{5,3},{10,12},{11,13},{12,10},{13,11},{18,20},{1... | collective-permute-start | bytes 811016 | tf_op jit(solution)/shard_map/ppermute | solution.py:978
  235.5 7.0 %collective-permute-start.50 = (bf16[384,384]{1,0:T(8,128)(2,1)}, bf16[384,384]{1,0:T(8,128)(2,1)S(1)}, u32[]{:S(2)}, u32[]{:S(2)}) collective-permute-start(bf16[384,384]{1,0:T(8,128)(2,1)} %constant_dynamic-update-slice_fusion.refs_0_), channel_id=1, source_target_pairs={{0,1},{1,0},{2,3},{3,2},{4,5},{5,4},{6,7},{7,6},{8,9},{9,8},{10,11... | collective-permute-start | bytes 884744 | tf_op jit(solution)/shard_map/ppermute | solution.py:974
  236.4 6.1 %collective-permute-start.51 = (bf16[384,384]{1,0:T(8,128)(2,1)}, bf16[384,384]{1,0:T(8,128)(2,1)S(1)}, u32[]{:S(2)}, u32[]{:S(2)}) collective-permute-start(bf16[384,384]{1,0:T(8,128)(2,1)} %collective-permute-done.45.refs_1_), channel_id=1, source_target_pairs={{0,1},{1,0},{2,3},{3,2},{4,5},{5,4},{6,7},{7,6},{8,9},{9,8},{10,11... | collective-permute-start | bytes 884744 | tf_op jit(solution)/shard_map/ppermute | solution.py:974
  239.5 3.0 %collective-permute-start.52 = (bf16[384,384]{1,0:T(8,128)(2,1)S(1)}, bf16[384,384]{1,0:T(8,128)(2,1)S(1)}, u32[]{:S(2)}, u32[]{:S(2)}) collective-permute-start(bf16[384,384]{1,0:T(8,128)(2,1)S(1)} %broadcast_select_fusion.3.refs_2_), channel_id=1, source_target_pairs={{0,1},{1,0},{2,3},{3,2},{4,5},{5,4},{6,7},{7,6},{8,9},{9,8},{10,11... | collective-permute-start | bytes 884744 | tf_op jit(solution)/shard_map/ppermute | solution.py:974
  240.8 1.7 collective-permute-start.53
  240.9 14.2 %collective-permute-start.37 = (bf16[352,384]{1,0:T(8,128)(2,1)S(1)}, bf16[352,384]{1,0:T(8,128)(2,1)S(1)}, u32[]{:S(2)}, u32[]{:S(2)}) collective-permute-start(bf16[352,384]{1,0:T(8,128)(2,1)S(1)} %pad_maximum_fusion.6), channel_id=1, source_target_pairs={{2,0},{3,1},{4,6},{5,7},{10,8},{11,9},{12,14},{13,15},{18,16},{19,... | collective-permute-start | bytes 811016 | tf_op jit(solution)/shard_map/ppermute | solution.py:978
  248.2 11.3 %collective-permute-start.38 = (bf16[160,384]{1,0:T(8,128)(2,1)S(1)}, bf16[160,384]{1,0:T(8,128)(2,1)S(1)}, u32[]{:S(2)}, u32[]{:S(2)}) collective-permute-start(bf16[160,384]{1,0:T(8,128)(2,1)S(1)} %slice.118.refs_0_), channel_id=1, source_target_pairs={{0,1},{1,0},{2,3},{3,2},{4,5},{5,4},{6,7},{7,6},{8,9},{9,8},{10,11... | collective-permute-start | bytes 368648 | tf_op jit(solution)/shard_map/ppermute | solution.py:974
  248.8 10.7 %collective-permute-start.39 = (bf16[160,384]{1,0:T(8,128)(2,1)S(1)}, bf16[160,384]{1,0:T(8,128)(2,1)S(1)}, u32[]{:S(2)}, u32[]{:S(2)}) collective-permute-start(bf16[160,384]{1,0:T(8,128)(2,1)S(1)} %slice.140.refs_1_), channel_id=1, source_target_pairs={{0,1},{1,0},{2,3},{3,2},{4,5},{5,4},{6,7},{7,6},{8,9},{9,8},{10,11... | collective-permute-start | bytes 368648 | tf_op jit(solution)/shard_map/ppermute | solution.py:974
  252.0 5.2 %collective-permute-start.36 = (f32[128,768]{1,0:T(8,128)}, f32[128,768]{1,0:T(8,128)S(1)}, u32[]{:S(2)}, u32[]{:S(2)}) collective-permute-start(f32[128,768]{1,0:T(8,128)} %get-tuple-element.182), channel_id=1, source_target_pairs={{0,1},{1,0},{2,3},{3,2},{4,5},{5,4},{6,7},{7,6},{8,9},{9,8},{10,11... | collective-permute-start | bytes 1179656 | tf_op jit(solution)/shard_map/ppermute | solution.py:974
  255.2 3.0 %collective-permute-start.41 = (bf16[352,384]{1,0:T(8,128)(2,1)S(1)}, bf16[352,384]{1,0:T(8,128)(2,1)S(1)}, u32[]{:S(2)}, u32[]{:S(2)}) collective-permute-start(bf16[352,384]{1,0:T(8,128)(2,1)S(1)} %broadcast_select_fusion.4), channel_id=1, source_target_pairs={{0,1},{1,0},{2,3},{3,2},{4,5},{5,4},{6,7},{7,6},{8,9},{9,8},{10,11... | collective-permute-start | bytes 811016 | tf_op jit(solution)/shard_map/ppermute | solution.py:974
  255.3 4.2 %collective-permute-start.40 = (bf16[160,384]{1,0:T(8,128)(2,1)S(1)}, bf16[160,384]{1,0:T(8,128)(2,1)S(1)}, u32[]{:S(2)}, u32[]{:S(2)}) collective-permute-start(bf16[160,384]{1,0:T(8,128)(2,1)S(1)} %broadcast_select_fusion.5.refs_2_), channel_id=1, source_target_pairs={{0,1},{1,0},{2,3},{3,2},{4,5},{5,4},{6,7},{7,6},{8,9},{9,8},{10,11... | collective-permute-start | bytes 368648 | tf_op jit(solution)/shard_map/ppermute | solution.py:974
  (44 other events, 155.3 us)
Sparse Core Ops, SparseCore 0:
  129.3 38.1 reduce-scatter.1

commit v6 on v5

--- a/solution.py
+++ b/solution.py
@@ -1049,10 +1049,11 @@
     x_on, y_on = across_w(x_on, 1), across_w(y_on, 2)
     x_on, y_on, w_heads = tied(x_on, y_on, jnp.concatenate([w_heads, gains]))
     heads = gather_plane(w_heads)
+    x_rest, y_rest, x_on, y_on, *heads = tied(x_rest, y_rest, x_on, y_on, *heads)
     corner_a, corner_b = across_w(x_on, 2), across_w(y_on, 1)
-    x_rest, y_rest, corner_a, corner_b = tied(x_rest, y_rest, corner_a, corner_b)
     x_rest, y_rest = across_w(x_rest, 1), across_w(y_rest, 2)
     normed_all, kv, mixt, att, att_low, lse, w_full, gains = attend(x_all, heads)
+    att_low, corner_a, corner_b = tied(att_low, corner_a, corner_b)
     shared = x_on, x_rest, y_on, y_rest, corner_a, corner_b
     att_home = lax.all_to_all(att_low, "ctx", 0, 0, tiled=True, axis_index_groups=Z_GROUPS).reshape(D, -1)
     wout_full, up, cots = assemble(cot, w_out, w_up, shared)

time: 273 us -> 269 us (0.985)
  waiting for transfers between devices: 66.8 us -> 61.1 us
    ppermute x27, waiting for transfers between devices: 34.1 us -> 27.1 us  [across_w(): return lax.ppermute(value, 'wshard', [(i, i ^ flip) for i in range(4)])]
    unnamed x105 -> x101, local copies, waits for them, and re-layouts: 13.4 us -> 12.7 us
  transfers between devices with their start and end apart: 58 -> 58, of which waited for: 22 -> 22; matrix products, arithmetic and copies ran while one was open for 7% -> 7% of each run, Pallas kernels for 26% -> 27%
where the time goes in v6:
time: 269 us; the launch traced here: 267 us
  Pallas kernels  83.8 us (31%)
  starting transfers between devices  76.5 us (28%)
  waiting for transfers between devices  61.1 us (23%)
  local copies, waits for them, and re-layouts  24.3 us (9%)
  between operations  15 us (6%)
  other arithmetic  5.93 us (2%)
    pallas_call x14, Pallas kernels, call(): pl.pallas_call(kernel, in_specs=ins, out_specs=out_specs or [WHOLE] * len...  66.7 us
    ppermute x27, starting transfers between devices, across_w(): return lax.ppermute(value, 'wshard', [(i, i ^ flip) for i in range(4)])  29.5 us
    ppermute x15, starting transfers between devices, between_z(): lax.ppermute(value, 'ctx', [(2 * a + c, 2 * b + c) for a, b in pairs for...  29.1 us
    ppermute x27, waiting for transfers between devices, across_w(): return lax.ppermute(value, 'wshard', [(i, i ^ flip) for i in range(4)])  27.1 us
    pallas_call x1, Pallas kernels, attend_back(): pl.pallas_call(attend_back_kernel, in_specs=[WHOLE] * 5 + [ANYWHERE] * 2...  17.1 us
    ppermute x15, waiting for transfers between devices, between_z(): lax.ppermute(value, 'ctx', [(2 * a + c, 2 * b + c) for a, b in pairs for...  17.1 us
    unnamed x101, local copies, waits for them, and re-layouts  12.7 us
    all_to_all x1, waiting for transfers between devices, local_grid(): lax.all_to_all(d_att, 'ctx', 0, 0, tiled=True, axis_index_groups=Z_GROUPS)  11.1 us
  transfers between devices with their start and end apart: 58, of which 22 were waited for; matrix products, arithmetic and copies ran while one was open for 7% of the time, Pallas kernels for 27%

profile of v6, /device:TPU:0, one launch (start us, length us, event | category | flops | bytes accessed | tf_op | source)
XLA Modules:
  0.0 266.6 jit_solution(6834834047684611018)
XLA Ops:
  7.2 1.3 dynamic-slice_bitcast_fusion.2
  9.0 1.3 collective-permute-done
  10.6 1.3 broadcast_in_dim.10
  11.9 6.2 %all-to-all-start = ((bf16[4,256,768]{2,1,0:T(8,128)(2,1)}), bf16[4,256,768]{2,1,0:T(8,128)(2,1)S(1)}, u32[]{:S(2)}, u32[]{:S(2)}) async-start(bf16[4,256,768]{2,1,0:T(8,128)(2,1)} %broadcast_in_dim.10), calls=%async_computation | async-start | bytes 3145728 | tf_op jit(solution)/shard_map/all_to_all | solution.py:1045
  18.9 3.1 %parcels.1 = (bf16[320,768]{1,0:T(8,128)(2,1)}, bf16[416,768]{1,0:T(8,128)(2,1)}, bf16[320,768]{1,0:T(8,128)(2,1)}, bf16[416,768]{1,0:T(8,128)(2,1)}) custom-call(bf16[256,768]{1,0:T(8,128)(2,1)} %pad_maximum_fusion.3.cot_ref, bf16[192,768]{1,0:T(8,128)(2,1)} %own_ref.1, bf16[192,3072]{1,0:T(8,128)(2,1)} %wup_ref.3), custom_call_target="tpu_custom_call" | custom-call | flops 1000 | bytes 1000 | tf_op jit(solution)/shard_map/parcels/pallas_call | solution.py:303
  22.0 1.6 collective-permute-start.1
  23.5 1.5 collective-permute-start.2
  25.1 2.9 %reshape.155 = bf16[192,3,4,192]{3,2,1,0:T(4,128)(2,1)S(1)} reshape(bf16[192,2304]{1,0:T(8,128)(2,1)} %param.10) | data formatting | bytes 1769472 | tf_op jit(solution)/shard_map/reshape | solution.py:1043
  29.7 5.6 %collective-permute-done.1.x_on = bf16[320,768]{1,0:T(8,128)(2,1)} collective-permute-done((bf16[320,768]{1,0:T(8,128)(2,1)}, bf16[320,768]{1,0:T(8,128)(2,1)}, u32[]{:S(2)}, u32[]{:S(2)}) %collective-permute-start.1) | collective-permute-done | bytes 491552 | tf_op jit(solution)/shard_map/ppermute | solution.py:970
  35.3 1.2 collective-permute-done.2.y_on
  36.5 1.5 collective-permute-start.4
  38.6 5.3 %collective-permute-done.4.w2 = bf16[224,576]{1,0:T(8,128)(2,1)S(1)} collective-permute-done((bf16[224,576]{1,0:T(8,128)(2,1)S(1)}, bf16[224,576]{1,0:T(8,128)(2,1)S(1)}, u32[]{:S(2)}, u32[]{:S(2)}) %collective-permute-start.4) | collective-permute-done | bytes 258080 | tf_op jit(solution)/shard_map/ppermute | solution.py:970
  44.6 1.3 collective-permute-done.3.w1
  46.2 2.9 %collective-permute-done.6.w4 = bf16[112,576]{1,0:T(8,128)(2,1)S(1)} collective-permute-done((bf16[112,576]{1,0:T(8,128)(2,1)S(1)}, bf16[112,576]{1,0:T(8,128)(2,1)S(1)}, u32[]{:S(2)}, u32[]{:S(2)}) %collective-permute-start.6) | collective-permute-done | bytes 129056 | tf_op jit(solution)/shard_map/ppermute | solution.py:970
  49.1 3.3 %collective-permute-done.5.w3 = bf16[112,576]{1,0:T(8,128)(2,1)S(1)} collective-permute-done((bf16[112,576]{1,0:T(8,128)(2,1)S(1)}, bf16[112,576]{1,0:T(8,128)(2,1)S(1)}, u32[]{:S(2)}, u32[]{:S(2)}) %collective-permute-start.5) | collective-permute-done | bytes 129056 | tf_op jit(solution)/shard_map/ppermute | solution.py:970
  54.5 2.0 collective-permute-start.10
  57.7 12.4 %attend.1 = (bf16[1024,768]{1,0:T(8,128)(2,1)}, bf16[3,1024,128]{2,1,0:T(8,128)(2,1)}, bf16[576,1024]{1,0:T(8,128)(2,1)}, f32[192,1024]{1,0:T(8,128)}, bf16[4,19...) custom-call(bf16[4,256,768]{2,1,0:T(8,128)(2,1)} %copy-done, ...), custom_call_target="tpu_custom_call" | custom-call | flops 1000 | bytes 1000 | tf_op jit(solution)/shard_map/attend/pallas_call | solution.py:303
  70.1 5.0 %all-to-all-start.1 = ((bf16[4,192,256]{2,1,0:T(8,128)(2,1)}), bf16[4,192,256]{2,1,0:T(8,128)(2,1)S(1)}, u32[]{:S(2)}, u32[]{:S(2)}) async-start(bf16[4,192,256]{2,1,0:T(8,128)(2,1)} %get-tuple-element.127), calls=%async_computation.1 | async-start | bytes 786432 | tf_op jit(solution)/shard_map/all_to_all | solution.py:1058
  76.0 4.1 %assemble.1 = (bf16[768,768]{1,0:T(8,128)(2,1)}, bf16[768,768]{1,0:T(8,128)(2,1)}, bf16[1024,768]{1,0:T(8,128)(2,1)}) custom-call(bf16[256,768]{1,0:T(8,128)(2,1)} %pad_maximum_fusion.3.cot_ref, bf16[192,768]{1,0:T(8,128)(2,1)} %own_ref.1, bf16[192,3072]{1,0:T(8,128)(2,1)} %wup_ref.3, bf16[320,768]{1,0:T(8,128)(2,1)} %collective-permute-done.1.x_on, ...), custom_call_target="tpu_custom_call" | custom-call | flops 1000 | bytes 1000 | tf_op jit(solution)/shard_map/assemble/pallas_call | solution.py:303
  80.1 3.9 %all-to-all-done.1 = bf16[4,192,256]{2,1,0:T(8,128)(2,1)S(1)} async-done(((bf16[4,192,256]{2,1,0:T(8,128)(2,1)}), bf16[4,192,256]{2,1,0:T(8,128)(2,1)S(1)}, u32[]{:S(2)}, u32[]{:S(2)}) %all-to-all-start.1) | async-done | bytes 393248 | tf_op jit(solution)/shard_map/all_to_all | solution.py:1058
  84.8 3.0 %project.1 = (f32[256,768]{1,0:T(8,128)}, bf16[256,768]{1,0:T(8,128)(2,1)}) custom-call(bf16[768,256]{1,0:T(8,128)(2,1)} %bitcast.48, bf16[256,768]{1,0:T(8,128)(2,1)} %copy-done.1, f32[8,768]{1,0:T(8,128)} %get-tuple-element.128.gain_ref, bf16[768,768]{1,0:T(8,128)(2,1)} %get-tuple-element.133.wout_ref), custom_call_target="tpu_custom_call" | custom-call | flops 1000 | bytes 1000 | tf_op jit(solution)/shard_map/project/pallas_call | solution.py:303
  87.8 1.2 collective-permute-start.12
  89.0 1.5 collective-permute-start.11
  90.5 4.6 %feed_own.1 = (bf16[256,768]{1,0:T(8,128)(2,1)}, bf16[256,768]{1,0:T(8,128)(2,1)}, f32[256,768]{1,0:T(8,128)}, f32[256,768]{1,0:T(8,128)}) custom-call(bf16[256,768]{1,0:T(8,128)(2,1)} %get-tuple-element.135.n_ref.n0, bf16[1024,768]{1,0:T(8,128)(2,1)} %get-tuple-element.136.cot_ref, bf16[768,768]{1,0:T(8,128)(2,1)} %get-tuple-element.137.up_ref, ...), custom_call_target="tpu_custom_call" | custom-call | flops 1000 | bytes 1000 | tf_op jit(solution)/shard_map/feed_own/pallas_call | solution.py:303
  96.1 2.1 collective-permute-done.11.nx_ref.n1
  98.5 1.5 collective-permute-start.14
  100.0 6.1 %feed_near.1 = (bf16[512,768]{1,0:T(8,128)(2,1)}, bf16[512,768]{1,0:T(8,128)(2,1)}, bf16[512,768]{1,0:T(8,128)(2,1)}, bf16[512,768]{1,0:T(8,128)(2,1)}) custom-call(bf16[256,768]{1,0:T(8,128)(2,1)} %copy-done.4, bf16[256,768]{1,0:T(8,128)(2,1)} %copy-done.3, bf16[1024,768]{1,0:T(8,128)(2,1)} %get-tuple-element.136.cot_ref, ...), custom_call_target="tpu_custom_call" | custom-call | flops 1000 | bytes 1000 | tf_op jit(solution)/shard_map/feed_near/pallas_call | solution.py:303
  106.8 5.6 %feed_far.1 = (bf16[256,768]{1,0:T(8,128)(2,1)}, bf16[256,768]{1,0:T(8,128)(2,1)}, bf16[2,128,768]{2,1,0:T(8,128)(2,1)}, bf16[128,768]{1,0:T(8,128)(2,1)}, bf16[...) custom-call(bf16[128,768]{1,0:T(8,128)(2,1)} %copy-done.14, ...), custom_call_target="tpu_custom_call" | custom-call | flops 1000 | bytes 1000 | tf_op jit(solution)/shard_map/feed_far/pallas_call | solution.py:303
  113.0 1.8 collective-permute-start.16
  114.8 7.6 %feed_grads.1 = bf16[8,8,48,384]{3,2,1,0:T(8,128)(2,1)} custom-call(bf16[256,768]{1,0:T(8,128)(2,1)} %get-tuple-element.135.n_ref.n0, bf16[256,768]{1,0:T(8,128)(2,1)} %copy-done.4, bf16[256,768]{1,0:T(8,128)(2,1)} %copy-done.3, bf16[128,768]{1,0:T(8,128)(2,1)} %copy-done.14, bf16[128,768]{1,0:T(8,128)(2,1)} %copy-done.15, ...), custom_call_target="tpu_custom_call" | custom-call | flops 1000 | bytes 1000 | tf_op jit(solution)/shard_map/feed_grads/pallas_call | solution.py:303
  123.5 1.4 collective-permute-start.18
  125.0 1.8 collective-permute-start.17
  126.8 2.5 collective-permute-done.18.b_more_ref
  129.3 1.5 collective-permute-done.17.a_more_ref
  131.4 4.3 %turn.1 = (f32[256,768]{1,0:T(8,128)}, bf16[4,192,256]{2,1,0:T(8,128)(2,1)}, bf16[256,768]{1,0:T(8,128)(2,1)}, f32[1,768]{1,0:T(1,128)}) custom-call(f32[256,768]{1,0:T(8,128)} %get-tuple-element.134.hidden_ref, f32[8,768]{1,0:T(8,128)} %get-tuple-element.128.gain_ref, f32[256,768]{1,0:T(8,128)} %get-tuple-element.138.dkeep_ref, ...), custom_call_target="tpu_custom_call" | custom-call | flops 1000 | bytes 1000 | tf_op jit(solution)/shard_map/turn/pallas_call | solution.py:303
  135.7 3.7 %all-to-all-start.2 = ((bf16[4,192,256]{2,1,0:T(8,128)(2,1)}), bf16[4,192,256]{2,1,0:T(8,128)(2,1)S(1)}, u32[]{:S(2)}, u32[]{:S(2)}) async-start(bf16[4,192,256]{2,1,0:T(8,128)(2,1)} %get-tuple-element.155), calls=%async_computation.2 | async-start | bytes 786432 | tf_op jit(solution)/shard_map/all_to_all | solution.py:1075
  140.1 1.2 collective-permute-start.20
  141.3 2.6 out_grad.1
  143.9 11.1 %all-to-all-done.2.dout_ref = bf16[4,192,256]{2,1,0:T(8,128)(2,1)S(1)} async-done(((bf16[4,192,256]{2,1,0:T(8,128)(2,1)}), bf16[4,192,256]{2,1,0:T(8,128)(2,1)S(1)}, u32[]{:S(2)}, u32[]{:S(2)}) %all-to-all-start.2) | async-done | bytes 393248 | tf_op jit(solution)/shard_map/all_to_all | solution.py:1075
  155.7 17.1 %attend_back.1 = (bf16[256,768]{1,0:T(8,128)(2,1)}, bf16[256,768]{1,0:T(8,128)(2,1)}, bf16[256,768]{1,0:T(8,128)(2,1)}, bf16[256,768]{1,0:T(8,128)(2,1)}, bf16[2...) custom-call(bf16[3,1024,128]{2,1,0:T(8,128)(2,1)} %get-tuple-element.1, ...), custom_call_target="tpu_custom_call", output_to_operand_aliasing={{4}: (9, {}), {5}: (10, {})} | custom-call | flops 1000 | bytes 1000 | tf_op jit(solution)/shard_map/attend_back/pallas_call | solution.py:841
  174.8 1.4 bitcast_dynamic-update-slice_fusion
  177.1 1.8 collective-permute-start.44
  180.4 1.5 add.71
  182.0 1.2 collective-permute-start.27
  185.1 1.4 collective-permute-start.46
  187.5 3.7 %collective-permute-start.21 = (bf16[256,768]{1,0:T(8,128)(2,1)S(1)}, bf16[256,768]{1,0:T(8,128)(2,1)}, u32[]{:S(2)}, u32[]{:S(2)}) collective-permute-start(bf16[256,768]{1,0:T(8,128)(2,1)S(1)} %copy-done.23), channel_id=1, source_target_pairs={{0,2},{1,3},{6,4},{7,5},{8,10},{9,11},{14,12},{15,13},{16,18},{17,... | collective-permute-start | bytes 1179656 | tf_op jit(solution)/shard_map/ppermute | solution.py:978
  191.2 1.3 collective-permute-start.47
  192.5 2.8 %collective-permute-done.45.refs_1_ = bf16[384,384]{1,0:T(8,128)(2,1)} collective-permute-done((bf16[384,384]{1,0:T(8,128)(2,1)}, bf16[384,384]{1,0:T(8,128)(2,1)}, u32[]{:S(2)}, u32[]{:S(2)}) %collective-permute-start.45) | collective-permute-done | bytes 294944 | tf_op jit(solution)/shard_map/ppermute | solution.py:978
  196.8 4.7 %collective-permute-done.21 = bf16[256,768]{1,0:T(8,128)(2,1)} collective-permute-done((bf16[256,768]{1,0:T(8,128)(2,1)S(1)}, bf16[256,768]{1,0:T(8,128)(2,1)}, u32[]{:S(2)}, u32[]{:S(2)}) %collective-permute-start.21) | collective-permute-done | bytes 393248 | tf_op jit(solution)/shard_map/ppermute | solution.py:978
  202.6 4.8 %collective-permute-start.24 = (bf16[256,768]{1,0:T(8,128)(2,1)S(1)}, bf16[256,768]{1,0:T(8,128)(2,1)S(1)}, u32[]{:S(2)}, u32[]{:S(2)}) collective-permute-start(bf16[256,768]{1,0:T(8,128)(2,1)S(1)} %select_add_fusion.1), channel_id=1, source_target_pairs={{0,2},{1,3},{6,4},{7,5},{8,10},{9,11},{14,12},{15,13},{16,18},{17,... | collective-permute-start | bytes 1179656 | tf_op jit(solution)/shard_map/ppermute | solution.py:978
  208.2 3.0 %collective-permute-start.32 = (bf16[352,384]{1,0:T(8,128)(2,1)S(1)}, bf16[352,384]{1,0:T(8,128)(2,1)S(1)}, u32[]{:S(2)}, u32[]{:S(2)}) collective-permute-start(bf16[352,384]{1,0:T(8,128)(2,1)S(1)} %fusion.2), channel_id=1, source_target_pairs={{0,2},{1,3},{2,0},{3,1},{4,6},{5,7},{6,4},{7,5},{8,10},{9,11},{10,... | collective-permute-start | bytes 811016 | tf_op jit(solution)/shard_map/ppermute | solution.py:978
  212.5 1.4 collective-permute-start.29
  214.0 2.8 %collective-permute-done.24 = bf16[256,768]{1,0:T(8,128)(2,1)S(1)} collective-permute-done((bf16[256,768]{1,0:T(8,128)(2,1)S(1)}, bf16[256,768]{1,0:T(8,128)(2,1)S(1)}, u32[]{:S(2)}, u32[]{:S(2)}) %collective-permute-start.24) | collective-permute-done | bytes 393248 | tf_op jit(solution)/shard_map/ppermute | solution.py:978
  216.8 1.3 collective-permute-start.49
  218.9 6.5 %collective-permute-start.23 = (bf16[256,768]{1,0:T(8,128)(2,1)S(1)}, bf16[256,768]{1,0:T(8,128)(2,1)S(1)}, u32[]{:S(2)}, u32[]{:S(2)}) collective-permute-start(bf16[256,768]{1,0:T(8,128)(2,1)S(1)} %select_add_fusion), channel_id=1, source_target_pairs={{0,2},{1,3},{2,0},{3,1},{4,6},{5,7},{6,4},{7,5},{8,10},{9,11},{10,... | collective-permute-start | bytes 1179656 | tf_op jit(solution)/shard_map/ppermute | solution.py:978
  225.4 1.3 collective-permute-start.35
  226.7 2.6 give.1
  232.4 2.1 collective-permute-done.23.pair_ref
  234.5 1.3 collective-permute-done.35
  235.9 1.6 collective-permute-start.37
  239.1 4.1 %finish_feed.1 = (f32[192,3072]{1,0:T(8,128)}, f32[768,768]{1,0:T(8,128)}) custom-call(bf16[384,384]{1,0:T(8,128)(2,1)} %constant_dynamic-update-slice_fusion.refs_0_, bf16[384,384]{1,0:T(8,128)(2,1)} %collective-permute-done.45.refs_1_, bf16[384,384]{1,0:T(8,128)(2,1)} %copy-done.6, bf16[384,384]{1,0:T(8,128)(2,1)} %copy-done.7, ...), custom_call_target="tpu_custom_call" | custom-call | flops 1000 | bytes 1000 | tf_op jit(solution)/shard_map/finish_feed/pallas_call | solution.py:303
  243.8 3.1 %last.1 = (f32[128,768]{1,0:T(8,128)}, f32[128,768]{1,0:T(8,128)}) custom-call(bf16[256,768]{1,0:T(8,128)(2,1)} %get-tuple-element.193.first_ref, bf16[256,768]{1,0:T(8,128)(2,1)} %copy-done.22, bf16[256,768]{1,0:T(8,128)(2,1)} %copy-done.21, bf16[256,768]{1,0:T(8,128)(2,1)} %copy-done.1, f32[8,768]{1,0:T(8,128)} %get-tuple-element.128.gain_ref, ...), custom_call_target="tpu_custom_call" | custom-call | flops 1000 | bytes 1000 | tf_op jit(solution)/shard_map/last/pallas_call | solution.py:303
  247.5 3.2 %collective-permute-done.37 = bf16[352,384]{1,0:T(8,128)(2,1)S(1)} collective-permute-done((bf16[352,384]{1,0:T(8,128)(2,1)S(1)}, bf16[352,384]{1,0:T(8,128)(2,1)S(1)}, u32[]{:S(2)}, u32[]{:S(2)}) %collective-permute-start.37) | collective-permute-done | bytes 270368 | tf_op jit(solution)/shard_map/ppermute | solution.py:978
  256.4 3.4 %finish_heads.1 = (f32[192,768]{1,0:T(8,128)}, f32[192,2304]{1,0:T(8,128)}, f32[192]{0:T(256)}, f32[192]{0:T(256)}) custom-call(bf16[160,384]{1,0:T(8,128)(2,1)} %copy-done.19, bf16[160,384]{1,0:T(8,128)(2,1)} %copy-done.9, bf16[160,384]{1,0:T(8,128)(2,1)} %copy-done.20, bf16[160,384]{1,0:T(8,128)(2,1)} %slice.142.refs_3_, bf16[160,384]{1,0:T(8,128)(2,1)} %copy-done.41, ...), custom_call_target="tpu_custom_call" | custom-call | flops 1000 | bytes 1000 | tf_op jit(solution)/shard_map/finish_heads/pallas_call | solution.py:303
  (219 shorter events, 39.6 us)
Async XLA Ops:
  8.5 1.9 collective-permute-start
  11.9 44.6 %all-to-all-start = ((bf16[4,256,768]{2,1,0:T(8,128)(2,1)}), bf16[4,256,768]{2,1,0:T(8,128)(2,1)S(1)}, u32[]{:S(2)}, u32[]{:S(2)}) async-start(bf16[4,256,768]{2,1,0:T(8,128)(2,1)} %broadcast_in_dim.10), calls=%async_computation | async-start | bytes 3145728 | tf_op jit(solution)/shard_map/all_to_all | solution.py:1045
  22.0 13.4 %collective-permute-start.1 = (bf16[320,768]{1,0:T(8,128)(2,1)}, bf16[320,768]{1,0:T(8,128)(2,1)}, u32[]{:S(2)}, u32[]{:S(2)}) collective-permute-start(bf16[320,768]{1,0:T(8,128)(2,1)} %get-tuple-element.110), channel_id=1, source_target_pairs={{0,8},{8,0},{16,24},{24,16},{1,9},{9,1},{17,25},{25,17},{2,10},{10... | collective-permute-start | bytes 1474568 | tf_op jit(solution)/shard_map/ppermute | solution.py:970
  23.5 13.0 %collective-permute-start.2 = (bf16[320,768]{1,0:T(8,128)(2,1)}, bf16[320,768]{1,0:T(8,128)(2,1)}, u32[]{:S(2)}, u32[]{:S(2)}) collective-permute-start(bf16[320,768]{1,0:T(8,128)(2,1)} %get-tuple-element.111), channel_id=1, source_target_pairs={{0,16},{8,24},{16,0},{24,8},{1,17},{9,25},{17,1},{25,9},{2,18},{10... | collective-permute-start | bytes 1474568 | tf_op jit(solution)/shard_map/ppermute | solution.py:970
  29.7 26.8 %copy-start.8 = (bf16[224,576]{1,0:T(8,128)(2,1)}, bf16[224,576]{1,0:T(8,128)(2,1)S(1)}, u32[]{:S(2)}) copy-start(bf16[224,576]{1,0:T(8,128)(2,1)S(1)} %pad_maximum_fusion.4.w0) | copy-start | bytes 774148
  36.5 7.4 %collective-permute-start.4 = (bf16[224,576]{1,0:T(8,128)(2,1)S(1)}, bf16[224,576]{1,0:T(8,128)(2,1)S(1)}, u32[]{:S(2)}, u32[]{:S(2)}) collective-permute-start(bf16[224,576]{1,0:T(8,128)(2,1)S(1)} %pad_maximum_fusion.4.w0), channel_id=1, source_target_pairs={{0,16},{8,24},{16,0},{24,8},{1,17},{9,25},{17,1},{25,9},{2,18},{10... | collective-permute-start | bytes 774152 | tf_op jit(solution)/shard_map/ppermute | solution.py:970
  38.1 7.9 %collective-permute-start.3 = (bf16[224,576]{1,0:T(8,128)(2,1)S(1)}, bf16[224,576]{1,0:T(8,128)(2,1)S(1)}, u32[]{:S(2)}, u32[]{:S(2)}) collective-permute-start(bf16[224,576]{1,0:T(8,128)(2,1)S(1)} %pad_maximum_fusion.4.w0), channel_id=1, source_target_pairs={{0,8},{8,0},{16,24},{24,16},{1,9},{9,1},{17,25},{25,17},{2,10},{10... | collective-permute-start | bytes 774152 | tf_op jit(solution)/shard_map/ppermute | solution.py:970
  44.0 5.2 %collective-permute-start.6 = (bf16[112,576]{1,0:T(8,128)(2,1)S(1)}, bf16[112,576]{1,0:T(8,128)(2,1)S(1)}, u32[]{:S(2)}, u32[]{:S(2)}) collective-permute-start(bf16[112,576]{1,0:T(8,128)(2,1)S(1)} %slice.135), channel_id=1, source_target_pairs={{0,8},{8,0},{16,24},{24,16},{1,9},{9,1},{17,25},{25,17},{2,10},{10... | collective-permute-start | bytes 387080 | tf_op jit(solution)/shard_map/ppermute | solution.py:970
  45.9 6.5 %collective-permute-start.5 = (bf16[112,576]{1,0:T(8,128)(2,1)S(1)}, bf16[112,576]{1,0:T(8,128)(2,1)S(1)}, u32[]{:S(2)}, u32[]{:S(2)}) collective-permute-start(bf16[112,576]{1,0:T(8,128)(2,1)S(1)} %slice.134), channel_id=1, source_target_pairs={{0,16},{8,24},{16,0},{24,8},{1,17},{9,25},{17,1},{25,9},{2,18},{10... | collective-permute-start | bytes 387080 | tf_op jit(solution)/shard_map/ppermute | solution.py:970
  52.5 17.6 %collective-permute-start.7 = (bf16[320,768]{1,0:T(8,128)(2,1)}, bf16[320,768]{1,0:T(8,128)(2,1)}, u32[]{:S(2)}, u32[]{:S(2)}) collective-permute-start(bf16[320,768]{1,0:T(8,128)(2,1)} %collective-permute-done.1.x_on), channel_id=1, source_target_pairs={{0,16},{8,24},{16,0},{24,8},{1,17},{9,25},{17,1},{25,9},{2,18},{10... | collective-permute-start | bytes 1474568 | tf_op jit(solution)/shard_map/ppermute | solution.py:970
  52.5 17.6 %collective-permute-start.8 = (bf16[320,768]{1,0:T(8,128)(2,1)}, bf16[320,768]{1,0:T(8,128)(2,1)}, u32[]{:S(2)}, u32[]{:S(2)}) collective-permute-start(bf16[320,768]{1,0:T(8,128)(2,1)} %collective-permute-done.2.y_on), channel_id=1, source_target_pairs={{0,8},{8,0},{16,24},{24,16},{1,9},{9,1},{17,25},{25,17},{2,10},{10... | collective-permute-start | bytes 1474568 | tf_op jit(solution)/shard_map/ppermute | solution.py:970
  53.4 21.8 %collective-permute-start.9 = (bf16[416,768]{1,0:T(8,128)(2,1)}, bf16[416,768]{1,0:T(8,128)(2,1)S(1)}, u32[]{:S(2)}, u32[]{:S(2)}) collective-permute-start(bf16[416,768]{1,0:T(8,128)(2,1)} %get-tuple-element.129), channel_id=1, source_target_pairs={{0,8},{8,0},{16,24},{24,16},{1,9},{9,1},{17,25},{25,17},{2,10},{10... | collective-permute-start | bytes 1916936 | tf_op jit(solution)/shard_map/ppermute | solution.py:970
  54.5 21.0 %collective-permute-start.10 = (bf16[416,768]{1,0:T(8,128)(2,1)}, bf16[416,768]{1,0:T(8,128)(2,1)}, u32[]{:S(2)}, u32[]{:S(2)}) collective-permute-start(bf16[416,768]{1,0:T(8,128)(2,1)} %get-tuple-element.130), channel_id=1, source_target_pairs={{0,16},{8,24},{16,0},{24,8},{1,17},{9,25},{17,1},{25,9},{2,18},{10... | collective-permute-start | bytes 1916936 | tf_op jit(solution)/shard_map/ppermute | solution.py:970
  70.1 13.9 %all-to-all-start.1 = ((bf16[4,192,256]{2,1,0:T(8,128)(2,1)}), bf16[4,192,256]{2,1,0:T(8,128)(2,1)S(1)}, u32[]{:S(2)}, u32[]{:S(2)}) async-start(bf16[4,192,256]{2,1,0:T(8,128)(2,1)} %get-tuple-element.127), calls=%async_computation.1 | async-start | bytes 786432 | tf_op jit(solution)/shard_map/all_to_all | solution.py:1058
  75.1 97.7 %reduce-scatter.2.cloned.1.call-start = ((), (), s32[]{:S(2)}) async-start(), calls=%async_computation.4 | async-start | bytes 2654208 | tf_op jit(solution)/shard_map/reduce_scatter | solution.py:1070
  87.8 8.3 %collective-permute-start.12 = (bf16[256,768]{1,0:T(8,128)(2,1)}, bf16[256,768]{1,0:T(8,128)(2,1)S(1)}, u32[]{:S(2)}, u32[]{:S(2)}) collective-permute-start(bf16[256,768]{1,0:T(8,128)(2,1)} %get-tuple-element.135.n_ref.n0), channel_id=1, source_target_pairs={{0,16},{8,24},{16,0},{24,8},{1,17},{9,25},{17,1},{25,9},{2,18},{10... | collective-permute-start | bytes 1179656 | tf_op jit(solution)/shard_map/ppermute | solution.py:970
  89.0 9.2 %collective-permute-start.11 = (bf16[256,768]{1,0:T(8,128)(2,1)}, bf16[256,768]{1,0:T(8,128)(2,1)S(1)}, u32[]{:S(2)}, u32[]{:S(2)}) collective-permute-start(bf16[256,768]{1,0:T(8,128)(2,1)} %get-tuple-element.135.n_ref.n0), channel_id=1, source_target_pairs={{0,8},{8,0},{16,24},{24,16},{1,9},{9,1},{17,25},{25,17},{2,10},{10... | collective-permute-start | bytes 1179656 | tf_op jit(solution)/shard_map/ppermute | solution.py:970
  98.2 7.9 %collective-permute-start.13 = (bf16[128,768]{1,0:T(8,128)(2,1)S(1)}, bf16[128,768]{1,0:T(8,128)(2,1)S(1)}, u32[]{:S(2)}, u32[]{:S(2)}) collective-permute-start(bf16[128,768]{1,0:T(8,128)(2,1)S(1)} %slice.136), channel_id=1, source_target_pairs={{0,16},{8,24},{16,0},{24,8},{1,17},{9,25},{17,1},{25,9},{2,18},{10... | collective-permute-start | bytes 589832 | tf_op jit(solution)/shard_map/ppermute | solution.py:970
  98.5 7.6 %collective-permute-start.14 = (bf16[128,768]{1,0:T(8,128)(2,1)S(1)}, bf16[128,768]{1,0:T(8,128)(2,1)S(1)}, u32[]{:S(2)}, u32[]{:S(2)}) collective-permute-start(bf16[128,768]{1,0:T(8,128)(2,1)S(1)} %slice.137), channel_id=1, source_target_pairs={{0,8},{8,0},{16,24},{24,16},{1,9},{9,1},{17,25},{25,17},{2,10},{10... | collective-permute-start | bytes 589832 | tf_op jit(solution)/shard_map/ppermute | solution.py:970
  112.4 10.0 %collective-permute-start.15 = (bf16[2,128,768]{2,1,0:T(8,128)(2,1)}, bf16[2,128,768]{2,1,0:T(8,128)(2,1)S(1)}, u32[]{:S(2)}, u32[]{:S(2)}) collective-permute-start(bf16[2,128,768]{2,1,0:T(8,128)(2,1)} %get-tuple-element.149), channel_id=1, source_target_pairs={{0,8},{8,0},{16,24},{24,16},{1,9},{9,1},{17,25},{25,17},{2,10},{10... | collective-permute-start | bytes 1179656 | tf_op jit(solution)/shard_map/ppermute | solution.py:970
  113.0 9.5 %collective-permute-start.16 = (bf16[2,128,768]{2,1,0:T(8,128)(2,1)}, bf16[2,128,768]{2,1,0:T(8,128)(2,1)S(1)}, u32[]{:S(2)}, u32[]{:S(2)}) collective-permute-start(bf16[2,128,768]{2,1,0:T(8,128)(2,1)} %get-tuple-element.150), channel_id=1, source_target_pairs={{0,16},{8,24},{16,0},{24,8},{1,17},{9,25},{17,1},{25,9},{2,18},{10... | collective-permute-start | bytes 1179656 | tf_op jit(solution)/shard_map/ppermute | solution.py:970
  123.5 5.7 %collective-permute-start.18 = (bf16[128,768]{1,0:T(8,128)(2,1)S(1)}, bf16[128,768]{1,0:T(8,128)(2,1)S(1)}, u32[]{:S(2)}, u32[]{:S(2)}) collective-permute-start(bf16[128,768]{1,0:T(8,128)(2,1)S(1)} %bitcast_add_fusion.2), channel_id=1, source_target_pairs={{0,8},{8,0},{16,24},{24,16},{1,9},{9,1},{17,25},{25,17},{2,10},{10... | collective-permute-start | bytes 589832 | tf_op jit(solution)/shard_map/ppermute | solution.py:970
  125.0 5.7 %collective-permute-start.17 = (bf16[128,768]{1,0:T(8,128)(2,1)S(1)}, bf16[128,768]{1,0:T(8,128)(2,1)S(1)}, u32[]{:S(2)}, u32[]{:S(2)}) collective-permute-start(bf16[128,768]{1,0:T(8,128)(2,1)S(1)} %bitcast_add_fusion.3), channel_id=1, source_target_pairs={{0,16},{8,24},{16,0},{24,8},{1,17},{9,25},{17,1},{25,9},{2,18},{10... | collective-permute-start | bytes 589832 | tf_op jit(solution)/shard_map/ppermute | solution.py:970
  135.7 19.2 %all-to-all-start.2 = ((bf16[4,192,256]{2,1,0:T(8,128)(2,1)}), bf16[4,192,256]{2,1,0:T(8,128)(2,1)S(1)}, u32[]{:S(2)}, u32[]{:S(2)}) async-start(bf16[4,192,256]{2,1,0:T(8,128)(2,1)} %get-tuple-element.155), calls=%async_computation.2 | async-start | bytes 786432 | tf_op jit(solution)/shard_map/all_to_all | solution.py:1075
  139.4 33.4 %collective-permute-start.19 = (bf16[2,128,768]{2,1,0:T(8,128)(2,1)S(1)}, bf16[2,128,768]{2,1,0:T(8,128)(2,1)S(1)}, u32[]{:S(2)}, u32[]{:S(2)}) collective-permute-start(bf16[2,128,768]{2,1,0:T(8,128)(2,1)S(1)} %copy-done.45), channel_id=1, source_target_pairs={{0,8},{8,0},{16,24},{24,16},{1,9},{9,1},{17,25},{25,17},{2,10},{10... | collective-permute-start | bytes 1179656 | tf_op jit(solution)/shard_map/ppermute | solution.py:970
  140.1 32.7 %collective-permute-start.20 = (bf16[2,128,768]{2,1,0:T(8,128)(2,1)S(1)}, bf16[2,128,768]{2,1,0:T(8,128)(2,1)S(1)}, u32[]{:S(2)}, u32[]{:S(2)}) collective-permute-start(bf16[2,128,768]{2,1,0:T(8,128)(2,1)S(1)} %copy-done.44), channel_id=1, source_target_pairs={{0,16},{8,24},{16,0},{24,8},{1,17},{9,25},{17,1},{25,9},{2,18},{10... | collective-permute-start | bytes 1179656 | tf_op jit(solution)/shard_map/ppermute | solution.py:970
  172.8 39.1 %copy-start.12 = (bf16[2,128,768]{2,1,0:T(8,128)(2,1)}, bf16[2,128,768]{2,1,0:T(8,128)(2,1)S(1)}, u32[]{:S(2)}) copy-start(bf16[2,128,768]{2,1,0:T(8,128)(2,1)S(1)} %collective-permute-done.19.a_ref) | copy-start | bytes 1179652
  172.8 39.1 %copy-start.13 = (bf16[2,128,768]{2,1,0:T(8,128)(2,1)}, bf16[2,128,768]{2,1,0:T(8,128)(2,1)S(1)}, u32[]{:S(2)}) copy-start(bf16[2,128,768]{2,1,0:T(8,128)(2,1)S(1)} %collective-permute-done.20.b_ref) | copy-start | bytes 1179652
  172.9 7.6 %collective-permute-start.26 = (bf16[2,2,352,384]{3,2,1,0:T(8,128)(2,1)}, bf16[2,2,352,384]{3,2,1,0:T(8,128)(2,1)S(1)}, u32[]{:S(2)}, u32[]{:S(2)}) collective-permute-start(bf16[2,2,352,384]{3,2,1,0:T(8,128)(2,1)} %get-tuple-element.180), channel_id=1, source_target_pairs={{0,1},{1,0},{2,3},{3,2},{4,5},{5,4},{6,7},{7,6},{8,9},{9,8},{10,11... | collective-permute-start | bytes 3244040 | tf_op jit(solution)/shard_map/ppermute | solution.py:974
  173.9 5.9 %collective-permute-start.42 = (bf16[48,384]{1,0:T(8,128)(2,1)S(1)}, bf16[48,384]{1,0:T(8,128)(2,1)S(1)}, u32[]{:S(2)}, u32[]{:S(2)}) collective-permute-start(bf16[48,384]{1,0:T(8,128)(2,1)S(1)} %get-tuple-element.220), channel_id=1, source_target_pairs={{0,8},{8,0},{16,24},{24,16},{1,9},{9,1},{17,25},{25,17},{2,10},{10... | collective-permute-start | bytes 110600 | tf_op jit(solution)/shard_map/ppermute | solution.py:970
  177.1 6.7 %collective-permute-start.44 = (bf16[48,384]{1,0:T(8,128)(2,1)S(1)}, bf16[48,384]{1,0:T(8,128)(2,1)S(1)}, u32[]{:S(2)}, u32[]{:S(2)}) collective-permute-start(bf16[48,384]{1,0:T(8,128)(2,1)S(1)} %get-tuple-element.218), channel_id=1, source_target_pairs={{0,24},{8,16},{16,8},{24,0},{1,25},{9,17},{17,9},{25,1},{2,26},{10... | collective-permute-start | bytes 110600 | tf_op jit(solution)/shard_map/ppermute | solution.py:970
  178.9 4.3 %collective-permute-start.43 = (bf16[48,384]{1,0:T(8,128)(2,1)S(1)}, bf16[48,384]{1,0:T(8,128)(2,1)S(1)}, u32[]{:S(2)}, u32[]{:S(2)}) collective-permute-start(bf16[48,384]{1,0:T(8,128)(2,1)S(1)} %get-tuple-element.219), channel_id=1, source_target_pairs={{0,16},{8,24},{16,0},{24,8},{1,17},{9,25},{17,1},{25,9},{2,18},{10... | collective-permute-start | bytes 110600 | tf_op jit(solution)/shard_map/ppermute | solution.py:970
  182.0 13.9 %collective-permute-start.27 = (bf16[2,352,384]{2,1,0:T(8,128)(2,1)S(1)}, bf16[2,352,384]{2,1,0:T(8,128)(2,1)S(1)}, u32[]{:S(2)}, u32[]{:S(2)}) collective-permute-start(bf16[2,352,384]{2,1,0:T(8,128)(2,1)S(1)} %slice_bitcast_fusion), channel_id=1, source_target_pairs={{0,16},{8,24},{16,0},{24,8},{1,17},{9,25},{17,1},{25,9},{2,18},{10... | collective-permute-start | bytes 1622024 | tf_op jit(solution)/shard_map/ppermute | solution.py:970
  185.1 6.1 %collective-permute-start.46 = (bf16[384,384]{1,0:T(8,128)(2,1)}, bf16[384,384]{1,0:T(8,128)(2,1)}, u32[]{:S(2)}, u32[]{:S(2)}) collective-permute-start(bf16[384,384]{1,0:T(8,128)(2,1)} %constant_dynamic-update-slice_fusion.refs_0_), channel_id=1, source_target_pairs={{2,4},{3,5},{4,2},{5,3},{10,12},{11,13},{12,10},{13,11},{18,20},{1... | collective-permute-start | bytes 884744 | tf_op jit(solution)/shard_map/ppermute | solution.py:978
  186.5 8.7 %collective-permute-start.45 = (bf16[384,384]{1,0:T(8,128)(2,1)}, bf16[384,384]{1,0:T(8,128)(2,1)}, u32[]{:S(2)}, u32[]{:S(2)}) collective-permute-start(bf16[384,384]{1,0:T(8,128)(2,1)} %constant_dynamic-update-slice_fusion.refs_0_), channel_id=1, source_target_pairs={{0,2},{1,3},{2,0},{3,1},{4,6},{5,7},{6,4},{7,5},{8,10},{9,11},{10,... | collective-permute-start | bytes 884744 | tf_op jit(solution)/shard_map/ppermute | solution.py:978
  187.5 14.0 %collective-permute-start.21 = (bf16[256,768]{1,0:T(8,128)(2,1)S(1)}, bf16[256,768]{1,0:T(8,128)(2,1)}, u32[]{:S(2)}, u32[]{:S(2)}) collective-permute-start(bf16[256,768]{1,0:T(8,128)(2,1)S(1)} %copy-done.23), channel_id=1, source_target_pairs={{0,2},{1,3},{6,4},{7,5},{8,10},{9,11},{14,12},{15,13},{16,18},{17,... | collective-permute-start | bytes 1179656 | tf_op jit(solution)/shard_map/ppermute | solution.py:978
  191.2 16.8 %collective-permute-start.47 = (bf16[384,384]{1,0:T(8,128)(2,1)}, bf16[384,384]{1,0:T(8,128)(2,1)S(1)}, u32[]{:S(2)}, u32[]{:S(2)}) collective-permute-start(bf16[384,384]{1,0:T(8,128)(2,1)} %collective-permute-done.46), channel_id=1, source_target_pairs={{2,0},{3,1},{4,6},{5,7},{10,8},{11,9},{12,14},{13,15},{18,16},{19,... | collective-permute-start | bytes 884744 | tf_op jit(solution)/shard_map/ppermute | solution.py:978
  195.3 16.7 %collective-permute-start.48 = (bf16[384,384]{1,0:T(8,128)(2,1)}, bf16[384,384]{1,0:T(8,128)(2,1)S(1)}, u32[]{:S(2)}, u32[]{:S(2)}) collective-permute-start(bf16[384,384]{1,0:T(8,128)(2,1)} %collective-permute-done.45.refs_1_), channel_id=1, source_target_pairs={{2,4},{3,5},{4,2},{5,3},{10,12},{11,13},{12,10},{13,11},{18,20},{1... | collective-permute-start | bytes 884744 | tf_op jit(solution)/shard_map/ppermute | solution.py:978
  196.0 12.1 %collective-permute-start.28 = (bf16[352,384]{1,0:T(8,128)(2,1)S(1)}, bf16[352,384]{1,0:T(8,128)(2,1)S(1)}, u32[]{:S(2)}, u32[]{:S(2)}) collective-permute-start(bf16[352,384]{1,0:T(8,128)(2,1)S(1)} %fusion), channel_id=1, source_target_pairs={{0,8},{8,0},{16,24},{24,16},{1,9},{9,1},{17,25},{25,17},{2,10},{10... | collective-permute-start | bytes 811016 | tf_op jit(solution)/shard_map/ppermute | solution.py:970
  202.6 14.2 %collective-permute-start.24 = (bf16[256,768]{1,0:T(8,128)(2,1)S(1)}, bf16[256,768]{1,0:T(8,128)(2,1)S(1)}, u32[]{:S(2)}, u32[]{:S(2)}) collective-permute-start(bf16[256,768]{1,0:T(8,128)(2,1)S(1)} %select_add_fusion.1), channel_id=1, source_target_pairs={{0,2},{1,3},{6,4},{7,5},{8,10},{9,11},{14,12},{15,13},{16,18},{17,... | collective-permute-start | bytes 1179656 | tf_op jit(solution)/shard_map/ppermute | solution.py:978
  207.3 5.2 %collective-permute-start.22 = (bf16[256,768]{1,0:T(8,128)(2,1)S(1)}, bf16[256,768]{1,0:T(8,128)(2,1)S(1)}, u32[]{:S(2)}, u32[]{:S(2)}) collective-permute-start(bf16[256,768]{1,0:T(8,128)(2,1)S(1)} %select_add_fusion.1), channel_id=1, source_target_pairs={{2,4},{3,5},{4,2},{5,3},{10,12},{11,13},{12,10},{13,11},{18,20},{1... | collective-permute-start | bytes 1179656 | tf_op jit(solution)/shard_map/ppermute | solution.py:978
  208.1 26.4 %copy-start.6 = (bf16[384,384]{1,0:T(8,128)(2,1)}, bf16[384,384]{1,0:T(8,128)(2,1)S(1)}, u32[]{:S(2)}) copy-start(bf16[384,384]{1,0:T(8,128)(2,1)S(1)} %broadcast_select_fusion.3.refs_2_) | copy-start | bytes 884740
  208.2 34.9 %copy-start.19 = (bf16[160,384]{1,0:T(8,128)(2,1)}, bf16[160,384]{1,0:T(8,128)(2,1)S(1)}, u32[]{:S(2)}) copy-start(bf16[160,384]{1,0:T(8,128)(2,1)S(1)} %slice.118.refs_0_) | copy-start | bytes 368644
  208.2 21.1 %collective-permute-start.32 = (bf16[352,384]{1,0:T(8,128)(2,1)S(1)}, bf16[352,384]{1,0:T(8,128)(2,1)S(1)}, u32[]{:S(2)}, u32[]{:S(2)}) collective-permute-start(bf16[352,384]{1,0:T(8,128)(2,1)S(1)} %fusion.2), channel_id=1, source_target_pairs={{0,2},{1,3},{2,0},{3,1},{4,6},{5,7},{6,4},{7,5},{8,10},{9,11},{10,... | collective-permute-start | bytes 811016 | tf_op jit(solution)/shard_map/ppermute | solution.py:978
  211.2 6.9 %collective-permute-start.34 = (bf16[160,384]{1,0:T(8,128)(2,1)S(1)}, bf16[160,384]{1,0:T(8,128)(2,1)S(1)}, u32[]{:S(2)}, u32[]{:S(2)}) collective-permute-start(bf16[160,384]{1,0:T(8,128)(2,1)S(1)} %slice.118.refs_0_), channel_id=1, source_target_pairs={{2,4},{3,5},{4,2},{5,3},{10,12},{11,13},{12,10},{13,11},{18,20},{1... | collective-permute-start | bytes 368648 | tf_op jit(solution)/shard_map/ppermute | solution.py:978
  212.0 6.9 %collective-permute-start.30 = (bf16[128,768]{1,0:T(8,128)(2,1)S(1)}, bf16[128,768]{1,0:T(8,128)(2,1)S(1)}, u32[]{:S(2)}, u32[]{:S(2)}) collective-permute-start(bf16[128,768]{1,0:T(8,128)(2,1)S(1)} %bitcast_add_fusion), channel_id=1, source_target_pairs={{0,8},{8,0},{16,24},{24,16},{1,9},{9,1},{17,25},{25,17},{2,10},{10... | collective-permute-start | bytes 589832 | tf_op jit(solution)/shard_map/ppermute | solution.py:970
  212.5 12.9 %collective-permute-start.29 = (bf16[128,768]{1,0:T(8,128)(2,1)S(1)}, bf16[128,768]{1,0:T(8,128)(2,1)S(1)}, u32[]{:S(2)}, u32[]{:S(2)}) collective-permute-start(bf16[128,768]{1,0:T(8,128)(2,1)S(1)} %bitcast_add_fusion.1), channel_id=1, source_target_pairs={{0,16},{8,24},{16,0},{24,8},{1,17},{9,25},{17,1},{25,9},{2,18},{10... | collective-permute-start | bytes 589832 | tf_op jit(solution)/shard_map/ppermute | solution.py:970
  216.8 12.9 %collective-permute-start.49 = (bf16[384,384]{1,0:T(8,128)(2,1)S(1)}, bf16[384,384]{1,0:T(8,128)(2,1)S(1)}, u32[]{:S(2)}, u32[]{:S(2)}) collective-permute-start(bf16[384,384]{1,0:T(8,128)(2,1)S(1)} %collective-permute-done.48), channel_id=1, source_target_pairs={{2,0},{3,1},{4,6},{5,7},{10,8},{11,9},{12,14},{13,15},{18,16},{19,... | collective-permute-start | bytes 884744 | tf_op jit(solution)/shard_map/ppermute | solution.py:978
  218.2 13.8 %collective-permute-start.25 = (bf16[256,768]{1,0:T(8,128)(2,1)S(1)}, bf16[256,768]{1,0:T(8,128)(2,1)S(1)}, u32[]{:S(2)}, u32[]{:S(2)}) collective-permute-start(bf16[256,768]{1,0:T(8,128)(2,1)S(1)} %add.70), channel_id=1, source_target_pairs={{2,4},{3,5},{4,2},{5,3},{10,12},{11,13},{12,10},{13,11},{18,20},{1... | collective-permute-start | bytes 1179656 | tf_op jit(solution)/shard_map/ppermute | solution.py:978
  218.9 15.6 %collective-permute-start.23 = (bf16[256,768]{1,0:T(8,128)(2,1)S(1)}, bf16[256,768]{1,0:T(8,128)(2,1)S(1)}, u32[]{:S(2)}, u32[]{:S(2)}) collective-permute-start(bf16[256,768]{1,0:T(8,128)(2,1)S(1)} %select_add_fusion), channel_id=1, source_target_pairs={{0,2},{1,3},{2,0},{3,1},{4,6},{5,7},{6,4},{7,5},{8,10},{9,11},{10,... | collective-permute-start | bytes 1179656 | tf_op jit(solution)/shard_map/ppermute | solution.py:978
  225.4 10.4 %collective-permute-start.35 = (bf16[160,384]{1,0:T(8,128)(2,1)S(1)}, bf16[160,384]{1,0:T(8,128)(2,1)S(1)}, u32[]{:S(2)}, u32[]{:S(2)}) collective-permute-start(bf16[160,384]{1,0:T(8,128)(2,1)S(1)} %collective-permute-done.34), channel_id=1, source_target_pairs={{2,0},{3,1},{4,6},{5,7},{10,8},{11,9},{12,14},{13,15},{18,16},{19,... | collective-permute-start | bytes 368648 | tf_op jit(solution)/shard_map/ppermute | solution.py:978
  229.3 1.7 collective-permute-start.31
  229.4 14.3 %copy-start.9 = (bf16[160,384]{1,0:T(8,128)(2,1)}, bf16[160,384]{1,0:T(8,128)(2,1)S(1)}, u32[]{:S(2)}) copy-start(bf16[160,384]{1,0:T(8,128)(2,1)S(1)} %slice.140.refs_1_) | copy-start | bytes 368644
  229.7 6.1 %collective-permute-start.33 = (bf16[352,384]{1,0:T(8,128)(2,1)S(1)}, bf16[352,384]{1,0:T(8,128)(2,1)S(1)}, u32[]{:S(2)}, u32[]{:S(2)}) collective-permute-start(bf16[352,384]{1,0:T(8,128)(2,1)S(1)} %pad_maximum_fusion.5), channel_id=1, source_target_pairs={{2,4},{3,5},{4,2},{5,3},{10,12},{11,13},{12,10},{13,11},{18,20},{1... | collective-permute-start | bytes 811016 | tf_op jit(solution)/shard_map/ppermute | solution.py:978
  231.1 6.4 %collective-permute-start.50 = (bf16[384,384]{1,0:T(8,128)(2,1)}, bf16[384,384]{1,0:T(8,128)(2,1)S(1)}, u32[]{:S(2)}, u32[]{:S(2)}) collective-permute-start(bf16[384,384]{1,0:T(8,128)(2,1)} %constant_dynamic-update-slice_fusion.refs_0_), channel_id=1, source_target_pairs={{0,1},{1,0},{2,3},{3,2},{4,5},{5,4},{6,7},{7,6},{8,9},{9,8},{10,11... | collective-permute-start | bytes 884744 | tf_op jit(solution)/shard_map/ppermute | solution.py:974
  232.0 5.5 %collective-permute-start.51 = (bf16[384,384]{1,0:T(8,128)(2,1)}, bf16[384,384]{1,0:T(8,128)(2,1)S(1)}, u32[]{:S(2)}, u32[]{:S(2)}) collective-permute-start(bf16[384,384]{1,0:T(8,128)(2,1)} %collective-permute-done.45.refs_1_), channel_id=1, source_target_pairs={{0,1},{1,0},{2,3},{3,2},{4,5},{5,4},{6,7},{7,6},{8,9},{9,8},{10,11... | collective-permute-start | bytes 884744 | tf_op jit(solution)/shard_map/ppermute | solution.py:974
  234.5 3.0 %collective-permute-start.52 = (bf16[384,384]{1,0:T(8,128)(2,1)S(1)}, bf16[384,384]{1,0:T(8,128)(2,1)S(1)}, u32[]{:S(2)}, u32[]{:S(2)}) collective-permute-start(bf16[384,384]{1,0:T(8,128)(2,1)S(1)} %broadcast_select_fusion.3.refs_2_), channel_id=1, source_target_pairs={{0,1},{1,0},{2,3},{3,2},{4,5},{5,4},{6,7},{7,6},{8,9},{9,8},{10,11... | collective-permute-start | bytes 884744 | tf_op jit(solution)/shard_map/ppermute | solution.py:974
  235.8 1.7 collective-permute-start.53
  235.9 14.8 %collective-permute-start.37 = (bf16[352,384]{1,0:T(8,128)(2,1)S(1)}, bf16[352,384]{1,0:T(8,128)(2,1)S(1)}, u32[]{:S(2)}, u32[]{:S(2)}) collective-permute-start(bf16[352,384]{1,0:T(8,128)(2,1)S(1)} %pad_maximum_fusion.6), channel_id=1, source_target_pairs={{2,0},{3,1},{4,6},{5,7},{10,8},{11,9},{12,14},{13,15},{18,16},{19,... | collective-permute-start | bytes 811016 | tf_op jit(solution)/shard_map/ppermute | solution.py:978
  243.2 11.9 %collective-permute-start.38 = (bf16[160,384]{1,0:T(8,128)(2,1)S(1)}, bf16[160,384]{1,0:T(8,128)(2,1)S(1)}, u32[]{:S(2)}, u32[]{:S(2)}) collective-permute-start(bf16[160,384]{1,0:T(8,128)(2,1)S(1)} %slice.118.refs_0_), channel_id=1, source_target_pairs={{0,1},{1,0},{2,3},{3,2},{4,5},{5,4},{6,7},{7,6},{8,9},{9,8},{10,11... | collective-permute-start | bytes 368648 | tf_op jit(solution)/shard_map/ppermute | solution.py:974
  243.8 11.3 %collective-permute-start.39 = (bf16[160,384]{1,0:T(8,128)(2,1)S(1)}, bf16[160,384]{1,0:T(8,128)(2,1)S(1)}, u32[]{:S(2)}, u32[]{:S(2)}) collective-permute-start(bf16[160,384]{1,0:T(8,128)(2,1)S(1)} %slice.140.refs_1_), channel_id=1, source_target_pairs={{0,1},{1,0},{2,3},{3,2},{4,5},{5,4},{6,7},{7,6},{8,9},{9,8},{10,11... | collective-permute-start | bytes 368648 | tf_op jit(solution)/shard_map/ppermute | solution.py:974
  247.0 5.8 %collective-permute-start.36 = (f32[128,768]{1,0:T(8,128)}, f32[128,768]{1,0:T(8,128)S(1)}, u32[]{:S(2)}, u32[]{:S(2)}) collective-permute-start(f32[128,768]{1,0:T(8,128)} %get-tuple-element.198), channel_id=1, source_target_pairs={{0,1},{1,0},{2,3},{3,2},{4,5},{5,4},{6,7},{7,6},{8,9},{9,8},{10,11... | collective-permute-start | bytes 1179656 | tf_op jit(solution)/shard_map/ppermute | solution.py:974
  250.7 3.0 %collective-permute-start.41 = (bf16[352,384]{1,0:T(8,128)(2,1)S(1)}, bf16[352,384]{1,0:T(8,128)(2,1)S(1)}, u32[]{:S(2)}, u32[]{:S(2)}) collective-permute-start(bf16[352,384]{1,0:T(8,128)(2,1)S(1)} %broadcast_select_fusion.4), channel_id=1, source_target_pairs={{0,1},{1,0},{2,3},{3,2},{4,5},{5,4},{6,7},{7,6},{8,9},{9,8},{10,11... | collective-permute-start | bytes 811016 | tf_op jit(solution)/shard_map/ppermute | solution.py:974
  250.8 4.2 %collective-permute-start.40 = (bf16[160,384]{1,0:T(8,128)(2,1)S(1)}, bf16[160,384]{1,0:T(8,128)(2,1)S(1)}, u32[]{:S(2)}, u32[]{:S(2)}) collective-permute-start(bf16[160,384]{1,0:T(8,128)(2,1)S(1)} %broadcast_select_fusion.5.refs_2_), channel_id=1, source_target_pairs={{0,1},{1,0},{2,3},{3,2},{4,5},{5,4},{6,7},{7,6},{8,9},{9,8},{10,11... | collective-permute-start | bytes 368648 | tf_op jit(solution)/shard_map/ppermute | solution.py:974
  (42 other events, 163.0 us)
Sparse Core Ops, SparseCore 0:
  122.6 39.6 reduce-scatter.1
